TPU v7x, 32 devices: a whole 2x2x4 slice. The times are simulated.
32 devices in a mesh: img: 16 (over z, y, x), row: 2 (over core).
Axes of the slice: x: 2, y: 2, z: 4, core: 2. Of those that a mesh axis runs over, the one named last changes fastest.
Arguments:
- features: bfloat16 [32, 32, 32, 512], P('img', 'row'), may hold values from -6 to 6
- validity: int32 [32, 32, 32], P('img', 'row'), may hold values from 0 to 1, as said below
- upstream: bfloat16 [32, 32, 32, 512], P('img', 'row'), may hold values from -6 to 6
- normgain: bfloat16 [512], replicated, may hold values from 0.25 to 1.75
- normshift: bfloat16 [512], replicated, may hold values from -1.75 to 1.75
- inweight: bfloat16 [512, 1024], P(('img', 'row')), may hold values from -0.25 to 0.25
- inbias: bfloat16 [1024], replicated, may hold values from -1.75 to 1.75
- dwkernel: bfloat16 [7, 7, 992], replicated, may hold values from -2.5 to 2.5
- dwbias: bfloat16 [992], replicated, may hold values from -3 to 3
- gatefirst: bfloat16 [32, 64], replicated, may hold values from -1 to 1
- gatesecond: bfloat16 [64, 128], replicated, may hold values from -0.75 to 0.75
- gatethird: bfloat16 [128, 256], replicated, may hold values from -0.5 to 0.5
- gatefourth: bfloat16 [256, 512], replicated, may hold values from -0.375 to 0.375
- gatebias: bfloat16 [960], replicated, may hold values from -1.75 to 1.75
- outweight: bfloat16 [512, 512], P(('img', 'row')), may hold values from -0.25 to 0.25
- outbias: bfloat16 [512], replicated, may hold values from -1.75 to 1.75
- mixscale: bfloat16 [512], replicated, may hold values from 0.5 to 2
- mlpgain: bfloat16 [512], replicated, may hold values from 0.25 to 1.75
- mlpshift: bfloat16 [512], replicated, may hold values from -1.75 to 1.75
- expandweight: bfloat16 [512, 2048], P(('img', 'row')), may hold values from -0.25 to 0.25
- expandbias: bfloat16 [2048], replicated, may hold values from -1.75 to 1.75
- reduceweight: bfloat16 [2048, 512], P(('img', 'row')), may hold values from -0.125 to 0.125
- reducebias: bfloat16 [512], replicated, may hold values from -1.75 to 1.75
- mlpscale: bfloat16 [512], replicated, may hold values from 0.5 to 2
Outputs:
- produced: bfloat16 [32, 32, 32, 512], P('img', 'row')
- features_grad: bfloat16 [32, 32, 32, 512], P('img', 'row')
- normgain_grad: float32 [512], replicated
- normshift_grad: float32 [512], replicated
- inweight_grad: float32 [512, 1024], P(('img', 'row'))
- inbias_grad: float32 [1024], replicated
- dwkernel_grad: float32 [7, 7, 992], replicated
- dwbias_grad: float32 [992], replicated
- gatefirst_grad: float32 [32, 64], replicated
- gatesecond_grad: float32 [64, 128], replicated
- gatethird_grad: float32 [128, 256], replicated
- gatefourth_grad: float32 [256, 512], replicated
- gatebias_grad: float32 [960], replicated
- outweight_grad: float32 [512, 512], P(('img', 'row'))
- outbias_grad: float32 [512], replicated
- mixscale_grad: float32 [512], replicated
- mlpgain_grad: float32 [512], replicated
- mlpshift_grad: float32 [512], replicated
- expandweight_grad: float32 [512, 2048], P(('img', 'row'))
- expandbias_grad: float32 [2048], replicated
- reduceweight_grad: float32 [2048, 512], P(('img', 'row'))
- reducebias_grad: float32 [512], replicated
- mlpscale_grad: float32 [512], replicated
Inputs may be any that keep to these rules, and one draw needn't show every extreme that they name: `validity`: in every image the pixels marked 1 form one rectangle at the top-left corner of the grid, more than 16 rows high.
All inputs are finite; a program needn't handle non-finite values.
Results may differ from a plain program's by a relative error of at most 0.015.
Values may be sent and summed in bfloat16 or wider, within the bound.
No kernel may reach another device: no remote copies, remote signals or barrier semaphores. Data moves between devices by JAX's collectives and lax.ppermute only.
A program may use at most 320 MiB of HBM per device.

v0:
```python
import functools
import math

import jax
import jax.numpy as jnp
from jax import lax
from jax.experimental import pallas as pl
from jax.experimental.pallas import tpu as pltpu
from jax.sharding import PartitionSpec as P

f32 = jnp.float32
bf16 = jnp.bfloat16
i32 = jnp.int32
norm_eps = 1e-06
conv_scale = 1.0 / 3.0
inv_root_two = 1.0 / math.sqrt(2.0)
inv_root_tau = 1.0 / math.sqrt(2.0 * math.pi)
vmem_bytes = 60 * 1024 * 1024


def dot(left, right):
    return jnp.dot(left, right, preferred_element_type=f32)


def dot_tn(left, right):
    return lax.dot_general(left, right, (((0,), (0,)), ((), ())), preferred_element_type=f32)


def dot_nt(left, right):
    return lax.dot_general(left, right, (((1,), (1,)), ((), ())), preferred_element_type=f32)


def column_sum(values):
    return jnp.sum(values, axis=0, keepdims=True)


def permutation():
    out = lax.broadcasted_iota(i32, (256, 256), 0)
    src = lax.broadcasted_iota(i32, (256, 256), 1)
    row_par, col_par = out >> 7, (out >> 6) & 1
    pair, ccp, img, blk = (out >> 5) & 1, (out >> 4) & 1, (out >> 3) & 1, out & 7
    want = img * 128 + (2 * pair + row_par) * 32 + 4 * blk + 2 * ccp + col_par
    return (src == want).astype(f32).astype(bf16)


def normalize(values):
    center = jnp.mean(values, axis=-1, keepdims=True)
    shifted = values - center
    spread = jnp.mean(shifted * shifted, axis=-1, keepdims=True)
    inverse = lax.rsqrt(spread + norm_eps)
    return shifted * inverse, inverse


def norm_backward(grad_norm, normed, inverse, gain):
    scaled = grad_norm * gain
    return inverse * (
        scaled
        - jnp.mean(scaled, axis=-1, keepdims=True)
        - normed * jnp.mean(scaled * normed, axis=-1, keepdims=True)
    )


def extents(valid_ref):
    heights = [sum(valid_ref[16 * n + r, 0] for r in range(16)) for n in range(2)]
    widths = [sum(valid_ref[16 * n, c] for c in range(32)) for n in range(2)]
    return heights, widths


def chunk_mask(sizes, row_par, col_par, count=256, first_row=0):
    (high_a, high_b), (wide_a, wide_b) = sizes
    at = lax.broadcasted_iota(i32, (count, 1), 0)
    pair, ccp, img, blk = at >> 5, (at >> 4) & 1, (at >> 3) & 1, at & 7
    row = 2 * pair + row_par + first_row
    col = 4 * blk + 2 * ccp + col_par
    high = jnp.where(img == 1, high_b, high_a)
    wide = jnp.where(img == 1, wide_b, wide_a)
    return jnp.where((row < high) & (col < wide), 1.0, 0.0).astype(f32)


def halo_sizes(valid_ref, halo_ref):
    heights, widths = extents(valid_ref)
    below, _ = extents(halo_ref)
    upper = lax.axis_index("row") == 0
    return [jnp.where(upper, h, 4) for h in below], widths


def halo_base():
    return jnp.where(lax.axis_index("row") == 0, 8, -2).astype(i32)


def vectors_kernel(in_ref, dw_ref, gate_ref, exp_ref, *rest):
    small, out_ref = rest[:8], rest[8]

    def line(ref):
        return ref[...].astype(f32).reshape(1, ref.shape[0])

    out_ref[0:1] = line(in_ref)
    out_ref[1:2, 0:32] = jnp.zeros((1, 32), f32)
    out_ref[1:2, 32:1024] = line(dw_ref)
    out_ref[2:3, 0:64] = jnp.zeros((1, 64), f32)
    out_ref[2:3, 64:1024] = line(gate_ref)
    wide = line(exp_ref)
    out_ref[3:4] = wide[:, 0:1024]
    out_ref[4:5] = wide[:, 1024:2048]
    for k, ref in enumerate(small):
        out_ref[5 + k // 2 : 6 + k // 2, k % 2 * 512 : k % 2 * 512 + 512] = line(ref)


def gather_vectors(large, small, deps=()):
    vmem = pl.BlockSpec(memory_space=pltpu.VMEM)
    return launch(
        deps,
        vectors_kernel,
        out_shape=jax.ShapeDtypeStruct((9, 1024), f32),
        in_specs=[vmem] * 12,
        out_specs=vmem,
        cost_estimate=takes(1),
        name="vectors",
    )(*large, *small)


def prepare_kernel(valid_ref, halo_valid_ref, x_ref, xh_ref, g_ref, vec_ref, xp_ref, gp_ref, y1_ref, y1h_ref):
    perm = permutation()
    gain, shift = vec_ref[8:9, 0:512], vec_ref[8:9, 512:1024]
    own, halo = extents(valid_ref), halo_sizes(valid_ref, halo_valid_ref)
    start = pl.multiple_of(lax.axis_index("row") * 384, 128)
    for b in range(5):
        if b == 4:
            rows = pl.ds(start, 128)
            block = jnp.concatenate([xh_ref[0, rows], xh_ref[1, rows]], axis=0)
        else:
            rows = slice(b * 128, (b + 1) * 128)
            block = jnp.concatenate([x_ref[0, rows], x_ref[1, rows]], axis=0)
            gblock = dot(perm, jnp.concatenate([g_ref[0, rows], g_ref[1, rows]], axis=0)).astype(bf16)
        block = dot(perm, block)
        lowered = block.astype(bf16)
        normed, _ = normalize(block)
        value = normed * gain + shift
        for q in range(4):
            part = slice(q * 64, (q + 1) * 64)
            if b == 4:
                y1h_ref[q] = (chunk_mask(halo, q // 2, q % 2, 64) * value[part]).astype(bf16)
            else:
                dest = slice(b * 64, (b + 1) * 64)
                xp_ref[q, dest] = lowered[part]
                gp_ref[q, dest] = gblock[part]
                y1_ref[q, dest] = (chunk_mask(own, q // 2, q % 2, 64, 4 * b) * value[part]).astype(bf16)


def whole(shape):
    return pl.BlockSpec(shape, lambda *_: (0,) * len(shape))


SMEM = pl.BlockSpec(memory_space=pltpu.SMEM)


def params():
    return pltpu.CompilerParams(vmem_limit_bytes=vmem_bytes)


def takes(micros):
    return pl.CostEstimate(flops=int(micros * 1.0e9), bytes_accessed=0, transcendentals=0)


def launch(deps, kernel, *, out_shape, in_specs, out_specs, **rest):
    single = not isinstance(out_shape, tuple)
    shapes = (out_shape,) if single else out_shape
    specs = (out_specs,) if single else out_specs
    anywhere = pl.BlockSpec(memory_space=pl.ANY)
    count = len(in_specs)

    def body(*refs):
        at = count + len(deps)
        kernel(*refs[:count], *refs[at : at + len(shapes)], *refs[at + len(shapes) + 1 :])

    call = pl.pallas_call(
        body,
        out_shape=(*shapes, jax.ShapeDtypeStruct((8, 128), f32)),
        in_specs=list(in_specs) + [anywhere] * len(deps),
        out_specs=(*specs, anywhere),
        compiler_params=params(),
        **rest,
    )
    return lambda *args: call(*args, *deps)


def own_number(dealt):
    return lax.axis_index("img") * 2 + lax.axis_index("row") if dealt else 0


def place_rows(scratch, refs, order, number, rows):
    each = 32 // len(refs)
    for k, ref in enumerate(refs):
        for b in range(each):
            at = pl.multiple_of((order[k * each + b] ^ number) * rows, 16)
            scratch[pl.ds(at, rows), :] = ref[b * rows : (b + 1) * rows, :]


def dealt_owner(place, order):
    if order == "none":
        return place
    if order == "plain":
        return (2 * (place % 16) + place // 16) ^ lax.axis_index("row")
    return (2 * masks_of(order)[place % 16] + place // 16) ^ own_number(True)


def deal_rows(outs, lead, value_ref, order, rows):
    for p in range(32):
        at = pl.multiple_of(dealt_owner(p, order) * rows, 16)
        outs[p // 16][(slice(p % 16 * rows, (p % 16 + 1) * rows),) + lead] = value_ref[pl.ds(at, rows), :].astype(bf16)


def prepare(valid, halo_valid, x, xh, g, wide, deps=()):
    vmem = pl.BlockSpec(memory_space=pltpu.VMEM)
    return launch(
        deps,
        prepare_kernel,
        out_shape=(
            jax.ShapeDtypeStruct((4, 256, 512), bf16),
            jax.ShapeDtypeStruct((4, 256, 512), bf16),
            jax.ShapeDtypeStruct((4, 256, 512), bf16),
            jax.ShapeDtypeStruct((4, 64, 512), bf16),
        ),
        in_specs=[SMEM] * 2 + [vmem] * 4,
        out_specs=(vmem,) * 4,
        cost_estimate=takes(4),
        name="prepare",
    )(valid, halo_valid, x, xh, g, wide)


def low_lanes(shape):
    return lax.broadcasted_iota(i32, shape, len(shape) - 1) < 64


def swap_lanes(value):
    return pltpu.roll(value, 64, axis=1)


def shifted_block(value, step):
    if step == 0:
        return value
    blk = lax.broadcasted_iota(i32, value.shape, 1)
    if step > 0:
        return jnp.where(blk < 7, pltpu.roll(value, 7, axis=1), 0.0)
    return jnp.where(blk > 0, pltpu.roll(value, 1, axis=1), 0.0)


ODD = ((-1, 0), (-1, 1), (0, 0), (0, 1), (1, 0))
EVEN = ((-1, 1), (0, 0), (0, 1), (1, 0), (1, 1))


def lane_pairs(chunks):
    res = {}
    for row_par in range(2):
        odd, even = chunks[2 * row_par + 1], chunks[2 * row_par]
        odd_s, even_s = swap_lanes(odd), swap_lanes(even)
        res[row_par, 0] = (odd, even_s)
        res[row_par, 1] = (odd_s, even)
    return res


def fill_band(ref, lead, pairs, n, start, row_par):
    odd, even = (v.reshape(n, 2, 2, 8, 128) for v in pairs)
    half = 1 - row_par
    lanes = slice(half * 128, half * 128 + 128)
    low = low_lanes((n * 2, 8, 128))
    cache = {}

    def take(name, value, step, ccp):
        if (name, step, ccp) not in cache:
            cache[name, step, ccp] = shifted_block(value[:, ccp].reshape(n * 2, 8, 128), step)
        return cache[name, step, ccp]

    for k in range(5):
        both = jnp.where(low, take("o", odd, *ODD[k]), take("e", even, *EVEN[k]))
        ref[lead + (pl.ds(start, n), k, slice(None), lanes)] = both.reshape(n, 16, 128).astype(bf16)


def fill_group(ref, lead, own, halo, base):
    other = 6 - base
    for row_par in range(2):
        first = 2 + row_par
        half = 1 - row_par
        fill_band(ref, lead, own[row_par], 8, first, row_par)
        fill_band(ref, lead, halo[row_par], 2, base + first, row_par)
        ref[lead + (pl.ds(other + first, 2), slice(None), slice(None), slice(half * 128, half * 128 + 128))] = jnp.zeros(
            (2, 5, 16, 128), bf16
        )


def diagonal(rows):
    return (lax.broadcasted_iota(i32, (rows, 128), 0) % 64) == (lax.broadcasted_iota(i32, (rows, 128), 1) % 64)


def build_weights(w_ref, slot, tap_ref, group, flip=False):
    mask = diagonal(64)
    low = low_lanes((1, 128))
    tile, side = group // 2, group % 2
    cols = slice(tile * 128, tile * 128 + 128)
    for i in range(7):
        rows = tap_ref[6 - i if flip else i, :, cols]
        turned = swap_lanes(rows)
        first, second = (rows, turned) if side == 0 else (turned, rows)
        for jj in range(8):
            a, b = (6 - jj, 7 - jj) if flip else (jj, jj - 1)
            left = first[a : a + 1] if 0 <= a <= 6 else jnp.zeros((1, 128), f32)
            right = second[b : b + 1] if 0 <= b <= 6 else jnp.zeros((1, 128), f32)
            vector = jnp.where(low, left, right)
            block = jnp.where(mask, jnp.broadcast_to(vector, (64, 128)), 0.0).astype(bf16)
            for out_par in range(2):
                top = i + out_par
                ti, rp, tj, cp = top // 2, top % 2, jj // 2, jj % 2
                at = (rp * 2 + cp) * 64
                w_ref[slot, ti * 4 + tj, at : at + 64, out_par * 128 : out_par * 128 + 128] = block


def clear_weights(w_ref):
    for slot in range(2):
        for tj in range(4):
            w_ref[slot, tj, 0:128, 128:256] = jnp.zeros((128, 128), bf16)
            w_ref[slot, 12 + tj, 128:256, 0:128] = jnp.zeros((128, 128), bf16)


def band_block(ref, lead, ti, tj):
    return ref[lead + (slice(1 + ti, 9 + ti), slice(tj, tj + 2))].reshape(256, 256)


def convolve(ref, lead, w_ref, slot):
    total = None
    for ti in range(4):
        for tj in range(4):
            part = dot(band_block(ref, lead, ti, tj), w_ref[slot, ti * 4 + tj])
            total = part if total is None else total + part
    return total


def split_lanes(low_group, high_group):
    low = low_lanes((256, 128))
    chunks = []
    for rp in range(2):
        lg = low_group[:, rp * 128 : rp * 128 + 128]
        hg = high_group[:, rp * 128 : rp * 128 + 128]
        chunks.append(jnp.where(low, lg, swap_lanes(hg)))
        chunks.append(jnp.where(low, swap_lanes(lg), hg))
    return chunks


def forward_kernel(valid_ref, halo_valid_ref, y1_ref, y1h_ref, *rest, order, dealt):
    weights, (wide_ref, tap_ref, d_ref, band_ref, j0_ref, w_ref, win_ref) = rest[:8], rest[8:]
    step = pl.program_id(0)

    @pl.when(step == 0)
    def _():
        clear_weights(w_ref)

    base = halo_base()
    sizes, around = extents(valid_ref), halo_sizes(valid_ref, halo_valid_ref)
    place_rows(win_ref, weights, order, own_number(dealt), 16)
    weight = win_ref[...]
    bias = wide_ref[0:1]
    joined = [dot(y1_ref[q], weight) + bias for q in range(4)]

    @pl.when(step == 0)
    def _():
        for q in range(4):
            j0_ref[q] = joined[q][:, 0:128]

    own, halo = [], []
    for q in range(4):
        own.append((joined[q] * chunk_mask(sizes, q // 2, q % 2)).astype(bf16).astype(f32))
        part = dot(y1h_ref[q], weight) + bias
        halo.append((part * chunk_mask(around, q // 2, q % 2, 64)).astype(bf16).astype(f32))
    for tile in range(2):
        cols = slice(tile * 128, tile * 128 + 128)
        own_pairs = lane_pairs([v[:, cols] for v in own])
        halo_pairs = lane_pairs([v[:, cols] for v in halo])
        sums = []
        for side in range(2):
            group = tile * 2 + side
            fill_group(
                band_ref,
                (group,),
                [own_pairs[rp, side] for rp in range(2)],
                [halo_pairs[rp, side] for rp in range(2)],
                base,
            )
            build_weights(w_ref, side, tap_ref, group)
            sums.append(convolve(band_ref, (group,), w_ref, side))
        for q, value in enumerate(split_lanes(*sums)):
            d_ref[q, :, cols] = (value + wide_ref[1:2, cols]) * conv_scale


def forward(valid, halo_valid, y1, y1h, w_in, wide, taps, order, dealt, deps=()):
    return launch(
        deps,
        functools.partial(forward_kernel, order=order, dealt=dealt),
        grid=(4,),
        out_shape=(
            jax.ShapeDtypeStruct((4, 256, 1024), f32),
            jax.ShapeDtypeStruct((16, 13, 5, 16, 256), bf16),
            jax.ShapeDtypeStruct((4, 256, 128), f32),
        ),
        in_specs=[SMEM, SMEM, whole((4, 256, 512)), whole((4, 64, 512))]
        + [pl.BlockSpec((64, 256), lambda t: (0, t))] * 8
        + [pl.BlockSpec((9, 256), lambda t: (0, t)), pl.BlockSpec((7, 7, 256), lambda t: (0, 0, t))],
        out_specs=(
            pl.BlockSpec((4, 256, 256), lambda t: (0, 0, t)),
            pl.BlockSpec((4, 13, 5, 16, 256), lambda t: (t, 0, 0, 0, 0)),
            whole((4, 256, 128)),
        ),
        scratch_shapes=[pltpu.VMEM((2, 16, 256, 256), bf16), pltpu.VMEM((512, 256), bf16)],
        cost_estimate=takes(24),
        name="forward",
    )(valid, halo_valid, y1, y1h, *w_in, wide, taps)


def middle_kernel(
    valid_ref,
    d_ref,
    j0_ref,
    xp_ref,
    gp_ref,
    oa,
    ob,
    oc,
    od,
    ea,
    eb4,
    ec,
    ed,
    ra,
    rb,
    first_ref,
    second_ref,
    g3_ref,
    g4_ref,
    wide_ref,
    out_ref,
    act_ref,
    dh_ref,
    y2_ref,
    df_ref,
    dz_ref,
    u_ref,
    dv_ref,
    dd_ref,
    dx2_ref,
    s512_ref,
    s2048_ref,
    s1024_ref,
    held_ref,
    w_out_ref,
    w_exp_ref,
    w_red_ref,
    g1_ref,
    g2_ref,
    *,
    order,
    dealt,
):
    q = pl.program_id(0)
    mask = chunk_mask(extents(valid_ref), q // 2, q % 2)
    out_bias, mix, gain, shift, red_bias, ffn = (
        wide_ref[5 + k // 2 : 6 + k // 2, k % 2 * 512 : k % 2 * 512 + 512] for k in range(6)
    )
    lane = lax.broadcasted_iota(i32, (256, 128), 1)
    is0 = (lane >= 32) & (lane < 64)
    is1 = lane >= 64

    @pl.when(q == 0)
    def _():
        s512_ref[...] = jnp.zeros_like(s512_ref)
        s2048_ref[...] = jnp.zeros_like(s2048_ref)
        s1024_ref[...] = jnp.zeros_like(s1024_ref)
        g1_ref[...] = jnp.zeros_like(g1_ref)
        g2_ref[...] = jnp.zeros_like(g2_ref)
        g1_ref[32:64, 64:128] = first_ref[...]
        g2_ref[64:128] = second_ref[...]
        number = own_number(dealt)
        place_rows(w_out_ref, (oa, ob, oc, od), order, number, 16)
        place_rows(w_exp_ref, (ea, eb4, ec, ed), order, number, 16)
        for p in range(32):
            at = pl.multiple_of(dealt_owner(p, "plain" if dealt else "none") * 64, 64)
            w_red_ref[pl.ds(at, 64), :] = (ra, rb)[p // 16][p % 16 * 64 : (p % 16 + 1) * 64, :]

    d01, d2, d3, d4 = d_ref[:, 0:128], d_ref[:, 128:256], d_ref[:, 256:512], d_ref[:, 512:1024]
    pointwise = pltpu.roll(j0_ref[...], 32, axis=1)
    u0 = jnp.where(is0, pointwise * d01, 0.0).astype(bf16)
    v1 = dot(u0, g1_ref[...]) + wide_ref[2:3, 0:128]
    u1 = jnp.where(is1, v1 * d01, 0.0).astype(bf16)
    v2 = dot(u1, g2_ref[...]) + wide_ref[2:3, 128:256]
    u2 = (v2 * d2).astype(bf16)
    v3 = dot(u2, g3_ref[...]) + wide_ref[2:3, 256:512]
    u3 = (v3 * d3).astype(bf16)
    v4 = dot(u3, g4_ref[...]) + wide_ref[2:3, 512:1024]
    u4 = (v4 * d4).astype(bf16)
    u_ref[:, 0:128] = jnp.where(is1, u1, u0)
    u_ref[:, 128:256] = u2
    u_ref[:, 256:512] = u3
    u_ref[:, 512:1024] = u4
    branch = dot(u4, w_out_ref[...]) + out_bias
    middle = xp_ref[...].astype(f32) + mask * mix * branch
    normed, inverse = normalize(middle)
    y2 = (mask * (normed * gain + shift)).astype(bf16)
    y2_ref[...] = y2
    grad = gp_ref[...].astype(f32)
    df = (mask * ffn * grad).astype(bf16)
    df_ref[...] = df
    reduced = red_bias
    back = jnp.zeros((256, 512), f32)
    for k in range(4):
        cols = slice(k * 512, (k + 1) * 512)
        hidden = dot(y2, w_exp_ref[:, cols]) + wide_ref[3 + k // 2 : 4 + k // 2, k % 2 * 512 : k % 2 * 512 + 512]
        cdf = 0.5 * (1.0 + lax.erf(hidden * inv_root_two))
        act = (hidden * cdf).astype(bf16)
        act_ref[:, cols] = act
        reduced = reduced + dot(act, w_red_ref[cols, :])
        density = jnp.exp(-0.5 * hidden * hidden) * inv_root_tau
        dh = (dot_nt(df, w_red_ref[cols, :]) * (cdf + hidden * density)).astype(bf16)
        dh_ref[:, cols] = dh
        s2048_ref[:, cols] += column_sum(dh.astype(f32))
        back = back + dot_nt(dh, w_exp_ref[:, cols])
    held_ref[q] = (middle + mask * ffn * reduced).astype(bf16)
    s512_ref[0:1] += column_sum(grad * mask * reduced)
    s512_ref[1:2] += column_sum(df.astype(f32))
    back = mask * back
    s512_ref[2:3] += column_sum(back * normed)
    s512_ref[3:4] += column_sum(back)
    dx2 = grad + norm_backward(back, normed, inverse, gain)
    dx2_ref[...] = dx2
    dz = (mask * mix * dx2).astype(bf16)
    dz_ref[...] = dz
    s512_ref[4:5] += column_sum(dx2 * mask * branch)
    s512_ref[5:6] += column_sum(dz.astype(f32))
    du4 = dot_nt(dz, w_out_ref[...])
    dv4 = (du4 * d4).astype(bf16)
    dd4 = (du4 * v4).astype(bf16)
    du3 = dot_nt(dv4, g4_ref[...])
    dv3 = (du3 * d3).astype(bf16)
    dd3 = (du3 * v3).astype(bf16)
    du2 = dot_nt(dv3, g3_ref[...])
    dv2 = (du2 * d2).astype(bf16)
    dd2 = (du2 * v2).astype(bf16)
    du1 = dot_nt(dv2, g2_ref[...])
    dv1 = (du1 * d01).astype(bf16)
    du0 = dot_nt(dv1, g1_ref[...])
    dpw = pltpu.roll(du0 * d01, 96, axis=1)
    dd01 = jnp.where(is1, du1 * v1, jnp.where(is0, du0 * pointwise, dpw)).astype(bf16)
    dv_ref[:, 0:128] = dv1
    dv_ref[:, 128:256] = dv2
    dv_ref[:, 256:512] = dv3
    dv_ref[:, 512:1024] = dv4
    dd_ref[:, 0:128] = dd01
    dd_ref[:, 128:256] = dd2
    dd_ref[:, 256:512] = dd3
    dd_ref[:, 512:1024] = dd4
    for k, ref in enumerate((dv_ref, dd_ref)):
        s1024_ref[k : k + 1] += column_sum(ref[...].astype(f32))

    @pl.when(q == 3)
    def _():
        unpermute(held_ref, out_ref)


def unpermute(held_ref, out_ref):
    perm = permutation()
    for b in range(4):
        block = jnp.concatenate([held_ref[k, b * 64 : (b + 1) * 64] for k in range(4)], axis=0)
        block = dot_tn(perm, block).astype(bf16)
        out_ref[0, b * 128 : (b + 1) * 128] = block[0:128]
        out_ref[1, b * 128 : (b + 1) * 128] = block[128:256]


def middle_call(valid, d, j0, xp, gp, w_exp, w_red, g1, g2, g3, g4, wide, order, dealt, deps=()):
    def chunk(width):
        return pl.BlockSpec((None, 256, width), lambda q: (q, 0, 0))

    def out(width, dtype=bf16):
        return jax.ShapeDtypeStruct((4, 256, width), dtype)

    widths = (2048, 2048, 512, 512, 512, 1024, 1024, 1024)
    return launch(
        deps,
        functools.partial(middle_kernel, order=order, dealt=dealt),
        grid=(4,),
        out_shape=(jax.ShapeDtypeStruct((2, 512, 512), bf16),)
        + tuple(out(w) for w in widths)
        + (
            out(512, f32),
            jax.ShapeDtypeStruct((8, 512), f32),
            jax.ShapeDtypeStruct((1, 2048), f32),
            jax.ShapeDtypeStruct((8, 1024), f32),
        ),
        in_specs=[SMEM, chunk(1024), chunk(128), chunk(512), chunk(512)]
        + [pl.BlockSpec((128, 512), lambda q: (0, 4))] * 4
        + [pl.BlockSpec((128, 2048), lambda q: (0, 0))] * 4
        + [whole((1024, 512))] * 2
        + [whole(v.shape) for v in (g1, g2, g3, g4, wide)],
        out_specs=(whole((2, 512, 512)),)
        + tuple(chunk(w) for w in widths)
        + (chunk(512), whole((8, 512)), whole((1, 2048)), whole((8, 1024))),
        scratch_shapes=[
            pltpu.VMEM((4, 256, 512), bf16),
            pltpu.VMEM((512, 512), bf16),
            pltpu.VMEM((512, 2048), bf16),
            pltpu.VMEM((2048, 512), bf16),
            pltpu.VMEM((128, 128), bf16),
            pltpu.VMEM((128, 128), bf16),
        ],
        cost_estimate=takes(30),
        name="middle",
    )(valid, d, j0, xp, gp, *w_exp, *w_exp, *w_red, g1, g2, g3, g4, wide)


def expand_grad_kernel(y2_ref, dh_ref, keep, send, sum_ref, *, order):
    sum_ref[...] = dot_tn(y2_ref[...], dh_ref[...])
    deal_rows((keep, send), (slice(None),), sum_ref, order, 16)


def expand_grad(y2, dh, order, deps=()):
    return launch(
        deps,
        functools.partial(expand_grad_kernel, order=order),
        grid=(4,),
        out_shape=(jax.ShapeDtypeStruct((256, 2048), bf16),) * 2,
        in_specs=[whole((1024, 512)), pl.BlockSpec((1024, 512), lambda k: (0, k))],
        out_specs=(pl.BlockSpec((256, 512), lambda k: (0, k)),) * 2,
        scratch_shapes=[pltpu.VMEM((512, 512), f32)],
        cost_estimate=takes(5),
        name="expand_grad",
    )(y2, dh)


def reduce_grad_kernel(act_ref, df_ref, u_ref, dz_ref, keep, send, red_ref, out_ref, *, order):
    step = pl.program_id(0)
    red_ref[pl.ds(pl.multiple_of(step * 512, 512), 512), :] = dot_tn(act_ref[...], df_ref[...])

    @pl.when(step == 0)
    def _():
        out_ref[...] = dot_tn(u_ref[...], dz_ref[...])

    @pl.when(step == 3)
    def _():
        for p in range(32):
            owner = dealt_owner(p, order)
            ref, first = (keep, send)[p // 16], p % 16 * 80
            ref[first : first + 64] = red_ref[pl.ds(pl.multiple_of(owner * 64, 64), 64), :].astype(bf16)
            ref[first + 64 : first + 80] = out_ref[pl.ds(pl.multiple_of(owner * 16, 16), 16), :].astype(bf16)


def reduce_grad(act, df, u, dz, order, deps=()):
    return launch(
        deps,
        functools.partial(reduce_grad_kernel, order=order),
        grid=(4,),
        out_shape=(jax.ShapeDtypeStruct((1280, 512), bf16),) * 2,
        in_specs=[
            pl.BlockSpec((1024, 512), lambda k: (0, k)),
            whole((1024, 512)),
            pl.BlockSpec((1024, 512), lambda k: (0, 1)),
            whole((1024, 512)),
        ],
        out_specs=(whole((1280, 512)),) * 2,
        scratch_shapes=[pltpu.VMEM((2048, 512), f32), pltpu.VMEM((512, 512), f32)],
        cost_estimate=takes(6),
        name="reduce_grad",
    )(act, df, u, dz)


def kernel_grad_kernel(dd_ref, band_ref, dk_ref):
    low = low_lanes((256, 128))
    low8 = low_lanes((8, 128))
    wide = diagonal(256)
    for tile in range(2):
        cols = slice(tile * 128, tile * 128 + 128)
        own = [dd_ref[q, :, cols].astype(f32) for q in range(4)]
        turned_own = [swap_lanes(v) for v in own]
        for side in range(2):
            group = tile * 2 + side
            halves = []
            for rp in range(2):
                if side == 0:
                    halves.append(jnp.where(low, own[2 * rp], turned_own[2 * rp + 1]))
                else:
                    halves.append(jnp.where(low, turned_own[2 * rp], own[2 * rp + 1]))
            left = jnp.concatenate(halves, axis=1).astype(bf16)
            rows = {}
            for ti in range(4):
                for tj in range(4):
                    cross = dot_tn(left, band_block(band_ref, (group,), ti, tj))
                    for rp in range(2):
                        half = jnp.where(wide, cross[:, rp * 128 : rp * 128 + 128], 0.0)
                        part = jnp.sum(half.reshape(4, 8, 8, 128), axis=1)
                        for out_rp in range(2):
                            i = 2 * ti + rp - out_rp
                            if 0 <= i <= 6:
                                for out_cp in range(2):
                                    key = (i, tj, out_cp)
                                    term = part[out_rp * 2 + out_cp]
                                    rows[key] = rows[key] + term if key in rows else term
            for i in range(7):
                turned = [swap_lanes(rows[i, tj, 1]) for tj in range(4)] + [jnp.zeros((8, 128), f32)]
                for tj in range(4):
                    value = rows[i, tj, 0] + jnp.where(low8, turned[tj], turned[tj + 1])
                    dk_ref[group, i * 4 + tj : i * 4 + tj + 1] = column_sum(value) * conv_scale
            dk_ref[group, 28:32] = jnp.zeros((4, 128), f32)


def kernel_grad(dd, band, deps=()):
    return launch(
        deps,
        kernel_grad_kernel,
        grid=(4,),
        out_shape=jax.ShapeDtypeStruct((16, 32, 128), f32),
        in_specs=[
            pl.BlockSpec((4, 256, 256), lambda t: (0, 0, t)),
            pl.BlockSpec((4, 13, 5, 16, 256), lambda t: (t, 0, 0, 0, 0)),
        ],
        out_specs=pl.BlockSpec((4, 32, 128), lambda t: (t, 0, 0)),
        cost_estimate=takes(13),
        name="kernel_grad",
    )(dd, band)


def gate_grads_kernel(u_ref, dv_ref, s512_ref, s2048_ref, s1024_ref, dk_ref, keep, send, small_ref, *, order):
    small_ref[0:256] = dot_tn(u_ref[:, 256:512], dv_ref[:, 512:1024])
    g3 = dot_tn(u_ref[:, 128:256], dv_ref[:, 256:512])
    small_ref[256:320, 0:256] = g3[0:64]
    small_ref[256:320, 256:512] = g3[64:128]
    g12 = dot_tn(u_ref[:, 0:128], dv_ref[:, 0:256])
    for k in range(4):
        cols = slice(k * 128, (k + 1) * 128)
        small_ref[320:336, cols] = g12[64 + 16 * k : 80 + 16 * k, 128:256]
        small_ref[336:344, cols] = g12[32 + 8 * k : 40 + 8 * k, 0:128]
        small_ref[384:512, cols] = dk_ref[k * 128 : (k + 1) * 128]
        small_ref[352 + k : 353 + k] = s2048_ref[:, k * 512 : (k + 1) * 512]
        small_ref[356 + k : 357 + k] = s1024_ref[k // 2 : k // 2 + 1, k % 2 * 512 : k % 2 * 512 + 512]
    small_ref[344:352] = s512_ref[...]
    small_ref[360:384] = jnp.zeros((24, 512), f32)
    deal_rows((keep, send), (slice(None),), small_ref, order, 16)


def gate_grads(u, dv, s512, s2048, s1024, dk, order, deps=()):
    return launch(
        deps,
        functools.partial(gate_grads_kernel, order=order),
        grid=(1,),
        out_shape=(jax.ShapeDtypeStruct((256, 512), bf16),) * 2,
        in_specs=[whole((1024, 512))] + [whole(v.shape) for v in (dv, s512, s2048, s1024, dk)],
        out_specs=(whole((256, 512)),) * 2,
        scratch_shapes=[pltpu.VMEM((512, 512), f32)],
        cost_estimate=takes(3),
        name="gate_grads",
    )(u, dv, s512, s2048, s1024, dk)


def unpack_kernel(own_ref, oth_ref, *rest):
    outs, (table_ref, all_ref) = rest[:-2], rest[-2:]
    in_ref, dk_ref, dwb_ref, g1_ref, g2_ref, g3_ref, g4_ref, gb_ref = outs[:8]
    outb_ref, mix_ref, gain_ref, shift_ref, expb_ref, redb_ref, ffn_ref = outs[8:]
    row = lax.axis_index("row")
    total = own_ref[0:16, 0:1024].astype(f32)
    for k in range(1, 16):
        total = total + own_ref[k * 16 : (k + 1) * 16, 0:1024].astype(f32)
    in_ref[...] = total
    for k in range(16):
        block = slice(k * 16, (k + 1) * 16)
        table_ref[pl.ds(pl.multiple_of((2 * k + row) * 16, 16), 16), :] = own_ref[block, 1024:1536]
        table_ref[pl.ds(pl.multiple_of((2 * k + 1 - row) * 16, 16), 16), :] = oth_ref[block, 1024:1536]
    all_ref[...] = table_ref[...].astype(f32)
    g4_ref[...] = all_ref[0:256]
    g3_ref[0:64] = all_ref[256:320, 0:256]
    g3_ref[64:128] = all_ref[256:320, 256:512]
    for k in range(4):
        cols = slice(k * 128, (k + 1) * 128)
        g2_ref[16 * k : 16 * k + 16] = all_ref[320:336, cols]
        g1_ref[8 * k : 8 * k + 8] = swap_lanes(all_ref[336:344, cols])[:, 0:64]
        expb_ref[k * 512 : (k + 1) * 512] = all_ref[352 + k : 353 + k].reshape(512)
    for k, ref in enumerate((ffn_ref, redb_ref, gain_ref, shift_ref, mix_ref, outb_ref)):
        ref[...] = all_ref[344 + k : 345 + k].reshape(512)

    def line(first):
        return jnp.concatenate([all_ref[first : first + 1], all_ref[first + 1 : first + 2]], axis=1)

    gb_ref[...] = line(356)[:, 64:1024].reshape(960)
    dwb_ref[...] = line(358)[:, 32:1024].reshape(992) * conv_scale
    low = low_lanes((32, 128))
    lane = lax.broadcasted_iota(i32, (32, 128), 1)
    rows = []
    for t in range(8):
        cols = slice(t // 2 * 128, t // 2 * 128 + 128)
        first = 384 + t % 2 * 64
        left = all_ref[first : first + 32, cols]
        right = all_ref[first + 32 : first + 64, cols]
        pair = (jnp.where(low, left, swap_lanes(right)), jnp.where(low, swap_lanes(left), right))
        rows.append([pltpu.roll(v, 96, axis=1) for v in pair])
    for t in range(8):
        size = 128 if t < 7 else 96
        for odd in range(2):
            value = jnp.where(lane < 96, rows[t][odd], rows[t + 1][odd]) if t < 7 else rows[t][odd]
            for i in range(7):
                for j in range(odd, 7, 2):
                    at = i * 4 + j // 2
                    dk_ref[i, j : j + 1, t * 128 : t * 128 + size] = value[at : at + 1, 0:size]


def unpack(own, oth, deps=()):
    vmem = pl.BlockSpec(memory_space=pltpu.VMEM)
    shapes = ((16, 1024), (7, 7, 992), (992,), (32, 64), (64, 128), (128, 256), (256, 512), (960,))
    shapes += ((512,),) * 4 + ((2048,), (512,), (512,))
    return launch(
        deps,
        unpack_kernel,
        out_shape=tuple(jax.ShapeDtypeStruct(v, f32) for v in shapes),
        in_specs=[vmem] * 2,
        out_specs=(vmem,) * len(shapes),
        scratch_shapes=[pltpu.VMEM((512, 512), bf16), pltpu.VMEM((512, 512), f32)],
        cost_estimate=takes(3),
        name="unpack",
    )(own, oth)


def conv_back_kernel(valid_ref, dd_ref, ddh_ref, tap_ref, df_ref, w_ref, back_ref, *, offset):
    step = pl.program_id(0)

    @pl.when(step == 0)
    def _():
        clear_weights(w_ref)

    base = halo_base()
    sizes = extents(valid_ref)
    masks = [chunk_mask(sizes, q // 2, q % 2) for q in range(4)]
    lane = lax.broadcasted_iota(i32, (256, 128), 1)
    keep = (lane < 32) & (step == 0)
    for tile in range(2):
        cols = slice(tile * 128, tile * 128 + 128)
        own = [dd_ref[q, :, cols].astype(f32) for q in range(4)]
        own_pairs = lane_pairs(own)
        halo_pairs = lane_pairs([ddh_ref[q, :, cols].astype(f32) for q in range(4)])
        sums = []
        for side in range(2):
            group = tile * 2 + side
            fill_group(
                back_ref,
                (group,),
                [own_pairs[rp, side] for rp in range(2)],
                [halo_pairs[rp, side] for rp in range(2)],
                base,
            )
            build_weights(w_ref, side, tap_ref, group, True)
            sums.append(convolve(back_ref, (group,), w_ref, side))
        for q, value in enumerate(split_lanes(*sums)):
            value = value * (masks[q] * conv_scale)
            if tile == 0 and offset == 0:
                value = jnp.where(keep, own[q], value)
            df_ref[q, :, cols] = value.astype(bf16)


def conv_back(valid, dd, ddh, taps, offset, steps, deps=()):
    return launch(
        deps,
        functools.partial(conv_back_kernel, offset=offset),
        grid=(steps,),
        out_shape=jax.ShapeDtypeStruct((4, 256, 256 * steps), bf16),
        in_specs=[
            SMEM,
            pl.BlockSpec((4, 256, 256), lambda t: (0, 0, t + offset)),
            pl.BlockSpec((4, 64, 256), lambda t: (0, 0, t + offset)),
            pl.BlockSpec((7, 7, 256), lambda t: (0, 0, t + offset)),
        ],
        out_specs=pl.BlockSpec((4, 256, 256), lambda t: (0, 0, t)),
        scratch_shapes=[pltpu.VMEM((2, 16, 256, 256), bf16), pltpu.VMEM((4, 13, 5, 16, 256), bf16)],
        cost_estimate=takes(4.5 * steps),
        name="conv_back",
    )(valid, dd, ddh, taps)


def in_grad_kernel(y1_ref, da_ref, db_ref, keep, send, sum_ref, *, order):
    for k, ref in enumerate((da_ref, db_ref)):
        sum_ref[k] = dot_tn(y1_ref[...], ref[...])
        deal_rows((keep, send), (slice(k * 512, (k + 1) * 512),), sum_ref.at[k], order, 16)


def in_grad(y1, da, db, order, deps=()):
    vmem = pl.BlockSpec(memory_space=pltpu.VMEM)
    return launch(
        deps,
        functools.partial(in_grad_kernel, order=order),
        out_shape=(jax.ShapeDtypeStruct((256, 1024), bf16),) * 2,
        in_specs=[vmem] * 3,
        out_specs=(vmem, vmem),
        scratch_shapes=[pltpu.VMEM((2, 512, 512), f32)],
        cost_estimate=takes(4),
        name="in_grad",
    )(y1, da, db)


def last_kernel(valid_ref, da_ref, db_ref, xp_ref, dx2_ref, *rest, order, dealt):
    weights, (wide_ref, out_ref, late_ref, held_ref, win_ref) = rest[:8], rest[8:]
    q = pl.program_id(0)

    @pl.when(q == 0)
    def _():
        late_ref[...] = jnp.zeros_like(late_ref)
        place_rows(win_ref, weights, order, own_number(dealt), 16)

    mask = chunk_mask(extents(valid_ref), q // 2, q % 2)
    da, db = da_ref[...], db_ref[...]
    late_ref[2:3] += column_sum(da.astype(f32))
    late_ref[3:4] += column_sum(db.astype(f32))
    grad = mask * (dot_nt(da, win_ref[:, 0:512]) + dot_nt(db, win_ref[:, 512:1024]))
    normed, inverse = normalize(xp_ref[...].astype(f32))
    late_ref[0:1] += column_sum(grad * normed)
    late_ref[1:2] += column_sum(grad)
    held_ref[q] = (dx2_ref[...] + norm_backward(grad, normed, inverse, wide_ref[8:9, 0:512])).astype(bf16)

    @pl.when(q == 3)
    def _():
        unpermute(held_ref, out_ref)


def last_call(valid, da, db, xp, dx2, w_in, wide, order, dealt, deps=()):
    def chunk(width):
        return pl.BlockSpec((None, 256, width), lambda q: (q, 0, 0))

    return launch(
        deps,
        functools.partial(last_kernel, order=order, dealt=dealt),
        grid=(4,),
        out_shape=(jax.ShapeDtypeStruct((2, 512, 512), bf16), jax.ShapeDtypeStruct((8, 512), f32)),
        in_specs=[SMEM] + [chunk(512)] * 4 + [whole((64, 1024))] * 8 + [whole(wide.shape)],
        out_specs=(whole((2, 512, 512)), whole((8, 512))),
        scratch_shapes=[pltpu.VMEM((4, 256, 512), bf16), pltpu.VMEM((512, 1024), bf16)],
        cost_estimate=takes(7),
        name="last",
    )(valid, da, db, xp, dx2, *w_in, wide)


def repeat(value):
    rows, cols = value.shape
    return jnp.broadcast_to(value[None], (16, rows, cols)).reshape(16 * rows, cols)


def join_kernel(*refs, counts):
    ins = list(refs[: sum(counts)])
    for out, count in zip(refs[sum(counts) :], counts):
        at = 0
        for _ in range(count):
            ref = ins.pop(0)
            out[at : at + ref.shape[0]] = ref[...]
            at += ref.shape[0]


def join(*lists, deps=()):
    vmem = pl.BlockSpec(memory_space=pltpu.VMEM)
    shapes = [(sum(v.shape[0] for v in group), group[0].shape[1]) for group in lists]
    return launch(
        deps,
        functools.partial(join_kernel, counts=[len(v) for v in lists]),
        out_shape=tuple(jax.ShapeDtypeStruct(v, bf16) for v in shapes),
        in_specs=[vmem] * sum(len(v) for v in lists),
        out_specs=(vmem,) * len(lists),
        cost_estimate=takes(1),
        name="join",
    )(*sum((list(v) for v in lists), []))


def add_kernel(a_ref, b_ref, out_ref):
    out_ref[...] = a_ref[...] + b_ref[...]


def add(a, b, deps=()):
    vmem = pl.BlockSpec(memory_space=pltpu.VMEM)
    return launch(
        deps,
        add_kernel,
        out_shape=jax.ShapeDtypeStruct(a.shape, a.dtype),
        in_specs=[vmem] * 2,
        out_specs=vmem,
        cost_estimate=takes(1),
        name="add",
    )(a, b)


def combine_kernel(*refs, parts):
    count = len(parts)
    ins, outs = refs[: 2 * count], list(refs[2 * count :])
    for k, n in enumerate(parts):
        for part in range(n):
            total = ins[2 * k][part, 0].astype(f32) + ins[2 * k + 1][part, 0].astype(f32)
            outs.pop(0)[0] = total.astype(bf16)


def combine(*items, deps=()):
    steps = next(n for n in (4, 2, 1) if all(v.shape[0] % (16 * n * p) == 0 for v, _, p in items))
    ins, in_specs, outs, out_specs = [], [], [], []
    for keep, got, parts in items:
        rows, cols = keep.shape
        size = rows // parts // steps
        ins += [v.reshape(parts, steps, size, cols) for v in (keep, got)]
        in_specs += [pl.BlockSpec((parts, 1, size, cols), lambda t: (0, t, 0, 0))] * 2
        outs += [jax.ShapeDtypeStruct((steps, size, cols), bf16)] * parts
        out_specs += [pl.BlockSpec((1, size, cols), lambda t: (t, 0, 0))] * parts
    *values, token = launch(
        deps,
        functools.partial(combine_kernel, parts=[p for _, _, p in items]),
        grid=(steps,),
        out_shape=tuple(outs),
        in_specs=in_specs,
        out_specs=tuple(out_specs),
        cost_estimate=takes(2),
        name="combine",
    )(*ins)
    return [v.reshape(-1, v.shape[-1]) for v in values] + [token]


def merge_kernel(ro_a, ro_b, e_a, e_b, keep, send):
    for z in range(4):
        ref, first = (keep, send)[z // 2], z % 2 * 144
        rows = slice(z * 80, (z + 1) * 80)
        ref[first : first + 80] = (ro_a[rows].astype(f32) + ro_b[rows].astype(f32)).astype(bf16)
        total = e_a[z * 16 : (z + 1) * 16].astype(f32) + e_b[z * 16 : (z + 1) * 16].astype(f32)
        for c in range(4):
            at = first + 80 + c * 16
            ref[at : at + 16] = total[:, c * 512 : (c + 1) * 512].astype(bf16)


def merge(ro_a, ro_b, e_a, e_b, deps=()):
    vmem = pl.BlockSpec(memory_space=pltpu.VMEM)
    return launch(
        deps,
        merge_kernel,
        out_shape=(jax.ShapeDtypeStruct((288, 512), bf16),) * 2,
        in_specs=[vmem] * 4,
        out_specs=(vmem,) * 2,
        cost_estimate=takes(2),
        name="merge",
    )(ro_a, ro_b, e_a, e_b)


def finish_kernel(a_ref, b_ref, red_ref, out_ref, exp_ref):
    red_ref[...] = a_ref[0:64].astype(f32) + b_ref[0:64].astype(f32)
    out_ref[...] = a_ref[64:80].astype(f32) + b_ref[64:80].astype(f32)
    for c in range(4):
        rows = slice(80 + c * 16, 96 + c * 16)
        exp_ref[:, c * 512 : (c + 1) * 512] = a_ref[rows].astype(f32) + b_ref[rows].astype(f32)


def finish(a, b, deps=()):
    vmem = pl.BlockSpec(memory_space=pltpu.VMEM)
    shapes = ((64, 512), (16, 512), (16, 2048))
    return launch(
        deps,
        finish_kernel,
        out_shape=tuple(jax.ShapeDtypeStruct(v, f32) for v in shapes),
        in_specs=[vmem] * 2,
        out_specs=(vmem,) * 3,
        cost_estimate=takes(1),
        name="finish",
    )(a, b)


def deal_kernel(i_a, i_b, s_a, s_b, out_ref):
    small = (s_a[...].astype(f32) + s_b[...].astype(f32)).astype(bf16)
    out_ref[:, 0:1024] = (i_a[...].astype(f32) + i_b[...].astype(f32)).astype(bf16)
    for k in range(16):
        out_ref[k * 16 : (k + 1) * 16, 1024:1536] = small


def deal(i_a, i_b, s_a, s_b, deps=()):
    vmem = pl.BlockSpec(memory_space=pltpu.VMEM)
    return launch(
        deps,
        deal_kernel,
        out_shape=jax.ShapeDtypeStruct((256, 1536), bf16),
        in_specs=[vmem] * 4,
        out_specs=vmem,
        cost_estimate=takes(2),
        name="deal",
    )(i_a, i_b, s_a, s_b)


def late_kernel(a_ref, b_ref, gain_ref, shift_ref, bias_ref):
    total = a_ref[...] + b_ref[...]
    gain_ref[...] = total[0:1].reshape(512)
    shift_ref[...] = total[1:2].reshape(512)
    bias_ref[0:512] = total[2:3].reshape(512)
    bias_ref[512:1024] = total[3:4].reshape(512)


def late_sums(a, b, deps=()):
    vmem = pl.BlockSpec(memory_space=pltpu.VMEM)
    return launch(
        deps,
        late_kernel,
        out_shape=tuple(jax.ShapeDtypeStruct((v,), f32) for v in (512, 512, 1024)),
        in_specs=[vmem] * 2,
        out_specs=(vmem,) * 3,
        cost_estimate=takes(1),
        name="late",
    )(a, b)


ROW = "row"


def img_bits():
    return lax.axis_size("img").bit_length() - 1


def swap_img(value, mask):
    return lax.ppermute(value, "img", [(k, k ^ mask) for k in range(lax.axis_size("img"))])


def swap_row(value):
    return lax.ppermute(value, "row", [(0, 1), (1, 0)])


def masks_of(stage):
    masks = [0]
    for bit in stage:
        masks = [m | v for m in masks for v in (0, 1 << bit)]
    return masks


def gather_order(groups):
    rel = [0]
    for bits in groups:
        rel = [m ^ r for m in masks_of(bits) for r in rel]
    return [2 * r + side for side in (0, 1) for r in rel]


def swaps(value, bits):
    return [value] + [swap_img(value, m) for m in masks_of(bits)[1:]]


def after(value, *others):
    return lax.optimization_barrier((value, others))[0]


def spread(value):
    return lax.all_to_all(value, "img", split_axis=0, concat_axis=0, tiled=True)


def sum_all(value):
    value = value + swap_row(value)
    for bit in range(img_bits() - 1):
        value = value + swap_img(value, 1 << bit)
    return value, swap_img(value, 1 << (img_bits() - 1))


def own_bit(bit):
    return lax.axis_index("row") if bit == ROW else (lax.axis_index("img") >> bit) & 1


def swap_bit(value, bit):
    return swap_row(value) if bit == ROW else swap_img(value, 1 << bit)


def plain_gather(shard):
    value = shard
    for bit in [ROW] + list(range(img_bits())):
        other = swap_bit(value, bit)
        mine = own_bit(bit) == 0
        value = jnp.concatenate([jnp.where(mine, value, other), jnp.where(mine, other, value)], axis=0)
    return value


def plain_scatter(value):
    for bit in list(range(img_bits()))[::-1] + [ROW]:
        half = value.shape[0] // 2
        mine = own_bit(bit) == 0
        first, second = value[:half], value[half:]
        sent = swap_bit(jnp.where(mine, second, first).astype(bf16), bit)
        value = jnp.where(mine, first, second).astype(f32) + sent.astype(f32)
    return value


def per_device(
    features,
    validity,
    upstream,
    normgain,
    normshift,
    inweight,
    inbias,
    dwkernel,
    dwbias,
    gatefirst,
    gatesecond,
    gatethird,
    gatefourth,
    gatebias,
    outweight,
    outbias,
    mixscale,
    mlpgain,
    mlpshift,
    expandweight,
    expandbias,
    reduceweight,
    reducebias,
    mlpscale,
):
    bits = img_bits()
    dealt = bits == 4
    lower = lax.axis_index("row") == 1

    x = features.reshape(2, 512, 512)
    g = upstream.reshape(2, 512, 512)
    valid = validity.reshape(32, 32)
    x_halo = swap_row(x)
    halo_valid = swap_row(valid)
    taps = jnp.pad(dwkernel.astype(f32), ((0, 0), (0, 0), (32, 0)))
    wide, token = gather_vectors(
        (inbias, dwbias, gatebias, expandbias),
        (outbias, mixscale, mlpgain, mlpshift, reducebias, mlpscale, normgain, normshift),
    )
    exp_out = jnp.concatenate([expandweight, outweight], axis=1)
    deep, flat_pair = (3, 2), (1, 0)
    if dealt:
        in_order = gather_order((deep, flat_pair))
        exp_order = gather_order((deep, (1,), (0,)))
        in_z, token = join(swaps(inweight, deep))
        exp_parts = swaps(exp_out, deep)
        red_own = spread(repeat(reduceweight))
        w_in = swaps(in_z, flat_pair)
        xp, gp, y1, y1h, token = prepare(valid, halo_valid, x, x_halo, g, wide, [token])
        exp_z, token = join(exp_parts, deps=[token] + w_in[1:])
        w_in = w_in + [swap_row(v) for v in w_in]
        exp_y, token = join(swaps(exp_z, (1,)), deps=[token])
        w_exp = swaps(exp_y, (0,))
        d, band, j0, token = forward(
            valid, halo_valid, y1, y1h, w_in, wide, taps, in_order, dealt, [token]
        )
        w_exp = w_exp + [swap_row(w_exp[0]), swap_row(after(w_exp[1], d))]
        w_red = [red_own, swap_row(after(red_own, d))]
    else:
        in_order = exp_order = list(range(32))
        w_in = jnp.split(plain_gather(inweight), 8, axis=0)
        w_exp = jnp.split(plain_gather(exp_out), 4, axis=0)
        w_red = jnp.split(plain_gather(reduceweight), 2, axis=0)
        xp, gp, y1, y1h, token = prepare(valid, halo_valid, x, x_halo, g, wide)
        d, band, j0, token = forward(valid, halo_valid, y1, y1h, w_in, wide, taps, in_order, dealt)
    (produced, act, dh, y2, df, dz, u, dv, dd, dx2, s512, s2048, s1024, token) = middle_call(
        valid, d, j0, xp, gp, w_exp, w_red, gatefirst, gatesecond, gatethird, gatefourth, wide, exp_order, dealt
    )
    dd_halo = swap_row(jnp.where(lower, dd[:, 0:64], dd[:, 192:256]))

    def flat(value):
        return value.reshape(1024, -1)

    r_order, e_order, plain = ((1, 0, 3, 2), (0, 1, 3, 2), "plain") if dealt else ("none",) * 3
    dk, token = kernel_grad(dd, band)
    dk = dk.reshape(512, 128)
    s_keep, s_send, token = gate_grads(flat(u), flat(dv), s512, s2048, s1024, dk, e_order, [token])
    if dealt:
        s_got = swap_row(s_send)
        e_keep, e_send, token = expand_grad(flat(y2), flat(dh), e_order, [token])
        e_got = swap_row(e_send)
        s_keep, s_send, token = combine((s_keep, s_got, 2), deps=[token])
        s_got = swap_img(s_send, 1)
        r_keep, r_send, token = reduce_grad(flat(act), flat(df), flat(u), flat(dz), r_order, [token])
        r_got = swap_row(r_send)
        s_keep, s_send, token = combine((s_keep, s_got, 2), deps=[token])
        s_got = swap_img(s_send, 2)
        df_a, token = conv_back(valid, dd, dd_halo, taps, 0, 2, [token])
        r_keep, r_send, e_keep, e_send, s_keep, s_send, token = combine(
            (r_keep, r_got, 2), (e_keep, e_got, 2), (s_keep, s_got, 2), deps=[token]
        )
        r_got, e_got, s_got = swap_img(r_send, 2), swap_img(e_send, 1), swap_img(s_send, 8)
        df_b, token = conv_back(valid, dd, dd_halo, taps, 2, 2, [token])
        s_keep, s_send, token = combine((s_keep, s_got, 2), deps=[token])
        s_got = swap_img(s_send, 4)
        i_keep, i_send, token = in_grad(flat(y1), flat(df_a), flat(df_b), plain, [token])
        i_got = swap_row(i_send)
        r_keep, r_send, e_keep, e_send, token = combine((r_keep, r_got, 2), (e_keep, e_got, 2), deps=[token])
        r_got, e_got = swap_img(r_send, 1), swap_img(e_send, 2)
        dealt_rows, token = deal(i_keep, i_got, s_keep, s_got, [token])
        mixed = spread(dealt_rows)
        fgrad, late, token = last_call(valid, df_a, df_b, xp, dx2, w_in, wide, in_order, dealt, [token])
        got = swap_row(late)
        m_keep, m_send, token = merge(r_keep, r_got, e_keep, e_got, [token])
        m_got = swap_img(m_send, 8)
        late, token = add(late, got, [token])
        got = swap_img(late, 1)
        late, token = add(late, got, [token])
        got = swap_img(late, 2)
        late, token = add(late, got, [token])
        got = swap_img(late, 4)
        m_keep, m_send, token = combine((m_keep, m_got, 2), deps=[token])
        m_got = swap_img(m_send, 4)
        late, token = add(late, got, [token])
        got = swap_img(late, 8)
        red_sum, out_sum, exp_sum, token = finish(m_keep, m_got, [token])
        sums = late_sums(late, got, [token])
        own, oth = mixed, swap_row(after(mixed, late))
    else:

        def total(parts, rows):
            value = jnp.concatenate(parts, axis=0)
            return plain_scatter(value.reshape(32, -1, value.shape[1])[:, rows].reshape(-1, value.shape[1]))

        everything = slice(None)
        e_parts = expand_grad(flat(y2), flat(dh), e_order)[:2]
        r_parts = reduce_grad(flat(act), flat(df), flat(u), flat(dz), r_order)[:2]
        df_a, _ = conv_back(valid, dd, dd_halo, taps, 0, 2)
        df_b, _ = conv_back(valid, dd, dd_halo, taps, 2, 2)
        i_parts = in_grad(flat(y1), flat(df_a), flat(df_b), plain)[:2]
        fgrad, late, token = last_call(valid, df_a, df_b, xp, dx2, w_in, wide, in_order, dealt)
        sums = late_sums(*sum_all(late))
        exp_sum, in_sum = total(e_parts, everything), total(i_parts, everything)
        red_sum, out_sum = total(r_parts, slice(0, 64)), total(r_parts, slice(64, 80))
        small = plain_gather(total((s_keep, s_send), everything).astype(bf16)).reshape(16, 2, 16, 512)
        lower_row = lax.axis_index("row")
        own, oth = (
            jnp.pad(lax.dynamic_index_in_dim(small, v, 1, keepdims=False).reshape(256, 512), ((0, 0), (1024, 0)))
            for v in (lower_row, 1 - lower_row)
        )

    unpacked = unpack(own, oth)
    if dealt:
        in_sum = unpacked[0]
    dk_sum, dwb_sum, gate1, gate2, gate3, gate4, gb_sum, outb, mix, gain, shift, expb, redb, ffn = unpacked[1:-1]
    return (
        produced.reshape(features.shape),
        fgrad.reshape(features.shape),
        sums[0],
        sums[1],
        in_sum,
        sums[2],
        dk_sum,
        dwb_sum,
        gate1,
        gate2,
        gate3,
        gate4,
        gb_sum,
        out_sum,
        outb,
        mix,
        gain,
        shift,
        exp_sum,
        expb,
        red_sum,
        redb,
        ffn,
    )


def solution(mesh):
    band = P("img", "row", None, None)
    rows = P(("img", "row"), None)
    copy = P()
    ins = [band, P("img", "row", None), band] + [copy] * 21
    for k in (5, 14, 19, 21):
        ins[k] = rows
    outs = [band, band] + [copy] * 21
    for k in (4, 13, 18, 20):
        outs[k] = rows
    return jax.shard_map(per_device, mesh=mesh, in_specs=tuple(ins), out_specs=tuple(outs), check_vma=False)
```

profile of v0, /device:TPU:0, one launch (start us, length us, event | category | flops | bytes accessed | tf_op | source)
XLA Modules:
  0.0 251.8 jit_solution(8165584534972688078)
XLA Ops:
  1.2 2.7 %collective-permute-start.2 = (bf16[16,1024]{1,0:T(8,128)(2,1)}, bf16[16,1024]{1,0:T(8,128)(2,1)S(1)}, u32[]{:S(2)}, u32[]{:S(2)}) collective-permute-start(bf16[16,1024]{1,0:T(8,128)(2,1)} %refs_0_.3), channel_id=1, source_target_pairs={{0,8},{2,10},{4,12},{6,14},{8,0},{10,2},{12,4},{14,6},{16,24},{18,... | collective-permute-start | bytes 98312 | tf_op jit(solution)/shard_map/ppermute | solution.py:1112
  3.8 2.6 %collective-permute-start.3 = (bf16[16,1024]{1,0:T(8,128)(2,1)}, bf16[16,1024]{1,0:T(8,128)(2,1)S(1)}, u32[]{:S(2)}, u32[]{:S(2)}) collective-permute-start(bf16[16,1024]{1,0:T(8,128)(2,1)} %refs_0_.3), channel_id=1, source_target_pairs={{0,16},{2,18},{4,20},{6,22},{8,24},{10,26},{12,28},{14,30},{16,0},... | collective-permute-start | bytes 98312 | tf_op jit(solution)/shard_map/ppermute | solution.py:1112
  6.4 0.8 constant_dynamic-update-slice_fusion.1
  8.0 0.9 collective-permute-start.12
  8.9 1.6 vectors.1
  10.5 3.6 %collective-permute-start.13 = (bf16[16,2560]{1,0:T(8,128)(2,1)S(1)}, bf16[16,2560]{1,0:T(8,128)(2,1)S(1)}, u32[]{:S(2)}, u32[]{:S(2)}) collective-permute-start(bf16[16,2560]{1,0:T(8,128)(2,1)S(1)} %constant_dynamic-update-slice_fusion.refs_0_), channel_id=1, source_target_pairs={{0,16},{2,18},{4,20},{6,22},{8,24},{10,26},{12,28},{14,30},{16,0},... | collective-permute-start | bytes 245768 | tf_op jit(solution)/shard_map/ppermute | solution.py:1112
  14.7 1.5 join.3
  16.1 1.8 collective-permute-start.5
  17.9 1.5 collective-permute-start.6
  20.4 4.5 %prepare.1 = (bf16[4,256,512]{2,1,0:T(8,128)(2,1)}, bf16[4,256,512]{2,1,0:T(8,128)(2,1)}, bf16[4,256,512]{2,1,0:T(8,128)(2,1)}, bf16[4,64,512]{2,1,0:T(8,128)(2,1)}, f32[8,128]{1,0:T(8,128)}) custom-call(s32[32,32]{1,0:T(8,128)} %bitcast.74, s32[32,32]{1,0:T(8,128)} %copy-done.48, bf16[2,512,512]{2,1,0:T(8,128)(2,1)} %bitcast.57, ...), custom_call_target="tpu_custom_call" | custom-call | flops 4000000000 | tf_op jit(solution)/shard_map/prepare/pallas_call | solution.py:184
  25.0 1.1 collective-permute-done.6.refs_6_.refs_7_
  26.7 1.8 join.4
  28.5 1.6 collective-permute-start.15
  30.1 1.1 broadcast_in_dim.2
  31.1 5.6 %all-to-all-start = ((bf16[16,64,512]{2,1,0:T(8,128)(2,1)}), bf16[16,64,512]{2,1,0:T(8,128)(2,1)S(1)}, u32[]{:S(2)}, u32[]{:S(2)}) async-start(bf16[16,64,512]{2,1,0:T(8,128)(2,1)} %broadcast_in_dim.2), calls=%async_computation | async-start | bytes 2097152 | tf_op jit(solution)/shard_map/all_to_all | solution.py:1142
  37.8 0.8 pad_convert_fusion.refs_13_.refs_3_
  39.3 2.0 join.5
  41.3 1.9 collective-permute-start.16
  44.0 22.8 %forward.1 = (f32[4,256,1024]{2,1,0:T(8,128)}, bf16[16,13,5,16,256]{4,3,2,1,0:T(8,128)(2,1)}, f32[4,256,128]{2,1,0:T(8,128)}, f32[8,128]{1,0:T(8,128)}) custom-call(s32[32,32]{1,0:T(8,128)} %bitcast.75, s32[32,32]{1,0:T(8,128)} %copy-done.48, bf16[4,256,512]{2,1,0:T(8,128)(2,1)} %get-tuple-element.136.refs_2_, ...), custom_call_target="tpu_custom_call" | custom-call | flops 24000000000 | tf_op jit(solution)/shard_map/forward/pallas_call | solution.py:184
  67.5 3.1 %collective-permute-done.17.refs_7_.refs_11_ = bf16[128,2560]{1,0:T(8,128)(2,1)} collective-permute-done((bf16[128,2560]{1,0:T(8,128)(2,1)S(1)}, bf16[128,2560]{1,0:T(8,128)(2,1)}, u32[]{:S(2)}, u32[]{:S(2)}) %collective-permute-start.17) | collective-permute-done | bytes 655392 | tf_op jit(solution)/shard_map/ppermute | solution.py:1116
  70.7 0.9 collective-permute-done.18.refs_8_.refs_12_
  71.6 1.0 copy-done.9
  72.6 29.3 %middle.1 = (bf16[2,512,512]{2,1,0:T(8,128)(2,1)}, bf16[4,256,2048]{2,1,0:T(8,128)(2,1)}, bf16[4,256,2048]{2,1,0:T(8,128)(2,1)}, bf16[4,256,512]{2,1,0:T(8,128)(...) custom-call(s32[32,32]{1,0:T(8,128)} %bitcast.76, ...), custom_call_target="tpu_custom_call" | custom-call | flops 30000001024 | tf_op jit(solution)/shard_map/middle/pallas_call | solution.py:184
  101.9 13.0 %kernel_grad.1 = (f32[16,32,128]{2,1,0:T(8,128)}, f32[8,128]{1,0:T(8,128)}) custom-call(bf16[4,256,1024]{2,1,0:T(8,128)(2,1)} %get-tuple-element.151.refs_0_.refs_1_, bf16[16,13,5,16,256]{4,3,2,1,0:T(8,128)(2,1)} %get-tuple-element.157.refs_1_), custom_call_target="tpu_custom_call" | custom-call | flops 12999999488 | tf_op jit(solution)/shard_map/kernel_grad/pallas_call | solution.py:184
  114.9 3.5 %gate_grads.1 = (bf16[256,512]{1,0:T(8,128)(2,1)}, bf16[256,512]{1,0:T(8,128)(2,1)}, f32[8,128]{1,0:T(8,128)}) custom-call(bf16[1024,1024]{1,0:T(8,128)(2,1)} %bitcast.84, bf16[1024,1024]{1,0:T(8,128)(2,1)} %bitcast.86, f32[8,512]{1,0:T(8,128)} %get-tuple-element.154.refs_2_, f32[1,2048]{1,0:T(1,128)} %get-tuple-element.155.refs_3_, ...), custom_call_target="tpu_custom_call" | custom-call | flops 3000000000 | tf_op jit(solution)/shard_map/gate_grads/pallas_call | solution.py:184
  119.1 6.2 %expand_grad.1 = (bf16[256,2048]{1,0:T(8,128)(2,1)}, bf16[256,2048]{1,0:T(8,128)(2,1)}, f32[8,128]{1,0:T(8,128)}) custom-call(bf16[1024,512]{1,0:T(8,128)(2,1)} %bitcast.96, bf16[1024,2048]{1,0:T(8,128)(2,1)} %bitcast.83, f32[8,128]{1,0:T(8,128)} %get-tuple-element.164.refs_2_), custom_call_target="tpu_custom_call" | custom-call | flops 5000000000 | tf_op jit(solution)/shard_map/expand_grad/pallas_call | solution.py:184
  126.0 3.0 %combine.6 = (bf16[4,32,512]{2,1,0:T(8,128)(2,1)}, bf16[4,32,512]{2,1,0:T(8,128)(2,1)}, f32[8,128]{1,0:T(8,128)}) custom-call(bf16[2,4,32,512]{3,2,1,0:T(8,128)(2,1)} %bitcast.102, bf16[2,4,32,512]{3,2,1,0:T(8,128)(2,1)} %bitcast.66, f32[8,128]{1,0:T(8,128)} %get-tuple-element.165.refs_2_), custom_call_target="tpu_custom_call" | custom-call | flops 2000000000 | tf_op jit(solution)/shard_map/combine/pallas_call | solution.py:184
  129.1 8.3 %reduce_grad.1 = (bf16[1280,512]{1,0:T(8,128)(2,1)}, bf16[1280,512]{1,0:T(8,128)(2,1)}, f32[8,128]{1,0:T(8,128)}) custom-call(bf16[1024,2048]{1,0:T(8,128)(2,1)} %bitcast.82, bf16[1024,512]{1,0:T(8,128)(2,1)} %bitcast.94, bf16[1024,1024]{1,0:T(8,128)(2,1)} %bitcast.85, bf16[1024,512]{1,0:T(8,128)(2,1)} %bitcast.95, f32[8,128]{1,0:T(8,128)} %get-tuple-element.171.refs_4_), custom_call_target="tpu_custom_call" | custom-call | flops 6000000000 | tf_op jit(solution)/shard_map/reduce_grad/pallas_call | solution.py:184
  137.9 5.3 %collective-permute-done.22 = bf16[128,512]{1,0:T(8,128)(2,1)S(1)} collective-permute-done((bf16[128,512]{1,0:T(8,128)(2,1)S(1)}, bf16[128,512]{1,0:T(8,128)(2,1)S(1)}, u32[]{:S(2)}, u32[]{:S(2)}) %collective-permute-start.22) | collective-permute-done | bytes 131104 | tf_op jit(solution)/shard_map/ppermute | solution.py:1112
  143.9 2.8 %combine.7 = (bf16[4,16,512]{2,1,0:T(8,128)(2,1)}, bf16[4,16,512]{2,1,0:T(8,128)(2,1)}, f32[8,128]{1,0:T(8,128)}) custom-call(bf16[2,4,16,512]{3,2,1,0:T(8,128)(2,1)} %bitcast.105, bf16[2,4,16,512]{3,2,1,0:T(8,128)(2,1)} %bitcast.69, f32[8,128]{1,0:T(8,128)} %get-tuple-element.172.refs_2_), custom_call_target="tpu_custom_call" | custom-call | flops 2000000000 | tf_op jit(solution)/shard_map/combine/pallas_call | solution.py:184
  146.7 1.4 collective-permute-start.25
  148.2 0.8 copy-done.14
  149.0 8.9 %conv_back.2 = (bf16[4,256,512]{2,1,0:T(8,128)(2,1)}, f32[8,128]{1,0:T(8,128)}) custom-call(s32[32,32]{1,0:T(8,128)} %bitcast.77, bf16[4,256,1024]{2,1,0:T(8,128)(2,1)} %get-tuple-element.151.refs_0_.refs_1_, bf16[4,64,1024]{2,1,0:T(8,128)(2,1)} %copy-done.14, f32[7,7,1024]{2,1,0:T(8,128)} %pad_convert_fusion.refs_13_.refs_3_, ...), custom_call_target="tpu_custom_call" | custom-call | flops 8999999488 | tf_op jit(solution)/shard_map/conv_back/pallas_call | solution.py:184
  159.0 3.6 %combine.8 = (bf16[2,320,512]{2,1,0:T(8,128)(2,1)}, bf16[2,320,512]{2,1,0:T(8,128)(2,1)}, bf16[2,64,2048]{2,1,0:T(8,128)(2,1)}, bf16[2,64,2048]{2,1,0:T(8,128)(2...) custom-call(bf16[2,2,320,512]{3,2,1,0:T(8,128)(2,1)} %bitcast.87, ...), custom_call_target="tpu_custom_call" | custom-call | flops 2000000000 | tf_op jit(solution)/shard_map/combine/pallas_call | solution.py:184
  162.6 2.4 collective-permute-start.26
  166.2 8.8 %conv_back.3 = (bf16[4,256,512]{2,1,0:T(8,128)(2,1)}, f32[8,128]{1,0:T(8,128)}) custom-call(s32[32,32]{1,0:T(8,128)} %bitcast.78, bf16[4,256,1024]{2,1,0:T(8,128)(2,1)} %get-tuple-element.151.refs_0_.refs_1_, bf16[4,64,1024]{2,1,0:T(8,128)(2,1)} %copy-done.14, f32[7,7,1024]{2,1,0:T(8,128)} %pad_convert_fusion.refs_13_.refs_3_, ...), custom_call_target="tpu_custom_call" | custom-call | flops 8999999488 | tf_op jit(solution)/shard_map/conv_back/pallas_call | solution.py:184
  175.6 1.4 combine.9
  177.0 4.2 %in_grad.1 = (bf16[256,1024]{1,0:T(8,128)(2,1)}, bf16[256,1024]{1,0:T(8,128)(2,1)}, f32[8,128]{1,0:T(8,128)}) custom-call(bf16[1024,512]{1,0:T(8,128)(2,1)} %bitcast.89, bf16[1024,512]{1,0:T(8,128)(2,1)} %bitcast.91, bf16[1024,512]{1,0:T(8,128)(2,1)} %bitcast.92, f32[8,128]{1,0:T(8,128)} %get-tuple-element.188.refs_3_), custom_call_target="tpu_custom_call" | custom-call | flops 4000000000 | tf_op jit(solution)/shard_map/in_grad/pallas_call | solution.py:184
  181.2 1.5 collective-permute-start.28
  182.7 0.8 copy-done.15
  183.7 3.8 %combine.10 = (bf16[4,80,512]{2,1,0:T(8,128)(2,1)}, bf16[4,80,512]{2,1,0:T(8,128)(2,1)}, bf16[4,16,2048]{2,1,0:T(8,128)(2,1)}, bf16[4,16,2048]{2,1,0:T(8,128)(2,1)}, f32[8,128]{1,0:T(8,128)}) custom-call(bf16[2,4,80,512]{3,2,1,0:T(8,128)(2,1)} %bitcast.97, bf16[2,4,80,512]{3,2,1,0:T(8,128)(2,1)} %bitcast.60, bf16[2,4,16,2048]{3,2,1,0:T(8,128)(2,1)} %bitcast.98, ...), custom_call_target="tpu_custom_call" | custom-call | flops 2000000000 | tf_op jit(solution)/shard_map/combine/pallas_call | solution.py:184
  188.3 2.4 deal.1
  190.6 3.7 %all-to-all-start.1 = ((bf16[16,16,1536]{2,1,0:T(8,128)(2,1)}), bf16[16,16,1536]{2,1,0:T(8,128)(2,1)S(1)}, u32[]{:S(2)}, u32[]{:S(2)}) async-start(bf16[16,16,1536]{2,1,0:T(8,128)(2,1)} %bitcast.54), calls=%async_computation.1 | async-start | bytes 1572864 | tf_op jit(solution)/shard_map/all_to_all | solution.py:1142
  194.4 2.0 collective-permute-start.32
  196.4 1.5 collective-permute-start.33
  197.8 6.9 %last.1 = (bf16[2,512,512]{2,1,0:T(8,128)(2,1)}, f32[8,512]{1,0:T(8,128)}, f32[8,128]{1,0:T(8,128)}) custom-call(s32[32,32]{1,0:T(8,128)} %bitcast.79, bf16[4,256,512]{2,1,0:T(8,128)(2,1)} %get-tuple-element.174.refs_1_, bf16[4,256,512]{2,1,0:T(8,128)(2,1)} %get-tuple-element.183.refs_2_, bf16[4,256,512]{2,1,0:T(8,128)(2,1)} %get-tuple-element.145.refs_3_, ...), custom_call_target="tpu_custom_call" | custom-call | flops 7000000000 | tf_op jit(solution)/shard_map/last/pallas_call | solution.py:184
  204.9 4.5 %collective-permute-done.33.refs_3_ = bf16[64,2048]{1,0:T(8,128)(2,1)S(1)} collective-permute-done((bf16[64,2048]{1,0:T(8,128)(2,1)S(1)}, bf16[64,2048]{1,0:T(8,128)(2,1)S(1)}, u32[]{:S(2)}, u32[]{:S(2)}) %collective-permute-start.33) | collective-permute-done | bytes 262176 | tf_op jit(solution)/shard_map/ppermute | solution.py:1112
  209.4 1.1 collective-permute-done.32.refs_1_
  211.3 2.1 merge.1
  213.4 4.2 %collective-permute-start.37 = (bf16[288,512]{1,0:T(8,128)(2,1)}, bf16[288,512]{1,0:T(8,128)(2,1)S(1)}, u32[]{:S(2)}, u32[]{:S(2)}) collective-permute-start(bf16[288,512]{1,0:T(8,128)(2,1)} %get-tuple-element.214), channel_id=1, source_target_pairs={{0,16},{2,18},{4,20},{6,22},{8,24},{10,26},{12,28},{14,30},{16,0},... | collective-permute-start | bytes 884744 | tf_op jit(solution)/shard_map/ppermute | solution.py:1112
  218.1 1.3 add.6
  220.0 3.4 %collective-permute-done.34.refs_1_ = f32[8,512]{1,0:T(8,128)S(1)} collective-permute-done((f32[8,512]{1,0:T(8,128)}, f32[8,512]{1,0:T(8,128)S(1)}, u32[]{:S(2)}, u32[]{:S(2)}) %collective-permute-start.34) | collective-permute-done | bytes 16416 | tf_op jit(solution)/shard_map/ppermute | solution.py:1112
  224.0 1.3 add.7
  225.4 1.7 collective-permute-start.35
  227.1 2.2 collective-permute-done.35.refs_1_
  229.9 1.3 add.8
  232.0 1.8 combine.11
  233.8 1.4 collective-permute-done.36.refs_1_
  235.8 1.3 add.9
  237.9 5.9 %collective-permute-done.39.refs_1_ = bf16[144,512]{1,0:T(8,128)(2,1)S(1)} collective-permute-done((bf16[144,512]{1,0:T(8,128)(2,1)S(1)}, bf16[144,512]{1,0:T(8,128)(2,1)S(1)}, u32[]{:S(2)}, u32[]{:S(2)}) %collective-permute-start.39) | collective-permute-done | bytes 147488 | tf_op jit(solution)/shard_map/ppermute | solution.py:1112
  244.5 1.7 finish.1
  246.8 1.3 late.1
  248.1 0.9 copy-done.10
  249.0 2.6 %unpack.1 = (f32[16,1024]{1,0:T(8,128)}, f32[7,7,992]{2,1,0:T(8,128)}, f32[992]{0:T(1024)}, f32[32,64]{1,0:T(8,128)}, f32[64,128]{1,0:T(8,128)}, /*index=5*/f32[...) custom-call(bf16[256,1536]{1,0:T(8,128)(2,1)} %bitcast.53, ...), custom_call_target="tpu_custom_call" | custom-call | flops 3000000000 | tf_op jit(solution)/shard_map/unpack/pallas_call | solution.py:184
  (169 shorter events, 19.6 us)
Async XLA Ops:
  0.7 13.4 %copy-start.47 = (s32[2,16,32]{2,1,0:T(8,128)S(1)}, s32[2,16,32]{2,1,0:T(8,128)}, u32[]{:S(2)}) copy-start(s32[2,16,32]{2,1,0:T(8,128)} %param.25) | copy-start | bytes 12292
  0.7 18.8 %collective-permute-start.1 = (bf16[2,512,512]{2,1,0:T(8,128)(2,1)}, bf16[2,512,512]{2,1,0:T(8,128)(2,1)S(1)}, u32[]{:S(2)}, u32[]{:S(2)}) collective-permute-start(bf16[2,512,512]{2,1,0:T(8,128)(2,1)} %bitcast.56), channel_id=1, source_target_pairs={{0,1},{1,0},{2,3},{3,2},{4,5},{5,4},{6,7},{7,6},{8,9},{9,8},{10,11... | collective-permute-start | bytes 3145736 | tf_op jit(solution)/shard_map/ppermute | solution.py:1116
  1.2 9.3 %collective-permute-start.2 = (bf16[16,1024]{1,0:T(8,128)(2,1)}, bf16[16,1024]{1,0:T(8,128)(2,1)S(1)}, u32[]{:S(2)}, u32[]{:S(2)}) collective-permute-start(bf16[16,1024]{1,0:T(8,128)(2,1)} %refs_0_.3), channel_id=1, source_target_pairs={{0,8},{2,10},{4,12},{6,14},{8,0},{10,2},{12,4},{14,6},{16,24},{18,... | collective-permute-start | bytes 98312 | tf_op jit(solution)/shard_map/ppermute | solution.py:1112
  3.8 10.2 %collective-permute-start.3 = (bf16[16,1024]{1,0:T(8,128)(2,1)}, bf16[16,1024]{1,0:T(8,128)(2,1)S(1)}, u32[]{:S(2)}, u32[]{:S(2)}) collective-permute-start(bf16[16,1024]{1,0:T(8,128)(2,1)} %refs_0_.3), channel_id=1, source_target_pairs={{0,16},{2,18},{4,20},{6,22},{8,24},{10,26},{12,28},{14,30},{16,0},... | collective-permute-start | bytes 98312 | tf_op jit(solution)/shard_map/ppermute | solution.py:1112
  6.4 7.6 %collective-permute-start.4 = (bf16[16,1024]{1,0:T(8,128)(2,1)}, bf16[16,1024]{1,0:T(8,128)(2,1)S(1)}, u32[]{:S(2)}, u32[]{:S(2)}) collective-permute-start(bf16[16,1024]{1,0:T(8,128)(2,1)} %refs_0_.3), channel_id=1, source_target_pairs={{0,24},{2,26},{4,28},{6,30},{8,16},{10,18},{12,20},{14,22},{16,8},... | collective-permute-start | bytes 98312 | tf_op jit(solution)/shard_map/ppermute | solution.py:1112
  8.0 8.1 %copy-start.5 = (bf16[16,2560]{1,0:T(8,128)(2,1)}, bf16[16,2560]{1,0:T(8,128)(2,1)S(1)}, u32[]{:S(2)}) copy-start(bf16[16,2560]{1,0:T(8,128)(2,1)S(1)} %constant_dynamic-update-slice_fusion.refs_0_) | copy-start | bytes 245764
  8.0 9.9 %collective-permute-start.12 = (bf16[16,2560]{1,0:T(8,128)(2,1)S(1)}, bf16[16,2560]{1,0:T(8,128)(2,1)S(1)}, u32[]{:S(2)}, u32[]{:S(2)}) collective-permute-start(bf16[16,2560]{1,0:T(8,128)(2,1)S(1)} %constant_dynamic-update-slice_fusion.refs_0_), channel_id=1, source_target_pairs={{0,8},{2,10},{4,12},{6,14},{8,0},{10,2},{12,4},{14,6},{16,24},{18,... | collective-permute-start | bytes 245768 | tf_op jit(solution)/shard_map/ppermute | solution.py:1112
  10.5 3.7 %copy-start.43 = (bf16[16,1024]{1,0:T(8,128)(2,1)}, bf16[16,1024]{1,0:T(8,128)(2,1)S(1)}, u32[]{:S(2)}) copy-start(bf16[16,1024]{1,0:T(8,128)(2,1)S(1)} %collective-permute-done.2.refs_1_) | copy-start | bytes 98308
  10.5 14.4 %collective-permute-start.13 = (bf16[16,2560]{1,0:T(8,128)(2,1)S(1)}, bf16[16,2560]{1,0:T(8,128)(2,1)S(1)}, u32[]{:S(2)}, u32[]{:S(2)}) collective-permute-start(bf16[16,2560]{1,0:T(8,128)(2,1)S(1)} %constant_dynamic-update-slice_fusion.refs_0_), channel_id=1, source_target_pairs={{0,16},{2,18},{4,20},{6,22},{8,24},{10,26},{12,28},{14,30},{16,0},... | collective-permute-start | bytes 245768 | tf_op jit(solution)/shard_map/ppermute | solution.py:1112
  14.0 10.9 %collective-permute-start.14 = (bf16[16,2560]{1,0:T(8,128)(2,1)S(1)}, bf16[16,2560]{1,0:T(8,128)(2,1)S(1)}, u32[]{:S(2)}, u32[]{:S(2)}) collective-permute-start(bf16[16,2560]{1,0:T(8,128)(2,1)S(1)} %constant_dynamic-update-slice_fusion.refs_0_), channel_id=1, source_target_pairs={{0,24},{2,26},{4,28},{6,30},{8,16},{10,18},{12,20},{14,22},{16,8},... | collective-permute-start | bytes 245768 | tf_op jit(solution)/shard_map/ppermute | solution.py:1112
  14.1 2.1 collective-permute-start
  16.1 3.6 %copy-start.48 = (s32[32,32]{1,0:T(8,128)}, s32[32,32]{1,0:T(8,128)S(1)}, u32[]{:S(2)}) copy-start(s32[32,32]{1,0:T(8,128)S(1)} %collective-permute-done.refs_1_) | copy-start | bytes 12292
  16.1 8.8 %collective-permute-start.5 = (bf16[64,1024]{1,0:T(8,128)(2,1)}, bf16[64,1024]{1,0:T(8,128)(2,1)S(1)}, u32[]{:S(2)}, u32[]{:S(2)}) collective-permute-start(bf16[64,1024]{1,0:T(8,128)(2,1)} %get-tuple-element.138.refs_4_.refs_5_), channel_id=1, source_target_pairs={{0,2},{2,0},{4,6},{6,4},{8,10},{10,8},{12,14},{14,12},{16,18},{18,... | collective-permute-start | bytes 393224 | tf_op jit(solution)/shard_map/ppermute | solution.py:1112
  17.9 7.0 %copy-start.39 = (bf16[16,2560]{1,0:T(8,128)(2,1)}, bf16[16,2560]{1,0:T(8,128)(2,1)S(1)}, u32[]{:S(2)}) copy-start(bf16[16,2560]{1,0:T(8,128)(2,1)S(1)} %collective-permute-done.12.refs_1_) | copy-start | bytes 245764
  17.9 8.1 %collective-permute-start.6 = (bf16[64,1024]{1,0:T(8,128)(2,1)}, bf16[64,1024]{1,0:T(8,128)(2,1)S(1)}, u32[]{:S(2)}, u32[]{:S(2)}) collective-permute-start(bf16[64,1024]{1,0:T(8,128)(2,1)} %get-tuple-element.138.refs_4_.refs_5_), channel_id=1, source_target_pairs={{0,4},{2,6},{4,0},{6,2},{8,12},{10,14},{12,8},{14,10},{16,20},{18,... | collective-permute-start | bytes 393224 | tf_op jit(solution)/shard_map/ppermute | solution.py:1112
  19.4 6.6 %collective-permute-start.7 = (bf16[64,1024]{1,0:T(8,128)(2,1)}, bf16[64,1024]{1,0:T(8,128)(2,1)S(1)}, u32[]{:S(2)}, u32[]{:S(2)}) collective-permute-start(bf16[64,1024]{1,0:T(8,128)(2,1)} %get-tuple-element.138.refs_4_.refs_5_), channel_id=1, source_target_pairs={{0,6},{2,4},{4,2},{6,0},{8,14},{10,12},{12,10},{14,8},{16,22},{18,... | collective-permute-start | bytes 393224 | tf_op jit(solution)/shard_map/ppermute | solution.py:1112
  24.9 5.2 %copy-start.4 = (bf16[64,512]{1,0:T(8,128)(2,1)S(1)}, bf16[64,512]{1,0:T(8,128)(2,1)}, u32[]{:S(2)}) copy-start(bf16[64,512]{1,0:T(8,128)(2,1)} %param.45) | copy-start | bytes 196612
  28.5 8.3 %copy-start.26 = (bf16[64,1024]{1,0:T(8,128)(2,1)S(1)}, bf16[64,1024]{1,0:T(8,128)(2,1)}, u32[]{:S(2)}) copy-start(bf16[64,1024]{1,0:T(8,128)(2,1)} %get-tuple-element.138.refs_4_.refs_5_) | copy-start | bytes 393220
  28.5 8.3 %copy-start.30 = (bf16[64,1024]{1,0:T(8,128)(2,1)S(1)}, bf16[64,1024]{1,0:T(8,128)(2,1)}, u32[]{:S(2)}) copy-start(bf16[64,1024]{1,0:T(8,128)(2,1)} %copy-done.29) | copy-start | bytes 393220
  28.5 8.8 %copy-start.32 = (bf16[64,1024]{1,0:T(8,128)(2,1)S(1)}, bf16[64,1024]{1,0:T(8,128)(2,1)}, u32[]{:S(2)}) copy-start(bf16[64,1024]{1,0:T(8,128)(2,1)} %copy-done.31) | copy-start | bytes 393220
  28.5 8.9 %copy-start.28 = (bf16[64,1024]{1,0:T(8,128)(2,1)S(1)}, bf16[64,1024]{1,0:T(8,128)(2,1)}, u32[]{:S(2)}) copy-start(bf16[64,1024]{1,0:T(8,128)(2,1)} %copy-done.27) | copy-start | bytes 393220
  28.5 9.3 %copy-start.3 = (bf16[7,7,992]{2,1,0:T(8,128)(2,1)S(1)}, bf16[7,7,992]{2,1,0:T(8,128)(2,1)}, u32[]{:S(2)}) copy-start(bf16[7,7,992]{2,1,0:T(8,128)(2,1)} %param.31) | copy-start | bytes 291652
  28.5 10.1 %collective-permute-start.15 = (bf16[64,2560]{1,0:T(8,128)(2,1)}, bf16[64,2560]{1,0:T(8,128)(2,1)S(1)}, u32[]{:S(2)}, u32[]{:S(2)}) collective-permute-start(bf16[64,2560]{1,0:T(8,128)(2,1)} %get-tuple-element.140.refs_0_), channel_id=1, source_target_pairs={{0,4},{2,6},{4,0},{6,2},{8,12},{10,14},{12,8},{14,10},{16,20},{18,... | collective-permute-start | bytes 983048 | tf_op jit(solution)/shard_map/ppermute | solution.py:1112
  31.1 35.7 %all-to-all-start = ((bf16[16,64,512]{2,1,0:T(8,128)(2,1)}), bf16[16,64,512]{2,1,0:T(8,128)(2,1)S(1)}, u32[]{:S(2)}, u32[]{:S(2)}) async-start(bf16[16,64,512]{2,1,0:T(8,128)(2,1)} %broadcast_in_dim.2), calls=%async_computation | async-start | bytes 2097152 | tf_op jit(solution)/shard_map/all_to_all | solution.py:1142
  36.7 6.5 %collective-permute-start.8 = (bf16[64,1024]{1,0:T(8,128)(2,1)S(1)}, bf16[64,1024]{1,0:T(8,128)(2,1)S(1)}, u32[]{:S(2)}, u32[]{:S(2)}) collective-permute-start(bf16[64,1024]{1,0:T(8,128)(2,1)S(1)} %copy-done.26), channel_id=1, source_target_pairs={{0,1},{1,0},{2,3},{3,2},{4,5},{5,4},{6,7},{7,6},{8,9},{9,8},{10,11... | collective-permute-start | bytes 393224 | tf_op jit(solution)/shard_map/ppermute | solution.py:1116
  36.8 6.4 %collective-permute-start.10 = (bf16[64,1024]{1,0:T(8,128)(2,1)S(1)}, bf16[64,1024]{1,0:T(8,128)(2,1)S(1)}, u32[]{:S(2)}, u32[]{:S(2)}) collective-permute-start(bf16[64,1024]{1,0:T(8,128)(2,1)S(1)} %copy-done.30), channel_id=1, source_target_pairs={{0,1},{1,0},{2,3},{3,2},{4,5},{5,4},{6,7},{7,6},{8,9},{9,8},{10,11... | collective-permute-start | bytes 393224 | tf_op jit(solution)/shard_map/ppermute | solution.py:1116
  37.3 5.9 %collective-permute-start.11 = (bf16[64,1024]{1,0:T(8,128)(2,1)S(1)}, bf16[64,1024]{1,0:T(8,128)(2,1)S(1)}, u32[]{:S(2)}, u32[]{:S(2)}) collective-permute-start(bf16[64,1024]{1,0:T(8,128)(2,1)S(1)} %copy-done.32), channel_id=1, source_target_pairs={{0,1},{1,0},{2,3},{3,2},{4,5},{5,4},{6,7},{7,6},{8,9},{9,8},{10,11... | collective-permute-start | bytes 393224 | tf_op jit(solution)/shard_map/ppermute | solution.py:1116
  37.4 5.9 %collective-permute-start.9 = (bf16[64,1024]{1,0:T(8,128)(2,1)S(1)}, bf16[64,1024]{1,0:T(8,128)(2,1)S(1)}, u32[]{:S(2)}, u32[]{:S(2)}) collective-permute-start(bf16[64,1024]{1,0:T(8,128)(2,1)S(1)} %copy-done.28), channel_id=1, source_target_pairs={{0,1},{1,0},{2,3},{3,2},{4,5},{5,4},{6,7},{7,6},{8,9},{9,8},{10,11... | collective-permute-start | bytes 393224 | tf_op jit(solution)/shard_map/ppermute | solution.py:1116
  41.3 26.1 %collective-permute-start.16 = (bf16[128,2560]{1,0:T(8,128)(2,1)}, bf16[128,2560]{1,0:T(8,128)(2,1)S(1)}, u32[]{:S(2)}, u32[]{:S(2)}) collective-permute-start(bf16[128,2560]{1,0:T(8,128)(2,1)} %get-tuple-element.147.refs_5_.refs_9_), channel_id=1, source_target_pairs={{0,2},{2,0},{4,6},{6,4},{8,10},{10,8},{12,14},{14,12},{16,18},{18,... | collective-permute-start | bytes 1966088 | tf_op jit(solution)/shard_map/ppermute | solution.py:1112
  44.0 22.9 %copy-start.11 = (bf16[128,2560]{1,0:T(8,128)(2,1)S(1)}, bf16[128,2560]{1,0:T(8,128)(2,1)}, u32[]{:S(2)}) copy-start(bf16[128,2560]{1,0:T(8,128)(2,1)} %get-tuple-element.147.refs_5_.refs_9_) | copy-start | bytes 1966084
  66.8 4.8 %copy-start = (bf16[16,64,512]{2,1,0:T(8,128)(2,1)}, bf16[16,64,512]{2,1,0:T(8,128)(2,1)S(1)}, u32[]{:S(2)}) copy-start(bf16[16,64,512]{2,1,0:T(8,128)(2,1)S(1)} %all-to-all-done) | copy-start | bytes 3145732
  66.9 4.7 %collective-permute-start.19 = (bf16[1024,512]{1,0:T(8,128)(2,1)S(1)}, bf16[1024,512]{1,0:T(8,128)(2,1)S(1)}, u32[]{:S(2)}, u32[]{:S(2)}) collective-permute-start(bf16[1024,512]{1,0:T(8,128)(2,1)S(1)} %bitcast.50), channel_id=1, source_target_pairs={{0,1},{1,0},{2,3},{3,2},{4,5},{5,4},{6,7},{7,6},{8,9},{9,8},{10,11... | collective-permute-start | bytes 3145736 | tf_op jit(solution)/shard_map/ppermute | solution.py:1116
  66.9 3.7 %collective-permute-start.17 = (bf16[128,2560]{1,0:T(8,128)(2,1)S(1)}, bf16[128,2560]{1,0:T(8,128)(2,1)}, u32[]{:S(2)}, u32[]{:S(2)}) collective-permute-start(bf16[128,2560]{1,0:T(8,128)(2,1)S(1)} %copy-done.11), channel_id=1, source_target_pairs={{0,1},{1,0},{2,3},{3,2},{4,5},{5,4},{6,7},{7,6},{8,9},{9,8},{10,11... | collective-permute-start | bytes 1966088 | tf_op jit(solution)/shard_map/ppermute | solution.py:1116
  67.4 4.2 %copy-start.12 = (bf16[128,2560]{1,0:T(8,128)(2,1)}, bf16[128,2560]{1,0:T(8,128)(2,1)S(1)}, u32[]{:S(2)}) copy-start(bf16[128,2560]{1,0:T(8,128)(2,1)S(1)} %collective-permute-done.16.refs_6_.refs_10_) | copy-start | bytes 1966084
  67.4 4.1 %collective-permute-start.18 = (bf16[128,2560]{1,0:T(8,128)(2,1)S(1)}, bf16[128,2560]{1,0:T(8,128)(2,1)}, u32[]{:S(2)}, u32[]{:S(2)}) collective-permute-start(bf16[128,2560]{1,0:T(8,128)(2,1)S(1)} %collective-permute-done.16.refs_6_.refs_10_), channel_id=1, source_target_pairs={{0,1},{1,0},{2,3},{3,2},{4,5},{5,4},{6,7},{7,6},{8,9},{9,8},{10,11... | collective-permute-start | bytes 1966088 | tf_op jit(solution)/shard_map/ppermute | solution.py:1116
  114.9 3.7 %copy-start.2 = (bf16[4,256,1024]{2,1,0:T(8,128)(2,1)S(1)}, bf16[4,256,1024]{2,1,0:T(8,128)(2,1)}, u32[]{:S(2)}) copy-start(bf16[4,256,1024]{2,1,0:T(8,128)(2,1)} %get-tuple-element.151.refs_0_.refs_1_) | copy-start | bytes 6291460
  118.5 6.9 %collective-permute-start.21 = (bf16[256,512]{1,0:T(8,128)(2,1)}, bf16[256,512]{1,0:T(8,128)(2,1)S(1)}, u32[]{:S(2)}, u32[]{:S(2)}) collective-permute-start(bf16[256,512]{1,0:T(8,128)(2,1)} %get-tuple-element.161), channel_id=1, source_target_pairs={{0,1},{1,0},{2,3},{3,2},{4,5},{5,4},{6,7},{7,6},{8,9},{9,8},{10,11... | collective-permute-start | bytes 786440 | tf_op jit(solution)/shard_map/ppermute | solution.py:1116
  118.7 29.5 %collective-permute-start.20 = (bf16[4,64,1024]{2,1,0:T(8,128)(2,1)S(1)}, bf16[4,64,1024]{2,1,0:T(8,128)(2,1)S(1)}, u32[]{:S(2)}, u32[]{:S(2)}) collective-permute-start(bf16[4,64,1024]{2,1,0:T(8,128)(2,1)S(1)} %slice_select_fusion), channel_id=1, source_target_pairs={{0,1},{1,0},{2,3},{3,2},{4,5},{5,4},{6,7},{7,6},{8,9},{9,8},{10,11... | collective-permute-start | bytes 1572872 | tf_op jit(solution)/shard_map/ppermute | solution.py:1116
  129.1 8.4 %copy-start.37 = (bf16[4,32,512]{2,1,0:T(8,128)(2,1)S(1)}, bf16[4,32,512]{2,1,0:T(8,128)(2,1)}, u32[]{:S(2)}) copy-start(bf16[4,32,512]{2,1,0:T(8,128)(2,1)} %get-tuple-element.167) | copy-start | bytes 393220
  129.1 8.5 %copy-start.8 = (bf16[256,2048]{1,0:T(8,128)(2,1)S(1)}, bf16[256,2048]{1,0:T(8,128)(2,1)}, u32[]{:S(2)}) copy-start(bf16[256,2048]{1,0:T(8,128)(2,1)} %get-tuple-element.178) | copy-start | bytes 3145732
  137.3 20.6 %collective-permute-start.23 = (bf16[1280,512]{1,0:T(8,128)(2,1)}, bf16[1280,512]{1,0:T(8,128)(2,1)S(1)}, u32[]{:S(2)}, u32[]{:S(2)}) collective-permute-start(bf16[1280,512]{1,0:T(8,128)(2,1)} %get-tuple-element.176), channel_id=1, source_target_pairs={{0,1},{1,0},{2,3},{3,2},{4,5},{5,4},{6,7},{7,6},{8,9},{9,8},{10,11... | collective-permute-start | bytes 3932168 | tf_op jit(solution)/shard_map/ppermute | solution.py:1116
  137.5 5.8 %collective-permute-start.22 = (bf16[128,512]{1,0:T(8,128)(2,1)S(1)}, bf16[128,512]{1,0:T(8,128)(2,1)S(1)}, u32[]{:S(2)}, u32[]{:S(2)}) collective-permute-start(bf16[128,512]{1,0:T(8,128)(2,1)S(1)} %bitcast.68), channel_id=1, source_target_pairs={{0,2},{2,0},{4,6},{6,4},{8,10},{10,8},{12,14},{14,12},{16,18},{18,... | collective-permute-start | bytes 393224 | tf_op jit(solution)/shard_map/ppermute | solution.py:1112
  137.6 20.3 %collective-permute-start.24 = (bf16[256,2048]{1,0:T(8,128)(2,1)S(1)}, bf16[256,2048]{1,0:T(8,128)(2,1)}, u32[]{:S(2)}, u32[]{:S(2)}) collective-permute-start(bf16[256,2048]{1,0:T(8,128)(2,1)S(1)} %copy-done.8), channel_id=1, source_target_pairs={{0,1},{1,0},{2,3},{3,2},{4,5},{5,4},{6,7},{7,6},{8,9},{9,8},{10,11... | collective-permute-start | bytes 3145736 | tf_op jit(solution)/shard_map/ppermute | solution.py:1116
  146.7 11.2 %collective-permute-start.25 = (bf16[64,512]{1,0:T(8,128)(2,1)}, bf16[64,512]{1,0:T(8,128)(2,1)S(1)}, u32[]{:S(2)}, u32[]{:S(2)}) collective-permute-start(bf16[64,512]{1,0:T(8,128)(2,1)} %bitcast.71), channel_id=1, source_target_pairs={{0,4},{2,6},{4,0},{6,2},{8,12},{10,14},{12,8},{14,10},{16,20},{18,... | collective-permute-start | bytes 196616 | tf_op jit(solution)/shard_map/ppermute | solution.py:1112
  162.6 12.4 %collective-permute-start.26 = (bf16[32,512]{1,0:T(8,128)(2,1)}, bf16[32,512]{1,0:T(8,128)(2,1)S(1)}, u32[]{:S(2)}, u32[]{:S(2)}) collective-permute-start(bf16[32,512]{1,0:T(8,128)(2,1)} %bitcast.72), channel_id=1, source_target_pairs={{0,16},{2,18},{4,20},{6,22},{8,24},{10,26},{12,28},{14,30},{16,0},... | collective-permute-start | bytes 98312 | tf_op jit(solution)/shard_map/ppermute | solution.py:1112
  165.0 17.7 %collective-permute-start.29 = (bf16[640,512]{1,0:T(8,128)(2,1)}, bf16[640,512]{1,0:T(8,128)(2,1)S(1)}, u32[]{:S(2)}, u32[]{:S(2)}) collective-permute-start(bf16[640,512]{1,0:T(8,128)(2,1)} %bitcast.59), channel_id=1, source_target_pairs={{0,4},{2,6},{4,0},{6,2},{8,12},{10,14},{12,8},{14,10},{16,20},{18,... | collective-permute-start | bytes 1966088 | tf_op jit(solution)/shard_map/ppermute | solution.py:1112
  165.6 17.1 %collective-permute-start.30 = (bf16[128,2048]{1,0:T(8,128)(2,1)}, bf16[128,2048]{1,0:T(8,128)(2,1)S(1)}, u32[]{:S(2)}, u32[]{:S(2)}) collective-permute-start(bf16[128,2048]{1,0:T(8,128)(2,1)} %bitcast.61), channel_id=1, source_target_pairs={{0,2},{2,0},{4,6},{6,4},{8,10},{10,8},{12,14},{14,12},{16,18},{18,... | collective-permute-start | bytes 1572872 | tf_op jit(solution)/shard_map/ppermute | solution.py:1112
  177.0 4.2 %copy-start.49 = (bf16[1,16,512]{2,1,0:T(8,128)(2,1)S(1)}, bf16[1,16,512]{2,1,0:T(8,128)(2,1)}, u32[]{:S(2)}) copy-start(bf16[1,16,512]{2,1,0:T(8,128)(2,1)} %get-tuple-element.192) | copy-start | bytes 49156
  181.2 6.3 %collective-permute-start.27 = (bf16[256,1024]{1,0:T(8,128)(2,1)}, bf16[256,1024]{1,0:T(8,128)(2,1)S(1)}, u32[]{:S(2)}, u32[]{:S(2)}) collective-permute-start(bf16[256,1024]{1,0:T(8,128)(2,1)} %get-tuple-element.190), channel_id=1, source_target_pairs={{0,1},{1,0},{2,3},{3,2},{4,5},{5,4},{6,7},{7,6},{8,9},{9,8},{10,11... | collective-permute-start | bytes 1572872 | tf_op jit(solution)/shard_map/ppermute | solution.py:1116
  181.2 6.2 %collective-permute-start.28 = (bf16[16,512]{1,0:T(8,128)(2,1)S(1)}, bf16[16,512]{1,0:T(8,128)(2,1)S(1)}, u32[]{:S(2)}, u32[]{:S(2)}) collective-permute-start(bf16[16,512]{1,0:T(8,128)(2,1)S(1)} %bitcast.81), channel_id=1, source_target_pairs={{0,8},{2,10},{4,12},{6,14},{8,0},{10,2},{12,4},{14,6},{16,24},{18,... | collective-permute-start | bytes 49160 | tf_op jit(solution)/shard_map/ppermute | solution.py:1112
  188.3 6.1 %copy-start.17 = (bf16[4,80,512]{2,1,0:T(8,128)(2,1)S(1)}, bf16[4,80,512]{2,1,0:T(8,128)(2,1)}, u32[]{:S(2)}) copy-start(bf16[4,80,512]{2,1,0:T(8,128)(2,1)} %get-tuple-element.203) | copy-start | bytes 983044
  188.3 8.1 %copy-start.21 = (bf16[4,16,2048]{2,1,0:T(8,128)(2,1)S(1)}, bf16[4,16,2048]{2,1,0:T(8,128)(2,1)}, u32[]{:S(2)}) copy-start(bf16[4,16,2048]{2,1,0:T(8,128)(2,1)} %get-tuple-element.205) | copy-start | bytes 786436
  190.6 46.5 %all-to-all-start.1 = ((bf16[16,16,1536]{2,1,0:T(8,128)(2,1)}), bf16[16,16,1536]{2,1,0:T(8,128)(2,1)S(1)}, u32[]{:S(2)}, u32[]{:S(2)}) async-start(bf16[16,16,1536]{2,1,0:T(8,128)(2,1)} %bitcast.54), calls=%async_computation.1 | async-start | bytes 1572864 | tf_op jit(solution)/shard_map/all_to_all | solution.py:1142
  194.4 16.1 %collective-permute-start.32 = (bf16[320,512]{1,0:T(8,128)(2,1)S(1)}, bf16[320,512]{1,0:T(8,128)(2,1)S(1)}, u32[]{:S(2)}, u32[]{:S(2)}) collective-permute-start(bf16[320,512]{1,0:T(8,128)(2,1)S(1)} %bitcast.63), channel_id=1, source_target_pairs={{0,2},{2,0},{4,6},{6,4},{8,10},{10,8},{12,14},{14,12},{16,18},{18,... | collective-permute-start | bytes 983048 | tf_op jit(solution)/shard_map/ppermute | solution.py:1112
  196.4 13.0 %collective-permute-start.33 = (bf16[64,2048]{1,0:T(8,128)(2,1)S(1)}, bf16[64,2048]{1,0:T(8,128)(2,1)S(1)}, u32[]{:S(2)}, u32[]{:S(2)}) collective-permute-start(bf16[64,2048]{1,0:T(8,128)(2,1)S(1)} %bitcast.65), channel_id=1, source_target_pairs={{0,4},{2,6},{4,0},{6,2},{8,12},{10,14},{12,8},{14,10},{16,20},{18,... | collective-permute-start | bytes 786440 | tf_op jit(solution)/shard_map/ppermute | solution.py:1112
  204.8 12.8 %collective-permute-start.31 = (f32[8,512]{1,0:T(8,128)}, f32[8,512]{1,0:T(8,128)S(1)}, u32[]{:S(2)}, u32[]{:S(2)}) collective-permute-start(f32[8,512]{1,0:T(8,128)} %get-tuple-element.201.refs_0_), channel_id=1, source_target_pairs={{0,1},{1,0},{2,3},{3,2},{4,5},{5,4},{6,7},{7,6},{8,9},{9,8},{10,11... | collective-permute-start | bytes 49160 | tf_op jit(solution)/shard_map/ppermute | solution.py:1116
  213.4 17.9 %collective-permute-start.37 = (bf16[288,512]{1,0:T(8,128)(2,1)}, bf16[288,512]{1,0:T(8,128)(2,1)S(1)}, u32[]{:S(2)}, u32[]{:S(2)}) collective-permute-start(bf16[288,512]{1,0:T(8,128)(2,1)} %get-tuple-element.214), channel_id=1, source_target_pairs={{0,16},{2,18},{4,20},{6,22},{8,24},{10,26},{12,28},{14,30},{16,0},... | collective-permute-start | bytes 884744 | tf_op jit(solution)/shard_map/ppermute | solution.py:1112
  219.5 3.9 %collective-permute-start.34 = (f32[8,512]{1,0:T(8,128)}, f32[8,512]{1,0:T(8,128)S(1)}, u32[]{:S(2)}, u32[]{:S(2)}) collective-permute-start(f32[8,512]{1,0:T(8,128)} %get-tuple-element.208.refs_0_), channel_id=1, source_target_pairs={{0,2},{2,0},{4,6},{6,4},{8,10},{10,8},{12,14},{14,12},{16,18},{18,... | collective-permute-start | bytes 49160 | tf_op jit(solution)/shard_map/ppermute | solution.py:1112
  225.4 3.9 %collective-permute-start.35 = (f32[8,512]{1,0:T(8,128)}, f32[8,512]{1,0:T(8,128)S(1)}, u32[]{:S(2)}, u32[]{:S(2)}) collective-permute-start(f32[8,512]{1,0:T(8,128)} %get-tuple-element.210.refs_0_), channel_id=1, source_target_pairs={{0,4},{2,6},{4,0},{6,2},{8,12},{10,14},{12,8},{14,10},{16,20},{18,... | collective-permute-start | bytes 49160 | tf_op jit(solution)/shard_map/ppermute | solution.py:1112
  231.3 3.9 %collective-permute-start.36 = (f32[8,512]{1,0:T(8,128)}, f32[8,512]{1,0:T(8,128)S(1)}, u32[]{:S(2)}, u32[]{:S(2)}) collective-permute-start(f32[8,512]{1,0:T(8,128)} %get-tuple-element.212.refs_0_), channel_id=1, source_target_pairs={{0,8},{2,10},{4,12},{6,14},{8,0},{10,2},{12,4},{14,6},{16,24},{18,... | collective-permute-start | bytes 49160 | tf_op jit(solution)/shard_map/ppermute | solution.py:1112
  237.2 10.9 %copy-start.1 = (bf16[16,16,1536]{2,1,0:T(8,128)(2,1)}, bf16[16,16,1536]{2,1,0:T(8,128)(2,1)S(1)}, u32[]{:S(2)}) copy-start(bf16[16,16,1536]{2,1,0:T(8,128)(2,1)S(1)} %all-to-all-done.1) | copy-start | bytes 2359300
  237.2 10.9 %collective-permute-start.40 = (bf16[256,1536]{1,0:T(8,128)(2,1)S(1)}, bf16[256,1536]{1,0:T(8,128)(2,1)S(1)}, u32[]{:S(2)}, u32[]{:S(2)}) collective-permute-start(bf16[256,1536]{1,0:T(8,128)(2,1)S(1)} %bitcast.52), channel_id=1, source_target_pairs={{0,1},{1,0},{2,3},{3,2},{4,5},{5,4},{6,7},{7,6},{8,9},{9,8},{10,11... | collective-permute-start | bytes 2359304 | tf_op jit(solution)/shard_map/ppermute | solution.py:1116
  237.2 6.6 %collective-permute-start.39 = (bf16[144,512]{1,0:T(8,128)(2,1)S(1)}, bf16[144,512]{1,0:T(8,128)(2,1)S(1)}, u32[]{:S(2)}, u32[]{:S(2)}) collective-permute-start(bf16[144,512]{1,0:T(8,128)(2,1)S(1)} %bitcast.67), channel_id=1, source_target_pairs={{0,8},{2,10},{4,12},{6,14},{8,0},{10,2},{12,4},{14,6},{16,24},{18,... | collective-permute-start | bytes 442376 | tf_op jit(solution)/shard_map/ppermute | solution.py:1112
  237.9 8.3 %collective-permute-start.38 = (f32[8,512]{1,0:T(8,128)}, f32[8,512]{1,0:T(8,128)S(1)}, u32[]{:S(2)}, u32[]{:S(2)}) collective-permute-start(f32[8,512]{1,0:T(8,128)} %get-tuple-element.217.refs_0_), channel_id=1, source_target_pairs={{0,16},{2,18},{4,20},{6,22},{8,24},{10,26},{12,28},{14,30},{16,0},... | collective-permute-start | bytes 49160 | tf_op jit(solution)/shard_map/ppermute | solution.py:1112
  (35 other events, 29.7 us)
where the time goes:
time: 254 us; the launch traced here: 252 us
  Pallas kernels  155 us (61%)
  starting transfers between devices  46.6 us (18%)
  waiting for transfers between devices  29.3 us (12%)
  local copies, waits for them, and re-layouts  18.7 us (7%)
    pallas_call x30, Pallas kernels, launch(): return lambda *args: call(*args, *deps)  155 us
    ppermute x25, starting transfers between devices, swap_img(): lax.ppermute(value, 'img', [(k, k ^ mask) for k in range(lax.axis_size('i...  33.9 us
    ppermute x25, waiting for transfers between devices, swap_img(): lax.ppermute(value, 'img', [(k, k ^ mask) for k in range(lax.axis_size('i...  25.2 us
    unnamed x113, local copies, waits for them, and re-layouts  16.9 us
    all_to_all x2, starting transfers between devices, spread(): return lax.all_to_all(value, 'img', split_axis=0, concat_axis=0, tiled=True)  9.28 us
  transfers between devices with their start and end apart: 43, of which 10 were waited for; matrix products, arithmetic and copies ran while one was open for 1% of the time, Pallas kernels for 39%

commit v1 on v0

--- a/solution.py
+++ b/solution.py
@@ -77,6 +77,10 @@
     return jnp.where((row < high) & (col < wide), 1.0, 0.0).astype(f32)
 
 
+def pair_mask(sizes, row_par):
+    return jnp.concatenate([chunk_mask(sizes, row_par, col_par) for col_par in range(2)], axis=0)
+
+
 def halo_sizes(valid_ref, halo_ref):
     heights, widths = extents(valid_ref)
     below, _ = extents(halo_ref)
@@ -84,8 +88,8 @@
     return [jnp.where(upper, h, 4) for h in below], widths
 
 
-def halo_base():
-    return jnp.where(lax.axis_index("row") == 0, 8, -2).astype(i32)
+def is_upper():
+    return jnp.where(lax.axis_index("row") == 0, 1.0, 0.0).astype(f32)
 
 
 def vectors_kernel(in_ref, dw_ref, gate_ref, exp_ref, *rest):
@@ -119,7 +123,7 @@
     )(*large, *small)
 
 
-def prepare_kernel(valid_ref, halo_valid_ref, x_ref, xh_ref, g_ref, vec_ref, xp_ref, gp_ref, y1_ref, y1h_ref):
+def prepare_kernel(valid_ref, halo_valid_ref, x_ref, xh_ref, g_ref, vec_ref, xp_ref, gp_ref, y1_ref, y1h_ref, y1t_ref):
     perm = permutation()
     gain, shift = vec_ref[8:9, 0:512], vec_ref[8:9, 512:1024]
     own, halo = extents(valid_ref), halo_sizes(valid_ref, halo_valid_ref)
@@ -145,6 +149,8 @@
                 xp_ref[q, dest] = lowered[part]
                 gp_ref[q, dest] = gblock[part]
                 y1_ref[q, dest] = (chunk_mask(own, q // 2, q % 2, 64, 4 * b) * value[part]).astype(bf16)
+    for q in range(4):
+        y1t_ref[:, q * 256 : (q + 1) * 256] = y1_ref[q].T
 
 
 def whole(shape):
@@ -220,9 +226,10 @@
             jax.ShapeDtypeStruct((4, 256, 512), bf16),
             jax.ShapeDtypeStruct((4, 256, 512), bf16),
             jax.ShapeDtypeStruct((4, 64, 512), bf16),
+            jax.ShapeDtypeStruct((512, 1024), bf16),
         ),
         in_specs=[SMEM] * 2 + [vmem] * 4,
-        out_specs=(vmem,) * 4,
+        out_specs=(vmem,) * 5,
         cost_estimate=takes(4),
         name="prepare",
     )(valid, halo_valid, x, xh, g, wide)
@@ -271,21 +278,21 @@
             cache[name, step, ccp] = shifted_block(value[:, ccp].reshape(n * 2, 8, 128), step)
         return cache[name, step, ccp]
 
-    for k in range(5):
+    def write(k):
         both = jnp.where(low, take("o", odd, *ODD[k]), take("e", even, *EVEN[k]))
-        ref[lead + (pl.ds(start, n), k, slice(None), lanes)] = both.reshape(n, 16, 128).astype(bf16)
-
-
-def fill_group(ref, lead, own, halo, base):
-    other = 6 - base
+        ref[lead + (slice(start, start + n), k, slice(None), lanes)] = both.reshape(n, 16, 128).astype(bf16)
+
+    return [functools.partial(write, k) for k in range(5)]
+
+
+def fill_group(ref, lead, own, halo, upper):
+    steps = []
     for row_par in range(2):
         first = 2 + row_par
-        half = 1 - row_par
-        fill_band(ref, lead, own[row_par], 8, first, row_par)
-        fill_band(ref, lead, halo[row_par], 2, base + first, row_par)
-        ref[lead + (pl.ds(other + first, 2), slice(None), slice(None), slice(half * 128, half * 128 + 128))] = jnp.zeros(
-            (2, 5, 16, 128), bf16
-        )
+        steps += fill_band(ref, lead, own[row_par], 8, first, row_par)
+        steps += fill_band(ref, lead, [v * (1.0 - upper) for v in halo[row_par]], 2, first - 2, row_par)
+        steps += fill_band(ref, lead, [v * upper for v in halo[row_par]], 2, first + 8, row_par)
+    return steps
 
 
 def diagonal(rows):
@@ -297,21 +304,23 @@
     low = low_lanes((1, 128))
     tile, side = group // 2, group % 2
     cols = slice(tile * 128, tile * 128 + 128)
-    for i in range(7):
+
+    def write(i, jj):
         rows = tap_ref[6 - i if flip else i, :, cols]
         turned = swap_lanes(rows)
         first, second = (rows, turned) if side == 0 else (turned, rows)
-        for jj in range(8):
-            a, b = (6 - jj, 7 - jj) if flip else (jj, jj - 1)
-            left = first[a : a + 1] if 0 <= a <= 6 else jnp.zeros((1, 128), f32)
-            right = second[b : b + 1] if 0 <= b <= 6 else jnp.zeros((1, 128), f32)
-            vector = jnp.where(low, left, right)
-            block = jnp.where(mask, jnp.broadcast_to(vector, (64, 128)), 0.0).astype(bf16)
-            for out_par in range(2):
-                top = i + out_par
-                ti, rp, tj, cp = top // 2, top % 2, jj // 2, jj % 2
-                at = (rp * 2 + cp) * 64
-                w_ref[slot, ti * 4 + tj, at : at + 64, out_par * 128 : out_par * 128 + 128] = block
+        a, b = (6 - jj, 7 - jj) if flip else (jj, jj - 1)
+        left = first[a : a + 1] if 0 <= a <= 6 else jnp.zeros((1, 128), f32)
+        right = second[b : b + 1] if 0 <= b <= 6 else jnp.zeros((1, 128), f32)
+        vector = jnp.where(low, left, right)
+        block = jnp.where(mask, jnp.broadcast_to(vector, (64, 128)), 0.0).astype(bf16)
+        for out_par in range(2):
+            top = i + out_par
+            ti, rp, tj, cp = top // 2, top % 2, jj // 2, jj % 2
+            at = (rp * 2 + cp) * 64
+            w_ref[slot, ti * 4 + tj, at : at + 64, out_par * 128 : out_par * 128 + 128] = block
+
+    return [functools.partial(write, i, jj) for i in range(7) for jj in range(8)]
 
 
 def clear_weights(w_ref):
@@ -325,13 +334,28 @@
     return ref[lead + (slice(1 + ti, 9 + ti), slice(tj, tj + 2))].reshape(256, 256)
 
 
-def convolve(ref, lead, w_ref, slot):
+def convolve(ref, lead, w_ref, slot, meanwhile):
     total = None
-    for ti in range(4):
-        for tj in range(4):
-            part = dot(band_block(ref, lead, ti, tj), w_ref[slot, ti * 4 + tj])
-            total = part if total is None else total + part
+    for k in range(16):
+        part = dot(band_block(ref, lead, k // 4, k % 4), w_ref[slot, k])
+        total = part if total is None else total + part
+        for step in meanwhile[len(meanwhile) * k // 16 : len(meanwhile) * (k + 1) // 16]:
+            step()
     return total
+
+
+def convolve_groups(ref, w_ref, tap_ref, own, halo, upper, flip):
+    def steps(group):
+        cols = slice(group // 2 * 128, group // 2 * 128 + 128)
+        own_pairs = lane_pairs([v[:, cols] for v in own])
+        halo_pairs = lane_pairs([v[:, cols] for v in halo])
+        side = group % 2
+        band = [own_pairs[rp, side] for rp in range(2)], [halo_pairs[rp, side] for rp in range(2)]
+        return fill_group(ref, (group,), *band, upper) + build_weights(w_ref, side, tap_ref, group, flip)
+
+    for step in steps(0):
+        step()
+    return [convolve(ref, (group,), w_ref, group % 2, steps(group + 1) if group < 3 else []) for group in range(4)]
 
 
 def split_lanes(low_group, high_group):
@@ -353,12 +377,14 @@
     def _():
         clear_weights(w_ref)
 
-    base = halo_base()
+    upper = is_upper()
     sizes, around = extents(valid_ref), halo_sizes(valid_ref, halo_valid_ref)
     place_rows(win_ref, weights, order, own_number(dealt), 16)
     weight = win_ref[...]
     bias = wide_ref[0:1]
-    joined = [dot(y1_ref[q], weight) + bias for q in range(4)]
+    joined = dot(y1_ref[...].reshape(1024, 512), weight) + bias
+    joined = [joined[q * 256 : (q + 1) * 256] for q in range(4)]
+    around_rows = dot(y1h_ref[...].reshape(256, 512), weight) + bias
 
     @pl.when(step == 0)
     def _():
@@ -368,25 +394,12 @@
     own, halo = [], []
     for q in range(4):
         own.append((joined[q] * chunk_mask(sizes, q // 2, q % 2)).astype(bf16).astype(f32))
-        part = dot(y1h_ref[q], weight) + bias
+        part = around_rows[q * 64 : (q + 1) * 64]
         halo.append((part * chunk_mask(around, q // 2, q % 2, 64)).astype(bf16).astype(f32))
+    sums = convolve_groups(band_ref, w_ref, tap_ref, own, halo, upper, False)
     for tile in range(2):
         cols = slice(tile * 128, tile * 128 + 128)
-        own_pairs = lane_pairs([v[:, cols] for v in own])
-        halo_pairs = lane_pairs([v[:, cols] for v in halo])
-        sums = []
-        for side in range(2):
-            group = tile * 2 + side
-            fill_group(
-                band_ref,
-                (group,),
-                [own_pairs[rp, side] for rp in range(2)],
-                [halo_pairs[rp, side] for rp in range(2)],
-                base,
-            )
-            build_weights(w_ref, side, tap_ref, group)
-            sums.append(convolve(band_ref, (group,), w_ref, side))
-        for q, value in enumerate(split_lanes(*sums)):
+        for q, value in enumerate(split_lanes(*sums[2 * tile : 2 * tile + 2])):
             d_ref[q, :, cols] = (value + wide_ref[1:2, cols]) * conv_scale
 
 
@@ -437,11 +450,11 @@
     wide_ref,
     out_ref,
     act_ref,
+    y2_ref,
+    u_ref,
     dh_ref,
-    y2_ref,
     df_ref,
     dz_ref,
-    u_ref,
     dv_ref,
     dd_ref,
     dx2_ref,
@@ -459,11 +472,11 @@
     dealt,
 ):
     q = pl.program_id(0)
-    mask = chunk_mask(extents(valid_ref), q // 2, q % 2)
+    mask = pair_mask(extents(valid_ref), q)
     out_bias, mix, gain, shift, red_bias, ffn = (
         wide_ref[5 + k // 2 : 6 + k // 2, k % 2 * 512 : k % 2 * 512 + 512] for k in range(6)
     )
-    lane = lax.broadcasted_iota(i32, (256, 128), 1)
+    lane = lax.broadcasted_iota(i32, (512, 128), 1)
     is0 = (lane >= 32) & (lane < 64)
     is1 = lane >= 64
 
@@ -480,8 +493,9 @@
         place_rows(w_out_ref, (oa, ob, oc, od), order, number, 16)
         place_rows(w_exp_ref, (ea, eb4, ec, ed), order, number, 16)
         for p in range(32):
-            at = pl.multiple_of(dealt_owner(p, "plain" if dealt else "none") * 64, 64)
-            w_red_ref[pl.ds(at, 64), :] = (ra, rb)[p // 16][p % 16 * 64 : (p % 16 + 1) * 64, :]
+            owner = dealt_owner(p, "plain" if dealt else "none")
+            ref, first = (ra, rb)[p // 16], p % 16 * 64
+            w_red_ref[pl.ds(pl.multiple_of(owner * 64, 64), 64), :] = ref[first : first + 64, :]
 
     d01, d2, d3, d4 = d_ref[:, 0:128], d_ref[:, 128:256], d_ref[:, 256:512], d_ref[:, 512:1024]
     pointwise = pltpu.roll(j0_ref[...], 32, axis=1)
@@ -494,33 +508,33 @@
     u3 = (v3 * d3).astype(bf16)
     v4 = dot(u3, g4_ref[...]) + wide_ref[2:3, 512:1024]
     u4 = (v4 * d4).astype(bf16)
-    u_ref[:, 0:128] = jnp.where(is1, u1, u0)
-    u_ref[:, 128:256] = u2
-    u_ref[:, 256:512] = u3
-    u_ref[:, 512:1024] = u4
+    u_ref[0:128] = jnp.where(is1, u1, u0).T
+    u_ref[128:256] = u2.T
+    u_ref[256:512] = u3.T
+    u_ref[512:1024] = u4.T
     branch = dot(u4, w_out_ref[...]) + out_bias
     middle = xp_ref[...].astype(f32) + mask * mix * branch
     normed, inverse = normalize(middle)
     y2 = (mask * (normed * gain + shift)).astype(bf16)
-    y2_ref[...] = y2
+    y2_ref[...] = y2.T
     grad = gp_ref[...].astype(f32)
     df = (mask * ffn * grad).astype(bf16)
     df_ref[...] = df
     reduced = red_bias
-    back = jnp.zeros((256, 512), f32)
+    back = jnp.zeros((512, 512), f32)
     for k in range(4):
         cols = slice(k * 512, (k + 1) * 512)
         hidden = dot(y2, w_exp_ref[:, cols]) + wide_ref[3 + k // 2 : 4 + k // 2, k % 2 * 512 : k % 2 * 512 + 512]
         cdf = 0.5 * (1.0 + lax.erf(hidden * inv_root_two))
         act = (hidden * cdf).astype(bf16)
-        act_ref[:, cols] = act
+        act_ref[cols, :] = act.T
         reduced = reduced + dot(act, w_red_ref[cols, :])
         density = jnp.exp(-0.5 * hidden * hidden) * inv_root_tau
         dh = (dot_nt(df, w_red_ref[cols, :]) * (cdf + hidden * density)).astype(bf16)
         dh_ref[:, cols] = dh
         s2048_ref[:, cols] += column_sum(dh.astype(f32))
         back = back + dot_nt(dh, w_exp_ref[:, cols])
-    held_ref[q] = (middle + mask * ffn * reduced).astype(bf16)
+    held_ref[pl.ds(2 * q, 2)] = (middle + mask * ffn * reduced).astype(bf16).reshape(2, 256, 512)
     s512_ref[0:1] += column_sum(grad * mask * reduced)
     s512_ref[1:2] += column_sum(df.astype(f32))
     back = mask * back
@@ -557,7 +571,7 @@
     for k, ref in enumerate((dv_ref, dd_ref)):
         s1024_ref[k : k + 1] += column_sum(ref[...].astype(f32))
 
-    @pl.when(q == 3)
+    @pl.when(q == 1)
     def _():
         unpermute(held_ref, out_ref)
 
@@ -573,17 +587,25 @@
 
 def middle_call(valid, d, j0, xp, gp, w_exp, w_red, g1, g2, g3, g4, wide, order, dealt, deps=()):
     def chunk(width):
-        return pl.BlockSpec((None, 256, width), lambda q: (q, 0, 0))
+        return pl.BlockSpec((512, width), lambda q: (q, 0))
 
     def out(width, dtype=bf16):
-        return jax.ShapeDtypeStruct((4, 256, width), dtype)
-
-    widths = (2048, 2048, 512, 512, 512, 1024, 1024, 1024)
+        return jax.ShapeDtypeStruct((1024, width), dtype)
+
+    def turned(rows):
+        return pl.BlockSpec((rows, 512), lambda q: (0, q))
+
+    def out_turned(rows):
+        return jax.ShapeDtypeStruct((rows, 1024), bf16)
+
+    widths = (2048, 512, 512, 1024, 1024)
+    rows = (2048, 512, 1024)
     return launch(
         deps,
         functools.partial(middle_kernel, order=order, dealt=dealt),
-        grid=(4,),
+        grid=(2,),
         out_shape=(jax.ShapeDtypeStruct((2, 512, 512), bf16),)
+        + tuple(out_turned(r) for r in rows)
         + tuple(out(w) for w in widths)
         + (
             out(512, f32),
@@ -597,6 +619,7 @@
         + [whole((1024, 512))] * 2
         + [whole(v.shape) for v in (g1, g2, g3, g4, wide)],
         out_specs=(whole((2, 512, 512)),)
+        + tuple(turned(r) for r in rows)
         + tuple(chunk(w) for w in widths)
         + (chunk(512), whole((8, 512)), whole((1, 2048)), whole((8, 1024))),
         scratch_shapes=[
@@ -609,11 +632,11 @@
         ],
         cost_estimate=takes(30),
         name="middle",
-    )(valid, d, j0, xp, gp, *w_exp, *w_exp, *w_red, g1, g2, g3, g4, wide)
+    )(valid, *(v.reshape(1024, -1) for v in (d, j0, xp, gp)), *w_exp, *w_exp, *w_red, g1, g2, g3, g4, wide)
 
 
 def expand_grad_kernel(y2_ref, dh_ref, keep, send, sum_ref, *, order):
-    sum_ref[...] = dot_tn(y2_ref[...], dh_ref[...])
+    sum_ref[...] = dot(y2_ref[...], dh_ref[...])
     deal_rows((keep, send), (slice(None),), sum_ref, order, 16)
 
 
@@ -623,7 +646,7 @@
         functools.partial(expand_grad_kernel, order=order),
         grid=(4,),
         out_shape=(jax.ShapeDtypeStruct((256, 2048), bf16),) * 2,
-        in_specs=[whole((1024, 512)), pl.BlockSpec((1024, 512), lambda k: (0, k))],
+        in_specs=[whole((512, 1024)), pl.BlockSpec((1024, 512), lambda k: (0, k))],
         out_specs=(pl.BlockSpec((256, 512), lambda k: (0, k)),) * 2,
         scratch_shapes=[pltpu.VMEM((512, 512), f32)],
         cost_estimate=takes(5),
@@ -633,11 +656,11 @@
 
 def reduce_grad_kernel(act_ref, df_ref, u_ref, dz_ref, keep, send, red_ref, out_ref, *, order):
     step = pl.program_id(0)
-    red_ref[pl.ds(pl.multiple_of(step * 512, 512), 512), :] = dot_tn(act_ref[...], df_ref[...])
+    red_ref[pl.ds(pl.multiple_of(step * 512, 512), 512), :] = dot(act_ref[...], df_ref[...])
 
     @pl.when(step == 0)
     def _():
-        out_ref[...] = dot_tn(u_ref[...], dz_ref[...])
+        out_ref[...] = dot(u_ref[...], dz_ref[...])
 
     @pl.when(step == 3)
     def _():
@@ -655,9 +678,9 @@
         grid=(4,),
         out_shape=(jax.ShapeDtypeStruct((1280, 512), bf16),) * 2,
         in_specs=[
-            pl.BlockSpec((1024, 512), lambda k: (0, k)),
+            pl.BlockSpec((512, 1024), lambda k: (k, 0)),
             whole((1024, 512)),
-            pl.BlockSpec((1024, 512), lambda k: (0, 1)),
+            pl.BlockSpec((512, 1024), lambda k: (1, 0)),
             whole((1024, 512)),
         ],
         out_specs=(whole((1280, 512)),) * 2,
@@ -723,11 +746,11 @@
 
 
 def gate_grads_kernel(u_ref, dv_ref, s512_ref, s2048_ref, s1024_ref, dk_ref, keep, send, small_ref, *, order):
-    small_ref[0:256] = dot_tn(u_ref[:, 256:512], dv_ref[:, 512:1024])
-    g3 = dot_tn(u_ref[:, 128:256], dv_ref[:, 256:512])
+    small_ref[0:256] = dot(u_ref[256:512], dv_ref[:, 512:1024])
+    g3 = dot(u_ref[128:256], dv_ref[:, 256:512])
     small_ref[256:320, 0:256] = g3[0:64]
     small_ref[256:320, 256:512] = g3[64:128]
-    g12 = dot_tn(u_ref[:, 0:128], dv_ref[:, 0:256])
+    g12 = dot(u_ref[0:128], dv_ref[:, 0:256])
     for k in range(4):
         cols = slice(k * 128, (k + 1) * 128)
         small_ref[320:336, cols] = g12[64 + 16 * k : 80 + 16 * k, 128:256]
@@ -746,7 +769,7 @@
         functools.partial(gate_grads_kernel, order=order),
         grid=(1,),
         out_shape=(jax.ShapeDtypeStruct((256, 512), bf16),) * 2,
-        in_specs=[whole((1024, 512))] + [whole(v.shape) for v in (dv, s512, s2048, s1024, dk)],
+        in_specs=[whole((512, 1024))] + [whole(v.shape) for v in (dv, s512, s2048, s1024, dk)],
         out_specs=(whole((256, 512)),) * 2,
         scratch_shapes=[pltpu.VMEM((512, 512), f32)],
         cost_estimate=takes(3),
@@ -827,32 +850,18 @@
     def _():
         clear_weights(w_ref)
 
-    base = halo_base()
     sizes = extents(valid_ref)
-    masks = [chunk_mask(sizes, q // 2, q % 2) for q in range(4)]
     lane = lax.broadcasted_iota(i32, (256, 128), 1)
     keep = (lane < 32) & (step == 0)
+    own = [dd_ref[q].astype(f32) for q in range(4)]
+    halo = [ddh_ref[q].astype(f32) for q in range(4)]
+    sums = convolve_groups(back_ref, w_ref, tap_ref, own, halo, is_upper(), True)
     for tile in range(2):
         cols = slice(tile * 128, tile * 128 + 128)
-        own = [dd_ref[q, :, cols].astype(f32) for q in range(4)]
-        own_pairs = lane_pairs(own)
-        halo_pairs = lane_pairs([ddh_ref[q, :, cols].astype(f32) for q in range(4)])
-        sums = []
-        for side in range(2):
-            group = tile * 2 + side
-            fill_group(
-                back_ref,
-                (group,),
-                [own_pairs[rp, side] for rp in range(2)],
-                [halo_pairs[rp, side] for rp in range(2)],
-                base,
-            )
-            build_weights(w_ref, side, tap_ref, group, True)
-            sums.append(convolve(back_ref, (group,), w_ref, side))
-        for q, value in enumerate(split_lanes(*sums)):
-            value = value * (masks[q] * conv_scale)
+        for q, value in enumerate(split_lanes(*sums[2 * tile : 2 * tile + 2])):
+            value = value * (chunk_mask(sizes, q // 2, q % 2) * conv_scale)
             if tile == 0 and offset == 0:
-                value = jnp.where(keep, own[q], value)
+                value = jnp.where(keep, own[q][:, cols], value)
             df_ref[q, :, cols] = value.astype(bf16)
 
 
@@ -877,7 +886,7 @@
 
 def in_grad_kernel(y1_ref, da_ref, db_ref, keep, send, sum_ref, *, order):
     for k, ref in enumerate((da_ref, db_ref)):
-        sum_ref[k] = dot_tn(y1_ref[...], ref[...])
+        sum_ref[k] = dot(y1_ref[...], ref[...])
         deal_rows((keep, send), (slice(k * 512, (k + 1) * 512),), sum_ref.at[k], order, 16)
 
 
@@ -904,7 +913,7 @@
         late_ref[...] = jnp.zeros_like(late_ref)
         place_rows(win_ref, weights, order, own_number(dealt), 16)
 
-    mask = chunk_mask(extents(valid_ref), q // 2, q % 2)
+    mask = pair_mask(extents(valid_ref), q)
     da, db = da_ref[...], db_ref[...]
     late_ref[2:3] += column_sum(da.astype(f32))
     late_ref[3:4] += column_sum(db.astype(f32))
@@ -912,28 +921,29 @@
     normed, inverse = normalize(xp_ref[...].astype(f32))
     late_ref[0:1] += column_sum(grad * normed)
     late_ref[1:2] += column_sum(grad)
-    held_ref[q] = (dx2_ref[...] + norm_backward(grad, normed, inverse, wide_ref[8:9, 0:512])).astype(bf16)
-
-    @pl.when(q == 3)
+    total = dx2_ref[...] + norm_backward(grad, normed, inverse, wide_ref[8:9, 0:512])
+    held_ref[pl.ds(2 * q, 2)] = total.astype(bf16).reshape(2, 256, 512)
+
+    @pl.when(q == 1)
     def _():
         unpermute(held_ref, out_ref)
 
 
 def last_call(valid, da, db, xp, dx2, w_in, wide, order, dealt, deps=()):
     def chunk(width):
-        return pl.BlockSpec((None, 256, width), lambda q: (q, 0, 0))
+        return pl.BlockSpec((512, width), lambda q: (q, 0))
 
     return launch(
         deps,
         functools.partial(last_kernel, order=order, dealt=dealt),
-        grid=(4,),
+        grid=(2,),
         out_shape=(jax.ShapeDtypeStruct((2, 512, 512), bf16), jax.ShapeDtypeStruct((8, 512), f32)),
         in_specs=[SMEM] + [chunk(512)] * 4 + [whole((64, 1024))] * 8 + [whole(wide.shape)],
         out_specs=(whole((2, 512, 512)), whole((8, 512))),
         scratch_shapes=[pltpu.VMEM((4, 256, 512), bf16), pltpu.VMEM((512, 1024), bf16)],
         cost_estimate=takes(7),
         name="last",
-    )(valid, da, db, xp, dx2, *w_in, wide)
+    )(valid, *(v.reshape(1024, -1) for v in (da, db, xp, dx2)), *w_in, wide)
 
 
 def repeat(value):
@@ -982,28 +992,29 @@
     )(a, b)
 
 
-def combine_kernel(*refs, parts):
-    count = len(parts)
-    ins, outs = refs[: 2 * count], list(refs[2 * count :])
-    for k, n in enumerate(parts):
-        for part in range(n):
-            total = ins[2 * k][part, 0].astype(f32) + ins[2 * k + 1][part, 0].astype(f32)
+def combine_kernel(*refs, items):
+    at = sum(n for n, _ in items)
+    ins, outs = list(refs[:at]), list(refs[at:])
+    for count, parts in items:
+        terms = [ins.pop(0) for _ in range(count)]
+        for part in range(parts):
+            total = functools.reduce(lambda a, b: a + b, [v[part, 0].astype(f32) for v in terms])
             outs.pop(0)[0] = total.astype(bf16)
 
 
 def combine(*items, deps=()):
-    steps = next(n for n in (4, 2, 1) if all(v.shape[0] % (16 * n * p) == 0 for v, _, p in items))
+    steps = next(n for n in (4, 2, 1) if all(v[0].shape[0] % (16 * n * p) == 0 for v, p in items))
     ins, in_specs, outs, out_specs = [], [], [], []
-    for keep, got, parts in items:
-        rows, cols = keep.shape
+    for terms, parts in items:
+        rows, cols = terms[0].shape
         size = rows // parts // steps
-        ins += [v.reshape(parts, steps, size, cols) for v in (keep, got)]
-        in_specs += [pl.BlockSpec((parts, 1, size, cols), lambda t: (0, t, 0, 0))] * 2
+        ins += [v.reshape(parts, steps, size, cols) for v in terms]
+        in_specs += [pl.BlockSpec((parts, 1, size, cols), lambda t: (0, t, 0, 0))] * len(terms)
         outs += [jax.ShapeDtypeStruct((steps, size, cols), bf16)] * parts
         out_specs += [pl.BlockSpec((1, size, cols), lambda t: (t, 0, 0))] * parts
     *values, token = launch(
         deps,
-        functools.partial(combine_kernel, parts=[p for _, _, p in items]),
+        functools.partial(combine_kernel, items=[(len(v), p) for v, p in items]),
         grid=(steps,),
         out_shape=tuple(outs),
         in_specs=in_specs,
@@ -1014,14 +1025,13 @@
     return [v.reshape(-1, v.shape[-1]) for v in values] + [token]
 
 
-def merge_kernel(ro_a, ro_b, e_a, e_b, keep, send):
-    for z in range(4):
-        ref, first = (keep, send)[z // 2], z % 2 * 144
+def merge_kernel(ro_a, ro_b, e_a, e_b, *outs):
+    for z, ref in enumerate(outs):
         rows = slice(z * 80, (z + 1) * 80)
-        ref[first : first + 80] = (ro_a[rows].astype(f32) + ro_b[rows].astype(f32)).astype(bf16)
+        ref[0:80] = (ro_a[rows].astype(f32) + ro_b[rows].astype(f32)).astype(bf16)
         total = e_a[z * 16 : (z + 1) * 16].astype(f32) + e_b[z * 16 : (z + 1) * 16].astype(f32)
         for c in range(4):
-            at = first + 80 + c * 16
+            at = 80 + c * 16
             ref[at : at + 16] = total[:, c * 512 : (c + 1) * 512].astype(bf16)
 
 
@@ -1030,54 +1040,56 @@
     return launch(
         deps,
         merge_kernel,
-        out_shape=(jax.ShapeDtypeStruct((288, 512), bf16),) * 2,
+        out_shape=(jax.ShapeDtypeStruct((144, 512), bf16),) * 4,
         in_specs=[vmem] * 4,
-        out_specs=(vmem,) * 2,
+        out_specs=(vmem,) * 4,
         cost_estimate=takes(2),
         name="merge",
     )(ro_a, ro_b, e_a, e_b)
 
 
-def finish_kernel(a_ref, b_ref, red_ref, out_ref, exp_ref):
-    red_ref[...] = a_ref[0:64].astype(f32) + b_ref[0:64].astype(f32)
-    out_ref[...] = a_ref[64:80].astype(f32) + b_ref[64:80].astype(f32)
+def finish_kernel(*refs):
+    ins, (red_ref, out_ref, exp_ref) = refs[:-3], refs[-3:]
+    total = functools.reduce(lambda a, b: a + b, [v[...].astype(f32) for v in ins])
+    red_ref[...] = total[0:64]
+    out_ref[...] = total[64:80]
     for c in range(4):
-        rows = slice(80 + c * 16, 96 + c * 16)
-        exp_ref[:, c * 512 : (c + 1) * 512] = a_ref[rows].astype(f32) + b_ref[rows].astype(f32)
-
-
-def finish(a, b, deps=()):
+        exp_ref[:, c * 512 : (c + 1) * 512] = total[80 + c * 16 : 96 + c * 16]
+
+
+def finish(parts, deps=()):
     vmem = pl.BlockSpec(memory_space=pltpu.VMEM)
     shapes = ((64, 512), (16, 512), (16, 2048))
     return launch(
         deps,
         finish_kernel,
         out_shape=tuple(jax.ShapeDtypeStruct(v, f32) for v in shapes),
-        in_specs=[vmem] * 2,
+        in_specs=[vmem] * len(parts),
         out_specs=(vmem,) * 3,
         cost_estimate=takes(1),
         name="finish",
-    )(a, b)
-
-
-def deal_kernel(i_a, i_b, s_a, s_b, out_ref):
-    small = (s_a[...].astype(f32) + s_b[...].astype(f32)).astype(bf16)
+    )(*parts)
+
+
+def deal_kernel(i_a, i_b, *rest):
+    parts, out_ref = rest[:-1], rest[-1]
+    small = functools.reduce(lambda a, b: a + b, [v[...].astype(f32) for v in parts]).astype(bf16)
     out_ref[:, 0:1024] = (i_a[...].astype(f32) + i_b[...].astype(f32)).astype(bf16)
     for k in range(16):
         out_ref[k * 16 : (k + 1) * 16, 1024:1536] = small
 
 
-def deal(i_a, i_b, s_a, s_b, deps=()):
+def deal(i_a, i_b, parts, deps=()):
     vmem = pl.BlockSpec(memory_space=pltpu.VMEM)
     return launch(
         deps,
         deal_kernel,
         out_shape=jax.ShapeDtypeStruct((256, 1536), bf16),
-        in_specs=[vmem] * 4,
+        in_specs=[vmem] * (2 + len(parts)),
         out_specs=vmem,
         cost_estimate=takes(2),
         name="deal",
-    )(i_a, i_b, s_a, s_b)
+    )(i_a, i_b, *parts)
 
 
 def late_kernel(a_ref, b_ref, gain_ref, shift_ref, bias_ref):
@@ -1142,11 +1154,10 @@
     return lax.all_to_all(value, "img", split_axis=0, concat_axis=0, tiled=True)
 
 
-def sum_all(value):
-    value = value + swap_row(value)
-    for bit in range(img_bits() - 1):
+def sum_img(value, bits):
+    for bit in bits[:-1]:
         value = value + swap_img(value, 1 << bit)
-    return value, swap_img(value, 1 << (img_bits() - 1))
+    return value, swap_img(value, 1 << bits[-1])
 
 
 def own_bit(bit):
@@ -1225,14 +1236,12 @@
         exp_parts = swaps(exp_out, deep)
         red_own = spread(repeat(reduceweight))
         w_in = swaps(in_z, flat_pair)
-        xp, gp, y1, y1h, token = prepare(valid, halo_valid, x, x_halo, g, wide, [token])
+        xp, gp, y1, y1h, y1t, token = prepare(valid, halo_valid, x, x_halo, g, wide, [token])
         exp_z, token = join(exp_parts, deps=[token] + w_in[1:])
         w_in = w_in + [swap_row(v) for v in w_in]
         exp_y, token = join(swaps(exp_z, (1,)), deps=[token])
         w_exp = swaps(exp_y, (0,))
-        d, band, j0, token = forward(
-            valid, halo_valid, y1, y1h, w_in, wide, taps, in_order, dealt, [token]
-        )
+        d, band, j0, token = forward(valid, halo_valid, y1, y1h, w_in, wide, taps, in_order, dealt, [token])
         w_exp = w_exp + [swap_row(w_exp[0]), swap_row(after(w_exp[1], d))]
         w_red = [red_own, swap_row(after(red_own, d))]
     else:
@@ -1240,61 +1249,50 @@
         w_in = jnp.split(plain_gather(inweight), 8, axis=0)
         w_exp = jnp.split(plain_gather(exp_out), 4, axis=0)
         w_red = jnp.split(plain_gather(reduceweight), 2, axis=0)
-        xp, gp, y1, y1h, token = prepare(valid, halo_valid, x, x_halo, g, wide)
+        xp, gp, y1, y1h, y1t, token = prepare(valid, halo_valid, x, x_halo, g, wide)
         d, band, j0, token = forward(valid, halo_valid, y1, y1h, w_in, wide, taps, in_order, dealt)
-    (produced, act, dh, y2, df, dz, u, dv, dd, dx2, s512, s2048, s1024, token) = middle_call(
+    (produced, act, y2, u, dh, df, dz, dv, dd, dx2, s512, s2048, s1024, token) = middle_call(
         valid, d, j0, xp, gp, w_exp, w_red, gatefirst, gatesecond, gatethird, gatefourth, wide, exp_order, dealt
     )
+    dd = dd.reshape(4, 256, 1024)
     dd_halo = swap_row(jnp.where(lower, dd[:, 0:64], dd[:, 192:256]))
 
     def flat(value):
         return value.reshape(1024, -1)
 
     r_order, e_order, plain = ((1, 0, 3, 2), (0, 1, 3, 2), "plain") if dealt else ("none",) * 3
-    dk, token = kernel_grad(dd, band)
-    dk = dk.reshape(512, 128)
-    s_keep, s_send, token = gate_grads(flat(u), flat(dv), s512, s2048, s1024, dk, e_order, [token])
     if dealt:
+        e_keep, e_send, token = expand_grad(y2, flat(dh), e_order)
+        e_got = swap_row(e_send)
+        r_keep, r_send, token = reduce_grad(act, flat(df), u, flat(dz), r_order, [token])
+        r_got = swap_row(r_send)
+        dk, token = kernel_grad(dd, band, [token])
+        r_keep, r_send, e_keep, e_send, token = combine(([r_keep, r_got], 2), ([e_keep, e_got], 2), deps=[token])
+        r_got, e_got = swap_img(r_send, 2), swap_img(e_send, 1)
+        s_keep, s_send, token = gate_grads(
+            u, flat(dv), s512, s2048, s1024, dk.reshape(512, 128), flat_pair + deep, [token]
+        )
         s_got = swap_row(s_send)
-        e_keep, e_send, token = expand_grad(flat(y2), flat(dh), e_order, [token])
-        e_got = swap_row(e_send)
-        s_keep, s_send, token = combine((s_keep, s_got, 2), deps=[token])
-        s_got = swap_img(s_send, 1)
-        r_keep, r_send, token = reduce_grad(flat(act), flat(df), flat(u), flat(dz), r_order, [token])
-        r_got = swap_row(r_send)
-        s_keep, s_send, token = combine((s_keep, s_got, 2), deps=[token])
-        s_got = swap_img(s_send, 2)
         df_a, token = conv_back(valid, dd, dd_halo, taps, 0, 2, [token])
-        r_keep, r_send, e_keep, e_send, s_keep, s_send, token = combine(
-            (r_keep, r_got, 2), (e_keep, e_got, 2), (s_keep, s_got, 2), deps=[token]
+        *small, token = combine(([s_keep, s_got], 4), deps=[token])
+        small = small[:1] + [swap_img(v, m) for v, m in zip(small[1:], masks_of(flat_pair)[1:])]
+        df_b, token = conv_back(valid, dd, dd_halo, taps, 2, 2, [token])
+        r_keep, r_send, e_keep, e_send, *small, token = combine(
+            ([r_keep, r_got], 2), ([e_keep, e_got], 2), (small, 4), deps=[token]
         )
-        r_got, e_got, s_got = swap_img(r_send, 2), swap_img(e_send, 1), swap_img(s_send, 8)
-        df_b, token = conv_back(valid, dd, dd_halo, taps, 2, 2, [token])
-        s_keep, s_send, token = combine((s_keep, s_got, 2), deps=[token])
-        s_got = swap_img(s_send, 4)
-        i_keep, i_send, token = in_grad(flat(y1), flat(df_a), flat(df_b), plain, [token])
+        r_got, e_got = swap_img(r_send, 1), swap_img(e_send, 2)
+        small = small[:1] + [swap_img(v, m) for v, m in zip(small[1:], masks_of(deep)[1:])]
+        i_keep, i_send, token = in_grad(y1t, flat(df_a), flat(df_b), plain, [token])
         i_got = swap_row(i_send)
-        r_keep, r_send, e_keep, e_send, token = combine((r_keep, r_got, 2), (e_keep, e_got, 2), deps=[token])
-        r_got, e_got = swap_img(r_send, 1), swap_img(e_send, 2)
-        dealt_rows, token = deal(i_keep, i_got, s_keep, s_got, [token])
+        *parts, token = merge(r_keep, r_got, e_keep, e_got, [token])
+        parts = parts[:1] + [swap_img(v, m) for v, m in zip(parts[1:], masks_of(deep)[1:])]
+        fgrad, late, token = last_call(valid, df_a, df_b, xp, dx2, w_in, wide, in_order, dealt, [token])
+        red_sum, out_sum, exp_sum, token = finish(parts, [token])
+        dealt_rows, token = deal(i_keep, i_got, small, [token])
         mixed = spread(dealt_rows)
-        fgrad, late, token = last_call(valid, df_a, df_b, xp, dx2, w_in, wide, in_order, dealt, [token])
-        got = swap_row(late)
-        m_keep, m_send, token = merge(r_keep, r_got, e_keep, e_got, [token])
-        m_got = swap_img(m_send, 8)
-        late, token = add(late, got, [token])
-        got = swap_img(late, 1)
-        late, token = add(late, got, [token])
-        got = swap_img(late, 2)
-        late, token = add(late, got, [token])
-        got = swap_img(late, 4)
-        m_keep, m_send, token = combine((m_keep, m_got, 2), deps=[token])
-        m_got = swap_img(m_send, 4)
-        late, token = add(late, got, [token])
-        got = swap_img(late, 8)
-        red_sum, out_sum, exp_sum, token = finish(m_keep, m_got, [token])
+        late, got = sum_img(late + swap_row(late), (0, 1, 2, 3))
+        own, oth = mixed, swap_row(after(mixed, late))
         sums = late_sums(late, got, [token])
-        own, oth = mixed, swap_row(after(mixed, late))
     else:
 
         def total(parts, rows):
@@ -1302,13 +1300,15 @@
             return plain_scatter(value.reshape(32, -1, value.shape[1])[:, rows].reshape(-1, value.shape[1]))
 
         everything = slice(None)
-        e_parts = expand_grad(flat(y2), flat(dh), e_order)[:2]
-        r_parts = reduce_grad(flat(act), flat(df), flat(u), flat(dz), r_order)[:2]
+        dk, token = kernel_grad(dd, band)
+        s_keep, s_send, token = gate_grads(u, flat(dv), s512, s2048, s1024, dk.reshape(512, 128), plain)
+        e_parts = expand_grad(y2, flat(dh), e_order)[:2]
+        r_parts = reduce_grad(act, flat(df), u, flat(dz), r_order)[:2]
         df_a, _ = conv_back(valid, dd, dd_halo, taps, 0, 2)
         df_b, _ = conv_back(valid, dd, dd_halo, taps, 2, 2)
-        i_parts = in_grad(flat(y1), flat(df_a), flat(df_b), plain)[:2]
+        i_parts = in_grad(y1t, flat(df_a), flat(df_b), plain)[:2]
         fgrad, late, token = last_call(valid, df_a, df_b, xp, dx2, w_in, wide, in_order, dealt)
-        sums = late_sums(*sum_all(late))
+        sums = late_sums(*sum_img(late + swap_row(late), list(range(bits))))
         exp_sum, in_sum = total(e_parts, everything), total(i_parts, everything)
         red_sum, out_sum = total(r_parts, slice(0, 64)), total(r_parts, slice(64, 80))
         small = plain_gather(total((s_keep, s_send), everything).astype(bf16)).reshape(16, 2, 16, 512)

time: 254 us -> 235 us (0.925)
  Pallas kernels: 155 us -> 138 us
  starting transfers between devices: 46.6 us -> 52.2 us
  local copies, waits for them, and re-layouts: 18.7 us -> 14.3 us
    pallas_call x30 -> x23, Pallas kernels: 155 us -> 138 us  [launch(): return lambda *args: call(*args, *deps)]
    ppermute x25 -> x28, waiting for transfers between devices: 25.2 us -> 19.9 us  [swap_img(): lax.ppermute(value, 'img', [(k, k ^ mask) for k in range(lax.axis_size('i...]
    ppermute x25 -> x28, starting transfers between devices: 33.9 us -> 38.7 us  [swap_img(): lax.ppermute(value, 'img', [(k, k ^ mask) for k in range(lax.axis_size('i...]
    unnamed x113, local copies, waits for them, and re-layouts: 16.9 us -> 12.5 us
    all_to_all x2, waiting for transfers between devices: 0.01 us -> 2.81 us  [spread(): return lax.all_to_all(value, 'img', split_axis=0, concat_axis=0, tiled=True)]
  transfers between devices with their start and end apart: 43 -> 46, of which waited for: 10 -> 14; matrix products, arithmetic and copies ran while one was open for 1% -> 1% of each run, Pallas kernels for 39% -> 38%
where the time goes in v1:
time: 235 us; the launch traced here: 234 us
  Pallas kernels  138 us (59%)
  starting transfers between devices  52.2 us (22%)
  waiting for transfers between devices  27.2 us (12%)
  local copies, waits for them, and re-layouts  14.3 us (6%)
    pallas_call x23, Pallas kernels, launch(): return lambda *args: call(*args, *deps)  138 us
    ppermute x28, starting transfers between devices, swap_img(): lax.ppermute(value, 'img', [(k, k ^ mask) for k in range(lax.axis_size('i...  38.7 us
    ppermute x28, waiting for transfers between devices, swap_img(): lax.ppermute(value, 'img', [(k, k ^ mask) for k in range(lax.axis_size('i...  19.9 us
    unnamed x113, local copies, waits for them, and re-layouts  12.5 us
    all_to_all x2, starting transfers between devices, spread(): return lax.all_to_all(value, 'img', split_axis=0, concat_axis=0, tiled=True)  10.2 us
  transfers between devices with their start and end apart: 46, of which 14 were waited for; matrix products, arithmetic and copies ran while one was open for 1% of the time, Pallas kernels for 38%

profile of v1, /device:TPU:0, one launch (start us, length us, event | category | flops | bytes accessed | tf_op | source)
XLA Modules:
  0.0 234.0 jit_solution(11239188757336813645)
XLA Ops:
  1.2 2.7 %collective-permute-start.2 = (bf16[16,1024]{1,0:T(8,128)(2,1)}, bf16[16,1024]{1,0:T(8,128)(2,1)S(1)}, u32[]{:S(2)}, u32[]{:S(2)}) collective-permute-start(bf16[16,1024]{1,0:T(8,128)(2,1)} %refs_0_.3), channel_id=1, source_target_pairs={{0,8},{2,10},{4,12},{6,14},{8,0},{10,2},{12,4},{14,6},{16,24},{18,... | collective-permute-start | bytes 98312 | tf_op jit(solution)/shard_map/ppermute | solution.py:1124
  3.8 2.6 %collective-permute-start.3 = (bf16[16,1024]{1,0:T(8,128)(2,1)}, bf16[16,1024]{1,0:T(8,128)(2,1)S(1)}, u32[]{:S(2)}, u32[]{:S(2)}) collective-permute-start(bf16[16,1024]{1,0:T(8,128)(2,1)} %refs_0_.3), channel_id=1, source_target_pairs={{0,16},{2,18},{4,20},{6,22},{8,24},{10,26},{12,28},{14,30},{16,0},... | collective-permute-start | bytes 98312 | tf_op jit(solution)/shard_map/ppermute | solution.py:1124
  6.4 0.8 constant_dynamic-update-slice_fusion.1
  8.0 0.9 collective-permute-start.12
  8.9 1.6 vectors.1
  10.5 3.6 %collective-permute-start.13 = (bf16[16,2560]{1,0:T(8,128)(2,1)S(1)}, bf16[16,2560]{1,0:T(8,128)(2,1)S(1)}, u32[]{:S(2)}, u32[]{:S(2)}) collective-permute-start(bf16[16,2560]{1,0:T(8,128)(2,1)S(1)} %constant_dynamic-update-slice_fusion.refs_0_), channel_id=1, source_target_pairs={{0,16},{2,18},{4,20},{6,22},{8,24},{10,26},{12,28},{14,30},{16,0},... | collective-permute-start | bytes 245768 | tf_op jit(solution)/shard_map/ppermute | solution.py:1124
  14.7 1.5 join.3
  16.1 1.8 collective-permute-start.5
  17.9 1.5 collective-permute-start.6
  20.4 4.9 %prepare.1 = (bf16[4,256,512]{2,1,0:T(8,128)(2,1)}, bf16[4,256,512]{2,1,0:T(8,128)(2,1)}, bf16[4,256,512]{2,1,0:T(8,128)(2,1)}, bf16[4,64,512]{2,1,0:T(8,128)(2,...) custom-call(s32[32,32]{1,0:T(8,128)} %bitcast.69, s32[32,32]{1,0:T(8,128)} %copy-done.50, bf16[2,512,512]{2,1,0:T(8,128)(2,1)} %bitcast.54, ...), custom_call_target="tpu_custom_call" | custom-call | flops 4000000000 | tf_op jit(solution)/shard_map/prepare/pallas_call | solution.py:190
  26.7 1.8 join.4
  28.5 1.6 collective-permute-start.15
  30.1 1.1 broadcast_in_dim.2
  31.2 5.5 %all-to-all-start = ((bf16[16,64,512]{2,1,0:T(8,128)(2,1)}), bf16[16,64,512]{2,1,0:T(8,128)(2,1)S(1)}, u32[]{:S(2)}, u32[]{:S(2)}) async-start(bf16[16,64,512]{2,1,0:T(8,128)(2,1)} %broadcast_in_dim.2), calls=%async_computation | async-start | bytes 2097152 | tf_op jit(solution)/shard_map/all_to_all | solution.py:1154
  37.8 0.8 pad_convert_fusion.refs_13_.refs_3_
  39.3 2.0 join.5
  41.3 1.9 collective-permute-start.16
  44.0 20.9 %forward.1 = (f32[4,256,1024]{2,1,0:T(8,128)}, bf16[16,13,5,16,256]{4,3,2,1,0:T(8,128)(2,1)}, f32[4,256,128]{2,1,0:T(8,128)}, f32[8,128]{1,0:T(8,128)}) custom-call(s32[32,32]{1,0:T(8,128)} %bitcast.70, s32[32,32]{1,0:T(8,128)} %copy-done.50, bf16[4,256,512]{2,1,0:T(8,128)(2,1)} %get-tuple-element.126.refs_2_, ...), custom_call_target="tpu_custom_call" | custom-call | flops 24000000000 | tf_op jit(solution)/shard_map/forward/pallas_call | solution.py:190
  65.6 0.9 collective-permute-done.16.refs_6_.refs_10_
  66.5 2.3 collective-permute-done.17.refs_7_.refs_11_
  68.8 0.9 collective-permute-done.18.refs_8_.refs_12_
  69.8 1.0 copy-done.10
  70.7 25.9 %middle.1 = (bf16[2,512,512]{2,1,0:T(8,128)(2,1)}, bf16[2048,1024]{1,0:T(8,128)(2,1)}, bf16[512,1024]{1,0:T(8,128)(2,1)}, bf16[1024,1024]{1,0:T(8,128)(2,1)}, bf...) custom-call(s32[32,32]{1,0:T(8,128)} %bitcast.71, ...), custom_call_target="tpu_custom_call" | custom-call | flops 30000001024 | tf_op jit(solution)/shard_map/middle/pallas_call | solution.py:190
  96.6 6.5 %expand_grad.1 = (bf16[256,2048]{1,0:T(8,128)(2,1)}, bf16[256,2048]{1,0:T(8,128)(2,1)}, f32[8,128]{1,0:T(8,128)}) custom-call(bf16[512,1024]{1,0:T(8,128)(2,1)} %get-tuple-element.151.refs_0_, bf16[1024,2048]{1,0:T(8,128)(2,1)} %get-tuple-element.152.refs_1_), custom_call_target="tpu_custom_call" | custom-call | flops 5000000000 | tf_op jit(solution)/shard_map/expand_grad/pallas_call | solution.py:190
  103.1 8.2 %reduce_grad.1 = (bf16[1280,512]{1,0:T(8,128)(2,1)}, bf16[1280,512]{1,0:T(8,128)(2,1)}, f32[8,128]{1,0:T(8,128)}) custom-call(bf16[2048,1024]{1,0:T(8,128)(2,1)} %get-tuple-element.148.refs_0_, bf16[1024,512]{1,0:T(8,128)(2,1)} %get-tuple-element.149.refs_1_, bf16[1024,1024]{1,0:T(8,128)(2,1)} %get-tuple-element.142.refs_2_.refs_0_, ...), custom_call_target="tpu_custom_call" | custom-call | flops 6000000000 | tf_op jit(solution)/shard_map/reduce_grad/pallas_call | solution.py:190
  112.1 12.9 %kernel_grad.1 = (f32[16,32,128]{2,1,0:T(8,128)}, f32[8,128]{1,0:T(8,128)}) custom-call(bf16[4,256,1024]{2,1,0:T(8,128)(2,1)} %bitcast.48, bf16[16,13,5,16,256]{4,3,2,1,0:T(8,128)(2,1)} %get-tuple-element.147.refs_1_, f32[8,128]{1,0:T(8,128)} %get-tuple-element.154.refs_2_), custom_call_target="tpu_custom_call" | custom-call | flops 12999999488 | tf_op jit(solution)/shard_map/kernel_grad/pallas_call | solution.py:190
  125.0 1.0 copy-done.8
  126.0 4.3 %combine.3 = (bf16[4,160,512]{2,1,0:T(8,128)(2,1)}, bf16[4,160,512]{2,1,0:T(8,128)(2,1)}, bf16[4,32,2048]{2,1,0:T(8,128)(2,1)}, bf16[4,32,2048]{2,1,0:T(8,128)(2,1)}, f32[8,128]{1,0:T(8,128)}) custom-call(bf16[2,4,160,512]{3,2,1,0:T(8,128)(2,1)} %bitcast.80, bf16[2,4,160,512]{3,2,1,0:T(8,128)(2,1)} %bitcast.52, bf16[2,4,32,2048]{3,2,1,0:T(8,128)(2,1)} %bitcast.90, ...), custom_call_target="tpu_custom_call" | custom-call | flops 2000000000 | tf_op jit(solution)/shard_map/combine/pallas_call | solution.py:190
  130.3 3.4 %gate_grads.1 = (bf16[256,512]{1,0:T(8,128)(2,1)}, bf16[256,512]{1,0:T(8,128)(2,1)}, f32[8,128]{1,0:T(8,128)}) custom-call(bf16[1024,1024]{1,0:T(8,128)(2,1)} %get-tuple-element.142.refs_2_.refs_0_, bf16[1024,1024]{1,0:T(8,128)(2,1)} %get-tuple-element.143.refs_1_, f32[8,512]{1,0:T(8,128)} %get-tuple-element.144.refs_2_, ...), custom_call_target="tpu_custom_call" | custom-call | flops 3000000000 | tf_op jit(solution)/shard_map/gate_grads/pallas_call | solution.py:190
  134.0 1.5 collective-permute-start.24
  136.0 0.8 copy-done.17
  136.8 8.9 %conv_back.2 = (bf16[4,256,512]{2,1,0:T(8,128)(2,1)}, f32[8,128]{1,0:T(8,128)}) custom-call(s32[32,32]{1,0:T(8,128)} %bitcast.72, bf16[4,256,1024]{2,1,0:T(8,128)(2,1)} %bitcast.49, bf16[4,64,1024]{2,1,0:T(8,128)(2,1)} %copy-done.17, f32[7,7,1024]{2,1,0:T(8,128)} %pad_convert_fusion.refs_13_.refs_3_, f32[8,128]{1,0:T(8,128)} %get-tuple-element.162.refs_4_), custom_call_target="tpu_custom_call" | custom-call | flops 8999999488 | tf_op jit(solution)/shard_map/conv_back/pallas_call | solution.py:190
  146.5 3.1 %combine.4 = (bf16[4,16,512]{2,1,0:T(8,128)(2,1)}, bf16[4,16,512]{2,1,0:T(8,128)(2,1)}, bf16[4,16,512]{2,1,0:T(8,128)(2,1)}, bf16[4,16,512]{2,1,0:T(8,128)(2,1)}, f32[8,128]{1,0:T(8,128)}) custom-call(bf16[4,4,16,512]{3,2,1,0:T(8,128)(2,1)} %bitcast.96, bf16[4,4,16,512]{3,2,1,0:T(8,128)(2,1)} %bitcast.62, f32[8,128]{1,0:T(8,128)} %get-tuple-element.166.refs_2_), custom_call_target="tpu_custom_call" | custom-call | flops 2000000000 | tf_op jit(solution)/shard_map/combine/pallas_call | solution.py:190
  149.5 1.5 collective-permute-start.26
  151.6 1.5 collective-permute-start.28
  153.1 9.0 %conv_back.3 = (bf16[4,256,512]{2,1,0:T(8,128)(2,1)}, f32[8,128]{1,0:T(8,128)}) custom-call(s32[32,32]{1,0:T(8,128)} %bitcast.73, bf16[4,256,1024]{2,1,0:T(8,128)(2,1)} %bitcast.50, bf16[4,64,1024]{2,1,0:T(8,128)(2,1)} %copy-done.17, f32[7,7,1024]{2,1,0:T(8,128)} %pad_convert_fusion.refs_13_.refs_3_, f32[8,128]{1,0:T(8,128)} %get-tuple-element.167.refs_4_), custom_call_target="tpu_custom_call" | custom-call | flops 8999999488 | tf_op jit(solution)/shard_map/conv_back/pallas_call | solution.py:190
  163.1 2.8 %combine.5 = (bf16[1,320,512]{2,1,0:T(8,128)(2,1)}, bf16[1,320,512]{2,1,0:T(8,128)(2,1)}, bf16[1,64,2048]{2,1,0:T(8,128)(2,1)}, bf16[1,64,2048]{2,1,0:T(8,128)(2...) custom-call(bf16[2,1,320,512]{3,2,1,0:T(8,128)(2,1)} %bitcast.91, ...), custom_call_target="tpu_custom_call" | custom-call | flops 2000000000 | tf_op jit(solution)/shard_map/combine/pallas_call | solution.py:190
  165.9 1.5 collective-permute-start.29
  168.0 4.2 %in_grad.1 = (bf16[256,1024]{1,0:T(8,128)(2,1)}, bf16[256,1024]{1,0:T(8,128)(2,1)}, f32[8,128]{1,0:T(8,128)}) custom-call(bf16[512,1024]{1,0:T(8,128)(2,1)} %get-tuple-element.183.refs_0_, bf16[1024,512]{1,0:T(8,128)(2,1)} %bitcast.85, bf16[1024,512]{1,0:T(8,128)(2,1)} %bitcast.88, f32[8,128]{1,0:T(8,128)} %get-tuple-element.184.refs_3_), custom_call_target="tpu_custom_call" | custom-call | flops 4000000000 | tf_op jit(solution)/shard_map/in_grad/pallas_call | solution.py:190
  172.1 1.5 collective-permute-start.37
  173.6 0.8 collective-permute-done.30.refs_3_
  175.4 2.1 merge.1
  177.4 1.5 collective-permute-start.40
  178.9 2.4 %collective-permute-start.41 = (bf16[144,512]{1,0:T(8,128)(2,1)}, bf16[144,512]{1,0:T(8,128)(2,1)S(1)}, u32[]{:S(2)}, u32[]{:S(2)}) collective-permute-start(bf16[144,512]{1,0:T(8,128)(2,1)} %get-tuple-element.197), channel_id=1, source_target_pairs={{0,16},{2,18},{4,20},{6,22},{8,24},{10,26},{12,28},{14,30},{16,0},... | collective-permute-start | bytes 442376 | tf_op jit(solution)/shard_map/ppermute | solution.py:1124
  181.8 6.4 %last.1 = (bf16[2,512,512]{2,1,0:T(8,128)(2,1)}, f32[8,512]{1,0:T(8,128)}, f32[8,128]{1,0:T(8,128)}) custom-call(s32[32,32]{1,0:T(8,128)} %bitcast.74, bf16[1024,512]{1,0:T(8,128)(2,1)} %bitcast.86, bf16[1024,512]{1,0:T(8,128)(2,1)} %bitcast.89, bf16[1024,512]{1,0:T(8,128)(2,1)} %bitcast.83, f32[1024,512]{1,0:T(8,128)} %get-tuple-element.169.refs_4_, ...), custom_call_target="tpu_custom_call" | custom-call | flops 7000000000 | tf_op jit(solution)/shard_map/last/pallas_call | solution.py:190
  188.2 2.0 collective-permute-start.38
  190.2 2.5 %collective-permute-done.41.refs_2_ = bf16[144,512]{1,0:T(8,128)(2,1)S(1)} collective-permute-done((bf16[144,512]{1,0:T(8,128)(2,1)}, bf16[144,512]{1,0:T(8,128)(2,1)S(1)}, u32[]{:S(2)}, u32[]{:S(2)}) %collective-permute-start.41) | collective-permute-done | bytes 147488 | tf_op jit(solution)/shard_map/ppermute | solution.py:1124
  192.7 2.0 collective-permute-start.39
  195.3 1.9 finish.1
  197.2 1.0 collective-permute-done.39.refs_5_
  199.0 2.3 deal.1
  201.3 4.6 %all-to-all-start.1 = ((bf16[16,16,1536]{2,1,0:T(8,128)(2,1)}), bf16[16,16,1536]{2,1,0:T(8,128)(2,1)S(1)}, u32[]{:S(2)}, u32[]{:S(2)}) async-start(bf16[16,16,1536]{2,1,0:T(8,128)(2,1)} %bitcast.47), calls=%async_computation.1 | async-start | bytes 1572864 | tf_op jit(solution)/shard_map/all_to_all | solution.py:1154
  206.0 1.2 collective-permute-done.31
  207.2 1.9 collective-permute-start.32
  209.1 3.8 %collective-permute-done.32 = f32[8,512]{1,0:T(8,128)S(1)} collective-permute-done((f32[8,512]{1,0:T(8,128)S(1)}, f32[8,512]{1,0:T(8,128)S(1)}, u32[]{:S(2)}, u32[]{:S(2)}) %collective-permute-start.32) | collective-permute-done | bytes 16416 | tf_op jit(solution)/shard_map/ppermute | solution.py:1124
  212.9 1.4 collective-permute-start.33
  214.2 3.0 %collective-permute-done.33 = f32[8,512]{1,0:T(8,128)S(1)} collective-permute-done((f32[8,512]{1,0:T(8,128)S(1)}, f32[8,512]{1,0:T(8,128)S(1)}, u32[]{:S(2)}, u32[]{:S(2)}) %collective-permute-start.33) | collective-permute-done | bytes 16416 | tf_op jit(solution)/shard_map/ppermute | solution.py:1124
  217.2 3.7 %collective-permute-done.34 = f32[8,512]{1,0:T(8,128)S(1)} collective-permute-done((f32[8,512]{1,0:T(8,128)S(1)}, f32[8,512]{1,0:T(8,128)S(1)}, u32[]{:S(2)}, u32[]{:S(2)}) %collective-permute-start.34) | collective-permute-done | bytes 16416 | tf_op jit(solution)/shard_map/ppermute | solution.py:1124
  221.0 2.8 %all-to-all-done.1 = bf16[16,16,1536]{2,1,0:T(8,128)(2,1)S(1)} async-done(((bf16[16,16,1536]{2,1,0:T(8,128)(2,1)}), bf16[16,16,1536]{2,1,0:T(8,128)(2,1)S(1)}, u32[]{:S(2)}, u32[]{:S(2)}) %all-to-all-start.1) | async-done | bytes 786464 | tf_op jit(solution)/shard_map/all_to_all | solution.py:1154
  223.8 1.2 collective-permute-start.35
  225.0 3.4 %collective-permute-done.35.refs_1_ = f32[8,512]{1,0:T(8,128)S(1)} collective-permute-done((f32[8,512]{1,0:T(8,128)S(1)}, f32[8,512]{1,0:T(8,128)S(1)}, u32[]{:S(2)}, u32[]{:S(2)}) %collective-permute-start.35) | collective-permute-done | bytes 16416 | tf_op jit(solution)/shard_map/ppermute | solution.py:1124
  229.0 1.3 late.1
  230.4 0.9 copy-done.11
  231.3 2.6 %unpack.1 = (f32[16,1024]{1,0:T(8,128)}, f32[7,7,992]{2,1,0:T(8,128)}, f32[992]{0:T(1024)}, f32[32,64]{1,0:T(8,128)}, f32[64,128]{1,0:T(8,128)}, /*index=5*/f32[...) custom-call(bf16[256,1536]{1,0:T(8,128)(2,1)} %bitcast.46, ...), custom_call_target="tpu_custom_call" | custom-call | flops 3000000000 | tf_op jit(solution)/shard_map/unpack/pallas_call | solution.py:190
  (172 shorter events, 15.5 us)
Async XLA Ops:
  0.7 13.4 %copy-start.47 = (s32[2,16,32]{2,1,0:T(8,128)S(1)}, s32[2,16,32]{2,1,0:T(8,128)}, u32[]{:S(2)}) copy-start(s32[2,16,32]{2,1,0:T(8,128)} %param.25) | copy-start | bytes 12292
  0.7 18.8 %collective-permute-start.1 = (bf16[2,512,512]{2,1,0:T(8,128)(2,1)}, bf16[2,512,512]{2,1,0:T(8,128)(2,1)S(1)}, u32[]{:S(2)}, u32[]{:S(2)}) collective-permute-start(bf16[2,512,512]{2,1,0:T(8,128)(2,1)} %bitcast.53), channel_id=1, source_target_pairs={{0,1},{1,0},{2,3},{3,2},{4,5},{5,4},{6,7},{7,6},{8,9},{9,8},{10,11... | collective-permute-start | bytes 3145736 | tf_op jit(solution)/shard_map/ppermute | solution.py:1128
  1.2 9.3 %collective-permute-start.2 = (bf16[16,1024]{1,0:T(8,128)(2,1)}, bf16[16,1024]{1,0:T(8,128)(2,1)S(1)}, u32[]{:S(2)}, u32[]{:S(2)}) collective-permute-start(bf16[16,1024]{1,0:T(8,128)(2,1)} %refs_0_.3), channel_id=1, source_target_pairs={{0,8},{2,10},{4,12},{6,14},{8,0},{10,2},{12,4},{14,6},{16,24},{18,... | collective-permute-start | bytes 98312 | tf_op jit(solution)/shard_map/ppermute | solution.py:1124
  3.8 10.2 %collective-permute-start.3 = (bf16[16,1024]{1,0:T(8,128)(2,1)}, bf16[16,1024]{1,0:T(8,128)(2,1)S(1)}, u32[]{:S(2)}, u32[]{:S(2)}) collective-permute-start(bf16[16,1024]{1,0:T(8,128)(2,1)} %refs_0_.3), channel_id=1, source_target_pairs={{0,16},{2,18},{4,20},{6,22},{8,24},{10,26},{12,28},{14,30},{16,0},... | collective-permute-start | bytes 98312 | tf_op jit(solution)/shard_map/ppermute | solution.py:1124
  6.4 7.6 %collective-permute-start.4 = (bf16[16,1024]{1,0:T(8,128)(2,1)}, bf16[16,1024]{1,0:T(8,128)(2,1)S(1)}, u32[]{:S(2)}, u32[]{:S(2)}) collective-permute-start(bf16[16,1024]{1,0:T(8,128)(2,1)} %refs_0_.3), channel_id=1, source_target_pairs={{0,24},{2,26},{4,28},{6,30},{8,16},{10,18},{12,20},{14,22},{16,8},... | collective-permute-start | bytes 98312 | tf_op jit(solution)/shard_map/ppermute | solution.py:1124
  8.0 8.1 %copy-start.5 = (bf16[16,2560]{1,0:T(8,128)(2,1)}, bf16[16,2560]{1,0:T(8,128)(2,1)S(1)}, u32[]{:S(2)}) copy-start(bf16[16,2560]{1,0:T(8,128)(2,1)S(1)} %constant_dynamic-update-slice_fusion.refs_0_) | copy-start | bytes 245764
  8.0 9.9 %collective-permute-start.12 = (bf16[16,2560]{1,0:T(8,128)(2,1)S(1)}, bf16[16,2560]{1,0:T(8,128)(2,1)S(1)}, u32[]{:S(2)}, u32[]{:S(2)}) collective-permute-start(bf16[16,2560]{1,0:T(8,128)(2,1)S(1)} %constant_dynamic-update-slice_fusion.refs_0_), channel_id=1, source_target_pairs={{0,8},{2,10},{4,12},{6,14},{8,0},{10,2},{12,4},{14,6},{16,24},{18,... | collective-permute-start | bytes 245768 | tf_op jit(solution)/shard_map/ppermute | solution.py:1124
  10.5 14.9 %collective-permute-start.13 = (bf16[16,2560]{1,0:T(8,128)(2,1)S(1)}, bf16[16,2560]{1,0:T(8,128)(2,1)S(1)}, u32[]{:S(2)}, u32[]{:S(2)}) collective-permute-start(bf16[16,2560]{1,0:T(8,128)(2,1)S(1)} %constant_dynamic-update-slice_fusion.refs_0_), channel_id=1, source_target_pairs={{0,16},{2,18},{4,20},{6,22},{8,24},{10,26},{12,28},{14,30},{16,0},... | collective-permute-start | bytes 245768 | tf_op jit(solution)/shard_map/ppermute | solution.py:1124
  14.0 11.3 %collective-permute-start.14 = (bf16[16,2560]{1,0:T(8,128)(2,1)S(1)}, bf16[16,2560]{1,0:T(8,128)(2,1)S(1)}, u32[]{:S(2)}, u32[]{:S(2)}) collective-permute-start(bf16[16,2560]{1,0:T(8,128)(2,1)S(1)} %constant_dynamic-update-slice_fusion.refs_0_), channel_id=1, source_target_pairs={{0,24},{2,26},{4,28},{6,30},{8,16},{10,18},{12,20},{14,22},{16,8},... | collective-permute-start | bytes 245768 | tf_op jit(solution)/shard_map/ppermute | solution.py:1124
  14.1 2.1 collective-permute-start
  16.1 9.2 %collective-permute-start.5 = (bf16[64,1024]{1,0:T(8,128)(2,1)}, bf16[64,1024]{1,0:T(8,128)(2,1)S(1)}, u32[]{:S(2)}, u32[]{:S(2)}) collective-permute-start(bf16[64,1024]{1,0:T(8,128)(2,1)} %get-tuple-element.128.refs_4_.refs_5_), channel_id=1, source_target_pairs={{0,2},{2,0},{4,6},{6,4},{8,10},{10,8},{12,14},{14,12},{16,18},{18,... | collective-permute-start | bytes 393224 | tf_op jit(solution)/shard_map/ppermute | solution.py:1124
  17.9 7.4 %copy-start.38 = (bf16[16,2560]{1,0:T(8,128)(2,1)}, bf16[16,2560]{1,0:T(8,128)(2,1)S(1)}, u32[]{:S(2)}) copy-start(bf16[16,2560]{1,0:T(8,128)(2,1)S(1)} %collective-permute-done.12.refs_1_) | copy-start | bytes 245764
  17.9 8.1 %collective-permute-start.6 = (bf16[64,1024]{1,0:T(8,128)(2,1)}, bf16[64,1024]{1,0:T(8,128)(2,1)S(1)}, u32[]{:S(2)}, u32[]{:S(2)}) collective-permute-start(bf16[64,1024]{1,0:T(8,128)(2,1)} %get-tuple-element.128.refs_4_.refs_5_), channel_id=1, source_target_pairs={{0,4},{2,6},{4,0},{6,2},{8,12},{10,14},{12,8},{14,10},{16,20},{18,... | collective-permute-start | bytes 393224 | tf_op jit(solution)/shard_map/ppermute | solution.py:1124
  19.4 6.6 %collective-permute-start.7 = (bf16[64,1024]{1,0:T(8,128)(2,1)}, bf16[64,1024]{1,0:T(8,128)(2,1)S(1)}, u32[]{:S(2)}, u32[]{:S(2)}) collective-permute-start(bf16[64,1024]{1,0:T(8,128)(2,1)} %get-tuple-element.128.refs_4_.refs_5_), channel_id=1, source_target_pairs={{0,6},{2,4},{4,2},{6,0},{8,14},{10,12},{12,10},{14,8},{16,22},{18,... | collective-permute-start | bytes 393224 | tf_op jit(solution)/shard_map/ppermute | solution.py:1124
  25.3 4.8 %copy-start.4 = (bf16[64,512]{1,0:T(8,128)(2,1)S(1)}, bf16[64,512]{1,0:T(8,128)(2,1)}, u32[]{:S(2)}) copy-start(bf16[64,512]{1,0:T(8,128)(2,1)} %param.45) | copy-start | bytes 196612
  28.5 8.2 %copy-start.27 = (bf16[64,1024]{1,0:T(8,128)(2,1)S(1)}, bf16[64,1024]{1,0:T(8,128)(2,1)}, u32[]{:S(2)}) copy-start(bf16[64,1024]{1,0:T(8,128)(2,1)} %get-tuple-element.128.refs_4_.refs_5_) | copy-start | bytes 393220
  28.5 8.3 %copy-start.31 = (bf16[64,1024]{1,0:T(8,128)(2,1)S(1)}, bf16[64,1024]{1,0:T(8,128)(2,1)}, u32[]{:S(2)}) copy-start(bf16[64,1024]{1,0:T(8,128)(2,1)} %copy-done.30) | copy-start | bytes 393220
  28.5 8.8 %copy-start.33 = (bf16[64,1024]{1,0:T(8,128)(2,1)S(1)}, bf16[64,1024]{1,0:T(8,128)(2,1)}, u32[]{:S(2)}) copy-start(bf16[64,1024]{1,0:T(8,128)(2,1)} %copy-done.32) | copy-start | bytes 393220
  28.5 8.9 %copy-start.29 = (bf16[64,1024]{1,0:T(8,128)(2,1)S(1)}, bf16[64,1024]{1,0:T(8,128)(2,1)}, u32[]{:S(2)}) copy-start(bf16[64,1024]{1,0:T(8,128)(2,1)} %copy-done.28) | copy-start | bytes 393220
  28.5 9.3 %copy-start.3 = (bf16[7,7,992]{2,1,0:T(8,128)(2,1)S(1)}, bf16[7,7,992]{2,1,0:T(8,128)(2,1)}, u32[]{:S(2)}) copy-start(bf16[7,7,992]{2,1,0:T(8,128)(2,1)} %param.31) | copy-start | bytes 291652
  28.5 10.1 %collective-permute-start.15 = (bf16[64,2560]{1,0:T(8,128)(2,1)}, bf16[64,2560]{1,0:T(8,128)(2,1)S(1)}, u32[]{:S(2)}, u32[]{:S(2)}) collective-permute-start(bf16[64,2560]{1,0:T(8,128)(2,1)} %get-tuple-element.130.refs_0_), channel_id=1, source_target_pairs={{0,4},{2,6},{4,0},{6,2},{8,12},{10,14},{12,8},{14,10},{16,20},{18,... | collective-permute-start | bytes 983048 | tf_op jit(solution)/shard_map/ppermute | solution.py:1124
  31.2 33.8 %all-to-all-start = ((bf16[16,64,512]{2,1,0:T(8,128)(2,1)}), bf16[16,64,512]{2,1,0:T(8,128)(2,1)S(1)}, u32[]{:S(2)}, u32[]{:S(2)}) async-start(bf16[16,64,512]{2,1,0:T(8,128)(2,1)} %broadcast_in_dim.2), calls=%async_computation | async-start | bytes 2097152 | tf_op jit(solution)/shard_map/all_to_all | solution.py:1154
  36.7 6.5 %collective-permute-start.8 = (bf16[64,1024]{1,0:T(8,128)(2,1)S(1)}, bf16[64,1024]{1,0:T(8,128)(2,1)S(1)}, u32[]{:S(2)}, u32[]{:S(2)}) collective-permute-start(bf16[64,1024]{1,0:T(8,128)(2,1)S(1)} %copy-done.27), channel_id=1, source_target_pairs={{0,1},{1,0},{2,3},{3,2},{4,5},{5,4},{6,7},{7,6},{8,9},{9,8},{10,11... | collective-permute-start | bytes 393224 | tf_op jit(solution)/shard_map/ppermute | solution.py:1128
  36.8 6.4 %collective-permute-start.10 = (bf16[64,1024]{1,0:T(8,128)(2,1)S(1)}, bf16[64,1024]{1,0:T(8,128)(2,1)S(1)}, u32[]{:S(2)}, u32[]{:S(2)}) collective-permute-start(bf16[64,1024]{1,0:T(8,128)(2,1)S(1)} %copy-done.31), channel_id=1, source_target_pairs={{0,1},{1,0},{2,3},{3,2},{4,5},{5,4},{6,7},{7,6},{8,9},{9,8},{10,11... | collective-permute-start | bytes 393224 | tf_op jit(solution)/shard_map/ppermute | solution.py:1128
  37.3 6.0 %collective-permute-start.11 = (bf16[64,1024]{1,0:T(8,128)(2,1)S(1)}, bf16[64,1024]{1,0:T(8,128)(2,1)S(1)}, u32[]{:S(2)}, u32[]{:S(2)}) collective-permute-start(bf16[64,1024]{1,0:T(8,128)(2,1)S(1)} %copy-done.33), channel_id=1, source_target_pairs={{0,1},{1,0},{2,3},{3,2},{4,5},{5,4},{6,7},{7,6},{8,9},{9,8},{10,11... | collective-permute-start | bytes 393224 | tf_op jit(solution)/shard_map/ppermute | solution.py:1128
  37.4 5.9 %collective-permute-start.9 = (bf16[64,1024]{1,0:T(8,128)(2,1)S(1)}, bf16[64,1024]{1,0:T(8,128)(2,1)S(1)}, u32[]{:S(2)}, u32[]{:S(2)}) collective-permute-start(bf16[64,1024]{1,0:T(8,128)(2,1)S(1)} %copy-done.29), channel_id=1, source_target_pairs={{0,1},{1,0},{2,3},{3,2},{4,5},{5,4},{6,7},{7,6},{8,9},{9,8},{10,11... | collective-permute-start | bytes 393224 | tf_op jit(solution)/shard_map/ppermute | solution.py:1128
  41.3 25.2 %collective-permute-start.16 = (bf16[128,2560]{1,0:T(8,128)(2,1)}, bf16[128,2560]{1,0:T(8,128)(2,1)S(1)}, u32[]{:S(2)}, u32[]{:S(2)}) collective-permute-start(bf16[128,2560]{1,0:T(8,128)(2,1)} %get-tuple-element.137.refs_5_.refs_9_), channel_id=1, source_target_pairs={{0,2},{2,0},{4,6},{6,4},{8,10},{10,8},{12,14},{14,12},{16,18},{18,... | collective-permute-start | bytes 1966088 | tf_op jit(solution)/shard_map/ppermute | solution.py:1124
  44.0 21.1 %copy-start.13 = (bf16[128,2560]{1,0:T(8,128)(2,1)S(1)}, bf16[128,2560]{1,0:T(8,128)(2,1)}, u32[]{:S(2)}) copy-start(bf16[128,2560]{1,0:T(8,128)(2,1)} %get-tuple-element.137.refs_5_.refs_9_) | copy-start | bytes 1966084
  65.0 4.7 %collective-permute-start.19 = (bf16[1024,512]{1,0:T(8,128)(2,1)S(1)}, bf16[1024,512]{1,0:T(8,128)(2,1)S(1)}, u32[]{:S(2)}, u32[]{:S(2)}) collective-permute-start(bf16[1024,512]{1,0:T(8,128)(2,1)S(1)} %bitcast.43), channel_id=1, source_target_pairs={{0,1},{1,0},{2,3},{3,2},{4,5},{5,4},{6,7},{7,6},{8,9},{9,8},{10,11... | collective-permute-start | bytes 3145736 | tf_op jit(solution)/shard_map/ppermute | solution.py:1128
  65.1 3.7 %collective-permute-start.17 = (bf16[128,2560]{1,0:T(8,128)(2,1)S(1)}, bf16[128,2560]{1,0:T(8,128)(2,1)}, u32[]{:S(2)}, u32[]{:S(2)}) collective-permute-start(bf16[128,2560]{1,0:T(8,128)(2,1)S(1)} %copy-done.13), channel_id=1, source_target_pairs={{0,1},{1,0},{2,3},{3,2},{4,5},{5,4},{6,7},{7,6},{8,9},{9,8},{10,11... | collective-permute-start | bytes 1966088 | tf_op jit(solution)/shard_map/ppermute | solution.py:1128
  66.5 3.3 %collective-permute-start.18 = (bf16[128,2560]{1,0:T(8,128)(2,1)S(1)}, bf16[128,2560]{1,0:T(8,128)(2,1)}, u32[]{:S(2)}, u32[]{:S(2)}) collective-permute-start(bf16[128,2560]{1,0:T(8,128)(2,1)S(1)} %collective-permute-done.16.refs_6_.refs_10_), channel_id=1, source_target_pairs={{0,1},{1,0},{2,3},{3,2},{4,5},{5,4},{6,7},{7,6},{8,9},{9,8},{10,11... | collective-permute-start | bytes 1966088 | tf_op jit(solution)/shard_map/ppermute | solution.py:1128
  103.1 8.7 %copy-start.2 = (bf16[1024,1024]{1,0:T(8,128)(2,1)S(1)}, bf16[1024,1024]{1,0:T(8,128)(2,1)}, u32[]{:S(2)}) copy-start(bf16[1024,1024]{1,0:T(8,128)(2,1)} %get-tuple-element.141) | copy-start | bytes 6291460
  111.3 13.7 %collective-permute-start.21 = (bf16[1280,512]{1,0:T(8,128)(2,1)}, bf16[1280,512]{1,0:T(8,128)(2,1)S(1)}, u32[]{:S(2)}, u32[]{:S(2)}) collective-permute-start(bf16[1280,512]{1,0:T(8,128)(2,1)} %get-tuple-element.157), channel_id=1, source_target_pairs={{0,1},{1,0},{2,3},{3,2},{4,5},{5,4},{6,7},{7,6},{8,9},{9,8},{10,11... | collective-permute-start | bytes 3932168 | tf_op jit(solution)/shard_map/ppermute | solution.py:1128
  111.4 13.5 %collective-permute-start.22 = (bf16[256,2048]{1,0:T(8,128)(2,1)}, bf16[256,2048]{1,0:T(8,128)(2,1)}, u32[]{:S(2)}, u32[]{:S(2)}) collective-permute-start(bf16[256,2048]{1,0:T(8,128)(2,1)} %get-tuple-element.159), channel_id=1, source_target_pairs={{0,1},{1,0},{2,3},{3,2},{4,5},{5,4},{6,7},{7,6},{8,9},{9,8},{10,11... | collective-permute-start | bytes 3145736 | tf_op jit(solution)/shard_map/ppermute | solution.py:1128
  111.9 24.2 %collective-permute-start.20 = (bf16[4,64,1024]{2,1,0:T(8,128)(2,1)S(1)}, bf16[4,64,1024]{2,1,0:T(8,128)(2,1)S(1)}, u32[]{:S(2)}, u32[]{:S(2)}) collective-permute-start(bf16[4,64,1024]{2,1,0:T(8,128)(2,1)S(1)} %slice_select_fusion), channel_id=1, source_target_pairs={{0,1},{1,0},{2,3},{3,2},{4,5},{5,4},{6,7},{7,6},{8,9},{9,8},{10,11... | collective-permute-start | bytes 1572872 | tf_op jit(solution)/shard_map/ppermute | solution.py:1128
  130.3 5.2 %copy-start.18 = (bf16[4,32,2048]{2,1,0:T(8,128)(2,1)S(1)}, bf16[4,32,2048]{2,1,0:T(8,128)(2,1)}, u32[]{:S(2)}) copy-start(bf16[4,32,2048]{2,1,0:T(8,128)(2,1)} %get-tuple-element.173) | copy-start | bytes 1572868
  133.7 12.0 %collective-permute-start.23 = (bf16[256,512]{1,0:T(8,128)(2,1)}, bf16[256,512]{1,0:T(8,128)(2,1)S(1)}, u32[]{:S(2)}, u32[]{:S(2)}) collective-permute-start(bf16[256,512]{1,0:T(8,128)(2,1)} %get-tuple-element.165), channel_id=1, source_target_pairs={{0,1},{1,0},{2,3},{3,2},{4,5},{5,4},{6,7},{7,6},{8,9},{9,8},{10,11... | collective-permute-start | bytes 786440 | tf_op jit(solution)/shard_map/ppermute | solution.py:1128
  134.0 28.1 %collective-permute-start.24 = (bf16[640,512]{1,0:T(8,128)(2,1)S(1)}, bf16[640,512]{1,0:T(8,128)(2,1)S(1)}, u32[]{:S(2)}, u32[]{:S(2)}) collective-permute-start(bf16[640,512]{1,0:T(8,128)(2,1)S(1)} %bitcast.56), channel_id=1, source_target_pairs={{0,4},{2,6},{4,0},{6,2},{8,12},{10,14},{12,8},{14,10},{16,20},{18,... | collective-permute-start | bytes 1966088 | tf_op jit(solution)/shard_map/ppermute | solution.py:1124
  135.5 26.6 %collective-permute-start.25 = (bf16[128,2048]{1,0:T(8,128)(2,1)S(1)}, bf16[128,2048]{1,0:T(8,128)(2,1)S(1)}, u32[]{:S(2)}, u32[]{:S(2)}) collective-permute-start(bf16[128,2048]{1,0:T(8,128)(2,1)S(1)} %bitcast.58), channel_id=1, source_target_pairs={{0,2},{2,0},{4,6},{6,4},{8,10},{10,8},{12,14},{14,12},{16,18},{18,... | collective-permute-start | bytes 1572872 | tf_op jit(solution)/shard_map/ppermute | solution.py:1124
  149.5 12.5 %collective-permute-start.26 = (bf16[64,512]{1,0:T(8,128)(2,1)}, bf16[64,512]{1,0:T(8,128)(2,1)S(1)}, u32[]{:S(2)}, u32[]{:S(2)}) collective-permute-start(bf16[64,512]{1,0:T(8,128)(2,1)} %bitcast.68), channel_id=1, source_target_pairs={{0,2},{2,0},{4,6},{6,4},{8,10},{10,8},{12,14},{14,12},{16,18},{18,... | collective-permute-start | bytes 196616 | tf_op jit(solution)/shard_map/ppermute | solution.py:1124
  151.1 11.0 %collective-permute-start.27 = (bf16[64,512]{1,0:T(8,128)(2,1)}, bf16[64,512]{1,0:T(8,128)(2,1)S(1)}, u32[]{:S(2)}, u32[]{:S(2)}) collective-permute-start(bf16[64,512]{1,0:T(8,128)(2,1)} %bitcast.67), channel_id=1, source_target_pairs={{0,4},{2,6},{4,0},{6,2},{8,12},{10,14},{12,8},{14,10},{16,20},{18,... | collective-permute-start | bytes 196616 | tf_op jit(solution)/shard_map/ppermute | solution.py:1124
  151.6 10.5 %collective-permute-start.28 = (bf16[64,512]{1,0:T(8,128)(2,1)}, bf16[64,512]{1,0:T(8,128)(2,1)S(1)}, u32[]{:S(2)}, u32[]{:S(2)}) collective-permute-start(bf16[64,512]{1,0:T(8,128)(2,1)} %bitcast.66), channel_id=1, source_target_pairs={{0,6},{2,4},{4,2},{6,0},{8,14},{10,12},{12,10},{14,8},{16,22},{18,... | collective-permute-start | bytes 196616 | tf_op jit(solution)/shard_map/ppermute | solution.py:1124
  165.9 8.7 %collective-permute-start.29 = (bf16[320,512]{1,0:T(8,128)(2,1)}, bf16[320,512]{1,0:T(8,128)(2,1)S(1)}, u32[]{:S(2)}, u32[]{:S(2)}) collective-permute-start(bf16[320,512]{1,0:T(8,128)(2,1)} %bitcast.60), channel_id=1, source_target_pairs={{0,2},{2,0},{4,6},{6,4},{8,10},{10,8},{12,14},{14,12},{16,18},{18,... | collective-permute-start | bytes 983048 | tf_op jit(solution)/shard_map/ppermute | solution.py:1124
  167.4 7.0 %collective-permute-start.30 = (bf16[64,2048]{1,0:T(8,128)(2,1)}, bf16[64,2048]{1,0:T(8,128)(2,1)S(1)}, u32[]{:S(2)}, u32[]{:S(2)}) collective-permute-start(bf16[64,2048]{1,0:T(8,128)(2,1)} %bitcast.61), channel_id=1, source_target_pairs={{0,4},{2,6},{4,0},{6,2},{8,12},{10,14},{12,8},{14,10},{16,20},{18,... | collective-permute-start | bytes 786440 | tf_op jit(solution)/shard_map/ppermute | solution.py:1124
  172.1 26.1 %collective-permute-start.36 = (bf16[256,1024]{1,0:T(8,128)(2,1)}, bf16[256,1024]{1,0:T(8,128)(2,1)S(1)}, u32[]{:S(2)}, u32[]{:S(2)}) collective-permute-start(bf16[256,1024]{1,0:T(8,128)(2,1)} %get-tuple-element.190), channel_id=1, source_target_pairs={{0,1},{1,0},{2,3},{3,2},{4,5},{5,4},{6,7},{7,6},{8,9},{9,8},{10,11... | collective-permute-start | bytes 1572872 | tf_op jit(solution)/shard_map/ppermute | solution.py:1128
  172.1 25.1 %collective-permute-start.37 = (bf16[16,512]{1,0:T(8,128)(2,1)S(1)}, bf16[16,512]{1,0:T(8,128)(2,1)S(1)}, u32[]{:S(2)}, u32[]{:S(2)}) collective-permute-start(bf16[16,512]{1,0:T(8,128)(2,1)S(1)} %bitcast.78), channel_id=1, source_target_pairs={{0,8},{2,10},{4,12},{6,14},{8,0},{10,2},{12,4},{14,6},{16,24},{18,... | collective-permute-start | bytes 49160 | tf_op jit(solution)/shard_map/ppermute | solution.py:1124
  177.4 10.8 %collective-permute-start.40 = (bf16[144,512]{1,0:T(8,128)(2,1)}, bf16[144,512]{1,0:T(8,128)(2,1)S(1)}, u32[]{:S(2)}, u32[]{:S(2)}) collective-permute-start(bf16[144,512]{1,0:T(8,128)(2,1)} %get-tuple-element.196), channel_id=1, source_target_pairs={{0,8},{2,10},{4,12},{6,14},{8,0},{10,2},{12,4},{14,6},{16,24},{18,... | collective-permute-start | bytes 442376 | tf_op jit(solution)/shard_map/ppermute | solution.py:1124
  178.9 13.8 %collective-permute-start.41 = (bf16[144,512]{1,0:T(8,128)(2,1)}, bf16[144,512]{1,0:T(8,128)(2,1)S(1)}, u32[]{:S(2)}, u32[]{:S(2)}) collective-permute-start(bf16[144,512]{1,0:T(8,128)(2,1)} %get-tuple-element.197), channel_id=1, source_target_pairs={{0,16},{2,18},{4,20},{6,22},{8,24},{10,26},{12,28},{14,30},{16,0},... | collective-permute-start | bytes 442376 | tf_op jit(solution)/shard_map/ppermute | solution.py:1124
  181.3 13.4 %collective-permute-start.42 = (bf16[144,512]{1,0:T(8,128)(2,1)}, bf16[144,512]{1,0:T(8,128)(2,1)S(1)}, u32[]{:S(2)}, u32[]{:S(2)}) collective-permute-start(bf16[144,512]{1,0:T(8,128)(2,1)} %get-tuple-element.198), channel_id=1, source_target_pairs={{0,24},{2,26},{4,28},{6,30},{8,16},{10,18},{12,20},{14,22},{16,8},... | collective-permute-start | bytes 442376 | tf_op jit(solution)/shard_map/ppermute | solution.py:1124
  181.8 6.4 %copy-start.49 = (bf16[1,16,512]{2,1,0:T(8,128)(2,1)S(1)}, bf16[1,16,512]{2,1,0:T(8,128)(2,1)}, u32[]{:S(2)}) copy-start(bf16[1,16,512]{2,1,0:T(8,128)(2,1)} %get-tuple-element.193) | copy-start | bytes 49156
  181.8 10.8 %copy-start.48 = (bf16[1,16,512]{2,1,0:T(8,128)(2,1)S(1)}, bf16[1,16,512]{2,1,0:T(8,128)(2,1)}, u32[]{:S(2)}) copy-start(bf16[1,16,512]{2,1,0:T(8,128)(2,1)} %get-tuple-element.194) | copy-start | bytes 49156
  188.2 6.5 %copy-start.24 = (bf16[144,512]{1,0:T(8,128)(2,1)}, bf16[144,512]{1,0:T(8,128)(2,1)S(1)}, u32[]{:S(2)}) copy-start(bf16[144,512]{1,0:T(8,128)(2,1)S(1)} %collective-permute-done.40.refs_1_) | copy-start | bytes 442372
  188.2 9.0 %collective-permute-start.38 = (bf16[16,512]{1,0:T(8,128)(2,1)S(1)}, bf16[16,512]{1,0:T(8,128)(2,1)S(1)}, u32[]{:S(2)}, u32[]{:S(2)}) collective-permute-start(bf16[16,512]{1,0:T(8,128)(2,1)S(1)} %bitcast.77), channel_id=1, source_target_pairs={{0,16},{2,18},{4,20},{6,22},{8,24},{10,26},{12,28},{14,30},{16,0},... | collective-permute-start | bytes 49160 | tf_op jit(solution)/shard_map/ppermute | solution.py:1124
  192.7 5.5 %collective-permute-start.39 = (bf16[16,512]{1,0:T(8,128)(2,1)S(1)}, bf16[16,512]{1,0:T(8,128)(2,1)S(1)}, u32[]{:S(2)}, u32[]{:S(2)}) collective-permute-start(bf16[16,512]{1,0:T(8,128)(2,1)S(1)} %bitcast.76), channel_id=1, source_target_pairs={{0,24},{2,26},{4,28},{6,30},{8,16},{10,18},{12,20},{14,22},{16,8},... | collective-permute-start | bytes 49160 | tf_op jit(solution)/shard_map/ppermute | solution.py:1124
  199.0 6.9 %copy-start.6 = (f32[8,512]{1,0:T(8,128)S(1)}, f32[8,512]{1,0:T(8,128)}, u32[]{:S(2)}) copy-start(f32[8,512]{1,0:T(8,128)} %get-tuple-element.188) | copy-start | bytes 49156
  201.3 22.5 %all-to-all-start.1 = ((bf16[16,16,1536]{2,1,0:T(8,128)(2,1)}), bf16[16,16,1536]{2,1,0:T(8,128)(2,1)S(1)}, u32[]{:S(2)}, u32[]{:S(2)}) async-start(bf16[16,16,1536]{2,1,0:T(8,128)(2,1)} %bitcast.47), calls=%async_computation.1 | async-start | bytes 1572864 | tf_op jit(solution)/shard_map/all_to_all | solution.py:1154
  205.9 1.2 collective-permute-start.31
  207.2 5.7 %collective-permute-start.32 = (f32[8,512]{1,0:T(8,128)S(1)}, f32[8,512]{1,0:T(8,128)S(1)}, u32[]{:S(2)}, u32[]{:S(2)}) collective-permute-start(f32[8,512]{1,0:T(8,128)S(1)} %add.14), channel_id=1, source_target_pairs={{0,2},{2,0},{4,6},{6,4},{8,10},{10,8},{12,14},{14,12},{16,18},{18,... | collective-permute-start | bytes 49160 | tf_op jit(solution)/shard_map/ppermute | solution.py:1124
  212.9 4.4 %collective-permute-start.33 = (f32[8,512]{1,0:T(8,128)S(1)}, f32[8,512]{1,0:T(8,128)S(1)}, u32[]{:S(2)}, u32[]{:S(2)}) collective-permute-start(f32[8,512]{1,0:T(8,128)S(1)} %add.15), channel_id=1, source_target_pairs={{0,4},{2,6},{4,0},{6,2},{8,12},{10,14},{12,8},{14,10},{16,20},{18,... | collective-permute-start | bytes 49160 | tf_op jit(solution)/shard_map/ppermute | solution.py:1124
  217.2 3.7 %collective-permute-start.34 = (f32[8,512]{1,0:T(8,128)S(1)}, f32[8,512]{1,0:T(8,128)S(1)}, u32[]{:S(2)}, u32[]{:S(2)}) collective-permute-start(f32[8,512]{1,0:T(8,128)S(1)} %add.16), channel_id=1, source_target_pairs={{0,8},{2,10},{4,12},{6,14},{8,0},{10,2},{12,4},{14,6},{16,24},{18,... | collective-permute-start | bytes 49160 | tf_op jit(solution)/shard_map/ppermute | solution.py:1124
  221.0 7.5 %copy-start.7 = (f32[8,512]{1,0:T(8,128)}, f32[8,512]{1,0:T(8,128)S(1)}, u32[]{:S(2)}) copy-start(f32[8,512]{1,0:T(8,128)S(1)} %add.17.refs_0_) | copy-start | bytes 49156
  223.8 6.6 %copy-start.1 = (bf16[16,16,1536]{2,1,0:T(8,128)(2,1)}, bf16[16,16,1536]{2,1,0:T(8,128)(2,1)S(1)}, u32[]{:S(2)}) copy-start(bf16[16,16,1536]{2,1,0:T(8,128)(2,1)S(1)} %all-to-all-done.1) | copy-start | bytes 2359300
  223.8 6.6 %collective-permute-start.43 = (bf16[256,1536]{1,0:T(8,128)(2,1)S(1)}, bf16[256,1536]{1,0:T(8,128)(2,1)S(1)}, u32[]{:S(2)}, u32[]{:S(2)}) collective-permute-start(bf16[256,1536]{1,0:T(8,128)(2,1)S(1)} %bitcast.45), channel_id=1, source_target_pairs={{0,1},{1,0},{2,3},{3,2},{4,5},{5,4},{6,7},{7,6},{8,9},{9,8},{10,11... | collective-permute-start | bytes 2359304 | tf_op jit(solution)/shard_map/ppermute | solution.py:1128
  223.8 4.6 %collective-permute-start.35 = (f32[8,512]{1,0:T(8,128)S(1)}, f32[8,512]{1,0:T(8,128)S(1)}, u32[]{:S(2)}, u32[]{:S(2)}) collective-permute-start(f32[8,512]{1,0:T(8,128)S(1)} %add.17.refs_0_), channel_id=1, source_target_pairs={{0,16},{2,18},{4,20},{6,22},{8,24},{10,26},{12,28},{14,30},{16,0},... | collective-permute-start | bytes 49160 | tf_op jit(solution)/shard_map/ppermute | solution.py:1124
  (38 other events, 48.6 us)

commit v2 on v1

--- a/solution.py
+++ b/solution.py
@@ -635,28 +635,13 @@
     )(valid, *(v.reshape(1024, -1) for v in (d, j0, xp, gp)), *w_exp, *w_exp, *w_red, g1, g2, g3, g4, wide)
 
 
-def expand_grad_kernel(y2_ref, dh_ref, keep, send, sum_ref, *, order):
-    sum_ref[...] = dot(y2_ref[...], dh_ref[...])
-    deal_rows((keep, send), (slice(None),), sum_ref, order, 16)
-
-
-def expand_grad(y2, dh, order, deps=()):
-    return launch(
-        deps,
-        functools.partial(expand_grad_kernel, order=order),
-        grid=(4,),
-        out_shape=(jax.ShapeDtypeStruct((256, 2048), bf16),) * 2,
-        in_specs=[whole((512, 1024)), pl.BlockSpec((1024, 512), lambda k: (0, k))],
-        out_specs=(pl.BlockSpec((256, 512), lambda k: (0, k)),) * 2,
-        scratch_shapes=[pltpu.VMEM((512, 512), f32)],
-        cost_estimate=takes(5),
-        name="expand_grad",
-    )(y2, dh)
-
-
-def reduce_grad_kernel(act_ref, df_ref, u_ref, dz_ref, keep, send, red_ref, out_ref, *, order):
+def feed_grads_kernel(
+    y2_ref, dh_ref, act_ref, df_ref, u_ref, dz_ref, e_keep, e_send, r_keep, r_send, exp_ref, red_ref, out_ref, *, e_order, r_order
+):
     step = pl.program_id(0)
+    exp_ref[...] = dot(y2_ref[...], dh_ref[...])
     red_ref[pl.ds(pl.multiple_of(step * 512, 512), 512), :] = dot(act_ref[...], df_ref[...])
+    deal_rows((e_keep, e_send), (slice(None),), exp_ref, e_order, 16)
 
     @pl.when(step == 0)
     def _():
@@ -665,29 +650,31 @@
     @pl.when(step == 3)
     def _():
         for p in range(32):
-            owner = dealt_owner(p, order)
-            ref, first = (keep, send)[p // 16], p % 16 * 80
+            owner = dealt_owner(p, r_order)
+            ref, first = (r_keep, r_send)[p // 16], p % 16 * 80
             ref[first : first + 64] = red_ref[pl.ds(pl.multiple_of(owner * 64, 64), 64), :].astype(bf16)
             ref[first + 64 : first + 80] = out_ref[pl.ds(pl.multiple_of(owner * 16, 16), 16), :].astype(bf16)
 
 
-def reduce_grad(act, df, u, dz, order, deps=()):
-    return launch(
-        deps,
-        functools.partial(reduce_grad_kernel, order=order),
+def feed_grads(y2, dh, act, df, u, dz, e_order, r_order, deps=()):
+    return launch(
+        deps,
+        functools.partial(feed_grads_kernel, e_order=e_order, r_order=r_order),
         grid=(4,),
-        out_shape=(jax.ShapeDtypeStruct((1280, 512), bf16),) * 2,
+        out_shape=(jax.ShapeDtypeStruct((256, 2048), bf16),) * 2 + (jax.ShapeDtypeStruct((1280, 512), bf16),) * 2,
         in_specs=[
+            whole((512, 1024)),
+            pl.BlockSpec((1024, 512), lambda k: (0, k)),
             pl.BlockSpec((512, 1024), lambda k: (k, 0)),
             whole((1024, 512)),
             pl.BlockSpec((512, 1024), lambda k: (1, 0)),
             whole((1024, 512)),
         ],
-        out_specs=(whole((1280, 512)),) * 2,
-        scratch_shapes=[pltpu.VMEM((2048, 512), f32), pltpu.VMEM((512, 512), f32)],
-        cost_estimate=takes(6),
-        name="reduce_grad",
-    )(act, df, u, dz)
+        out_specs=(pl.BlockSpec((256, 512), lambda k: (0, k)),) * 2 + (whole((1280, 512)),) * 2,
+        scratch_shapes=[pltpu.VMEM((512, 512), f32), pltpu.VMEM((2048, 512), f32), pltpu.VMEM((512, 512), f32)],
+        cost_estimate=takes(11),
+        name="feed_grads",
+    )(y2, dh, act, df, u, dz)
 
 
 def kernel_grad_kernel(dd_ref, band_ref, dk_ref):
@@ -843,7 +830,7 @@
     )(own, oth)
 
 
-def conv_back_kernel(valid_ref, dd_ref, ddh_ref, tap_ref, df_ref, w_ref, back_ref, *, offset):
+def conv_back_kernel(valid_ref, dd_ref, ddh_ref, tap_ref, df_ref, w_ref, back_ref):
     step = pl.program_id(0)
 
     @pl.when(step == 0)
@@ -860,51 +847,50 @@
         cols = slice(tile * 128, tile * 128 + 128)
         for q, value in enumerate(split_lanes(*sums[2 * tile : 2 * tile + 2])):
             value = value * (chunk_mask(sizes, q // 2, q % 2) * conv_scale)
-            if tile == 0 and offset == 0:
+            if tile == 0:
                 value = jnp.where(keep, own[q][:, cols], value)
             df_ref[q, :, cols] = value.astype(bf16)
 
 
-def conv_back(valid, dd, ddh, taps, offset, steps, deps=()):
-    return launch(
-        deps,
-        functools.partial(conv_back_kernel, offset=offset),
-        grid=(steps,),
-        out_shape=jax.ShapeDtypeStruct((4, 256, 256 * steps), bf16),
+def conv_back(valid, dd, ddh, taps, deps=()):
+    return launch(
+        deps,
+        conv_back_kernel,
+        grid=(4,),
+        out_shape=jax.ShapeDtypeStruct((4, 256, 1024), bf16),
         in_specs=[
             SMEM,
-            pl.BlockSpec((4, 256, 256), lambda t: (0, 0, t + offset)),
-            pl.BlockSpec((4, 64, 256), lambda t: (0, 0, t + offset)),
-            pl.BlockSpec((7, 7, 256), lambda t: (0, 0, t + offset)),
+            pl.BlockSpec((4, 256, 256), lambda t: (0, 0, t)),
+            pl.BlockSpec((4, 64, 256), lambda t: (0, 0, t)),
+            pl.BlockSpec((7, 7, 256), lambda t: (0, 0, t)),
         ],
         out_specs=pl.BlockSpec((4, 256, 256), lambda t: (0, 0, t)),
         scratch_shapes=[pltpu.VMEM((2, 16, 256, 256), bf16), pltpu.VMEM((4, 13, 5, 16, 256), bf16)],
-        cost_estimate=takes(4.5 * steps),
+        cost_estimate=takes(16),
         name="conv_back",
     )(valid, dd, ddh, taps)
 
 
-def in_grad_kernel(y1_ref, da_ref, db_ref, keep, send, sum_ref, *, order):
-    for k, ref in enumerate((da_ref, db_ref)):
-        sum_ref[k] = dot(y1_ref[...], ref[...])
-        deal_rows((keep, send), (slice(k * 512, (k + 1) * 512),), sum_ref.at[k], order, 16)
-
-
-def in_grad(y1, da, db, order, deps=()):
-    vmem = pl.BlockSpec(memory_space=pltpu.VMEM)
+def in_grad_kernel(y1_ref, df_ref, keep, send, sum_ref, *, order):
+    sum_ref[...] = dot(y1_ref[...], df_ref[...])
+    deal_rows((keep, send), (slice(None),), sum_ref, order, 16)
+
+
+def in_grad(y1, df, order, deps=()):
     return launch(
         deps,
         functools.partial(in_grad_kernel, order=order),
+        grid=(2,),
         out_shape=(jax.ShapeDtypeStruct((256, 1024), bf16),) * 2,
-        in_specs=[vmem] * 3,
-        out_specs=(vmem, vmem),
-        scratch_shapes=[pltpu.VMEM((2, 512, 512), f32)],
+        in_specs=[whole((512, 1024)), pl.BlockSpec((1024, 512), lambda k: (0, k))],
+        out_specs=(pl.BlockSpec((256, 512), lambda k: (0, k)),) * 2,
+        scratch_shapes=[pltpu.VMEM((512, 512), f32)],
         cost_estimate=takes(4),
         name="in_grad",
-    )(y1, da, db)
-
-
-def last_kernel(valid_ref, da_ref, db_ref, xp_ref, dx2_ref, *rest, order, dealt):
+    )(y1, df)
+
+
+def last_kernel(valid_ref, df_ref, xp_ref, dx2_ref, *rest, order, dealt):
     weights, (wide_ref, out_ref, late_ref, held_ref, win_ref) = rest[:8], rest[8:]
     q = pl.program_id(0)
 
@@ -914,10 +900,11 @@
         place_rows(win_ref, weights, order, own_number(dealt), 16)
 
     mask = pair_mask(extents(valid_ref), q)
-    da, db = da_ref[...], db_ref[...]
-    late_ref[2:3] += column_sum(da.astype(f32))
-    late_ref[3:4] += column_sum(db.astype(f32))
-    grad = mask * (dot_nt(da, win_ref[:, 0:512]) + dot_nt(db, win_ref[:, 512:1024]))
+    df = df_ref[...]
+    sums = column_sum(df.astype(f32))
+    late_ref[2:3] += sums[:, 0:512]
+    late_ref[3:4] += sums[:, 512:1024]
+    grad = mask * dot_nt(df, win_ref[...])
     normed, inverse = normalize(xp_ref[...].astype(f32))
     late_ref[0:1] += column_sum(grad * normed)
     late_ref[1:2] += column_sum(grad)
@@ -929,7 +916,7 @@
         unpermute(held_ref, out_ref)
 
 
-def last_call(valid, da, db, xp, dx2, w_in, wide, order, dealt, deps=()):
+def last_call(valid, df, xp, dx2, w_in, wide, order, dealt, deps=()):
     def chunk(width):
         return pl.BlockSpec((512, width), lambda q: (q, 0))
 
@@ -938,12 +925,12 @@
         functools.partial(last_kernel, order=order, dealt=dealt),
         grid=(2,),
         out_shape=(jax.ShapeDtypeStruct((2, 512, 512), bf16), jax.ShapeDtypeStruct((8, 512), f32)),
-        in_specs=[SMEM] + [chunk(512)] * 4 + [whole((64, 1024))] * 8 + [whole(wide.shape)],
+        in_specs=[SMEM, chunk(1024), chunk(512), chunk(512)] + [whole((64, 1024))] * 8 + [whole(wide.shape)],
         out_specs=(whole((2, 512, 512)), whole((8, 512))),
         scratch_shapes=[pltpu.VMEM((4, 256, 512), bf16), pltpu.VMEM((512, 1024), bf16)],
         cost_estimate=takes(7),
         name="last",
-    )(valid, *(v.reshape(1024, -1) for v in (da, db, xp, dx2)), *w_in, wide)
+    )(valid, *(v.reshape(1024, -1) for v in (df, xp, dx2)), *w_in, wide)
 
 
 def repeat(value):
@@ -1262,34 +1249,36 @@
 
     r_order, e_order, plain = ((1, 0, 3, 2), (0, 1, 3, 2), "plain") if dealt else ("none",) * 3
     if dealt:
-        e_keep, e_send, token = expand_grad(y2, flat(dh), e_order)
-        e_got = swap_row(e_send)
-        r_keep, r_send, token = reduce_grad(act, flat(df), u, flat(dz), r_order, [token])
-        r_got = swap_row(r_send)
+        e_keep, e_send, r_keep, r_send, token = feed_grads(
+            y2, flat(dh), act, flat(df), u, flat(dz), e_order, r_order
+        )
+        e_got, r_got = swap_row(e_send), swap_row(r_send)
         dk, token = kernel_grad(dd, band, [token])
-        r_keep, r_send, e_keep, e_send, token = combine(([r_keep, r_got], 2), ([e_keep, e_got], 2), deps=[token])
-        r_got, e_got = swap_img(r_send, 2), swap_img(e_send, 1)
         s_keep, s_send, token = gate_grads(
             u, flat(dv), s512, s2048, s1024, dk.reshape(512, 128), flat_pair + deep, [token]
         )
         s_got = swap_row(s_send)
-        df_a, token = conv_back(valid, dd, dd_halo, taps, 0, 2, [token])
-        *small, token = combine(([s_keep, s_got], 4), deps=[token])
+        r_keep, r_send, e_keep, e_send, *small, token = combine(
+            ([r_keep, r_got], 2), ([e_keep, e_got], 2), ([s_keep, s_got], 4), deps=[token]
+        )
+        r_got, e_got = swap_img(r_send, 2), swap_img(e_send, 1)
         small = small[:1] + [swap_img(v, m) for v, m in zip(small[1:], masks_of(flat_pair)[1:])]
-        df_b, token = conv_back(valid, dd, dd_halo, taps, 2, 2, [token])
+        dfused, token = conv_back(valid, dd, dd_halo, taps, [token])
         r_keep, r_send, e_keep, e_send, *small, token = combine(
             ([r_keep, r_got], 2), ([e_keep, e_got], 2), (small, 4), deps=[token]
         )
         r_got, e_got = swap_img(r_send, 1), swap_img(e_send, 2)
         small = small[:1] + [swap_img(v, m) for v, m in zip(small[1:], masks_of(deep)[1:])]
-        i_keep, i_send, token = in_grad(y1t, flat(df_a), flat(df_b), plain, [token])
+        i_keep, i_send, token = in_grad(y1t, flat(dfused), plain, [token])
         i_got = swap_row(i_send)
         *parts, token = merge(r_keep, r_got, e_keep, e_got, [token])
         parts = parts[:1] + [swap_img(v, m) for v, m in zip(parts[1:], masks_of(deep)[1:])]
-        fgrad, late, token = last_call(valid, df_a, df_b, xp, dx2, w_in, wide, in_order, dealt, [token])
+        fgrad, late, token = last_call(
+            valid, dfused, xp, dx2, w_in, wide, in_order, dealt, [token] + small[1:]
+        )
+        dealt_rows, token = deal(i_keep, i_got, small, [token] + parts[1:])
+        mixed = spread(dealt_rows)
         red_sum, out_sum, exp_sum, token = finish(parts, [token])
-        dealt_rows, token = deal(i_keep, i_got, small, [token])
-        mixed = spread(dealt_rows)
         late, got = sum_img(late + swap_row(late), (0, 1, 2, 3))
         own, oth = mixed, swap_row(after(mixed, late))
         sums = late_sums(late, got, [token])
@@ -1302,12 +1291,11 @@
         everything = slice(None)
         dk, token = kernel_grad(dd, band)
         s_keep, s_send, token = gate_grads(u, flat(dv), s512, s2048, s1024, dk.reshape(512, 128), plain)
-        e_parts = expand_grad(y2, flat(dh), e_order)[:2]
-        r_parts = reduce_grad(act, flat(df), u, flat(dz), r_order)[:2]
-        df_a, _ = conv_back(valid, dd, dd_halo, taps, 0, 2)
-        df_b, _ = conv_back(valid, dd, dd_halo, taps, 2, 2)
-        i_parts = in_grad(y1t, flat(df_a), flat(df_b), plain)[:2]
-        fgrad, late, token = last_call(valid, df_a, df_b, xp, dx2, w_in, wide, in_order, dealt)
+        parts = feed_grads(y2, flat(dh), act, flat(df), u, flat(dz), e_order, r_order)
+        e_parts, r_parts = parts[:2], parts[2:4]
+        dfused, _ = conv_back(valid, dd, dd_halo, taps)
+        i_parts = in_grad(y1t, flat(dfused), plain)[:2]
+        fgrad, late, token = last_call(valid, dfused, xp, dx2, w_in, wide, in_order, dealt)
         sums = late_sums(*sum_img(late + swap_row(late), list(range(bits))))
         exp_sum, in_sum = total(e_parts, everything), total(i_parts, everything)
         red_sum, out_sum = total(r_parts, slice(0, 64)), total(r_parts, slice(64, 80))

time: 235 us -> 227 us (0.966)
  Pallas kernels: 138 us -> 130 us
  starting transfers between devices: 52.2 us -> 56 us
    pallas_call x23 -> x20, Pallas kernels: 138 us -> 130 us  [launch(): return lambda *args: call(*args, *deps)]
    ppermute x28, waiting for transfers between devices: 19.9 us -> 12.3 us  [swap_img(): lax.ppermute(value, 'img', [(k, k ^ mask) for k in range(lax.axis_size('i...]
    all_to_all x2, waiting for transfers between devices: 2.81 us -> 6.7 us  [spread(): return lax.all_to_all(value, 'img', split_axis=0, concat_axis=0, tiled=True)]
    unnamed x113 -> x103, local copies, waits for them, and re-layouts: 12.5 us -> 11.1 us
  transfers between devices with their start and end apart: 46 -> 46, of which waited for: 14 -> 12; matrix products, arithmetic and copies ran while one was open for 1% -> 2% of each run, Pallas kernels for 38% -> 37%
where the time goes in v2:
time: 227 us; the launch traced here: 226 us
  Pallas kernels  130 us (57%)
  starting transfers between devices  56 us (25%)
  waiting for transfers between devices  25 us (11%)
  local copies, waits for them, and re-layouts  12.9 us (6%)
    pallas_call x20, Pallas kernels, launch(): return lambda *args: call(*args, *deps)  130 us
    ppermute x28, starting transfers between devices, swap_img(): lax.ppermute(value, 'img', [(k, k ^ mask) for k in range(lax.axis_size('i...  40.5 us
    ppermute x28, waiting for transfers between devices, swap_img(): lax.ppermute(value, 'img', [(k, k ^ mask) for k in range(lax.axis_size('i...  12.3 us
    all_to_all x2, starting transfers between devices, spread(): return lax.all_to_all(value, 'img', split_axis=0, concat_axis=0, tiled=True)  12.1 us
    unnamed x103, local copies, waits for them, and re-layouts  11.1 us
    all_to_all x2, waiting for transfers between devices, spread(): return lax.all_to_all(value, 'img', split_axis=0, concat_axis=0, tiled=True)  6.7 us
    ppermute x16, waiting for transfers between devices, swap_row(): return lax.ppermute(value, 'row', [(0, 1), (1, 0)])  5.93 us
  transfers between devices with their start and end apart: 46, of which 12 were waited for; matrix products, arithmetic and copies ran while one was open for 2% of the time, Pallas kernels for 37%

profile of v2, /device:TPU:0, one launch (start us, length us, event | category | flops | bytes accessed | tf_op | source)
XLA Modules:
  0.0 225.7 jit_solution(13097021511138295476)
XLA Ops:
  1.2 2.7 %collective-permute-start.2 = (bf16[16,1024]{1,0:T(8,128)(2,1)}, bf16[16,1024]{1,0:T(8,128)(2,1)S(1)}, u32[]{:S(2)}, u32[]{:S(2)}) collective-permute-start(bf16[16,1024]{1,0:T(8,128)(2,1)} %refs_0_.3), channel_id=1, source_target_pairs={{0,8},{2,10},{4,12},{6,14},{8,0},{10,2},{12,4},{14,6},{16,24},{18,... | collective-permute-start | bytes 98312 | tf_op jit(solution)/shard_map/ppermute | solution.py:1111
  3.8 2.6 %collective-permute-start.3 = (bf16[16,1024]{1,0:T(8,128)(2,1)}, bf16[16,1024]{1,0:T(8,128)(2,1)S(1)}, u32[]{:S(2)}, u32[]{:S(2)}) collective-permute-start(bf16[16,1024]{1,0:T(8,128)(2,1)} %refs_0_.3), channel_id=1, source_target_pairs={{0,16},{2,18},{4,20},{6,22},{8,24},{10,26},{12,28},{14,30},{16,0},... | collective-permute-start | bytes 98312 | tf_op jit(solution)/shard_map/ppermute | solution.py:1111
  6.4 0.8 constant_dynamic-update-slice_fusion.1
  7.3 0.7 constant_dynamic-update-slice_fusion.refs_0_
  8.0 0.9 collective-permute-start.12
  8.9 1.6 vectors.1
  10.5 3.6 %collective-permute-start.13 = (bf16[16,2560]{1,0:T(8,128)(2,1)S(1)}, bf16[16,2560]{1,0:T(8,128)(2,1)S(1)}, u32[]{:S(2)}, u32[]{:S(2)}) collective-permute-start(bf16[16,2560]{1,0:T(8,128)(2,1)S(1)} %constant_dynamic-update-slice_fusion.refs_0_), channel_id=1, source_target_pairs={{0,16},{2,18},{4,20},{6,22},{8,24},{10,26},{12,28},{14,30},{16,0},... | collective-permute-start | bytes 245768 | tf_op jit(solution)/shard_map/ppermute | solution.py:1111
  14.7 1.5 join.3
  16.1 1.8 collective-permute-start.5
  17.9 1.5 collective-permute-start.6
  19.7 0.7 copy-done.9
  20.4 4.9 %prepare.1 = (bf16[4,256,512]{2,1,0:T(8,128)(2,1)}, bf16[4,256,512]{2,1,0:T(8,128)(2,1)}, bf16[4,256,512]{2,1,0:T(8,128)(2,1)}, bf16[4,64,512]{2,1,0:T(8,128)(2,...) custom-call(s32[32,32]{1,0:T(8,128)} %bitcast.67, s32[32,32]{1,0:T(8,128)} %copy-done.46, bf16[2,512,512]{2,1,0:T(8,128)(2,1)} %bitcast.52, ...), custom_call_target="tpu_custom_call" | custom-call | flops 4000000000 | tf_op jit(solution)/shard_map/prepare/pallas_call | solution.py:190
  25.4 0.6 collective-permute-done.6.refs_6_
  26.1 0.6 copy-done.28
  26.7 1.8 join.4
  28.5 1.6 collective-permute-start.15
  30.1 1.1 broadcast_in_dim.2
  31.1 5.5 %all-to-all-start = ((bf16[16,64,512]{2,1,0:T(8,128)(2,1)}), bf16[16,64,512]{2,1,0:T(8,128)(2,1)S(1)}, u32[]{:S(2)}, u32[]{:S(2)}) async-start(bf16[16,64,512]{2,1,0:T(8,128)(2,1)} %broadcast_in_dim.2), calls=%async_computation | async-start | bytes 2097152 | tf_op jit(solution)/shard_map/all_to_all | solution.py:1141
  37.8 0.8 pad_convert_fusion.refs_13_.refs_3_
  38.6 0.7 copy-done.19
  39.3 1.9 join.5
  41.3 1.9 collective-permute-start.16
  44.0 20.9 %forward.1 = (f32[4,256,1024]{2,1,0:T(8,128)}, bf16[16,13,5,16,256]{4,3,2,1,0:T(8,128)(2,1)}, f32[4,256,128]{2,1,0:T(8,128)}, f32[8,128]{1,0:T(8,128)}) custom-call(s32[32,32]{1,0:T(8,128)} %bitcast.68, s32[32,32]{1,0:T(8,128)} %copy-done.46, bf16[4,256,512]{2,1,0:T(8,128)(2,1)} %get-tuple-element.122.refs_2_, ...), custom_call_target="tpu_custom_call" | custom-call | flops 24000000000 | tf_op jit(solution)/shard_map/forward/pallas_call | solution.py:190
  65.6 0.9 collective-permute-done.16.refs_6_.refs_10_
  66.5 2.3 %collective-permute-done.17.refs_7_.refs_11_ = bf16[128,2560]{1,0:T(8,128)(2,1)} collective-permute-done((bf16[128,2560]{1,0:T(8,128)(2,1)S(1)}, bf16[128,2560]{1,0:T(8,128)(2,1)}, u32[]{:S(2)}, u32[]{:S(2)}) %collective-permute-start.17) | collective-permute-done | bytes 655392 | tf_op jit(solution)/shard_map/ppermute | solution.py:1115
  68.8 0.9 collective-permute-done.18.refs_8_.refs_12_
  69.7 1.0 copy-done.10
  70.7 25.8 %middle.1 = (bf16[2,512,512]{2,1,0:T(8,128)(2,1)}, bf16[2048,1024]{1,0:T(8,128)(2,1)}, bf16[512,1024]{1,0:T(8,128)(2,1)}, bf16[1024,1024]{1,0:T(8,128)(2,1)}, bf...) custom-call(s32[32,32]{1,0:T(8,128)} %bitcast.69, ...), custom_call_target="tpu_custom_call" | custom-call | flops 30000001024 | tf_op jit(solution)/shard_map/middle/pallas_call | solution.py:190
  96.6 11.3 %feed_grads.1 = (bf16[256,2048]{1,0:T(8,128)(2,1)}, bf16[256,2048]{1,0:T(8,128)(2,1)}, bf16[1280,512]{1,0:T(8,128)(2,1)}, bf16[1280,512]{1,0:T(8,128)(2,1)}, f32[8,128]{1,0:T(8,128)}) custom-call(bf16[512,1024]{1,0:T(8,128)(2,1)} %get-tuple-element.138.refs_0_, bf16[1024,2048]{1,0:T(8,128)(2,1)} %get-tuple-element.139.refs_1_, ...), custom_call_target="tpu_custom_call" | custom-call | flops 11000000512 | tf_op jit(solution)/shard_map/feed_grads/pallas_call | solution.py:190
  108.7 12.9 %kernel_grad.1 = (f32[16,32,128]{2,1,0:T(8,128)}, f32[8,128]{1,0:T(8,128)}) custom-call(bf16[4,256,1024]{2,1,0:T(8,128)(2,1)} %bitcast.47, bf16[16,13,5,16,256]{4,3,2,1,0:T(8,128)(2,1)} %get-tuple-element.152.refs_1_, f32[8,128]{1,0:T(8,128)} %get-tuple-element.153.refs_2_), custom_call_target="tpu_custom_call" | custom-call | flops 12999999488 | tf_op jit(solution)/shard_map/kernel_grad/pallas_call | solution.py:190
  121.6 3.4 %gate_grads.1 = (bf16[256,512]{1,0:T(8,128)(2,1)}, bf16[256,512]{1,0:T(8,128)(2,1)}, f32[8,128]{1,0:T(8,128)}) custom-call(bf16[1024,1024]{1,0:T(8,128)(2,1)} %get-tuple-element.142.refs_4_.refs_0_, bf16[1024,1024]{1,0:T(8,128)(2,1)} %get-tuple-element.148.refs_1_, f32[8,512]{1,0:T(8,128)} %get-tuple-element.149.refs_2_, ...), custom_call_target="tpu_custom_call" | custom-call | flops 3000000000 | tf_op jit(solution)/shard_map/gate_grads/pallas_call | solution.py:190
  125.2 1.5 collective-permute-done.23
  126.7 0.7 copy-done.21
  127.8 4.5 %combine.2 = (bf16[4,160,512]{2,1,0:T(8,128)(2,1)}, bf16[4,160,512]{2,1,0:T(8,128)(2,1)}, bf16[4,32,2048]{2,1,0:T(8,128)(2,1)}, bf16[4,32,2048]{2,1,0:T(8,128)(2...) custom-call(bf16[2,4,160,512]{3,2,1,0:T(8,128)(2,1)} %bitcast.79, ...), custom_call_target="tpu_custom_call" | custom-call | flops 2000000000 | tf_op jit(solution)/shard_map/combine/pallas_call | solution.py:190
  132.3 1.5 collective-permute-start.24
  134.4 1.5 collective-permute-start.26
  136.4 1.5 collective-permute-start.28
  137.9 15.9 %conv_back.1 = (bf16[4,256,1024]{2,1,0:T(8,128)(2,1)}, f32[8,128]{1,0:T(8,128)}) custom-call(s32[32,32]{1,0:T(8,128)} %bitcast.70, bf16[4,256,1024]{2,1,0:T(8,128)(2,1)} %bitcast.48, bf16[4,64,1024]{2,1,0:T(8,128)(2,1)} %copy-done.15, f32[7,7,1024]{2,1,0:T(8,128)} %pad_convert_fusion.refs_13_.refs_3_, f32[8,128]{1,0:T(8,128)} %get-tuple-element.159.refs_4_), custom_call_target="tpu_custom_call" | custom-call | flops 16000000000 | tf_op jit(solution)/shard_map/conv_back/pallas_call | solution.py:190
  154.8 2.8 %combine.3 = (bf16[1,320,512]{2,1,0:T(8,128)(2,1)}, bf16[1,320,512]{2,1,0:T(8,128)(2,1)}, bf16[1,64,2048]{2,1,0:T(8,128)(2,1)}, bf16[1,64,2048]{2,1,0:T(8,128)(2...) custom-call(bf16[2,1,320,512]{3,2,1,0:T(8,128)(2,1)} %bitcast.86, ...), custom_call_target="tpu_custom_call" | custom-call | flops 2000000000 | tf_op jit(solution)/shard_map/combine/pallas_call | solution.py:190
  157.6 1.5 collective-permute-start.29
  159.6 1.5 collective-permute-start.31
  161.1 2.4 %collective-permute-start.32 = (bf16[16,512]{1,0:T(8,128)(2,1)}, bf16[16,512]{1,0:T(8,128)(2,1)S(1)}, u32[]{:S(2)}, u32[]{:S(2)}) collective-permute-start(bf16[16,512]{1,0:T(8,128)(2,1)} %bitcast.74), channel_id=1, source_target_pairs={{0,16},{2,18},{4,20},{6,22},{8,24},{10,26},{12,28},{14,30},{16,0},... | collective-permute-start | bytes 49160 | tf_op jit(solution)/shard_map/ppermute | solution.py:1111
  164.0 4.2 %in_grad.1 = (bf16[256,1024]{1,0:T(8,128)(2,1)}, bf16[256,1024]{1,0:T(8,128)(2,1)}, f32[8,128]{1,0:T(8,128)}) custom-call(bf16[512,1024]{1,0:T(8,128)(2,1)} %get-tuple-element.175.refs_0_, bf16[1024,1024]{1,0:T(8,128)(2,1)} %bitcast.77, f32[8,128]{1,0:T(8,128)} %get-tuple-element.176.refs_2_), custom_call_target="tpu_custom_call" | custom-call | flops 4000000000 | tf_op jit(solution)/shard_map/in_grad/pallas_call | solution.py:190
  169.0 2.1 merge.1
  171.7 3.3 %collective-permute-start.40 = (bf16[144,512]{1,0:T(8,128)(2,1)}, bf16[144,512]{1,0:T(8,128)(2,1)S(1)}, u32[]{:S(2)}, u32[]{:S(2)}) collective-permute-start(bf16[144,512]{1,0:T(8,128)(2,1)} %get-tuple-element.186), channel_id=1, source_target_pairs={{0,16},{2,18},{4,20},{6,22},{8,24},{10,26},{12,28},{14,30},{16,0},... | collective-permute-start | bytes 442376 | tf_op jit(solution)/shard_map/ppermute | solution.py:1111
  176.1 6.3 %last.1 = (bf16[2,512,512]{2,1,0:T(8,128)(2,1)}, f32[8,512]{1,0:T(8,128)}, f32[8,128]{1,0:T(8,128)}) custom-call(s32[32,32]{1,0:T(8,128)} %bitcast.71, bf16[1024,1024]{1,0:T(8,128)(2,1)} %bitcast.78, bf16[1024,512]{1,0:T(8,128)(2,1)} %bitcast.82, f32[1024,512]{1,0:T(8,128)} %get-tuple-element.161.refs_3_, bf16[64,1024]{1,0:T(8,128)(2,1)} %get-tuple-element.124.refs_4_, ...), custom_call_target="tpu_custom_call" | custom-call | flops 7000000000 | tf_op jit(solution)/shard_map/last/pallas_call | solution.py:190
  182.5 3.7 %collective-permute-done.40.refs_8_.refs_2_ = bf16[144,512]{1,0:T(8,128)(2,1)S(1)} collective-permute-done((bf16[144,512]{1,0:T(8,128)(2,1)}, bf16[144,512]{1,0:T(8,128)(2,1)S(1)}, u32[]{:S(2)}, u32[]{:S(2)}) %collective-permute-start.40) | collective-permute-done | bytes 147488 | tf_op jit(solution)/shard_map/ppermute | solution.py:1111
  186.2 0.6 copy-done.23
  187.1 2.3 %deal.1 = (bf16[256,1536]{1,0:T(8,128)(2,1)}, f32[8,128]{1,0:T(8,128)}) custom-call(bf16[256,1024]{1,0:T(8,128)(2,1)} %get-tuple-element.188.refs_0_, bf16[256,1024]{1,0:T(8,128)(2,1)} %copy-done.16, bf16[16,512]{1,0:T(8,128)(2,1)} %bitcast.94, bf16[16,512]{1,0:T(8,128)(2,1)} %copy-done.47, bf16[16,512]{1,0:T(8,128)(2,1)} %copy-done.48, ...), custom_call_target="tpu_custom_call" | custom-call | flops 2000000000 | tf_op jit(solution)/shard_map/deal/pallas_call | solution.py:190
  189.3 6.5 %all-to-all-start.1 = ((bf16[16,16,1536]{2,1,0:T(8,128)(2,1)}), bf16[16,16,1536]{2,1,0:T(8,128)(2,1)S(1)}, u32[]{:S(2)}, u32[]{:S(2)}) async-start(bf16[16,16,1536]{2,1,0:T(8,128)(2,1)} %bitcast.46), calls=%async_computation.1 | async-start | bytes 1572864 | tf_op jit(solution)/shard_map/all_to_all | solution.py:1141
  196.0 1.2 collective-permute-done.34
  197.1 1.9 collective-permute-start.35
  199.1 1.9 collective-permute-done.35
  201.0 1.9 collective-permute-start.36
  202.8 1.9 collective-permute-done.36
  204.7 1.8 collective-permute-start.37
  206.5 2.2 collective-permute-done.37
  208.8 6.7 %all-to-all-done.1 = bf16[16,16,1536]{2,1,0:T(8,128)(2,1)S(1)} async-done(((bf16[16,16,1536]{2,1,0:T(8,128)(2,1)}), bf16[16,16,1536]{2,1,0:T(8,128)(2,1)S(1)}, u32[]{:S(2)}, u32[]{:S(2)}) %all-to-all-start.1) | async-done | bytes 786464 | tf_op jit(solution)/shard_map/all_to_all | solution.py:1141
  215.5 1.7 collective-permute-start.38
  217.2 1.9 finish.1
  219.1 1.1 collective-permute-done.38.refs_1_
  220.8 1.3 late.1
  222.1 0.9 copy-done.11
  223.0 2.6 %unpack.1 = (f32[16,1024]{1,0:T(8,128)}, f32[7,7,992]{2,1,0:T(8,128)}, f32[992]{0:T(1024)}, f32[32,64]{1,0:T(8,128)}, f32[64,128]{1,0:T(8,128)}, /*index=5*/f32[...) custom-call(bf16[256,1536]{1,0:T(8,128)(2,1)} %bitcast.45, ...), custom_call_target="tpu_custom_call" | custom-call | flops 3000000000 | tf_op jit(solution)/shard_map/unpack/pallas_call | solution.py:190
  (159 shorter events, 12.2 us)
Async XLA Ops:
  0.7 13.4 %copy-start.45 = (s32[2,16,32]{2,1,0:T(8,128)S(1)}, s32[2,16,32]{2,1,0:T(8,128)}, u32[]{:S(2)}) copy-start(s32[2,16,32]{2,1,0:T(8,128)} %param.25) | copy-start | bytes 12292
  0.7 18.8 %collective-permute-start.1 = (bf16[2,512,512]{2,1,0:T(8,128)(2,1)}, bf16[2,512,512]{2,1,0:T(8,128)(2,1)S(1)}, u32[]{:S(2)}, u32[]{:S(2)}) collective-permute-start(bf16[2,512,512]{2,1,0:T(8,128)(2,1)} %bitcast.51), channel_id=1, source_target_pairs={{0,1},{1,0},{2,3},{3,2},{4,5},{5,4},{6,7},{7,6},{8,9},{9,8},{10,11... | collective-permute-start | bytes 3145736 | tf_op jit(solution)/shard_map/ppermute | solution.py:1115
  1.2 9.3 %collective-permute-start.2 = (bf16[16,1024]{1,0:T(8,128)(2,1)}, bf16[16,1024]{1,0:T(8,128)(2,1)S(1)}, u32[]{:S(2)}, u32[]{:S(2)}) collective-permute-start(bf16[16,1024]{1,0:T(8,128)(2,1)} %refs_0_.3), channel_id=1, source_target_pairs={{0,8},{2,10},{4,12},{6,14},{8,0},{10,2},{12,4},{14,6},{16,24},{18,... | collective-permute-start | bytes 98312 | tf_op jit(solution)/shard_map/ppermute | solution.py:1111
  3.8 10.2 %collective-permute-start.3 = (bf16[16,1024]{1,0:T(8,128)(2,1)}, bf16[16,1024]{1,0:T(8,128)(2,1)S(1)}, u32[]{:S(2)}, u32[]{:S(2)}) collective-permute-start(bf16[16,1024]{1,0:T(8,128)(2,1)} %refs_0_.3), channel_id=1, source_target_pairs={{0,16},{2,18},{4,20},{6,22},{8,24},{10,26},{12,28},{14,30},{16,0},... | collective-permute-start | bytes 98312 | tf_op jit(solution)/shard_map/ppermute | solution.py:1111
  6.4 7.6 %collective-permute-start.4 = (bf16[16,1024]{1,0:T(8,128)(2,1)}, bf16[16,1024]{1,0:T(8,128)(2,1)S(1)}, u32[]{:S(2)}, u32[]{:S(2)}) collective-permute-start(bf16[16,1024]{1,0:T(8,128)(2,1)} %refs_0_.3), channel_id=1, source_target_pairs={{0,24},{2,26},{4,28},{6,30},{8,16},{10,18},{12,20},{14,22},{16,8},... | collective-permute-start | bytes 98312 | tf_op jit(solution)/shard_map/ppermute | solution.py:1111
  8.0 8.1 %copy-start.5 = (bf16[16,2560]{1,0:T(8,128)(2,1)}, bf16[16,2560]{1,0:T(8,128)(2,1)S(1)}, u32[]{:S(2)}) copy-start(bf16[16,2560]{1,0:T(8,128)(2,1)S(1)} %constant_dynamic-update-slice_fusion.refs_0_) | copy-start | bytes 245764
  8.0 9.9 %collective-permute-start.12 = (bf16[16,2560]{1,0:T(8,128)(2,1)S(1)}, bf16[16,2560]{1,0:T(8,128)(2,1)S(1)}, u32[]{:S(2)}, u32[]{:S(2)}) collective-permute-start(bf16[16,2560]{1,0:T(8,128)(2,1)S(1)} %constant_dynamic-update-slice_fusion.refs_0_), channel_id=1, source_target_pairs={{0,8},{2,10},{4,12},{6,14},{8,0},{10,2},{12,4},{14,6},{16,24},{18,... | collective-permute-start | bytes 245768 | tf_op jit(solution)/shard_map/ppermute | solution.py:1111
  10.5 3.7 %copy-start.42 = (bf16[16,1024]{1,0:T(8,128)(2,1)}, bf16[16,1024]{1,0:T(8,128)(2,1)S(1)}, u32[]{:S(2)}) copy-start(bf16[16,1024]{1,0:T(8,128)(2,1)S(1)} %collective-permute-done.2.refs_1_) | copy-start | bytes 98308
  10.5 14.9 %collective-permute-start.13 = (bf16[16,2560]{1,0:T(8,128)(2,1)S(1)}, bf16[16,2560]{1,0:T(8,128)(2,1)S(1)}, u32[]{:S(2)}, u32[]{:S(2)}) collective-permute-start(bf16[16,2560]{1,0:T(8,128)(2,1)S(1)} %constant_dynamic-update-slice_fusion.refs_0_), channel_id=1, source_target_pairs={{0,16},{2,18},{4,20},{6,22},{8,24},{10,26},{12,28},{14,30},{16,0},... | collective-permute-start | bytes 245768 | tf_op jit(solution)/shard_map/ppermute | solution.py:1111
  14.0 11.3 %collective-permute-start.14 = (bf16[16,2560]{1,0:T(8,128)(2,1)S(1)}, bf16[16,2560]{1,0:T(8,128)(2,1)S(1)}, u32[]{:S(2)}, u32[]{:S(2)}) collective-permute-start(bf16[16,2560]{1,0:T(8,128)(2,1)S(1)} %constant_dynamic-update-slice_fusion.refs_0_), channel_id=1, source_target_pairs={{0,24},{2,26},{4,28},{6,30},{8,16},{10,18},{12,20},{14,22},{16,8},... | collective-permute-start | bytes 245768 | tf_op jit(solution)/shard_map/ppermute | solution.py:1111
  14.1 2.1 collective-permute-start
  16.1 9.2 %collective-permute-start.5 = (bf16[64,1024]{1,0:T(8,128)(2,1)}, bf16[64,1024]{1,0:T(8,128)(2,1)S(1)}, u32[]{:S(2)}, u32[]{:S(2)}) collective-permute-start(bf16[64,1024]{1,0:T(8,128)(2,1)} %get-tuple-element.124.refs_4_), channel_id=1, source_target_pairs={{0,2},{2,0},{4,6},{6,4},{8,10},{10,8},{12,14},{14,12},{16,18},{18,... | collective-permute-start | bytes 393224 | tf_op jit(solution)/shard_map/ppermute | solution.py:1111
  17.9 7.4 %copy-start.36 = (bf16[16,2560]{1,0:T(8,128)(2,1)}, bf16[16,2560]{1,0:T(8,128)(2,1)S(1)}, u32[]{:S(2)}) copy-start(bf16[16,2560]{1,0:T(8,128)(2,1)S(1)} %collective-permute-done.12.refs_1_) | copy-start | bytes 245764
  17.9 8.1 %collective-permute-start.6 = (bf16[64,1024]{1,0:T(8,128)(2,1)}, bf16[64,1024]{1,0:T(8,128)(2,1)S(1)}, u32[]{:S(2)}, u32[]{:S(2)}) collective-permute-start(bf16[64,1024]{1,0:T(8,128)(2,1)} %get-tuple-element.124.refs_4_), channel_id=1, source_target_pairs={{0,4},{2,6},{4,0},{6,2},{8,12},{10,14},{12,8},{14,10},{16,20},{18,... | collective-permute-start | bytes 393224 | tf_op jit(solution)/shard_map/ppermute | solution.py:1111
  19.4 6.6 %collective-permute-start.7 = (bf16[64,1024]{1,0:T(8,128)(2,1)}, bf16[64,1024]{1,0:T(8,128)(2,1)S(1)}, u32[]{:S(2)}, u32[]{:S(2)}) collective-permute-start(bf16[64,1024]{1,0:T(8,128)(2,1)} %get-tuple-element.124.refs_4_), channel_id=1, source_target_pairs={{0,6},{2,4},{4,2},{6,0},{8,14},{10,12},{12,10},{14,8},{16,22},{18,... | collective-permute-start | bytes 393224 | tf_op jit(solution)/shard_map/ppermute | solution.py:1111
  25.3 4.7 %copy-start.4 = (bf16[64,512]{1,0:T(8,128)(2,1)S(1)}, bf16[64,512]{1,0:T(8,128)(2,1)}, u32[]{:S(2)}) copy-start(bf16[64,512]{1,0:T(8,128)(2,1)} %param.45) | copy-start | bytes 196612
  28.5 8.2 %copy-start.25 = (bf16[64,1024]{1,0:T(8,128)(2,1)S(1)}, bf16[64,1024]{1,0:T(8,128)(2,1)}, u32[]{:S(2)}) copy-start(bf16[64,1024]{1,0:T(8,128)(2,1)} %get-tuple-element.124.refs_4_) | copy-start | bytes 393220
  28.5 8.3 %copy-start.29 = (bf16[64,1024]{1,0:T(8,128)(2,1)S(1)}, bf16[64,1024]{1,0:T(8,128)(2,1)}, u32[]{:S(2)}) copy-start(bf16[64,1024]{1,0:T(8,128)(2,1)} %copy-done.28) | copy-start | bytes 393220
  28.5 8.8 %copy-start.31 = (bf16[64,1024]{1,0:T(8,128)(2,1)S(1)}, bf16[64,1024]{1,0:T(8,128)(2,1)}, u32[]{:S(2)}) copy-start(bf16[64,1024]{1,0:T(8,128)(2,1)} %copy-done.30) | copy-start | bytes 393220
  28.5 8.9 %copy-start.27 = (bf16[64,1024]{1,0:T(8,128)(2,1)S(1)}, bf16[64,1024]{1,0:T(8,128)(2,1)}, u32[]{:S(2)}) copy-start(bf16[64,1024]{1,0:T(8,128)(2,1)} %copy-done.26) | copy-start | bytes 393220
  28.5 9.3 %copy-start.3 = (bf16[7,7,992]{2,1,0:T(8,128)(2,1)S(1)}, bf16[7,7,992]{2,1,0:T(8,128)(2,1)}, u32[]{:S(2)}) copy-start(bf16[7,7,992]{2,1,0:T(8,128)(2,1)} %param.31) | copy-start | bytes 291652
  28.5 10.1 %collective-permute-start.15 = (bf16[64,2560]{1,0:T(8,128)(2,1)}, bf16[64,2560]{1,0:T(8,128)(2,1)S(1)}, u32[]{:S(2)}, u32[]{:S(2)}) collective-permute-start(bf16[64,2560]{1,0:T(8,128)(2,1)} %get-tuple-element.126.refs_0_), channel_id=1, source_target_pairs={{0,4},{2,6},{4,0},{6,2},{8,12},{10,14},{12,8},{14,10},{16,20},{18,... | collective-permute-start | bytes 983048 | tf_op jit(solution)/shard_map/ppermute | solution.py:1111
  31.1 33.8 %all-to-all-start = ((bf16[16,64,512]{2,1,0:T(8,128)(2,1)}), bf16[16,64,512]{2,1,0:T(8,128)(2,1)S(1)}, u32[]{:S(2)}, u32[]{:S(2)}) async-start(bf16[16,64,512]{2,1,0:T(8,128)(2,1)} %broadcast_in_dim.2), calls=%async_computation | async-start | bytes 2097152 | tf_op jit(solution)/shard_map/all_to_all | solution.py:1141
  36.7 6.5 %collective-permute-start.8 = (bf16[64,1024]{1,0:T(8,128)(2,1)S(1)}, bf16[64,1024]{1,0:T(8,128)(2,1)S(1)}, u32[]{:S(2)}, u32[]{:S(2)}) collective-permute-start(bf16[64,1024]{1,0:T(8,128)(2,1)S(1)} %copy-done.25), channel_id=1, source_target_pairs={{0,1},{1,0},{2,3},{3,2},{4,5},{5,4},{6,7},{7,6},{8,9},{9,8},{10,11... | collective-permute-start | bytes 393224 | tf_op jit(solution)/shard_map/ppermute | solution.py:1115
  36.8 6.4 %collective-permute-start.10 = (bf16[64,1024]{1,0:T(8,128)(2,1)S(1)}, bf16[64,1024]{1,0:T(8,128)(2,1)S(1)}, u32[]{:S(2)}, u32[]{:S(2)}) collective-permute-start(bf16[64,1024]{1,0:T(8,128)(2,1)S(1)} %copy-done.29), channel_id=1, source_target_pairs={{0,1},{1,0},{2,3},{3,2},{4,5},{5,4},{6,7},{7,6},{8,9},{9,8},{10,11... | collective-permute-start | bytes 393224 | tf_op jit(solution)/shard_map/ppermute | solution.py:1115
  37.3 5.9 %collective-permute-start.11 = (bf16[64,1024]{1,0:T(8,128)(2,1)S(1)}, bf16[64,1024]{1,0:T(8,128)(2,1)S(1)}, u32[]{:S(2)}, u32[]{:S(2)}) collective-permute-start(bf16[64,1024]{1,0:T(8,128)(2,1)S(1)} %copy-done.31), channel_id=1, source_target_pairs={{0,1},{1,0},{2,3},{3,2},{4,5},{5,4},{6,7},{7,6},{8,9},{9,8},{10,11... | collective-permute-start | bytes 393224 | tf_op jit(solution)/shard_map/ppermute | solution.py:1115
  37.4 5.9 %collective-permute-start.9 = (bf16[64,1024]{1,0:T(8,128)(2,1)S(1)}, bf16[64,1024]{1,0:T(8,128)(2,1)S(1)}, u32[]{:S(2)}, u32[]{:S(2)}) collective-permute-start(bf16[64,1024]{1,0:T(8,128)(2,1)S(1)} %copy-done.27), channel_id=1, source_target_pairs={{0,1},{1,0},{2,3},{3,2},{4,5},{5,4},{6,7},{7,6},{8,9},{9,8},{10,11... | collective-permute-start | bytes 393224 | tf_op jit(solution)/shard_map/ppermute | solution.py:1115
  41.3 25.2 %collective-permute-start.16 = (bf16[128,2560]{1,0:T(8,128)(2,1)}, bf16[128,2560]{1,0:T(8,128)(2,1)S(1)}, u32[]{:S(2)}, u32[]{:S(2)}) collective-permute-start(bf16[128,2560]{1,0:T(8,128)(2,1)} %get-tuple-element.133.refs_5_.refs_9_), channel_id=1, source_target_pairs={{0,2},{2,0},{4,6},{6,4},{8,10},{10,8},{12,14},{14,12},{16,18},{18,... | collective-permute-start | bytes 1966088 | tf_op jit(solution)/shard_map/ppermute | solution.py:1111
  44.0 21.0 %copy-start.12 = (bf16[128,2560]{1,0:T(8,128)(2,1)S(1)}, bf16[128,2560]{1,0:T(8,128)(2,1)}, u32[]{:S(2)}) copy-start(bf16[128,2560]{1,0:T(8,128)(2,1)} %get-tuple-element.133.refs_5_.refs_9_) | copy-start | bytes 1966084
  65.0 4.8 %copy-start = (bf16[16,64,512]{2,1,0:T(8,128)(2,1)}, bf16[16,64,512]{2,1,0:T(8,128)(2,1)S(1)}, u32[]{:S(2)}) copy-start(bf16[16,64,512]{2,1,0:T(8,128)(2,1)S(1)} %all-to-all-done) | copy-start | bytes 3145732
  65.0 4.7 %collective-permute-start.19 = (bf16[1024,512]{1,0:T(8,128)(2,1)S(1)}, bf16[1024,512]{1,0:T(8,128)(2,1)S(1)}, u32[]{:S(2)}, u32[]{:S(2)}) collective-permute-start(bf16[1024,512]{1,0:T(8,128)(2,1)S(1)} %bitcast.42), channel_id=1, source_target_pairs={{0,1},{1,0},{2,3},{3,2},{4,5},{5,4},{6,7},{7,6},{8,9},{9,8},{10,11... | collective-permute-start | bytes 3145736 | tf_op jit(solution)/shard_map/ppermute | solution.py:1115
  65.1 3.7 %collective-permute-start.17 = (bf16[128,2560]{1,0:T(8,128)(2,1)S(1)}, bf16[128,2560]{1,0:T(8,128)(2,1)}, u32[]{:S(2)}, u32[]{:S(2)}) collective-permute-start(bf16[128,2560]{1,0:T(8,128)(2,1)S(1)} %copy-done.12), channel_id=1, source_target_pairs={{0,1},{1,0},{2,3},{3,2},{4,5},{5,4},{6,7},{7,6},{8,9},{9,8},{10,11... | collective-permute-start | bytes 1966088 | tf_op jit(solution)/shard_map/ppermute | solution.py:1115
  66.5 3.3 %collective-permute-start.18 = (bf16[128,2560]{1,0:T(8,128)(2,1)S(1)}, bf16[128,2560]{1,0:T(8,128)(2,1)}, u32[]{:S(2)}, u32[]{:S(2)}) collective-permute-start(bf16[128,2560]{1,0:T(8,128)(2,1)S(1)} %collective-permute-done.16.refs_6_.refs_10_), channel_id=1, source_target_pairs={{0,1},{1,0},{2,3},{3,2},{4,5},{5,4},{6,7},{7,6},{8,9},{9,8},{10,11... | collective-permute-start | bytes 1966088 | tf_op jit(solution)/shard_map/ppermute | solution.py:1115
  96.5 11.9 %copy-start.2 = (bf16[1024,1024]{1,0:T(8,128)(2,1)S(1)}, bf16[1024,1024]{1,0:T(8,128)(2,1)}, u32[]{:S(2)}) copy-start(bf16[1024,1024]{1,0:T(8,128)(2,1)} %get-tuple-element.137) | copy-start | bytes 6291460
  107.8 18.8 %collective-permute-start.21 = (bf16[1280,512]{1,0:T(8,128)(2,1)}, bf16[1280,512]{1,0:T(8,128)(2,1)S(1)}, u32[]{:S(2)}, u32[]{:S(2)}) collective-permute-start(bf16[1280,512]{1,0:T(8,128)(2,1)} %get-tuple-element.145), channel_id=1, source_target_pairs={{0,1},{1,0},{2,3},{3,2},{4,5},{5,4},{6,7},{7,6},{8,9},{9,8},{10,11... | collective-permute-start | bytes 3932168 | tf_op jit(solution)/shard_map/ppermute | solution.py:1115
  108.0 18.6 %collective-permute-start.22 = (bf16[256,2048]{1,0:T(8,128)(2,1)}, bf16[256,2048]{1,0:T(8,128)(2,1)}, u32[]{:S(2)}, u32[]{:S(2)}) collective-permute-start(bf16[256,2048]{1,0:T(8,128)(2,1)} %get-tuple-element.147), channel_id=1, source_target_pairs={{0,1},{1,0},{2,3},{3,2},{4,5},{5,4},{6,7},{7,6},{8,9},{9,8},{10,11... | collective-permute-start | bytes 3145736 | tf_op jit(solution)/shard_map/ppermute | solution.py:1115
  108.5 27.9 %collective-permute-start.20 = (bf16[4,64,1024]{2,1,0:T(8,128)(2,1)S(1)}, bf16[4,64,1024]{2,1,0:T(8,128)(2,1)S(1)}, u32[]{:S(2)}, u32[]{:S(2)}) collective-permute-start(bf16[4,64,1024]{2,1,0:T(8,128)(2,1)S(1)} %slice_select_fusion), channel_id=1, source_target_pairs={{0,1},{1,0},{2,3},{3,2},{4,5},{5,4},{6,7},{7,6},{8,9},{9,8},{10,11... | collective-permute-start | bytes 1572872 | tf_op jit(solution)/shard_map/ppermute | solution.py:1115
  124.9 1.7 collective-permute-start.23
  132.3 21.5 %collective-permute-start.24 = (bf16[640,512]{1,0:T(8,128)(2,1)}, bf16[640,512]{1,0:T(8,128)(2,1)S(1)}, u32[]{:S(2)}, u32[]{:S(2)}) collective-permute-start(bf16[640,512]{1,0:T(8,128)(2,1)} %bitcast.55), channel_id=1, source_target_pairs={{0,4},{2,6},{4,0},{6,2},{8,12},{10,14},{12,8},{14,10},{16,20},{18,... | collective-permute-start | bytes 1966088 | tf_op jit(solution)/shard_map/ppermute | solution.py:1111
  133.8 20.0 %collective-permute-start.25 = (bf16[128,2048]{1,0:T(8,128)(2,1)}, bf16[128,2048]{1,0:T(8,128)(2,1)S(1)}, u32[]{:S(2)}, u32[]{:S(2)}) collective-permute-start(bf16[128,2048]{1,0:T(8,128)(2,1)} %bitcast.57), channel_id=1, source_target_pairs={{0,2},{2,0},{4,6},{6,4},{8,10},{10,8},{12,14},{14,12},{16,18},{18,... | collective-permute-start | bytes 1572872 | tf_op jit(solution)/shard_map/ppermute | solution.py:1111
  134.4 19.4 %collective-permute-start.26 = (bf16[64,512]{1,0:T(8,128)(2,1)}, bf16[64,512]{1,0:T(8,128)(2,1)S(1)}, u32[]{:S(2)}, u32[]{:S(2)}) collective-permute-start(bf16[64,512]{1,0:T(8,128)(2,1)} %bitcast.65), channel_id=1, source_target_pairs={{0,2},{2,0},{4,6},{6,4},{8,10},{10,8},{12,14},{14,12},{16,18},{18,... | collective-permute-start | bytes 196616 | tf_op jit(solution)/shard_map/ppermute | solution.py:1111
  135.8 17.9 %collective-permute-start.27 = (bf16[64,512]{1,0:T(8,128)(2,1)}, bf16[64,512]{1,0:T(8,128)(2,1)S(1)}, u32[]{:S(2)}, u32[]{:S(2)}) collective-permute-start(bf16[64,512]{1,0:T(8,128)(2,1)} %bitcast.64), channel_id=1, source_target_pairs={{0,4},{2,6},{4,0},{6,2},{8,12},{10,14},{12,8},{14,10},{16,20},{18,... | collective-permute-start | bytes 196616 | tf_op jit(solution)/shard_map/ppermute | solution.py:1111
  136.4 17.4 %collective-permute-start.28 = (bf16[64,512]{1,0:T(8,128)(2,1)}, bf16[64,512]{1,0:T(8,128)(2,1)S(1)}, u32[]{:S(2)}, u32[]{:S(2)}) collective-permute-start(bf16[64,512]{1,0:T(8,128)(2,1)} %bitcast.62), channel_id=1, source_target_pairs={{0,6},{2,4},{4,2},{6,0},{8,14},{10,12},{12,10},{14,8},{16,22},{18,... | collective-permute-start | bytes 196616 | tf_op jit(solution)/shard_map/ppermute | solution.py:1111
  157.6 10.7 %collective-permute-start.29 = (bf16[320,512]{1,0:T(8,128)(2,1)}, bf16[320,512]{1,0:T(8,128)(2,1)S(1)}, u32[]{:S(2)}, u32[]{:S(2)}) collective-permute-start(bf16[320,512]{1,0:T(8,128)(2,1)} %bitcast.58), channel_id=1, source_target_pairs={{0,2},{2,0},{4,6},{6,4},{8,10},{10,8},{12,14},{14,12},{16,18},{18,... | collective-permute-start | bytes 983048 | tf_op jit(solution)/shard_map/ppermute | solution.py:1111
  159.1 9.1 %collective-permute-start.30 = (bf16[64,2048]{1,0:T(8,128)(2,1)}, bf16[64,2048]{1,0:T(8,128)(2,1)S(1)}, u32[]{:S(2)}, u32[]{:S(2)}) collective-permute-start(bf16[64,2048]{1,0:T(8,128)(2,1)} %bitcast.59), channel_id=1, source_target_pairs={{0,4},{2,6},{4,0},{6,2},{8,12},{10,14},{12,8},{14,10},{16,20},{18,... | collective-permute-start | bytes 786440 | tf_op jit(solution)/shard_map/ppermute | solution.py:1111
  159.6 12.0 %collective-permute-start.31 = (bf16[16,512]{1,0:T(8,128)(2,1)}, bf16[16,512]{1,0:T(8,128)(2,1)S(1)}, u32[]{:S(2)}, u32[]{:S(2)}) collective-permute-start(bf16[16,512]{1,0:T(8,128)(2,1)} %bitcast.75), channel_id=1, source_target_pairs={{0,8},{2,10},{4,12},{6,14},{8,0},{10,2},{12,4},{14,6},{16,24},{18,... | collective-permute-start | bytes 49160 | tf_op jit(solution)/shard_map/ppermute | solution.py:1111
  161.1 13.8 %collective-permute-start.32 = (bf16[16,512]{1,0:T(8,128)(2,1)}, bf16[16,512]{1,0:T(8,128)(2,1)S(1)}, u32[]{:S(2)}, u32[]{:S(2)}) collective-permute-start(bf16[16,512]{1,0:T(8,128)(2,1)} %bitcast.74), channel_id=1, source_target_pairs={{0,16},{2,18},{4,20},{6,22},{8,24},{10,26},{12,28},{14,30},{16,0},... | collective-permute-start | bytes 49160 | tf_op jit(solution)/shard_map/ppermute | solution.py:1111
  163.5 12.0 %collective-permute-start.33 = (bf16[16,512]{1,0:T(8,128)(2,1)}, bf16[16,512]{1,0:T(8,128)(2,1)S(1)}, u32[]{:S(2)}, u32[]{:S(2)}) collective-permute-start(bf16[16,512]{1,0:T(8,128)(2,1)} %bitcast.73), channel_id=1, source_target_pairs={{0,24},{2,26},{4,28},{6,30},{8,16},{10,18},{12,20},{14,22},{16,8},... | collective-permute-start | bytes 49160 | tf_op jit(solution)/shard_map/ppermute | solution.py:1111
  168.2 17.9 %collective-permute-start.42 = (bf16[256,1024]{1,0:T(8,128)(2,1)}, bf16[256,1024]{1,0:T(8,128)(2,1)S(1)}, u32[]{:S(2)}, u32[]{:S(2)}) collective-permute-start(bf16[256,1024]{1,0:T(8,128)(2,1)} %get-tuple-element.189), channel_id=1, source_target_pairs={{0,1},{1,0},{2,3},{3,2},{4,5},{5,4},{6,7},{7,6},{8,9},{9,8},{10,11... | collective-permute-start | bytes 1572872 | tf_op jit(solution)/shard_map/ppermute | solution.py:1115
  171.1 11.4 %collective-permute-start.39 = (bf16[144,512]{1,0:T(8,128)(2,1)}, bf16[144,512]{1,0:T(8,128)(2,1)S(1)}, u32[]{:S(2)}, u32[]{:S(2)}) collective-permute-start(bf16[144,512]{1,0:T(8,128)(2,1)} %get-tuple-element.185), channel_id=1, source_target_pairs={{0,8},{2,10},{4,12},{6,14},{8,0},{10,2},{12,4},{14,6},{16,24},{18,... | collective-permute-start | bytes 442376 | tf_op jit(solution)/shard_map/ppermute | solution.py:1111
  171.7 3.8 %copy-start.47 = (bf16[16,512]{1,0:T(8,128)(2,1)}, bf16[16,512]{1,0:T(8,128)(2,1)S(1)}, u32[]{:S(2)}) copy-start(bf16[16,512]{1,0:T(8,128)(2,1)S(1)} %collective-permute-done.31.refs_14_.refs_3_) | copy-start | bytes 49156
  171.7 14.5 %collective-permute-start.40 = (bf16[144,512]{1,0:T(8,128)(2,1)}, bf16[144,512]{1,0:T(8,128)(2,1)S(1)}, u32[]{:S(2)}, u32[]{:S(2)}) collective-permute-start(bf16[144,512]{1,0:T(8,128)(2,1)} %get-tuple-element.186), channel_id=1, source_target_pairs={{0,16},{2,18},{4,20},{6,22},{8,24},{10,26},{12,28},{14,30},{16,0},... | collective-permute-start | bytes 442376 | tf_op jit(solution)/shard_map/ppermute | solution.py:1111
  175.0 11.2 %collective-permute-start.41 = (bf16[144,512]{1,0:T(8,128)(2,1)}, bf16[144,512]{1,0:T(8,128)(2,1)S(1)}, u32[]{:S(2)}, u32[]{:S(2)}) collective-permute-start(bf16[144,512]{1,0:T(8,128)(2,1)} %get-tuple-element.187), channel_id=1, source_target_pairs={{0,24},{2,26},{4,28},{6,30},{8,16},{10,18},{12,20},{14,22},{16,8},... | collective-permute-start | bytes 442376 | tf_op jit(solution)/shard_map/ppermute | solution.py:1111
  182.5 3.7 %copy-start.22 = (bf16[144,512]{1,0:T(8,128)(2,1)}, bf16[144,512]{1,0:T(8,128)(2,1)S(1)}, u32[]{:S(2)}) copy-start(bf16[144,512]{1,0:T(8,128)(2,1)S(1)} %collective-permute-done.39.refs_7_.refs_1_) | copy-start | bytes 442372
  187.1 8.8 %copy-start.6 = (f32[8,512]{1,0:T(8,128)S(1)}, f32[8,512]{1,0:T(8,128)}, u32[]{:S(2)}) copy-start(f32[8,512]{1,0:T(8,128)} %get-tuple-element.183) | copy-start | bytes 49156
  189.3 26.2 %all-to-all-start.1 = ((bf16[16,16,1536]{2,1,0:T(8,128)(2,1)}), bf16[16,16,1536]{2,1,0:T(8,128)(2,1)S(1)}, u32[]{:S(2)}, u32[]{:S(2)}) async-start(bf16[16,16,1536]{2,1,0:T(8,128)(2,1)} %bitcast.46), calls=%async_computation.1 | async-start | bytes 1572864 | tf_op jit(solution)/shard_map/all_to_all | solution.py:1141
  195.9 1.2 collective-permute-start.34
  197.1 3.8 %collective-permute-start.35 = (f32[8,512]{1,0:T(8,128)S(1)}, f32[8,512]{1,0:T(8,128)S(1)}, u32[]{:S(2)}, u32[]{:S(2)}) collective-permute-start(f32[8,512]{1,0:T(8,128)S(1)} %add.14), channel_id=1, source_target_pairs={{0,2},{2,0},{4,6},{6,4},{8,10},{10,8},{12,14},{14,12},{16,18},{18,... | collective-permute-start | bytes 49160 | tf_op jit(solution)/shard_map/ppermute | solution.py:1111
  201.0 3.7 %collective-permute-start.36 = (f32[8,512]{1,0:T(8,128)S(1)}, f32[8,512]{1,0:T(8,128)S(1)}, u32[]{:S(2)}, u32[]{:S(2)}) collective-permute-start(f32[8,512]{1,0:T(8,128)S(1)} %add.15), channel_id=1, source_target_pairs={{0,4},{2,6},{4,0},{6,2},{8,12},{10,14},{12,8},{14,10},{16,20},{18,... | collective-permute-start | bytes 49160 | tf_op jit(solution)/shard_map/ppermute | solution.py:1111
  204.7 4.1 %collective-permute-start.37 = (f32[8,512]{1,0:T(8,128)S(1)}, f32[8,512]{1,0:T(8,128)S(1)}, u32[]{:S(2)}, u32[]{:S(2)}) collective-permute-start(f32[8,512]{1,0:T(8,128)S(1)} %add.16), channel_id=1, source_target_pairs={{0,8},{2,10},{4,12},{6,14},{8,0},{10,2},{12,4},{14,6},{16,24},{18,... | collective-permute-start | bytes 49160 | tf_op jit(solution)/shard_map/ppermute | solution.py:1111
  208.8 11.4 %copy-start.7 = (f32[8,512]{1,0:T(8,128)}, f32[8,512]{1,0:T(8,128)S(1)}, u32[]{:S(2)}) copy-start(f32[8,512]{1,0:T(8,128)S(1)} %add.17.refs_0_) | copy-start | bytes 49156
  215.5 6.6 %copy-start.1 = (bf16[16,16,1536]{2,1,0:T(8,128)(2,1)}, bf16[16,16,1536]{2,1,0:T(8,128)(2,1)S(1)}, u32[]{:S(2)}) copy-start(bf16[16,16,1536]{2,1,0:T(8,128)(2,1)S(1)} %all-to-all-done.1) | copy-start | bytes 2359300
  215.5 6.6 %collective-permute-start.43 = (bf16[256,1536]{1,0:T(8,128)(2,1)S(1)}, bf16[256,1536]{1,0:T(8,128)(2,1)S(1)}, u32[]{:S(2)}, u32[]{:S(2)}) collective-permute-start(bf16[256,1536]{1,0:T(8,128)(2,1)S(1)} %bitcast.44), channel_id=1, source_target_pairs={{0,1},{1,0},{2,3},{3,2},{4,5},{5,4},{6,7},{7,6},{8,9},{9,8},{10,11... | collective-permute-start | bytes 2359304 | tf_op jit(solution)/shard_map/ppermute | solution.py:1115
  215.5 4.6 %collective-permute-start.38 = (f32[8,512]{1,0:T(8,128)S(1)}, f32[8,512]{1,0:T(8,128)S(1)}, u32[]{:S(2)}, u32[]{:S(2)}) collective-permute-start(f32[8,512]{1,0:T(8,128)S(1)} %add.17.refs_0_), channel_id=1, source_target_pairs={{0,16},{2,18},{4,20},{6,22},{8,24},{10,26},{12,28},{14,30},{16,0},... | collective-permute-start | bytes 49160 | tf_op jit(solution)/shard_map/ppermute | solution.py:1111
  (33 other events, 30.4 us)

commit v3 on v2

--- a/solution.py
+++ b/solution.py
@@ -767,12 +767,23 @@
 def unpack_kernel(own_ref, oth_ref, *rest):
     outs, (table_ref, all_ref) = rest[:-2], rest[-2:]
     in_ref, dk_ref, dwb_ref, g1_ref, g2_ref, g3_ref, g4_ref, gb_ref = outs[:8]
-    outb_ref, mix_ref, gain_ref, shift_ref, expb_ref, redb_ref, ffn_ref = outs[8:]
+    outb_ref, mix_ref, gain_ref, shift_ref, expb_ref, redb_ref, ffn_ref = outs[8:15]
+    first_gain_ref, first_shift_ref, inb_ref = outs[15:]
     row = lax.axis_index("row")
     total = own_ref[0:16, 0:1024].astype(f32)
     for k in range(1, 16):
         total = total + own_ref[k * 16 : (k + 1) * 16, 0:1024].astype(f32)
     in_ref[...] = total
+    late = own_ref[0:16, 1536:1664].astype(f32)
+    for k in range(1, 16):
+        late = late + own_ref[k * 16 : (k + 1) * 16, 1536:1664].astype(f32)
+    lines = [
+        jnp.concatenate([late[r * 4 + c : r * 4 + c + 1] for c in range(4)], axis=1).reshape(512) for r in range(4)
+    ]
+    first_gain_ref[...] = lines[0]
+    first_shift_ref[...] = lines[1]
+    inb_ref[0:512] = lines[2]
+    inb_ref[512:1024] = lines[3]
     for k in range(16):
         block = slice(k * 16, (k + 1) * 16)
         table_ref[pl.ds(pl.multiple_of((2 * k + row) * 16, 16), 16), :] = own_ref[block, 1024:1536]
@@ -817,7 +828,7 @@
 def unpack(own, oth, deps=()):
     vmem = pl.BlockSpec(memory_space=pltpu.VMEM)
     shapes = ((16, 1024), (7, 7, 992), (992,), (32, 64), (64, 128), (128, 256), (256, 512), (960,))
-    shapes += ((512,),) * 4 + ((2048,), (512,), (512,))
+    shapes += ((512,),) * 4 + ((2048,), (512,), (512,), (512,), (512,), (1024,))
     return launch(
         deps,
         unpack_kernel,
@@ -1058,25 +1069,32 @@
     )(*parts)
 
 
-def deal_kernel(i_a, i_b, *rest):
-    parts, out_ref = rest[:-1], rest[-1]
+def deal_kernel(i_a, i_b, late_a, late_b, *rest):
+    parts, (out_ref, late_ref) = rest[:-2], rest[-2:]
     small = functools.reduce(lambda a, b: a + b, [v[...].astype(f32) for v in parts]).astype(bf16)
+    late = late_a[...] + late_b[...]
+    for r in range(4):
+        for c in range(4):
+            late_ref[r * 4 + c : r * 4 + c + 1] = late[r : r + 1, c * 128 : (c + 1) * 128]
+    last = late_ref[...].astype(bf16)
     out_ref[:, 0:1024] = (i_a[...].astype(f32) + i_b[...].astype(f32)).astype(bf16)
     for k in range(16):
         out_ref[k * 16 : (k + 1) * 16, 1024:1536] = small
-
-
-def deal(i_a, i_b, parts, deps=()):
+        out_ref[k * 16 : (k + 1) * 16, 1536:1664] = last
+
+
+def deal(i_a, i_b, late_a, late_b, parts, deps=()):
     vmem = pl.BlockSpec(memory_space=pltpu.VMEM)
     return launch(
         deps,
         deal_kernel,
-        out_shape=jax.ShapeDtypeStruct((256, 1536), bf16),
-        in_specs=[vmem] * (2 + len(parts)),
+        out_shape=jax.ShapeDtypeStruct((256, 1664), bf16),
+        in_specs=[vmem] * (4 + len(parts)),
         out_specs=vmem,
+        scratch_shapes=[pltpu.VMEM((16, 128), f32)],
         cost_estimate=takes(2),
         name="deal",
-    )(i_a, i_b, *parts)
+    )(i_a, i_b, late_a, late_b, *parts)
 
 
 def late_kernel(a_ref, b_ref, gain_ref, shift_ref, bias_ref):
@@ -1276,12 +1294,10 @@
         fgrad, late, token = last_call(
             valid, dfused, xp, dx2, w_in, wide, in_order, dealt, [token] + small[1:]
         )
-        dealt_rows, token = deal(i_keep, i_got, small, [token] + parts[1:])
+        dealt_rows, token = deal(i_keep, i_got, late, swap_row(late), small, [token] + parts[1:])
         mixed = spread(dealt_rows)
         red_sum, out_sum, exp_sum, token = finish(parts, [token])
-        late, got = sum_img(late + swap_row(late), (0, 1, 2, 3))
-        own, oth = mixed, swap_row(after(mixed, late))
-        sums = late_sums(late, got, [token])
+        own, oth = mixed, swap_row(mixed)
     else:
 
         def total(parts, rows):
@@ -1302,14 +1318,14 @@
         small = plain_gather(total((s_keep, s_send), everything).astype(bf16)).reshape(16, 2, 16, 512)
         lower_row = lax.axis_index("row")
         own, oth = (
-            jnp.pad(lax.dynamic_index_in_dim(small, v, 1, keepdims=False).reshape(256, 512), ((0, 0), (1024, 0)))
+            jnp.pad(lax.dynamic_index_in_dim(small, v, 1, keepdims=False).reshape(256, 512), ((0, 0), (1024, 128)))
             for v in (lower_row, 1 - lower_row)
         )
 
     unpacked = unpack(own, oth)
     if dealt:
-        in_sum = unpacked[0]
-    dk_sum, dwb_sum, gate1, gate2, gate3, gate4, gb_sum, outb, mix, gain, shift, expb, redb, ffn = unpacked[1:-1]
+        in_sum, sums = unpacked[0], unpacked[15:18]
+    dk_sum, dwb_sum, gate1, gate2, gate3, gate4, gb_sum, outb, mix, gain, shift, expb, redb, ffn = unpacked[1:15]
     return (
         produced.reshape(features.shape),
         fgrad.reshape(features.shape),

time: 227 us -> 226 us (level)
  blocking collectives: 0 us -> 29 us
  waiting for transfers between devices: 25 us -> 10.2 us
  starting transfers between devices: 56 us -> 42.1 us
    all_to_all x0 -> x1, blocking collectives: none -> 29 us  [spread(): return lax.all_to_all(value, 'img', split_axis=0, concat_axis=0, tiled=True)]
    ppermute x28 -> x24, waiting for transfers between devices: 12.3 us -> 3.91 us  [swap_img(): lax.ppermute(value, 'img', [(k, k ^ mask) for k in range(lax.axis_size('i...]
    ppermute x28 -> x24, starting transfers between devices: 40.5 us -> 33.2 us  [swap_img(): lax.ppermute(value, 'img', [(k, k ^ mask) for k in range(lax.axis_size('i...]
    all_to_all x2 -> x1, waiting for transfers between devices: 6.7 us -> 0.01 us  [spread(): return lax.all_to_all(value, 'img', split_axis=0, concat_axis=0, tiled=True)]
    all_to_all x2 -> x1, starting transfers between devices: 12.1 us -> 5.55 us  [spread(): return lax.all_to_all(value, 'img', split_axis=0, concat_axis=0, tiled=True)]
    pallas_call x20 -> x19, Pallas kernels: 130 us -> 129 us  [launch(): return lambda *args: call(*args, *deps)]
    unnamed x103 -> x99, local copies, waits for them, and re-layouts: 11.1 us -> 10.5 us
  transfers between devices with their start and end apart: 46 -> 41, of which waited for: 12 -> 8; matrix products, arithmetic and copies ran while one was open for 2% -> 2% of each run, Pallas kernels for 37% -> 37%
where the time goes in v3:
time: 226 us; the launch traced here: 225 us
  Pallas kernels  129 us (57%)
  starting transfers between devices  42.1 us (19%)
  blocking collectives  29 us (13%)
  local copies, waits for them, and re-layouts  12.3 us (5%)
  waiting for transfers between devices  10.2 us (5%)
    pallas_call x19, Pallas kernels, launch(): return lambda *args: call(*args, *deps)  129 us
    ppermute x24, starting transfers between devices, swap_img(): lax.ppermute(value, 'img', [(k, k ^ mask) for k in range(lax.axis_size('i...  33.2 us
    all_to_all x1, blocking collectives, spread(): return lax.all_to_all(value, 'img', split_axis=0, concat_axis=0, tiled=True)  29 us
    unnamed x99, local copies, waits for them, and re-layouts  10.5 us
    ppermute x16, waiting for transfers between devices, swap_row(): return lax.ppermute(value, 'row', [(0, 1), (1, 0)])  6.31 us
    all_to_all x1, starting transfers between devices, spread(): return lax.all_to_all(value, 'img', split_axis=0, concat_axis=0, tiled=True)  5.55 us
  transfers between devices with their start and end apart: 41, of which 8 were waited for; matrix products, arithmetic and copies ran while one was open for 2% of the time, Pallas kernels for 37%

profile of v3, /device:TPU:0, one launch (start us, length us, event | category | flops | bytes accessed | tf_op | source)
XLA Modules:
  0.0 224.6 jit_solution(13759076230840185969)
XLA Ops:
  1.2 2.7 %collective-permute-start.2 = (bf16[16,1024]{1,0:T(8,128)(2,1)}, bf16[16,1024]{1,0:T(8,128)(2,1)S(1)}, u32[]{:S(2)}, u32[]{:S(2)}) collective-permute-start(bf16[16,1024]{1,0:T(8,128)(2,1)} %refs_0_.3), channel_id=1, source_target_pairs={{0,8},{2,10},{4,12},{6,14},{8,0},{10,2},{12,4},{14,6},{16,24},{18,... | collective-permute-start | bytes 98312 | tf_op jit(solution)/shard_map/ppermute | solution.py:1129
  3.8 2.6 %collective-permute-start.3 = (bf16[16,1024]{1,0:T(8,128)(2,1)}, bf16[16,1024]{1,0:T(8,128)(2,1)S(1)}, u32[]{:S(2)}, u32[]{:S(2)}) collective-permute-start(bf16[16,1024]{1,0:T(8,128)(2,1)} %refs_0_.3), channel_id=1, source_target_pairs={{0,16},{2,18},{4,20},{6,22},{8,24},{10,26},{12,28},{14,30},{16,0},... | collective-permute-start | bytes 98312 | tf_op jit(solution)/shard_map/ppermute | solution.py:1129
  6.4 0.8 constant_dynamic-update-slice_fusion.1
  7.3 0.7 constant_dynamic-update-slice_fusion.refs_0_
  8.0 0.9 collective-permute-start.12
  8.9 1.6 vectors.1
  10.5 3.6 %collective-permute-start.13 = (bf16[16,2560]{1,0:T(8,128)(2,1)S(1)}, bf16[16,2560]{1,0:T(8,128)(2,1)S(1)}, u32[]{:S(2)}, u32[]{:S(2)}) collective-permute-start(bf16[16,2560]{1,0:T(8,128)(2,1)S(1)} %constant_dynamic-update-slice_fusion.refs_0_), channel_id=1, source_target_pairs={{0,16},{2,18},{4,20},{6,22},{8,24},{10,26},{12,28},{14,30},{16,0},... | collective-permute-start | bytes 245768 | tf_op jit(solution)/shard_map/ppermute | solution.py:1129
  14.7 1.5 join.3
  16.1 1.8 collective-permute-start.5
  17.9 1.5 collective-permute-start.6
  19.7 0.7 copy-done.7
  20.4 4.9 %prepare.1 = (bf16[4,256,512]{2,1,0:T(8,128)(2,1)}, bf16[4,256,512]{2,1,0:T(8,128)(2,1)}, bf16[4,256,512]{2,1,0:T(8,128)(2,1)}, bf16[4,64,512]{2,1,0:T(8,128)(2,...) custom-call(s32[32,32]{1,0:T(8,128)} %bitcast.67, s32[32,32]{1,0:T(8,128)} %copy-done.44, bf16[2,512,512]{2,1,0:T(8,128)(2,1)} %bitcast.52, ...), custom_call_target="tpu_custom_call" | custom-call | flops 4000000000 | tf_op jit(solution)/shard_map/prepare/pallas_call | solution.py:190
  25.4 0.6 collective-permute-done.6.refs_6_
  26.1 0.6 copy-done.26
  26.7 1.8 join.4
  28.5 1.6 collective-permute-start.15
  30.1 1.1 broadcast_in_dim.2
  31.1 5.5 %all-to-all-start = ((bf16[16,64,512]{2,1,0:T(8,128)(2,1)}), bf16[16,64,512]{2,1,0:T(8,128)(2,1)S(1)}, u32[]{:S(2)}, u32[]{:S(2)}) async-start(bf16[16,64,512]{2,1,0:T(8,128)(2,1)} %broadcast_in_dim.2), calls=%async_computation | async-start | bytes 2097152 | tf_op jit(solution)/shard_map/all_to_all | solution.py:1159
  37.8 0.8 pad_convert_fusion.refs_13_.refs_3_
  38.6 0.7 copy-done.17
  39.3 2.0 join.5
  41.3 1.9 collective-permute-start.16
  43.3 0.6 copy-done.30
  44.0 20.9 %forward.1 = (f32[4,256,1024]{2,1,0:T(8,128)}, bf16[16,13,5,16,256]{4,3,2,1,0:T(8,128)(2,1)}, f32[4,256,128]{2,1,0:T(8,128)}, f32[8,128]{1,0:T(8,128)}) custom-call(s32[32,32]{1,0:T(8,128)} %bitcast.68, s32[32,32]{1,0:T(8,128)} %copy-done.44, bf16[4,256,512]{2,1,0:T(8,128)(2,1)} %get-tuple-element.120.refs_2_, ...), custom_call_target="tpu_custom_call" | custom-call | flops 24000000000 | tf_op jit(solution)/shard_map/forward/pallas_call | solution.py:190
  65.5 0.9 collective-permute-done.16.refs_6_.refs_10_
  66.5 2.3 %collective-permute-done.17.refs_7_.refs_11_ = bf16[128,2560]{1,0:T(8,128)(2,1)} collective-permute-done((bf16[128,2560]{1,0:T(8,128)(2,1)S(1)}, bf16[128,2560]{1,0:T(8,128)(2,1)}, u32[]{:S(2)}, u32[]{:S(2)}) %collective-permute-start.17) | collective-permute-done | bytes 655392 | tf_op jit(solution)/shard_map/ppermute | solution.py:1133
  68.8 0.9 collective-permute-done.18.refs_8_.refs_12_
  69.7 0.9 copy-done.8
  70.7 25.8 %middle.1 = (bf16[2,512,512]{2,1,0:T(8,128)(2,1)}, bf16[2048,1024]{1,0:T(8,128)(2,1)}, bf16[512,1024]{1,0:T(8,128)(2,1)}, bf16[1024,1024]{1,0:T(8,128)(2,1)}, bf...) custom-call(s32[32,32]{1,0:T(8,128)} %bitcast.69, ...), custom_call_target="tpu_custom_call" | custom-call | flops 30000001024 | tf_op jit(solution)/shard_map/middle/pallas_call | solution.py:190
  96.5 11.3 %feed_grads.1 = (bf16[256,2048]{1,0:T(8,128)(2,1)}, bf16[256,2048]{1,0:T(8,128)(2,1)}, bf16[1280,512]{1,0:T(8,128)(2,1)}, bf16[1280,512]{1,0:T(8,128)(2,1)}, f32[8,128]{1,0:T(8,128)}) custom-call(bf16[512,1024]{1,0:T(8,128)(2,1)} %get-tuple-element.136.refs_0_, bf16[1024,2048]{1,0:T(8,128)(2,1)} %get-tuple-element.137.refs_1_, ...), custom_call_target="tpu_custom_call" | custom-call | flops 11000000512 | tf_op jit(solution)/shard_map/feed_grads/pallas_call | solution.py:190
  108.7 12.9 %kernel_grad.1 = (f32[16,32,128]{2,1,0:T(8,128)}, f32[8,128]{1,0:T(8,128)}) custom-call(bf16[4,256,1024]{2,1,0:T(8,128)(2,1)} %bitcast.47, bf16[16,13,5,16,256]{4,3,2,1,0:T(8,128)(2,1)} %get-tuple-element.150.refs_1_, f32[8,128]{1,0:T(8,128)} %get-tuple-element.151.refs_2_), custom_call_target="tpu_custom_call" | custom-call | flops 12999999488 | tf_op jit(solution)/shard_map/kernel_grad/pallas_call | solution.py:190
  121.5 3.4 %gate_grads.1 = (bf16[256,512]{1,0:T(8,128)(2,1)}, bf16[256,512]{1,0:T(8,128)(2,1)}, f32[8,128]{1,0:T(8,128)}) custom-call(bf16[1024,1024]{1,0:T(8,128)(2,1)} %get-tuple-element.140.refs_4_.refs_0_, bf16[1024,1024]{1,0:T(8,128)(2,1)} %get-tuple-element.146.refs_1_, f32[8,512]{1,0:T(8,128)} %get-tuple-element.147.refs_2_, ...), custom_call_target="tpu_custom_call" | custom-call | flops 3000000000 | tf_op jit(solution)/shard_map/gate_grads/pallas_call | solution.py:190
  125.2 1.5 collective-permute-done.23
  126.7 0.7 copy-done.19
  127.8 4.5 %combine.2 = (bf16[4,160,512]{2,1,0:T(8,128)(2,1)}, bf16[4,160,512]{2,1,0:T(8,128)(2,1)}, bf16[4,32,2048]{2,1,0:T(8,128)(2,1)}, bf16[4,32,2048]{2,1,0:T(8,128)(2...) custom-call(bf16[2,4,160,512]{3,2,1,0:T(8,128)(2,1)} %bitcast.79, ...), custom_call_target="tpu_custom_call" | custom-call | flops 2000000000 | tf_op jit(solution)/shard_map/combine/pallas_call | solution.py:190
  132.3 1.5 collective-permute-start.24
  133.8 0.6 collective-permute-start.25
  134.4 1.5 collective-permute-start.26
  135.9 0.6 collective-permute-start.27
  136.4 1.5 collective-permute-start.28
  137.9 15.9 %conv_back.1 = (bf16[4,256,1024]{2,1,0:T(8,128)(2,1)}, f32[8,128]{1,0:T(8,128)}) custom-call(s32[32,32]{1,0:T(8,128)} %bitcast.70, bf16[4,256,1024]{2,1,0:T(8,128)(2,1)} %bitcast.48, bf16[4,64,1024]{2,1,0:T(8,128)(2,1)} %copy-done.14, f32[7,7,1024]{2,1,0:T(8,128)} %pad_convert_fusion.refs_13_.refs_3_, f32[8,128]{1,0:T(8,128)} %get-tuple-element.157.refs_4_), custom_call_target="tpu_custom_call" | custom-call | flops 16000000000 | tf_op jit(solution)/shard_map/conv_back/pallas_call | solution.py:190
  153.9 0.5 copy-done.37
  154.8 2.8 %combine.3 = (bf16[1,320,512]{2,1,0:T(8,128)(2,1)}, bf16[1,320,512]{2,1,0:T(8,128)(2,1)}, bf16[1,64,2048]{2,1,0:T(8,128)(2,1)}, bf16[1,64,2048]{2,1,0:T(8,128)(2...) custom-call(bf16[2,1,320,512]{3,2,1,0:T(8,128)(2,1)} %bitcast.86, ...), custom_call_target="tpu_custom_call" | custom-call | flops 2000000000 | tf_op jit(solution)/shard_map/combine/pallas_call | solution.py:190
  157.6 1.5 collective-permute-start.29
  159.1 0.6 collective-permute-start.30
  159.7 1.5 collective-permute-start.31
  161.2 2.4 %collective-permute-start.32 = (bf16[16,512]{1,0:T(8,128)(2,1)}, bf16[16,512]{1,0:T(8,128)(2,1)S(1)}, u32[]{:S(2)}, u32[]{:S(2)}) collective-permute-start(bf16[16,512]{1,0:T(8,128)(2,1)} %bitcast.74), channel_id=1, source_target_pairs={{0,16},{2,18},{4,20},{6,22},{8,24},{10,26},{12,28},{14,30},{16,0},... | collective-permute-start | bytes 49160 | tf_op jit(solution)/shard_map/ppermute | solution.py:1129
  163.5 0.5 collective-permute-start.33
  164.1 4.2 %in_grad.1 = (bf16[256,1024]{1,0:T(8,128)(2,1)}, bf16[256,1024]{1,0:T(8,128)(2,1)}, f32[8,128]{1,0:T(8,128)}) custom-call(bf16[512,1024]{1,0:T(8,128)(2,1)} %get-tuple-element.173.refs_0_, bf16[1024,1024]{1,0:T(8,128)(2,1)} %bitcast.77, f32[8,128]{1,0:T(8,128)} %get-tuple-element.174.refs_2_), custom_call_target="tpu_custom_call" | custom-call | flops 4000000000 | tf_op jit(solution)/shard_map/in_grad/pallas_call | solution.py:190
  168.4 0.6 copy-done.18
  169.1 2.1 merge.1
  171.2 0.6 collective-permute-start.36
  171.7 3.3 %collective-permute-start.37 = (bf16[144,512]{1,0:T(8,128)(2,1)}, bf16[144,512]{1,0:T(8,128)(2,1)S(1)}, u32[]{:S(2)}, u32[]{:S(2)}) collective-permute-start(bf16[144,512]{1,0:T(8,128)(2,1)} %get-tuple-element.187), channel_id=1, source_target_pairs={{0,16},{2,18},{4,20},{6,22},{8,24},{10,26},{12,28},{14,30},{16,0},... | collective-permute-start | bytes 442376 | tf_op jit(solution)/shard_map/ppermute | solution.py:1129
  175.0 0.5 collective-permute-start.38
  175.6 0.5 copy-done.47
  176.2 6.3 %last.1 = (bf16[2,512,512]{2,1,0:T(8,128)(2,1)}, f32[8,512]{1,0:T(8,128)}, f32[8,128]{1,0:T(8,128)}) custom-call(s32[32,32]{1,0:T(8,128)} %bitcast.71, bf16[1024,1024]{1,0:T(8,128)(2,1)} %bitcast.78, bf16[1024,512]{1,0:T(8,128)(2,1)} %bitcast.81, f32[1024,512]{1,0:T(8,128)} %get-tuple-element.159.refs_3_, bf16[64,1024]{1,0:T(8,128)(2,1)} %get-tuple-element.122.refs_4_, ...), custom_call_target="tpu_custom_call" | custom-call | flops 7000000000 | tf_op jit(solution)/shard_map/last/pallas_call | solution.py:190
  182.5 1.4 collective-permute-done.35.refs_3_
  183.9 2.3 %collective-permute-done.37.refs_10_.refs_2_ = bf16[144,512]{1,0:T(8,128)(2,1)S(1)} collective-permute-done((bf16[144,512]{1,0:T(8,128)(2,1)}, bf16[144,512]{1,0:T(8,128)(2,1)S(1)}, u32[]{:S(2)}, u32[]{:S(2)}) %collective-permute-start.37) | collective-permute-done | bytes 147488 | tf_op jit(solution)/shard_map/ppermute | solution.py:1129
  186.2 0.6 copy-done.21
  187.1 2.4 %deal.1 = (bf16[256,1664]{1,0:T(8,128)(2,1)}, f32[8,128]{1,0:T(8,128)}) custom-call(bf16[256,1024]{1,0:T(8,128)(2,1)} %get-tuple-element.181.refs_0_, bf16[256,1024]{1,0:T(8,128)(2,1)} %copy-done.13, f32[8,512]{1,0:T(8,128)} %get-tuple-element.183.refs_2_, f32[8,512]{1,0:T(8,128)} %copy-done.48, bf16[16,512]{1,0:T(8,128)(2,1)} %bitcast.94, ...), custom_call_target="tpu_custom_call" | custom-call | flops 2000000000 | tf_op jit(solution)/shard_map/deal/pallas_call | solution.py:190
  189.5 29.0 %all_to_all.19 = bf16[16,16,1664]{2,1,0:T(8,128)(2,1)S(1)} all-to-all(bf16[16,16,1664]{2,1,0:T(8,128)(2,1)} %bitcast.46), channel_id=1, replica_groups=mesh['img'=16,'row'=2] {'img'}, dimensions={0} | all-to-all | bytes 1703936 | tf_op jit(solution)/shard_map/all_to_all | solution.py:1159
  218.5 2.2 finish.1
  220.9 0.9 copy-done.9
  221.8 2.6 %unpack.1 = (f32[16,1024]{1,0:T(8,128)}, f32[7,7,992]{2,1,0:T(8,128)}, f32[992]{0:T(1024)}, f32[32,64]{1,0:T(8,128)}, f32[64,128]{1,0:T(8,128)}, /*index=5*/f32[...) custom-call(bf16[256,1664]{1,0:T(8,128)(2,1)} %bitcast.45, ...), custom_call_target="tpu_custom_call" | custom-call | flops 3000000000 | tf_op jit(solution)/shard_map/unpack/pallas_call | solution.py:190
  (141 shorter events, 6.1 us)
Async XLA Ops:
  0.7 13.4 %copy-start.43 = (s32[2,16,32]{2,1,0:T(8,128)S(1)}, s32[2,16,32]{2,1,0:T(8,128)}, u32[]{:S(2)}) copy-start(s32[2,16,32]{2,1,0:T(8,128)} %param.25) | copy-start | bytes 12292
  0.7 18.8 %collective-permute-start.1 = (bf16[2,512,512]{2,1,0:T(8,128)(2,1)}, bf16[2,512,512]{2,1,0:T(8,128)(2,1)S(1)}, u32[]{:S(2)}, u32[]{:S(2)}) collective-permute-start(bf16[2,512,512]{2,1,0:T(8,128)(2,1)} %bitcast.51), channel_id=1, source_target_pairs={{0,1},{1,0},{2,3},{3,2},{4,5},{5,4},{6,7},{7,6},{8,9},{9,8},{10,11... | collective-permute-start | bytes 3145736 | tf_op jit(solution)/shard_map/ppermute | solution.py:1133
  1.2 9.3 %collective-permute-start.2 = (bf16[16,1024]{1,0:T(8,128)(2,1)}, bf16[16,1024]{1,0:T(8,128)(2,1)S(1)}, u32[]{:S(2)}, u32[]{:S(2)}) collective-permute-start(bf16[16,1024]{1,0:T(8,128)(2,1)} %refs_0_.3), channel_id=1, source_target_pairs={{0,8},{2,10},{4,12},{6,14},{8,0},{10,2},{12,4},{14,6},{16,24},{18,... | collective-permute-start | bytes 98312 | tf_op jit(solution)/shard_map/ppermute | solution.py:1129
  3.8 10.2 %collective-permute-start.3 = (bf16[16,1024]{1,0:T(8,128)(2,1)}, bf16[16,1024]{1,0:T(8,128)(2,1)S(1)}, u32[]{:S(2)}, u32[]{:S(2)}) collective-permute-start(bf16[16,1024]{1,0:T(8,128)(2,1)} %refs_0_.3), channel_id=1, source_target_pairs={{0,16},{2,18},{4,20},{6,22},{8,24},{10,26},{12,28},{14,30},{16,0},... | collective-permute-start | bytes 98312 | tf_op jit(solution)/shard_map/ppermute | solution.py:1129
  6.4 7.6 %collective-permute-start.4 = (bf16[16,1024]{1,0:T(8,128)(2,1)}, bf16[16,1024]{1,0:T(8,128)(2,1)S(1)}, u32[]{:S(2)}, u32[]{:S(2)}) collective-permute-start(bf16[16,1024]{1,0:T(8,128)(2,1)} %refs_0_.3), channel_id=1, source_target_pairs={{0,24},{2,26},{4,28},{6,30},{8,16},{10,18},{12,20},{14,22},{16,8},... | collective-permute-start | bytes 98312 | tf_op jit(solution)/shard_map/ppermute | solution.py:1129
  8.0 8.1 %copy-start.5 = (bf16[16,2560]{1,0:T(8,128)(2,1)}, bf16[16,2560]{1,0:T(8,128)(2,1)S(1)}, u32[]{:S(2)}) copy-start(bf16[16,2560]{1,0:T(8,128)(2,1)S(1)} %constant_dynamic-update-slice_fusion.refs_0_) | copy-start | bytes 245764
  8.0 9.9 %collective-permute-start.12 = (bf16[16,2560]{1,0:T(8,128)(2,1)S(1)}, bf16[16,2560]{1,0:T(8,128)(2,1)S(1)}, u32[]{:S(2)}, u32[]{:S(2)}) collective-permute-start(bf16[16,2560]{1,0:T(8,128)(2,1)S(1)} %constant_dynamic-update-slice_fusion.refs_0_), channel_id=1, source_target_pairs={{0,8},{2,10},{4,12},{6,14},{8,0},{10,2},{12,4},{14,6},{16,24},{18,... | collective-permute-start | bytes 245768 | tf_op jit(solution)/shard_map/ppermute | solution.py:1129
  10.5 3.7 %copy-start.40 = (bf16[16,1024]{1,0:T(8,128)(2,1)}, bf16[16,1024]{1,0:T(8,128)(2,1)S(1)}, u32[]{:S(2)}) copy-start(bf16[16,1024]{1,0:T(8,128)(2,1)S(1)} %collective-permute-done.2.refs_1_) | copy-start | bytes 98308
  10.5 14.8 %collective-permute-start.13 = (bf16[16,2560]{1,0:T(8,128)(2,1)S(1)}, bf16[16,2560]{1,0:T(8,128)(2,1)S(1)}, u32[]{:S(2)}, u32[]{:S(2)}) collective-permute-start(bf16[16,2560]{1,0:T(8,128)(2,1)S(1)} %constant_dynamic-update-slice_fusion.refs_0_), channel_id=1, source_target_pairs={{0,16},{2,18},{4,20},{6,22},{8,24},{10,26},{12,28},{14,30},{16,0},... | collective-permute-start | bytes 245768 | tf_op jit(solution)/shard_map/ppermute | solution.py:1129
  14.0 11.3 %collective-permute-start.14 = (bf16[16,2560]{1,0:T(8,128)(2,1)S(1)}, bf16[16,2560]{1,0:T(8,128)(2,1)S(1)}, u32[]{:S(2)}, u32[]{:S(2)}) collective-permute-start(bf16[16,2560]{1,0:T(8,128)(2,1)S(1)} %constant_dynamic-update-slice_fusion.refs_0_), channel_id=1, source_target_pairs={{0,24},{2,26},{4,28},{6,30},{8,16},{10,18},{12,20},{14,22},{16,8},... | collective-permute-start | bytes 245768 | tf_op jit(solution)/shard_map/ppermute | solution.py:1129
  14.1 2.1 collective-permute-start
  16.1 3.6 %copy-start.44 = (s32[32,32]{1,0:T(8,128)}, s32[32,32]{1,0:T(8,128)S(1)}, u32[]{:S(2)}) copy-start(s32[32,32]{1,0:T(8,128)S(1)} %collective-permute-done.refs_1_) | copy-start | bytes 12292
  16.1 9.2 %collective-permute-start.5 = (bf16[64,1024]{1,0:T(8,128)(2,1)}, bf16[64,1024]{1,0:T(8,128)(2,1)S(1)}, u32[]{:S(2)}, u32[]{:S(2)}) collective-permute-start(bf16[64,1024]{1,0:T(8,128)(2,1)} %get-tuple-element.122.refs_4_), channel_id=1, source_target_pairs={{0,2},{2,0},{4,6},{6,4},{8,10},{10,8},{12,14},{14,12},{16,18},{18,... | collective-permute-start | bytes 393224 | tf_op jit(solution)/shard_map/ppermute | solution.py:1129
  17.9 7.4 %copy-start.34 = (bf16[16,2560]{1,0:T(8,128)(2,1)}, bf16[16,2560]{1,0:T(8,128)(2,1)S(1)}, u32[]{:S(2)}) copy-start(bf16[16,2560]{1,0:T(8,128)(2,1)S(1)} %collective-permute-done.12.refs_1_) | copy-start | bytes 245764
  17.9 8.1 %collective-permute-start.6 = (bf16[64,1024]{1,0:T(8,128)(2,1)}, bf16[64,1024]{1,0:T(8,128)(2,1)S(1)}, u32[]{:S(2)}, u32[]{:S(2)}) collective-permute-start(bf16[64,1024]{1,0:T(8,128)(2,1)} %get-tuple-element.122.refs_4_), channel_id=1, source_target_pairs={{0,4},{2,6},{4,0},{6,2},{8,12},{10,14},{12,8},{14,10},{16,20},{18,... | collective-permute-start | bytes 393224 | tf_op jit(solution)/shard_map/ppermute | solution.py:1129
  19.4 1.0 copy-start.7
  19.4 6.6 %collective-permute-start.7 = (bf16[64,1024]{1,0:T(8,128)(2,1)}, bf16[64,1024]{1,0:T(8,128)(2,1)S(1)}, u32[]{:S(2)}, u32[]{:S(2)}) collective-permute-start(bf16[64,1024]{1,0:T(8,128)(2,1)} %get-tuple-element.122.refs_4_), channel_id=1, source_target_pairs={{0,6},{2,4},{4,2},{6,0},{8,14},{10,12},{12,10},{14,8},{16,22},{18,... | collective-permute-start | bytes 393224 | tf_op jit(solution)/shard_map/ppermute | solution.py:1129
  25.3 4.8 %copy-start.4 = (bf16[64,512]{1,0:T(8,128)(2,1)S(1)}, bf16[64,512]{1,0:T(8,128)(2,1)}, u32[]{:S(2)}) copy-start(bf16[64,512]{1,0:T(8,128)(2,1)} %param.45) | copy-start | bytes 196612
  28.5 8.2 %copy-start.23 = (bf16[64,1024]{1,0:T(8,128)(2,1)S(1)}, bf16[64,1024]{1,0:T(8,128)(2,1)}, u32[]{:S(2)}) copy-start(bf16[64,1024]{1,0:T(8,128)(2,1)} %get-tuple-element.122.refs_4_) | copy-start | bytes 393220
  28.5 8.3 %copy-start.27 = (bf16[64,1024]{1,0:T(8,128)(2,1)S(1)}, bf16[64,1024]{1,0:T(8,128)(2,1)}, u32[]{:S(2)}) copy-start(bf16[64,1024]{1,0:T(8,128)(2,1)} %copy-done.26) | copy-start | bytes 393220
  28.5 8.8 %copy-start.29 = (bf16[64,1024]{1,0:T(8,128)(2,1)S(1)}, bf16[64,1024]{1,0:T(8,128)(2,1)}, u32[]{:S(2)}) copy-start(bf16[64,1024]{1,0:T(8,128)(2,1)} %copy-done.28) | copy-start | bytes 393220
  28.5 8.9 %copy-start.25 = (bf16[64,1024]{1,0:T(8,128)(2,1)S(1)}, bf16[64,1024]{1,0:T(8,128)(2,1)}, u32[]{:S(2)}) copy-start(bf16[64,1024]{1,0:T(8,128)(2,1)} %copy-done.24) | copy-start | bytes 393220
  28.5 9.3 %copy-start.3 = (bf16[7,7,992]{2,1,0:T(8,128)(2,1)S(1)}, bf16[7,7,992]{2,1,0:T(8,128)(2,1)}, u32[]{:S(2)}) copy-start(bf16[7,7,992]{2,1,0:T(8,128)(2,1)} %param.31) | copy-start | bytes 291652
  28.5 10.1 %collective-permute-start.15 = (bf16[64,2560]{1,0:T(8,128)(2,1)}, bf16[64,2560]{1,0:T(8,128)(2,1)S(1)}, u32[]{:S(2)}, u32[]{:S(2)}) collective-permute-start(bf16[64,2560]{1,0:T(8,128)(2,1)} %get-tuple-element.124.refs_0_), channel_id=1, source_target_pairs={{0,4},{2,6},{4,0},{6,2},{8,12},{10,14},{12,8},{14,10},{16,20},{18,... | collective-permute-start | bytes 983048 | tf_op jit(solution)/shard_map/ppermute | solution.py:1129
  31.1 33.8 %all-to-all-start = ((bf16[16,64,512]{2,1,0:T(8,128)(2,1)}), bf16[16,64,512]{2,1,0:T(8,128)(2,1)S(1)}, u32[]{:S(2)}, u32[]{:S(2)}) async-start(bf16[16,64,512]{2,1,0:T(8,128)(2,1)} %broadcast_in_dim.2), calls=%async_computation | async-start | bytes 2097152 | tf_op jit(solution)/shard_map/all_to_all | solution.py:1159
  36.7 6.5 %collective-permute-start.8 = (bf16[64,1024]{1,0:T(8,128)(2,1)S(1)}, bf16[64,1024]{1,0:T(8,128)(2,1)S(1)}, u32[]{:S(2)}, u32[]{:S(2)}) collective-permute-start(bf16[64,1024]{1,0:T(8,128)(2,1)S(1)} %copy-done.23), channel_id=1, source_target_pairs={{0,1},{1,0},{2,3},{3,2},{4,5},{5,4},{6,7},{7,6},{8,9},{9,8},{10,11... | collective-permute-start | bytes 393224 | tf_op jit(solution)/shard_map/ppermute | solution.py:1133
  36.8 6.4 %collective-permute-start.10 = (bf16[64,1024]{1,0:T(8,128)(2,1)S(1)}, bf16[64,1024]{1,0:T(8,128)(2,1)S(1)}, u32[]{:S(2)}, u32[]{:S(2)}) collective-permute-start(bf16[64,1024]{1,0:T(8,128)(2,1)S(1)} %copy-done.27), channel_id=1, source_target_pairs={{0,1},{1,0},{2,3},{3,2},{4,5},{5,4},{6,7},{7,6},{8,9},{9,8},{10,11... | collective-permute-start | bytes 393224 | tf_op jit(solution)/shard_map/ppermute | solution.py:1133
  37.3 6.0 %collective-permute-start.11 = (bf16[64,1024]{1,0:T(8,128)(2,1)S(1)}, bf16[64,1024]{1,0:T(8,128)(2,1)S(1)}, u32[]{:S(2)}, u32[]{:S(2)}) collective-permute-start(bf16[64,1024]{1,0:T(8,128)(2,1)S(1)} %copy-done.29), channel_id=1, source_target_pairs={{0,1},{1,0},{2,3},{3,2},{4,5},{5,4},{6,7},{7,6},{8,9},{9,8},{10,11... | collective-permute-start | bytes 393224 | tf_op jit(solution)/shard_map/ppermute | solution.py:1133
  37.4 5.9 %collective-permute-start.9 = (bf16[64,1024]{1,0:T(8,128)(2,1)S(1)}, bf16[64,1024]{1,0:T(8,128)(2,1)S(1)}, u32[]{:S(2)}, u32[]{:S(2)}) collective-permute-start(bf16[64,1024]{1,0:T(8,128)(2,1)S(1)} %copy-done.25), channel_id=1, source_target_pairs={{0,1},{1,0},{2,3},{3,2},{4,5},{5,4},{6,7},{7,6},{8,9},{9,8},{10,11... | collective-permute-start | bytes 393224 | tf_op jit(solution)/shard_map/ppermute | solution.py:1133
  41.3 25.2 %collective-permute-start.16 = (bf16[128,2560]{1,0:T(8,128)(2,1)}, bf16[128,2560]{1,0:T(8,128)(2,1)S(1)}, u32[]{:S(2)}, u32[]{:S(2)}) collective-permute-start(bf16[128,2560]{1,0:T(8,128)(2,1)} %get-tuple-element.131.refs_5_.refs_9_), channel_id=1, source_target_pairs={{0,2},{2,0},{4,6},{6,4},{8,10},{10,8},{12,14},{14,12},{16,18},{18,... | collective-permute-start | bytes 1966088 | tf_op jit(solution)/shard_map/ppermute | solution.py:1129
  44.0 21.0 %copy-start.10 = (bf16[128,2560]{1,0:T(8,128)(2,1)S(1)}, bf16[128,2560]{1,0:T(8,128)(2,1)}, u32[]{:S(2)}) copy-start(bf16[128,2560]{1,0:T(8,128)(2,1)} %get-tuple-element.131.refs_5_.refs_9_) | copy-start | bytes 1966084
  65.0 4.8 %copy-start = (bf16[16,64,512]{2,1,0:T(8,128)(2,1)}, bf16[16,64,512]{2,1,0:T(8,128)(2,1)S(1)}, u32[]{:S(2)}) copy-start(bf16[16,64,512]{2,1,0:T(8,128)(2,1)S(1)} %all-to-all-done) | copy-start | bytes 3145732
  65.0 4.7 %collective-permute-start.19 = (bf16[1024,512]{1,0:T(8,128)(2,1)S(1)}, bf16[1024,512]{1,0:T(8,128)(2,1)S(1)}, u32[]{:S(2)}, u32[]{:S(2)}) collective-permute-start(bf16[1024,512]{1,0:T(8,128)(2,1)S(1)} %bitcast.42), channel_id=1, source_target_pairs={{0,1},{1,0},{2,3},{3,2},{4,5},{5,4},{6,7},{7,6},{8,9},{9,8},{10,11... | collective-permute-start | bytes 3145736 | tf_op jit(solution)/shard_map/ppermute | solution.py:1133
  65.1 3.7 %collective-permute-start.17 = (bf16[128,2560]{1,0:T(8,128)(2,1)S(1)}, bf16[128,2560]{1,0:T(8,128)(2,1)}, u32[]{:S(2)}, u32[]{:S(2)}) collective-permute-start(bf16[128,2560]{1,0:T(8,128)(2,1)S(1)} %copy-done.10), channel_id=1, source_target_pairs={{0,1},{1,0},{2,3},{3,2},{4,5},{5,4},{6,7},{7,6},{8,9},{9,8},{10,11... | collective-permute-start | bytes 1966088 | tf_op jit(solution)/shard_map/ppermute | solution.py:1133
  66.5 3.2 %copy-start.11 = (bf16[128,2560]{1,0:T(8,128)(2,1)}, bf16[128,2560]{1,0:T(8,128)(2,1)S(1)}, u32[]{:S(2)}) copy-start(bf16[128,2560]{1,0:T(8,128)(2,1)S(1)} %collective-permute-done.16.refs_6_.refs_10_) | copy-start | bytes 1966084
  66.5 3.2 %collective-permute-start.18 = (bf16[128,2560]{1,0:T(8,128)(2,1)S(1)}, bf16[128,2560]{1,0:T(8,128)(2,1)}, u32[]{:S(2)}, u32[]{:S(2)}) collective-permute-start(bf16[128,2560]{1,0:T(8,128)(2,1)S(1)} %collective-permute-done.16.refs_6_.refs_10_), channel_id=1, source_target_pairs={{0,1},{1,0},{2,3},{3,2},{4,5},{5,4},{6,7},{7,6},{8,9},{9,8},{10,11... | collective-permute-start | bytes 1966088 | tf_op jit(solution)/shard_map/ppermute | solution.py:1133
  96.5 11.9 %copy-start.2 = (bf16[1024,1024]{1,0:T(8,128)(2,1)S(1)}, bf16[1024,1024]{1,0:T(8,128)(2,1)}, u32[]{:S(2)}) copy-start(bf16[1024,1024]{1,0:T(8,128)(2,1)} %get-tuple-element.135) | copy-start | bytes 6291460
  107.8 18.8 %collective-permute-start.21 = (bf16[1280,512]{1,0:T(8,128)(2,1)}, bf16[1280,512]{1,0:T(8,128)(2,1)S(1)}, u32[]{:S(2)}, u32[]{:S(2)}) collective-permute-start(bf16[1280,512]{1,0:T(8,128)(2,1)} %get-tuple-element.143), channel_id=1, source_target_pairs={{0,1},{1,0},{2,3},{3,2},{4,5},{5,4},{6,7},{7,6},{8,9},{9,8},{10,11... | collective-permute-start | bytes 3932168 | tf_op jit(solution)/shard_map/ppermute | solution.py:1133
  108.0 18.6 %collective-permute-start.22 = (bf16[256,2048]{1,0:T(8,128)(2,1)}, bf16[256,2048]{1,0:T(8,128)(2,1)}, u32[]{:S(2)}, u32[]{:S(2)}) collective-permute-start(bf16[256,2048]{1,0:T(8,128)(2,1)} %get-tuple-element.145), channel_id=1, source_target_pairs={{0,1},{1,0},{2,3},{3,2},{4,5},{5,4},{6,7},{7,6},{8,9},{9,8},{10,11... | collective-permute-start | bytes 3145736 | tf_op jit(solution)/shard_map/ppermute | solution.py:1133
  108.5 28.0 %collective-permute-start.20 = (bf16[4,64,1024]{2,1,0:T(8,128)(2,1)S(1)}, bf16[4,64,1024]{2,1,0:T(8,128)(2,1)S(1)}, u32[]{:S(2)}, u32[]{:S(2)}) collective-permute-start(bf16[4,64,1024]{2,1,0:T(8,128)(2,1)S(1)} %slice_select_fusion), channel_id=1, source_target_pairs={{0,1},{1,0},{2,3},{3,2},{4,5},{5,4},{6,7},{7,6},{8,9},{9,8},{10,11... | collective-permute-start | bytes 1572872 | tf_op jit(solution)/shard_map/ppermute | solution.py:1133
  124.9 1.7 collective-permute-start.23
  126.7 1.1 copy-start.6
  132.3 21.5 %collective-permute-start.24 = (bf16[640,512]{1,0:T(8,128)(2,1)}, bf16[640,512]{1,0:T(8,128)(2,1)S(1)}, u32[]{:S(2)}, u32[]{:S(2)}) collective-permute-start(bf16[640,512]{1,0:T(8,128)(2,1)} %bitcast.55), channel_id=1, source_target_pairs={{0,4},{2,6},{4,0},{6,2},{8,12},{10,14},{12,8},{14,10},{16,20},{18,... | collective-permute-start | bytes 1966088 | tf_op jit(solution)/shard_map/ppermute | solution.py:1129
  133.8 20.0 %collective-permute-start.25 = (bf16[128,2048]{1,0:T(8,128)(2,1)}, bf16[128,2048]{1,0:T(8,128)(2,1)S(1)}, u32[]{:S(2)}, u32[]{:S(2)}) collective-permute-start(bf16[128,2048]{1,0:T(8,128)(2,1)} %bitcast.57), channel_id=1, source_target_pairs={{0,2},{2,0},{4,6},{6,4},{8,10},{10,8},{12,14},{14,12},{16,18},{18,... | collective-permute-start | bytes 1572872 | tf_op jit(solution)/shard_map/ppermute | solution.py:1129
  134.4 19.4 %collective-permute-start.26 = (bf16[64,512]{1,0:T(8,128)(2,1)}, bf16[64,512]{1,0:T(8,128)(2,1)S(1)}, u32[]{:S(2)}, u32[]{:S(2)}) collective-permute-start(bf16[64,512]{1,0:T(8,128)(2,1)} %bitcast.65), channel_id=1, source_target_pairs={{0,2},{2,0},{4,6},{6,4},{8,10},{10,8},{12,14},{14,12},{16,18},{18,... | collective-permute-start | bytes 196616 | tf_op jit(solution)/shard_map/ppermute | solution.py:1129
  135.9 17.9 %collective-permute-start.27 = (bf16[64,512]{1,0:T(8,128)(2,1)}, bf16[64,512]{1,0:T(8,128)(2,1)S(1)}, u32[]{:S(2)}, u32[]{:S(2)}) collective-permute-start(bf16[64,512]{1,0:T(8,128)(2,1)} %bitcast.64), channel_id=1, source_target_pairs={{0,4},{2,6},{4,0},{6,2},{8,12},{10,14},{12,8},{14,10},{16,20},{18,... | collective-permute-start | bytes 196616 | tf_op jit(solution)/shard_map/ppermute | solution.py:1129
  136.4 1.5 copy-start.14
  136.4 17.4 %collective-permute-start.28 = (bf16[64,512]{1,0:T(8,128)(2,1)}, bf16[64,512]{1,0:T(8,128)(2,1)S(1)}, u32[]{:S(2)}, u32[]{:S(2)}) collective-permute-start(bf16[64,512]{1,0:T(8,128)(2,1)} %bitcast.62), channel_id=1, source_target_pairs={{0,6},{2,4},{4,2},{6,0},{8,14},{10,12},{12,10},{14,8},{16,22},{18,... | collective-permute-start | bytes 196616 | tf_op jit(solution)/shard_map/ppermute | solution.py:1129
  153.9 1.0 copy-start.12
  157.6 10.7 %collective-permute-start.29 = (bf16[320,512]{1,0:T(8,128)(2,1)}, bf16[320,512]{1,0:T(8,128)(2,1)S(1)}, u32[]{:S(2)}, u32[]{:S(2)}) collective-permute-start(bf16[320,512]{1,0:T(8,128)(2,1)} %bitcast.58), channel_id=1, source_target_pairs={{0,2},{2,0},{4,6},{6,4},{8,10},{10,8},{12,14},{14,12},{16,18},{18,... | collective-permute-start | bytes 983048 | tf_op jit(solution)/shard_map/ppermute | solution.py:1129
  159.1 9.1 %collective-permute-start.30 = (bf16[64,2048]{1,0:T(8,128)(2,1)}, bf16[64,2048]{1,0:T(8,128)(2,1)S(1)}, u32[]{:S(2)}, u32[]{:S(2)}) collective-permute-start(bf16[64,2048]{1,0:T(8,128)(2,1)} %bitcast.59), channel_id=1, source_target_pairs={{0,4},{2,6},{4,0},{6,2},{8,12},{10,14},{12,8},{14,10},{16,20},{18,... | collective-permute-start | bytes 786440 | tf_op jit(solution)/shard_map/ppermute | solution.py:1129
  159.7 12.0 %collective-permute-start.31 = (bf16[16,512]{1,0:T(8,128)(2,1)}, bf16[16,512]{1,0:T(8,128)(2,1)S(1)}, u32[]{:S(2)}, u32[]{:S(2)}) collective-permute-start(bf16[16,512]{1,0:T(8,128)(2,1)} %bitcast.75), channel_id=1, source_target_pairs={{0,8},{2,10},{4,12},{6,14},{8,0},{10,2},{12,4},{14,6},{16,24},{18,... | collective-permute-start | bytes 49160 | tf_op jit(solution)/shard_map/ppermute | solution.py:1129
  161.2 13.8 %collective-permute-start.32 = (bf16[16,512]{1,0:T(8,128)(2,1)}, bf16[16,512]{1,0:T(8,128)(2,1)S(1)}, u32[]{:S(2)}, u32[]{:S(2)}) collective-permute-start(bf16[16,512]{1,0:T(8,128)(2,1)} %bitcast.74), channel_id=1, source_target_pairs={{0,16},{2,18},{4,20},{6,22},{8,24},{10,26},{12,28},{14,30},{16,0},... | collective-permute-start | bytes 49160 | tf_op jit(solution)/shard_map/ppermute | solution.py:1129
  163.5 12.0 %collective-permute-start.33 = (bf16[16,512]{1,0:T(8,128)(2,1)}, bf16[16,512]{1,0:T(8,128)(2,1)S(1)}, u32[]{:S(2)}, u32[]{:S(2)}) collective-permute-start(bf16[16,512]{1,0:T(8,128)(2,1)} %bitcast.73), channel_id=1, source_target_pairs={{0,24},{2,26},{4,28},{6,30},{8,16},{10,18},{12,20},{14,22},{16,8},... | collective-permute-start | bytes 49160 | tf_op jit(solution)/shard_map/ppermute | solution.py:1129
  168.3 17.9 %collective-permute-start.34 = (bf16[256,1024]{1,0:T(8,128)(2,1)}, bf16[256,1024]{1,0:T(8,128)(2,1)S(1)}, u32[]{:S(2)}, u32[]{:S(2)}) collective-permute-start(bf16[256,1024]{1,0:T(8,128)(2,1)} %get-tuple-element.182), channel_id=1, source_target_pairs={{0,1},{1,0},{2,3},{3,2},{4,5},{5,4},{6,7},{7,6},{8,9},{9,8},{10,11... | collective-permute-start | bytes 1572872 | tf_op jit(solution)/shard_map/ppermute | solution.py:1133
  171.2 12.8 %collective-permute-start.36 = (bf16[144,512]{1,0:T(8,128)(2,1)}, bf16[144,512]{1,0:T(8,128)(2,1)S(1)}, u32[]{:S(2)}, u32[]{:S(2)}) collective-permute-start(bf16[144,512]{1,0:T(8,128)(2,1)} %get-tuple-element.186), channel_id=1, source_target_pairs={{0,8},{2,10},{4,12},{6,14},{8,0},{10,2},{12,4},{14,6},{16,24},{18,... | collective-permute-start | bytes 442376 | tf_op jit(solution)/shard_map/ppermute | solution.py:1129
  171.7 3.8 %copy-start.45 = (bf16[16,512]{1,0:T(8,128)(2,1)}, bf16[16,512]{1,0:T(8,128)(2,1)S(1)}, u32[]{:S(2)}) copy-start(bf16[16,512]{1,0:T(8,128)(2,1)S(1)} %collective-permute-done.31.refs_14_.refs_5_) | copy-start | bytes 49156
  171.7 14.5 %collective-permute-start.37 = (bf16[144,512]{1,0:T(8,128)(2,1)}, bf16[144,512]{1,0:T(8,128)(2,1)S(1)}, u32[]{:S(2)}, u32[]{:S(2)}) collective-permute-start(bf16[144,512]{1,0:T(8,128)(2,1)} %get-tuple-element.187), channel_id=1, source_target_pairs={{0,16},{2,18},{4,20},{6,22},{8,24},{10,26},{12,28},{14,30},{16,0},... | collective-permute-start | bytes 442376 | tf_op jit(solution)/shard_map/ppermute | solution.py:1129
  175.0 11.2 %collective-permute-start.38 = (bf16[144,512]{1,0:T(8,128)(2,1)}, bf16[144,512]{1,0:T(8,128)(2,1)S(1)}, u32[]{:S(2)}, u32[]{:S(2)}) collective-permute-start(bf16[144,512]{1,0:T(8,128)(2,1)} %get-tuple-element.188), channel_id=1, source_target_pairs={{0,24},{2,26},{4,28},{6,30},{8,16},{10,18},{12,20},{14,22},{16,8},... | collective-permute-start | bytes 442376 | tf_op jit(solution)/shard_map/ppermute | solution.py:1129
  182.5 1.4 collective-permute-start.35
  183.9 2.3 %copy-start.48 = (f32[8,512]{1,0:T(8,128)}, f32[8,512]{1,0:T(8,128)S(1)}, u32[]{:S(2)}) copy-start(f32[8,512]{1,0:T(8,128)S(1)} %collective-permute-done.35.refs_3_) | copy-start | bytes 49156
  183.9 2.3 %copy-start.20 = (bf16[144,512]{1,0:T(8,128)(2,1)}, bf16[144,512]{1,0:T(8,128)(2,1)S(1)}, u32[]{:S(2)}) copy-start(bf16[144,512]{1,0:T(8,128)(2,1)S(1)} %collective-permute-done.36.refs_9_.refs_1_) | copy-start | bytes 442372
  218.5 2.4 %copy-start.1 = (bf16[16,16,1664]{2,1,0:T(8,128)(2,1)}, bf16[16,16,1664]{2,1,0:T(8,128)(2,1)S(1)}, u32[]{:S(2)}) copy-start(bf16[16,16,1664]{2,1,0:T(8,128)(2,1)S(1)} %all_to_all.19) | copy-start | bytes 2555908
  218.5 2.4 %collective-permute-start.39 = (bf16[256,1664]{1,0:T(8,128)(2,1)S(1)}, bf16[256,1664]{1,0:T(8,128)(2,1)S(1)}, u32[]{:S(2)}, u32[]{:S(2)}) collective-permute-start(bf16[256,1664]{1,0:T(8,128)(2,1)S(1)} %bitcast.44), channel_id=1, source_target_pairs={{0,1},{1,0},{2,3},{3,2},{4,5},{5,4},{6,7},{7,6},{8,9},{9,8},{10,11... | collective-permute-start | bytes 2555912 | tf_op jit(solution)/shard_map/ppermute | solution.py:1133
  (26 other events, 18.4 us)

commit v4 on v3

--- a/solution.py
+++ b/solution.py
@@ -110,22 +110,11 @@
         out_ref[5 + k // 2 : 6 + k // 2, k % 2 * 512 : k % 2 * 512 + 512] = line(ref)
 
 
-def gather_vectors(large, small, deps=()):
-    vmem = pl.BlockSpec(memory_space=pltpu.VMEM)
-    return launch(
-        deps,
-        vectors_kernel,
-        out_shape=jax.ShapeDtypeStruct((9, 1024), f32),
-        in_specs=[vmem] * 12,
-        out_specs=vmem,
-        cost_estimate=takes(1),
-        name="vectors",
-    )(*large, *small)
-
-
-def prepare_kernel(valid_ref, halo_valid_ref, x_ref, xh_ref, g_ref, vec_ref, xp_ref, gp_ref, y1_ref, y1h_ref, y1t_ref):
+def prepare_kernel(valid_ref, halo_valid_ref, x_ref, xh_ref, g_ref, *rest):
+    vectors, (xp_ref, gp_ref, y1_ref, y1h_ref, y1t_ref, wide_ref) = rest[:12], rest[12:]
+    vectors_kernel(*vectors, wide_ref)
     perm = permutation()
-    gain, shift = vec_ref[8:9, 0:512], vec_ref[8:9, 512:1024]
+    gain, shift = wide_ref[8:9, 0:512], wide_ref[8:9, 512:1024]
     own, halo = extents(valid_ref), halo_sizes(valid_ref, halo_valid_ref)
     start = pl.multiple_of(lax.axis_index("row") * 384, 128)
     for b in range(5):
@@ -216,7 +205,7 @@
         outs[p // 16][(slice(p % 16 * rows, (p % 16 + 1) * rows),) + lead] = value_ref[pl.ds(at, rows), :].astype(bf16)
 
 
-def prepare(valid, halo_valid, x, xh, g, wide, deps=()):
+def prepare(valid, halo_valid, x, xh, g, vectors, deps=()):
     vmem = pl.BlockSpec(memory_space=pltpu.VMEM)
     return launch(
         deps,
@@ -227,12 +216,13 @@
             jax.ShapeDtypeStruct((4, 256, 512), bf16),
             jax.ShapeDtypeStruct((4, 64, 512), bf16),
             jax.ShapeDtypeStruct((512, 1024), bf16),
+            jax.ShapeDtypeStruct((9, 1024), f32),
         ),
-        in_specs=[SMEM] * 2 + [vmem] * 4,
-        out_specs=(vmem,) * 5,
+        in_specs=[SMEM] * 2 + [vmem] * 15,
+        out_specs=(vmem,) * 6,
         cost_estimate=takes(4),
         name="prepare",
-    )(valid, halo_valid, x, xh, g, wide)
+    )(valid, halo_valid, x, xh, g, *vectors)
 
 
 def low_lanes(shape):
@@ -1228,10 +1218,8 @@
     x_halo = swap_row(x)
     halo_valid = swap_row(valid)
     taps = jnp.pad(dwkernel.astype(f32), ((0, 0), (0, 0), (32, 0)))
-    wide, token = gather_vectors(
-        (inbias, dwbias, gatebias, expandbias),
-        (outbias, mixscale, mlpgain, mlpshift, reducebias, mlpscale, normgain, normshift),
-    )
+    vectors = (inbias, dwbias, gatebias, expandbias)
+    vectors += (outbias, mixscale, mlpgain, mlpshift, reducebias, mlpscale, normgain, normshift)
     exp_out = jnp.concatenate([expandweight, outweight], axis=1)
     deep, flat_pair = (3, 2), (1, 0)
     if dealt:
@@ -1241,7 +1229,7 @@
         exp_parts = swaps(exp_out, deep)
         red_own = spread(repeat(reduceweight))
         w_in = swaps(in_z, flat_pair)
-        xp, gp, y1, y1h, y1t, token = prepare(valid, halo_valid, x, x_halo, g, wide, [token])
+        xp, gp, y1, y1h, y1t, wide, token = prepare(valid, halo_valid, x, x_halo, g, vectors, [token])
         exp_z, token = join(exp_parts, deps=[token] + w_in[1:])
         w_in = w_in + [swap_row(v) for v in w_in]
         exp_y, token = join(swaps(exp_z, (1,)), deps=[token])
@@ -1254,7 +1242,7 @@
         w_in = jnp.split(plain_gather(inweight), 8, axis=0)
         w_exp = jnp.split(plain_gather(exp_out), 4, axis=0)
         w_red = jnp.split(plain_gather(reduceweight), 2, axis=0)
-        xp, gp, y1, y1h, y1t, token = prepare(valid, halo_valid, x, x_halo, g, wide)
+        xp, gp, y1, y1h, y1t, wide, token = prepare(valid, halo_valid, x, x_halo, g, vectors)
         d, band, j0, token = forward(valid, halo_valid, y1, y1h, w_in, wide, taps, in_order, dealt)
     (produced, act, y2, u, dh, df, dz, dv, dd, dx2, s512, s2048, s1024, token) = middle_call(
         valid, d, j0, xp, gp, w_exp, w_red, gatefirst, gatesecond, gatethird, gatefourth, wide, exp_order, dealt

time: 226 us -> 224 us (level)
    pallas_call x19 -> x18, Pallas kernels: 129 us -> 127 us  [launch(): return lambda *args: call(*args, *deps)]
    unnamed x99 -> x97, local copies, waits for them, and re-layouts: 10.5 us -> 10.4 us
  transfers between devices with their start and end apart: 41 -> 41, of which waited for: 8 -> 8; matrix products, arithmetic and copies ran while one was open for 2% -> 2% of each run, Pallas kernels for 37% -> 36%
where the time goes in v4:
time: 224 us; the launch traced here: 223 us
  Pallas kernels  127 us (57%)
  starting transfers between devices  42.1 us (19%)
  blocking collectives  29 us (13%)
  local copies, waits for them, and re-layouts  12.2 us (5%)
  waiting for transfers between devices  10 us (4%)
    pallas_call x18, Pallas kernels, launch(): return lambda *args: call(*args, *deps)  127 us
    ppermute x24, starting transfers between devices, swap_img(): lax.ppermute(value, 'img', [(k, k ^ mask) for k in range(lax.axis_size('i...  33.4 us
    all_to_all x1, blocking collectives, spread(): return lax.all_to_all(value, 'img', split_axis=0, concat_axis=0, tiled=True)  29 us
    unnamed x97, local copies, waits for them, and re-layouts  10.4 us
    ppermute x16, waiting for transfers between devices, swap_row(): return lax.ppermute(value, 'row', [(0, 1), (1, 0)])  6.33 us
    all_to_all x1, starting transfers between devices, spread(): return lax.all_to_all(value, 'img', split_axis=0, concat_axis=0, tiled=True)  5.42 us
  transfers between devices with their start and end apart: 41, of which 8 were waited for; matrix products, arithmetic and copies ran while one was open for 2% of the time, Pallas kernels for 36%

profile of v4, /device:TPU:0, one launch (start us, length us, event | category | flops | bytes accessed | tf_op | source)
XLA Modules:
  0.0 222.9 jit_solution(86882114068638653)
XLA Ops:
  0.7 0.5 collective-permute-start.1
  1.2 2.7 %collective-permute-start.2 = (bf16[16,1024]{1,0:T(8,128)(2,1)}, bf16[16,1024]{1,0:T(8,128)(2,1)S(1)}, u32[]{:S(2)}, u32[]{:S(2)}) collective-permute-start(bf16[16,1024]{1,0:T(8,128)(2,1)} %refs_0_.1), channel_id=1, source_target_pairs={{0,8},{2,10},{4,12},{6,14},{8,0},{10,2},{12,4},{14,6},{16,24},{18,... | collective-permute-start | bytes 98312 | tf_op jit(solution)/shard_map/ppermute | solution.py:1119
  3.8 2.6 %collective-permute-start.3 = (bf16[16,1024]{1,0:T(8,128)(2,1)}, bf16[16,1024]{1,0:T(8,128)(2,1)S(1)}, u32[]{:S(2)}, u32[]{:S(2)}) collective-permute-start(bf16[16,1024]{1,0:T(8,128)(2,1)} %refs_0_.1), channel_id=1, source_target_pairs={{0,16},{2,18},{4,20},{6,22},{8,24},{10,26},{12,28},{14,30},{16,0},... | collective-permute-start | bytes 98312 | tf_op jit(solution)/shard_map/ppermute | solution.py:1119
  6.4 0.8 constant_dynamic-update-slice_fusion.1
  7.3 0.7 constant_dynamic-update-slice_fusion.refs_0_
  8.0 0.9 collective-permute-start.12
  8.9 3.5 %collective-permute-start.13 = (bf16[16,2560]{1,0:T(8,128)(2,1)S(1)}, bf16[16,2560]{1,0:T(8,128)(2,1)S(1)}, u32[]{:S(2)}, u32[]{:S(2)}) collective-permute-start(bf16[16,2560]{1,0:T(8,128)(2,1)S(1)} %constant_dynamic-update-slice_fusion.refs_0_), channel_id=1, source_target_pairs={{0,16},{2,18},{4,20},{6,22},{8,24},{10,26},{12,28},{14,30},{16,0},... | collective-permute-start | bytes 245768 | tf_op jit(solution)/shard_map/ppermute | solution.py:1119
  13.4 1.5 join.3
  14.8 1.5 collective-permute-start.5
  16.3 1.5 collective-permute-start.6
  18.3 0.5 copy-done.7
  18.8 5.0 %prepare.1 = (bf16[4,256,512]{2,1,0:T(8,128)(2,1)}, bf16[4,256,512]{2,1,0:T(8,128)(2,1)}, bf16[4,256,512]{2,1,0:T(8,128)(2,1)}, bf16[4,64,512]{2,1,0:T(8,128)(2,...) custom-call(s32[32,32]{1,0:T(8,128)} %bitcast.68, s32[32,32]{1,0:T(8,128)} %copy-done.43, ...), custom_call_target="tpu_custom_call" | custom-call | flops 4000000000 | tf_op jit(solution)/shard_map/prepare/pallas_call | solution.py:179
  25.1 1.8 join.4
  26.8 1.6 collective-permute-start.15
  28.4 1.1 broadcast_in_dim.2
  29.5 5.4 %all-to-all-start = ((bf16[16,64,512]{2,1,0:T(8,128)(2,1)}), bf16[16,64,512]{2,1,0:T(8,128)(2,1)S(1)}, u32[]{:S(2)}, u32[]{:S(2)}) async-start(bf16[16,64,512]{2,1,0:T(8,128)(2,1)} %broadcast_in_dim.2), calls=%async_computation | async-start | bytes 2097152 | tf_op jit(solution)/shard_map/all_to_all | solution.py:1149
  35.0 0.5 collective-permute-start.10
  36.0 0.8 pad_convert_fusion.refs_13_.refs_3_
  36.8 0.7 copy-done.17
  37.6 2.0 join.5
  39.6 1.9 collective-permute-start.16
  41.5 0.6 copy-done.30
  42.3 20.9 %forward.1 = (f32[4,256,1024]{2,1,0:T(8,128)}, bf16[16,13,5,16,256]{4,3,2,1,0:T(8,128)(2,1)}, f32[4,256,128]{2,1,0:T(8,128)}, f32[8,128]{1,0:T(8,128)}) custom-call(s32[32,32]{1,0:T(8,128)} %bitcast.69, s32[32,32]{1,0:T(8,128)} %copy-done.43, bf16[4,256,512]{2,1,0:T(8,128)(2,1)} %get-tuple-element.119.refs_2_, ...), custom_call_target="tpu_custom_call" | custom-call | flops 24000000000 | tf_op jit(solution)/shard_map/forward/pallas_call | solution.py:179
  63.3 0.5 collective-permute-start.17
  63.8 0.9 collective-permute-done.16.refs_6_.refs_10_
  64.7 2.3 %collective-permute-done.17.refs_7_.refs_11_ = bf16[128,2560]{1,0:T(8,128)(2,1)} collective-permute-done((bf16[128,2560]{1,0:T(8,128)(2,1)S(1)}, bf16[128,2560]{1,0:T(8,128)(2,1)}, u32[]{:S(2)}, u32[]{:S(2)}) %collective-permute-start.17) | collective-permute-done | bytes 655392 | tf_op jit(solution)/shard_map/ppermute | solution.py:1123
  67.0 0.9 collective-permute-done.18.refs_8_.refs_12_
  68.0 1.0 copy-done.8
  69.0 25.8 %middle.1 = (bf16[2,512,512]{2,1,0:T(8,128)(2,1)}, bf16[2048,1024]{1,0:T(8,128)(2,1)}, bf16[512,1024]{1,0:T(8,128)(2,1)}, bf16[1024,1024]{1,0:T(8,128)(2,1)}, bf...) custom-call(s32[32,32]{1,0:T(8,128)} %bitcast.70, ...), custom_call_target="tpu_custom_call" | custom-call | flops 30000001024 | tf_op jit(solution)/shard_map/middle/pallas_call | solution.py:179
  94.8 11.3 %feed_grads.1 = (bf16[256,2048]{1,0:T(8,128)(2,1)}, bf16[256,2048]{1,0:T(8,128)(2,1)}, bf16[1280,512]{1,0:T(8,128)(2,1)}, bf16[1280,512]{1,0:T(8,128)(2,1)}, f32[8,128]{1,0:T(8,128)}) custom-call(bf16[512,1024]{1,0:T(8,128)(2,1)} %get-tuple-element.136.refs_0_, bf16[1024,2048]{1,0:T(8,128)(2,1)} %get-tuple-element.137.refs_1_, ...), custom_call_target="tpu_custom_call" | custom-call | flops 11000000512 | tf_op jit(solution)/shard_map/feed_grads/pallas_call | solution.py:179
  106.9 12.9 %kernel_grad.1 = (f32[16,32,128]{2,1,0:T(8,128)}, f32[8,128]{1,0:T(8,128)}) custom-call(bf16[4,256,1024]{2,1,0:T(8,128)(2,1)} %bitcast.47, bf16[16,13,5,16,256]{4,3,2,1,0:T(8,128)(2,1)} %get-tuple-element.150.refs_1_, f32[8,128]{1,0:T(8,128)} %get-tuple-element.151.refs_2_), custom_call_target="tpu_custom_call" | custom-call | flops 12999999488 | tf_op jit(solution)/shard_map/kernel_grad/pallas_call | solution.py:179
  119.8 3.4 %gate_grads.1 = (bf16[256,512]{1,0:T(8,128)(2,1)}, bf16[256,512]{1,0:T(8,128)(2,1)}, f32[8,128]{1,0:T(8,128)}) custom-call(bf16[1024,1024]{1,0:T(8,128)(2,1)} %get-tuple-element.140.refs_4_.refs_0_, bf16[1024,1024]{1,0:T(8,128)(2,1)} %get-tuple-element.146.refs_1_, f32[8,512]{1,0:T(8,128)} %get-tuple-element.147.refs_2_, ...), custom_call_target="tpu_custom_call" | custom-call | flops 3000000000 | tf_op jit(solution)/shard_map/gate_grads/pallas_call | solution.py:179
  123.5 1.5 collective-permute-done.23
  125.0 0.7 copy-done.19
  126.1 4.5 %combine.2 = (bf16[4,160,512]{2,1,0:T(8,128)(2,1)}, bf16[4,160,512]{2,1,0:T(8,128)(2,1)}, bf16[4,32,2048]{2,1,0:T(8,128)(2,1)}, bf16[4,32,2048]{2,1,0:T(8,128)(2...) custom-call(bf16[2,4,160,512]{3,2,1,0:T(8,128)(2,1)} %bitcast.79, ...), custom_call_target="tpu_custom_call" | custom-call | flops 2000000000 | tf_op jit(solution)/shard_map/combine/pallas_call | solution.py:179
  130.6 1.5 collective-permute-start.24
  132.1 0.6 collective-permute-start.25
  132.7 1.5 collective-permute-start.26
  134.2 0.6 collective-permute-start.27
  134.7 1.5 collective-permute-start.28
  136.2 15.9 %conv_back.1 = (bf16[4,256,1024]{2,1,0:T(8,128)(2,1)}, f32[8,128]{1,0:T(8,128)}) custom-call(s32[32,32]{1,0:T(8,128)} %bitcast.71, bf16[4,256,1024]{2,1,0:T(8,128)(2,1)} %bitcast.48, bf16[4,64,1024]{2,1,0:T(8,128)(2,1)} %copy-done.14, f32[7,7,1024]{2,1,0:T(8,128)} %pad_convert_fusion.refs_13_.refs_3_, f32[8,128]{1,0:T(8,128)} %get-tuple-element.157.refs_4_), custom_call_target="tpu_custom_call" | custom-call | flops 16000000000 | tf_op jit(solution)/shard_map/conv_back/pallas_call | solution.py:179
  152.2 0.5 copy-done.37
  153.1 2.8 %combine.3 = (bf16[1,320,512]{2,1,0:T(8,128)(2,1)}, bf16[1,320,512]{2,1,0:T(8,128)(2,1)}, bf16[1,64,2048]{2,1,0:T(8,128)(2,1)}, bf16[1,64,2048]{2,1,0:T(8,128)(2...) custom-call(bf16[2,1,320,512]{3,2,1,0:T(8,128)(2,1)} %bitcast.86, ...), custom_call_target="tpu_custom_call" | custom-call | flops 2000000000 | tf_op jit(solution)/shard_map/combine/pallas_call | solution.py:179
  155.9 1.5 collective-permute-start.29
  157.4 0.6 collective-permute-start.30
  158.0 1.5 collective-permute-start.31
  159.5 2.4 %collective-permute-start.32 = (bf16[16,512]{1,0:T(8,128)(2,1)}, bf16[16,512]{1,0:T(8,128)(2,1)S(1)}, u32[]{:S(2)}, u32[]{:S(2)}) collective-permute-start(bf16[16,512]{1,0:T(8,128)(2,1)} %bitcast.74), channel_id=1, source_target_pairs={{0,16},{2,18},{4,20},{6,22},{8,24},{10,26},{12,28},{14,30},{16,0},... | collective-permute-start | bytes 49160 | tf_op jit(solution)/shard_map/ppermute | solution.py:1119
  161.8 0.6 collective-permute-start.33
  162.4 4.2 %in_grad.1 = (bf16[256,1024]{1,0:T(8,128)(2,1)}, bf16[256,1024]{1,0:T(8,128)(2,1)}, f32[8,128]{1,0:T(8,128)}) custom-call(bf16[512,1024]{1,0:T(8,128)(2,1)} %get-tuple-element.173.refs_0_, bf16[1024,1024]{1,0:T(8,128)(2,1)} %bitcast.77, f32[8,128]{1,0:T(8,128)} %get-tuple-element.174.refs_2_), custom_call_target="tpu_custom_call" | custom-call | flops 4000000000 | tf_op jit(solution)/shard_map/in_grad/pallas_call | solution.py:179
  166.7 0.6 copy-done.18
  167.4 2.1 merge.1
  169.5 0.6 collective-permute-start.36
  170.0 3.3 %collective-permute-start.37 = (bf16[144,512]{1,0:T(8,128)(2,1)}, bf16[144,512]{1,0:T(8,128)(2,1)S(1)}, u32[]{:S(2)}, u32[]{:S(2)}) collective-permute-start(bf16[144,512]{1,0:T(8,128)(2,1)} %get-tuple-element.187), channel_id=1, source_target_pairs={{0,16},{2,18},{4,20},{6,22},{8,24},{10,26},{12,28},{14,30},{16,0},... | collective-permute-start | bytes 442376 | tf_op jit(solution)/shard_map/ppermute | solution.py:1119
  173.3 0.6 collective-permute-start.38
  173.9 0.6 copy-done.46
  174.5 6.3 %last.1 = (bf16[2,512,512]{2,1,0:T(8,128)(2,1)}, f32[8,512]{1,0:T(8,128)}, f32[8,128]{1,0:T(8,128)}) custom-call(s32[32,32]{1,0:T(8,128)} %bitcast.72, bf16[1024,1024]{1,0:T(8,128)(2,1)} %bitcast.78, bf16[1024,512]{1,0:T(8,128)(2,1)} %bitcast.81, f32[1024,512]{1,0:T(8,128)} %get-tuple-element.159.refs_3_, bf16[64,1024]{1,0:T(8,128)(2,1)} %get-tuple-element.121.refs_4_, ...), custom_call_target="tpu_custom_call" | custom-call | flops 7000000000 | tf_op jit(solution)/shard_map/last/pallas_call | solution.py:179
  180.8 1.4 collective-permute-done.35.refs_3_
  182.2 2.3 %collective-permute-done.37.refs_10_.refs_2_ = bf16[144,512]{1,0:T(8,128)(2,1)S(1)} collective-permute-done((bf16[144,512]{1,0:T(8,128)(2,1)}, bf16[144,512]{1,0:T(8,128)(2,1)S(1)}, u32[]{:S(2)}, u32[]{:S(2)}) %collective-permute-start.37) | collective-permute-done | bytes 147488 | tf_op jit(solution)/shard_map/ppermute | solution.py:1119
  184.5 0.6 copy-done.21
  185.4 2.4 %deal.1 = (bf16[256,1664]{1,0:T(8,128)(2,1)}, f32[8,128]{1,0:T(8,128)}) custom-call(bf16[256,1024]{1,0:T(8,128)(2,1)} %get-tuple-element.181.refs_0_, bf16[256,1024]{1,0:T(8,128)(2,1)} %copy-done.13, f32[8,512]{1,0:T(8,128)} %get-tuple-element.183.refs_2_, f32[8,512]{1,0:T(8,128)} %copy-done.47, bf16[16,512]{1,0:T(8,128)(2,1)} %bitcast.94, ...), custom_call_target="tpu_custom_call" | custom-call | flops 2000000000 | tf_op jit(solution)/shard_map/deal/pallas_call | solution.py:179
  187.8 29.0 %all_to_all.19 = bf16[16,16,1664]{2,1,0:T(8,128)(2,1)S(1)} all-to-all(bf16[16,16,1664]{2,1,0:T(8,128)(2,1)} %bitcast.46), channel_id=1, replica_groups=mesh['img'=16,'row'=2] {'img'}, dimensions={0} | all-to-all | bytes 1703936 | tf_op jit(solution)/shard_map/all_to_all | solution.py:1149
  216.8 2.2 finish.1
  219.2 0.9 copy-done.9
  220.1 2.6 %unpack.1 = (f32[16,1024]{1,0:T(8,128)}, f32[7,7,992]{2,1,0:T(8,128)}, f32[992]{0:T(1024)}, f32[32,64]{1,0:T(8,128)}, f32[64,128]{1,0:T(8,128)}, /*index=5*/f32[...) custom-call(bf16[256,1664]{1,0:T(8,128)(2,1)} %bitcast.45, ...), custom_call_target="tpu_custom_call" | custom-call | flops 3000000000 | tf_op jit(solution)/shard_map/unpack/pallas_call | solution.py:179
  (138 shorter events, 6.3 us)
Async XLA Ops:
  0.7 17.2 %collective-permute-start.1 = (bf16[2,512,512]{2,1,0:T(8,128)(2,1)}, bf16[2,512,512]{2,1,0:T(8,128)(2,1)S(1)}, u32[]{:S(2)}, u32[]{:S(2)}) collective-permute-start(bf16[2,512,512]{2,1,0:T(8,128)(2,1)} %bitcast.51), channel_id=1, source_target_pairs={{0,1},{1,0},{2,3},{3,2},{4,5},{5,4},{6,7},{7,6},{8,9},{9,8},{10,11... | collective-permute-start | bytes 3145736 | tf_op jit(solution)/shard_map/ppermute | solution.py:1123
  1.2 7.7 %collective-permute-start.2 = (bf16[16,1024]{1,0:T(8,128)(2,1)}, bf16[16,1024]{1,0:T(8,128)(2,1)S(1)}, u32[]{:S(2)}, u32[]{:S(2)}) collective-permute-start(bf16[16,1024]{1,0:T(8,128)(2,1)} %refs_0_.1), channel_id=1, source_target_pairs={{0,8},{2,10},{4,12},{6,14},{8,0},{10,2},{12,4},{14,6},{16,24},{18,... | collective-permute-start | bytes 98312 | tf_op jit(solution)/shard_map/ppermute | solution.py:1119
  3.8 8.6 %collective-permute-start.3 = (bf16[16,1024]{1,0:T(8,128)(2,1)}, bf16[16,1024]{1,0:T(8,128)(2,1)S(1)}, u32[]{:S(2)}, u32[]{:S(2)}) collective-permute-start(bf16[16,1024]{1,0:T(8,128)(2,1)} %refs_0_.1), channel_id=1, source_target_pairs={{0,16},{2,18},{4,20},{6,22},{8,24},{10,26},{12,28},{14,30},{16,0},... | collective-permute-start | bytes 98312 | tf_op jit(solution)/shard_map/ppermute | solution.py:1119
  6.4 6.3 %collective-permute-start.4 = (bf16[16,1024]{1,0:T(8,128)(2,1)}, bf16[16,1024]{1,0:T(8,128)(2,1)S(1)}, u32[]{:S(2)}, u32[]{:S(2)}) collective-permute-start(bf16[16,1024]{1,0:T(8,128)(2,1)} %refs_0_.1), channel_id=1, source_target_pairs={{0,24},{2,26},{4,28},{6,30},{8,16},{10,18},{12,20},{14,22},{16,8},... | collective-permute-start | bytes 98312 | tf_op jit(solution)/shard_map/ppermute | solution.py:1119
  8.0 15.9 %copy-start.5 = (bf16[16,2560]{1,0:T(8,128)(2,1)}, bf16[16,2560]{1,0:T(8,128)(2,1)S(1)}, u32[]{:S(2)}) copy-start(bf16[16,2560]{1,0:T(8,128)(2,1)S(1)} %constant_dynamic-update-slice_fusion.refs_0_) | copy-start | bytes 245764
  8.0 8.3 %collective-permute-start.12 = (bf16[16,2560]{1,0:T(8,128)(2,1)S(1)}, bf16[16,2560]{1,0:T(8,128)(2,1)S(1)}, u32[]{:S(2)}, u32[]{:S(2)}) collective-permute-start(bf16[16,2560]{1,0:T(8,128)(2,1)S(1)} %constant_dynamic-update-slice_fusion.refs_0_), channel_id=1, source_target_pairs={{0,8},{2,10},{4,12},{6,14},{8,0},{10,2},{12,4},{14,6},{16,24},{18,... | collective-permute-start | bytes 245768 | tf_op jit(solution)/shard_map/ppermute | solution.py:1119
  8.9 3.9 %copy-start.40 = (bf16[16,1024]{1,0:T(8,128)(2,1)}, bf16[16,1024]{1,0:T(8,128)(2,1)S(1)}, u32[]{:S(2)}) copy-start(bf16[16,1024]{1,0:T(8,128)(2,1)S(1)} %collective-permute-done.2.refs_1_) | copy-start | bytes 98308
  8.9 15.0 %collective-permute-start.13 = (bf16[16,2560]{1,0:T(8,128)(2,1)S(1)}, bf16[16,2560]{1,0:T(8,128)(2,1)S(1)}, u32[]{:S(2)}, u32[]{:S(2)}) collective-permute-start(bf16[16,2560]{1,0:T(8,128)(2,1)S(1)} %constant_dynamic-update-slice_fusion.refs_0_), channel_id=1, source_target_pairs={{0,16},{2,18},{4,20},{6,22},{8,24},{10,26},{12,28},{14,30},{16,0},... | collective-permute-start | bytes 245768 | tf_op jit(solution)/shard_map/ppermute | solution.py:1119
  12.4 11.5 %collective-permute-start.14 = (bf16[16,2560]{1,0:T(8,128)(2,1)S(1)}, bf16[16,2560]{1,0:T(8,128)(2,1)S(1)}, u32[]{:S(2)}, u32[]{:S(2)}) collective-permute-start(bf16[16,2560]{1,0:T(8,128)(2,1)S(1)} %constant_dynamic-update-slice_fusion.refs_0_), channel_id=1, source_target_pairs={{0,24},{2,26},{4,28},{6,30},{8,16},{10,18},{12,20},{14,22},{16,8},... | collective-permute-start | bytes 245768 | tf_op jit(solution)/shard_map/ppermute | solution.py:1119
  12.7 2.1 collective-permute-start
  14.8 3.5 %copy-start.43 = (s32[32,32]{1,0:T(8,128)}, s32[32,32]{1,0:T(8,128)S(1)}, u32[]{:S(2)}) copy-start(s32[32,32]{1,0:T(8,128)S(1)} %collective-permute-done.refs_1_) | copy-start | bytes 12292
  14.8 9.1 %collective-permute-start.5 = (bf16[64,1024]{1,0:T(8,128)(2,1)}, bf16[64,1024]{1,0:T(8,128)(2,1)S(1)}, u32[]{:S(2)}, u32[]{:S(2)}) collective-permute-start(bf16[64,1024]{1,0:T(8,128)(2,1)} %get-tuple-element.121.refs_4_), channel_id=1, source_target_pairs={{0,2},{2,0},{4,6},{6,4},{8,10},{10,8},{12,14},{14,12},{16,18},{18,... | collective-permute-start | bytes 393224 | tf_op jit(solution)/shard_map/ppermute | solution.py:1119
  16.3 7.5 %copy-start.34 = (bf16[16,2560]{1,0:T(8,128)(2,1)}, bf16[16,2560]{1,0:T(8,128)(2,1)S(1)}, u32[]{:S(2)}) copy-start(bf16[16,2560]{1,0:T(8,128)(2,1)S(1)} %collective-permute-done.12.refs_1_) | copy-start | bytes 245764
  16.3 8.0 %collective-permute-start.6 = (bf16[64,1024]{1,0:T(8,128)(2,1)}, bf16[64,1024]{1,0:T(8,128)(2,1)S(1)}, u32[]{:S(2)}, u32[]{:S(2)}) collective-permute-start(bf16[64,1024]{1,0:T(8,128)(2,1)} %get-tuple-element.121.refs_4_), channel_id=1, source_target_pairs={{0,4},{2,6},{4,0},{6,2},{8,12},{10,14},{12,8},{14,10},{16,20},{18,... | collective-permute-start | bytes 393224 | tf_op jit(solution)/shard_map/ppermute | solution.py:1119
  17.8 1.0 copy-start.7
  17.9 6.5 %collective-permute-start.7 = (bf16[64,1024]{1,0:T(8,128)(2,1)}, bf16[64,1024]{1,0:T(8,128)(2,1)S(1)}, u32[]{:S(2)}, u32[]{:S(2)}) collective-permute-start(bf16[64,1024]{1,0:T(8,128)(2,1)} %get-tuple-element.121.refs_4_), channel_id=1, source_target_pairs={{0,6},{2,4},{4,2},{6,0},{8,14},{10,12},{12,10},{14,8},{16,22},{18,... | collective-permute-start | bytes 393224 | tf_op jit(solution)/shard_map/ppermute | solution.py:1119
  23.9 4.6 %copy-start.4 = (bf16[64,512]{1,0:T(8,128)(2,1)S(1)}, bf16[64,512]{1,0:T(8,128)(2,1)}, u32[]{:S(2)}) copy-start(bf16[64,512]{1,0:T(8,128)(2,1)} %param.45) | copy-start | bytes 196612
  26.8 8.1 %copy-start.23 = (bf16[64,1024]{1,0:T(8,128)(2,1)S(1)}, bf16[64,1024]{1,0:T(8,128)(2,1)}, u32[]{:S(2)}) copy-start(bf16[64,1024]{1,0:T(8,128)(2,1)} %get-tuple-element.121.refs_4_) | copy-start | bytes 393220
  26.8 8.2 %copy-start.27 = (bf16[64,1024]{1,0:T(8,128)(2,1)S(1)}, bf16[64,1024]{1,0:T(8,128)(2,1)}, u32[]{:S(2)}) copy-start(bf16[64,1024]{1,0:T(8,128)(2,1)} %copy-done.26) | copy-start | bytes 393220
  26.8 8.7 %copy-start.29 = (bf16[64,1024]{1,0:T(8,128)(2,1)S(1)}, bf16[64,1024]{1,0:T(8,128)(2,1)}, u32[]{:S(2)}) copy-start(bf16[64,1024]{1,0:T(8,128)(2,1)} %copy-done.28) | copy-start | bytes 393220
  26.8 8.8 %copy-start.25 = (bf16[64,1024]{1,0:T(8,128)(2,1)S(1)}, bf16[64,1024]{1,0:T(8,128)(2,1)}, u32[]{:S(2)}) copy-start(bf16[64,1024]{1,0:T(8,128)(2,1)} %copy-done.24) | copy-start | bytes 393220
  26.8 9.2 %copy-start.3 = (bf16[7,7,992]{2,1,0:T(8,128)(2,1)S(1)}, bf16[7,7,992]{2,1,0:T(8,128)(2,1)}, u32[]{:S(2)}) copy-start(bf16[7,7,992]{2,1,0:T(8,128)(2,1)} %param.31) | copy-start | bytes 291652
  26.8 10.0 %collective-permute-start.15 = (bf16[64,2560]{1,0:T(8,128)(2,1)}, bf16[64,2560]{1,0:T(8,128)(2,1)S(1)}, u32[]{:S(2)}, u32[]{:S(2)}) collective-permute-start(bf16[64,2560]{1,0:T(8,128)(2,1)} %get-tuple-element.124.refs_0_), channel_id=1, source_target_pairs={{0,4},{2,6},{4,0},{6,2},{8,12},{10,14},{12,8},{14,10},{16,20},{18,... | collective-permute-start | bytes 983048 | tf_op jit(solution)/shard_map/ppermute | solution.py:1119
  29.5 33.7 %all-to-all-start = ((bf16[16,64,512]{2,1,0:T(8,128)(2,1)}), bf16[16,64,512]{2,1,0:T(8,128)(2,1)S(1)}, u32[]{:S(2)}, u32[]{:S(2)}) async-start(bf16[16,64,512]{2,1,0:T(8,128)(2,1)} %broadcast_in_dim.2), calls=%async_computation | async-start | bytes 2097152 | tf_op jit(solution)/shard_map/all_to_all | solution.py:1149
  34.9 6.5 %collective-permute-start.8 = (bf16[64,1024]{1,0:T(8,128)(2,1)S(1)}, bf16[64,1024]{1,0:T(8,128)(2,1)S(1)}, u32[]{:S(2)}, u32[]{:S(2)}) collective-permute-start(bf16[64,1024]{1,0:T(8,128)(2,1)S(1)} %copy-done.23), channel_id=1, source_target_pairs={{0,1},{1,0},{2,3},{3,2},{4,5},{5,4},{6,7},{7,6},{8,9},{9,8},{10,11... | collective-permute-start | bytes 393224 | tf_op jit(solution)/shard_map/ppermute | solution.py:1123
  35.0 6.5 %collective-permute-start.10 = (bf16[64,1024]{1,0:T(8,128)(2,1)S(1)}, bf16[64,1024]{1,0:T(8,128)(2,1)S(1)}, u32[]{:S(2)}, u32[]{:S(2)}) collective-permute-start(bf16[64,1024]{1,0:T(8,128)(2,1)S(1)} %copy-done.27), channel_id=1, source_target_pairs={{0,1},{1,0},{2,3},{3,2},{4,5},{5,4},{6,7},{7,6},{8,9},{9,8},{10,11... | collective-permute-start | bytes 393224 | tf_op jit(solution)/shard_map/ppermute | solution.py:1123
  35.5 6.0 %collective-permute-start.11 = (bf16[64,1024]{1,0:T(8,128)(2,1)S(1)}, bf16[64,1024]{1,0:T(8,128)(2,1)S(1)}, u32[]{:S(2)}, u32[]{:S(2)}) collective-permute-start(bf16[64,1024]{1,0:T(8,128)(2,1)S(1)} %copy-done.29), channel_id=1, source_target_pairs={{0,1},{1,0},{2,3},{3,2},{4,5},{5,4},{6,7},{7,6},{8,9},{9,8},{10,11... | collective-permute-start | bytes 393224 | tf_op jit(solution)/shard_map/ppermute | solution.py:1123
  35.6 5.9 %collective-permute-start.9 = (bf16[64,1024]{1,0:T(8,128)(2,1)S(1)}, bf16[64,1024]{1,0:T(8,128)(2,1)S(1)}, u32[]{:S(2)}, u32[]{:S(2)}) collective-permute-start(bf16[64,1024]{1,0:T(8,128)(2,1)S(1)} %copy-done.25), channel_id=1, source_target_pairs={{0,1},{1,0},{2,3},{3,2},{4,5},{5,4},{6,7},{7,6},{8,9},{9,8},{10,11... | collective-permute-start | bytes 393224 | tf_op jit(solution)/shard_map/ppermute | solution.py:1123
  39.6 25.2 %collective-permute-start.16 = (bf16[128,2560]{1,0:T(8,128)(2,1)}, bf16[128,2560]{1,0:T(8,128)(2,1)S(1)}, u32[]{:S(2)}, u32[]{:S(2)}) collective-permute-start(bf16[128,2560]{1,0:T(8,128)(2,1)} %get-tuple-element.131.refs_5_.refs_9_), channel_id=1, source_target_pairs={{0,2},{2,0},{4,6},{6,4},{8,10},{10,8},{12,14},{14,12},{16,18},{18,... | collective-permute-start | bytes 1966088 | tf_op jit(solution)/shard_map/ppermute | solution.py:1119
  42.3 21.0 %copy-start.10 = (bf16[128,2560]{1,0:T(8,128)(2,1)S(1)}, bf16[128,2560]{1,0:T(8,128)(2,1)}, u32[]{:S(2)}) copy-start(bf16[128,2560]{1,0:T(8,128)(2,1)} %get-tuple-element.131.refs_5_.refs_9_) | copy-start | bytes 1966084
  63.2 4.8 %copy-start = (bf16[16,64,512]{2,1,0:T(8,128)(2,1)}, bf16[16,64,512]{2,1,0:T(8,128)(2,1)S(1)}, u32[]{:S(2)}) copy-start(bf16[16,64,512]{2,1,0:T(8,128)(2,1)S(1)} %all-to-all-done) | copy-start | bytes 3145732
  63.2 4.7 %collective-permute-start.19 = (bf16[1024,512]{1,0:T(8,128)(2,1)S(1)}, bf16[1024,512]{1,0:T(8,128)(2,1)S(1)}, u32[]{:S(2)}, u32[]{:S(2)}) collective-permute-start(bf16[1024,512]{1,0:T(8,128)(2,1)S(1)} %bitcast.42), channel_id=1, source_target_pairs={{0,1},{1,0},{2,3},{3,2},{4,5},{5,4},{6,7},{7,6},{8,9},{9,8},{10,11... | collective-permute-start | bytes 3145736 | tf_op jit(solution)/shard_map/ppermute | solution.py:1123
  63.3 3.7 %collective-permute-start.17 = (bf16[128,2560]{1,0:T(8,128)(2,1)S(1)}, bf16[128,2560]{1,0:T(8,128)(2,1)}, u32[]{:S(2)}, u32[]{:S(2)}) collective-permute-start(bf16[128,2560]{1,0:T(8,128)(2,1)S(1)} %copy-done.10), channel_id=1, source_target_pairs={{0,1},{1,0},{2,3},{3,2},{4,5},{5,4},{6,7},{7,6},{8,9},{9,8},{10,11... | collective-permute-start | bytes 1966088 | tf_op jit(solution)/shard_map/ppermute | solution.py:1123
  64.7 3.3 %copy-start.11 = (bf16[128,2560]{1,0:T(8,128)(2,1)}, bf16[128,2560]{1,0:T(8,128)(2,1)S(1)}, u32[]{:S(2)}) copy-start(bf16[128,2560]{1,0:T(8,128)(2,1)S(1)} %collective-permute-done.16.refs_6_.refs_10_) | copy-start | bytes 1966084
  64.7 3.2 %collective-permute-start.18 = (bf16[128,2560]{1,0:T(8,128)(2,1)S(1)}, bf16[128,2560]{1,0:T(8,128)(2,1)}, u32[]{:S(2)}, u32[]{:S(2)}) collective-permute-start(bf16[128,2560]{1,0:T(8,128)(2,1)S(1)} %collective-permute-done.16.refs_6_.refs_10_), channel_id=1, source_target_pairs={{0,1},{1,0},{2,3},{3,2},{4,5},{5,4},{6,7},{7,6},{8,9},{9,8},{10,11... | collective-permute-start | bytes 1966088 | tf_op jit(solution)/shard_map/ppermute | solution.py:1123
  68.0 1.0 copy-start.8
  94.8 11.9 %copy-start.2 = (bf16[1024,1024]{1,0:T(8,128)(2,1)S(1)}, bf16[1024,1024]{1,0:T(8,128)(2,1)}, u32[]{:S(2)}) copy-start(bf16[1024,1024]{1,0:T(8,128)(2,1)} %get-tuple-element.135) | copy-start | bytes 6291460
  106.1 18.9 %collective-permute-start.21 = (bf16[1280,512]{1,0:T(8,128)(2,1)}, bf16[1280,512]{1,0:T(8,128)(2,1)S(1)}, u32[]{:S(2)}, u32[]{:S(2)}) collective-permute-start(bf16[1280,512]{1,0:T(8,128)(2,1)} %get-tuple-element.143), channel_id=1, source_target_pairs={{0,1},{1,0},{2,3},{3,2},{4,5},{5,4},{6,7},{7,6},{8,9},{9,8},{10,11... | collective-permute-start | bytes 3932168 | tf_op jit(solution)/shard_map/ppermute | solution.py:1123
  106.3 18.6 %collective-permute-start.22 = (bf16[256,2048]{1,0:T(8,128)(2,1)}, bf16[256,2048]{1,0:T(8,128)(2,1)}, u32[]{:S(2)}, u32[]{:S(2)}) collective-permute-start(bf16[256,2048]{1,0:T(8,128)(2,1)} %get-tuple-element.145), channel_id=1, source_target_pairs={{0,1},{1,0},{2,3},{3,2},{4,5},{5,4},{6,7},{7,6},{8,9},{9,8},{10,11... | collective-permute-start | bytes 3145736 | tf_op jit(solution)/shard_map/ppermute | solution.py:1123
  106.8 28.0 %collective-permute-start.20 = (bf16[4,64,1024]{2,1,0:T(8,128)(2,1)S(1)}, bf16[4,64,1024]{2,1,0:T(8,128)(2,1)S(1)}, u32[]{:S(2)}, u32[]{:S(2)}) collective-permute-start(bf16[4,64,1024]{2,1,0:T(8,128)(2,1)S(1)} %slice_select_fusion), channel_id=1, source_target_pairs={{0,1},{1,0},{2,3},{3,2},{4,5},{5,4},{6,7},{7,6},{8,9},{9,8},{10,11... | collective-permute-start | bytes 1572872 | tf_op jit(solution)/shard_map/ppermute | solution.py:1123
  123.2 1.7 collective-permute-start.23
  125.0 1.2 copy-start.6
  130.6 21.5 %collective-permute-start.24 = (bf16[640,512]{1,0:T(8,128)(2,1)}, bf16[640,512]{1,0:T(8,128)(2,1)S(1)}, u32[]{:S(2)}, u32[]{:S(2)}) collective-permute-start(bf16[640,512]{1,0:T(8,128)(2,1)} %bitcast.55), channel_id=1, source_target_pairs={{0,4},{2,6},{4,0},{6,2},{8,12},{10,14},{12,8},{14,10},{16,20},{18,... | collective-permute-start | bytes 1966088 | tf_op jit(solution)/shard_map/ppermute | solution.py:1119
  132.1 20.0 %collective-permute-start.25 = (bf16[128,2048]{1,0:T(8,128)(2,1)}, bf16[128,2048]{1,0:T(8,128)(2,1)S(1)}, u32[]{:S(2)}, u32[]{:S(2)}) collective-permute-start(bf16[128,2048]{1,0:T(8,128)(2,1)} %bitcast.57), channel_id=1, source_target_pairs={{0,2},{2,0},{4,6},{6,4},{8,10},{10,8},{12,14},{14,12},{16,18},{18,... | collective-permute-start | bytes 1572872 | tf_op jit(solution)/shard_map/ppermute | solution.py:1119
  132.7 19.4 %collective-permute-start.26 = (bf16[64,512]{1,0:T(8,128)(2,1)}, bf16[64,512]{1,0:T(8,128)(2,1)S(1)}, u32[]{:S(2)}, u32[]{:S(2)}) collective-permute-start(bf16[64,512]{1,0:T(8,128)(2,1)} %bitcast.65), channel_id=1, source_target_pairs={{0,2},{2,0},{4,6},{6,4},{8,10},{10,8},{12,14},{14,12},{16,18},{18,... | collective-permute-start | bytes 196616 | tf_op jit(solution)/shard_map/ppermute | solution.py:1119
  134.2 17.9 %collective-permute-start.27 = (bf16[64,512]{1,0:T(8,128)(2,1)}, bf16[64,512]{1,0:T(8,128)(2,1)S(1)}, u32[]{:S(2)}, u32[]{:S(2)}) collective-permute-start(bf16[64,512]{1,0:T(8,128)(2,1)} %bitcast.64), channel_id=1, source_target_pairs={{0,4},{2,6},{4,0},{6,2},{8,12},{10,14},{12,8},{14,10},{16,20},{18,... | collective-permute-start | bytes 196616 | tf_op jit(solution)/shard_map/ppermute | solution.py:1119
  134.7 1.5 copy-start.14
  134.7 17.4 %collective-permute-start.28 = (bf16[64,512]{1,0:T(8,128)(2,1)}, bf16[64,512]{1,0:T(8,128)(2,1)S(1)}, u32[]{:S(2)}, u32[]{:S(2)}) collective-permute-start(bf16[64,512]{1,0:T(8,128)(2,1)} %bitcast.62), channel_id=1, source_target_pairs={{0,6},{2,4},{4,2},{6,0},{8,14},{10,12},{12,10},{14,8},{16,22},{18,... | collective-permute-start | bytes 196616 | tf_op jit(solution)/shard_map/ppermute | solution.py:1119
  152.2 1.0 copy-start.12
  155.9 10.7 %collective-permute-start.29 = (bf16[320,512]{1,0:T(8,128)(2,1)}, bf16[320,512]{1,0:T(8,128)(2,1)S(1)}, u32[]{:S(2)}, u32[]{:S(2)}) collective-permute-start(bf16[320,512]{1,0:T(8,128)(2,1)} %bitcast.58), channel_id=1, source_target_pairs={{0,2},{2,0},{4,6},{6,4},{8,10},{10,8},{12,14},{14,12},{16,18},{18,... | collective-permute-start | bytes 983048 | tf_op jit(solution)/shard_map/ppermute | solution.py:1119
  157.4 9.1 %collective-permute-start.30 = (bf16[64,2048]{1,0:T(8,128)(2,1)}, bf16[64,2048]{1,0:T(8,128)(2,1)S(1)}, u32[]{:S(2)}, u32[]{:S(2)}) collective-permute-start(bf16[64,2048]{1,0:T(8,128)(2,1)} %bitcast.59), channel_id=1, source_target_pairs={{0,4},{2,6},{4,0},{6,2},{8,12},{10,14},{12,8},{14,10},{16,20},{18,... | collective-permute-start | bytes 786440 | tf_op jit(solution)/shard_map/ppermute | solution.py:1119
  158.0 12.0 %collective-permute-start.31 = (bf16[16,512]{1,0:T(8,128)(2,1)}, bf16[16,512]{1,0:T(8,128)(2,1)S(1)}, u32[]{:S(2)}, u32[]{:S(2)}) collective-permute-start(bf16[16,512]{1,0:T(8,128)(2,1)} %bitcast.75), channel_id=1, source_target_pairs={{0,8},{2,10},{4,12},{6,14},{8,0},{10,2},{12,4},{14,6},{16,24},{18,... | collective-permute-start | bytes 49160 | tf_op jit(solution)/shard_map/ppermute | solution.py:1119
  159.5 13.8 %collective-permute-start.32 = (bf16[16,512]{1,0:T(8,128)(2,1)}, bf16[16,512]{1,0:T(8,128)(2,1)S(1)}, u32[]{:S(2)}, u32[]{:S(2)}) collective-permute-start(bf16[16,512]{1,0:T(8,128)(2,1)} %bitcast.74), channel_id=1, source_target_pairs={{0,16},{2,18},{4,20},{6,22},{8,24},{10,26},{12,28},{14,30},{16,0},... | collective-permute-start | bytes 49160 | tf_op jit(solution)/shard_map/ppermute | solution.py:1119
  161.8 12.0 %collective-permute-start.33 = (bf16[16,512]{1,0:T(8,128)(2,1)}, bf16[16,512]{1,0:T(8,128)(2,1)S(1)}, u32[]{:S(2)}, u32[]{:S(2)}) collective-permute-start(bf16[16,512]{1,0:T(8,128)(2,1)} %bitcast.73), channel_id=1, source_target_pairs={{0,24},{2,26},{4,28},{6,30},{8,16},{10,18},{12,20},{14,22},{16,8},... | collective-permute-start | bytes 49160 | tf_op jit(solution)/shard_map/ppermute | solution.py:1119
  166.6 17.9 %collective-permute-start.34 = (bf16[256,1024]{1,0:T(8,128)(2,1)}, bf16[256,1024]{1,0:T(8,128)(2,1)S(1)}, u32[]{:S(2)}, u32[]{:S(2)}) collective-permute-start(bf16[256,1024]{1,0:T(8,128)(2,1)} %get-tuple-element.182), channel_id=1, source_target_pairs={{0,1},{1,0},{2,3},{3,2},{4,5},{5,4},{6,7},{7,6},{8,9},{9,8},{10,11... | collective-permute-start | bytes 1572872 | tf_op jit(solution)/shard_map/ppermute | solution.py:1123
  169.5 12.8 %collective-permute-start.36 = (bf16[144,512]{1,0:T(8,128)(2,1)}, bf16[144,512]{1,0:T(8,128)(2,1)S(1)}, u32[]{:S(2)}, u32[]{:S(2)}) collective-permute-start(bf16[144,512]{1,0:T(8,128)(2,1)} %get-tuple-element.186), channel_id=1, source_target_pairs={{0,8},{2,10},{4,12},{6,14},{8,0},{10,2},{12,4},{14,6},{16,24},{18,... | collective-permute-start | bytes 442376 | tf_op jit(solution)/shard_map/ppermute | solution.py:1119
  170.0 3.8 %copy-start.44 = (bf16[16,512]{1,0:T(8,128)(2,1)}, bf16[16,512]{1,0:T(8,128)(2,1)S(1)}, u32[]{:S(2)}) copy-start(bf16[16,512]{1,0:T(8,128)(2,1)S(1)} %collective-permute-done.31.refs_14_.refs_5_) | copy-start | bytes 49156
  170.0 14.5 %collective-permute-start.37 = (bf16[144,512]{1,0:T(8,128)(2,1)}, bf16[144,512]{1,0:T(8,128)(2,1)S(1)}, u32[]{:S(2)}, u32[]{:S(2)}) collective-permute-start(bf16[144,512]{1,0:T(8,128)(2,1)} %get-tuple-element.187), channel_id=1, source_target_pairs={{0,16},{2,18},{4,20},{6,22},{8,24},{10,26},{12,28},{14,30},{16,0},... | collective-permute-start | bytes 442376 | tf_op jit(solution)/shard_map/ppermute | solution.py:1119
  173.3 11.2 %collective-permute-start.38 = (bf16[144,512]{1,0:T(8,128)(2,1)}, bf16[144,512]{1,0:T(8,128)(2,1)S(1)}, u32[]{:S(2)}, u32[]{:S(2)}) collective-permute-start(bf16[144,512]{1,0:T(8,128)(2,1)} %get-tuple-element.188), channel_id=1, source_target_pairs={{0,24},{2,26},{4,28},{6,30},{8,16},{10,18},{12,20},{14,22},{16,8},... | collective-permute-start | bytes 442376 | tf_op jit(solution)/shard_map/ppermute | solution.py:1119
  180.8 1.4 collective-permute-start.35
  182.2 2.3 %copy-start.47 = (f32[8,512]{1,0:T(8,128)}, f32[8,512]{1,0:T(8,128)S(1)}, u32[]{:S(2)}) copy-start(f32[8,512]{1,0:T(8,128)S(1)} %collective-permute-done.35.refs_3_) | copy-start | bytes 49156
  182.2 2.3 %copy-start.20 = (bf16[144,512]{1,0:T(8,128)(2,1)}, bf16[144,512]{1,0:T(8,128)(2,1)S(1)}, u32[]{:S(2)}) copy-start(bf16[144,512]{1,0:T(8,128)(2,1)S(1)} %collective-permute-done.36.refs_9_.refs_1_) | copy-start | bytes 442372
  216.8 2.4 %copy-start.1 = (bf16[16,16,1664]{2,1,0:T(8,128)(2,1)}, bf16[16,16,1664]{2,1,0:T(8,128)(2,1)S(1)}, u32[]{:S(2)}) copy-start(bf16[16,16,1664]{2,1,0:T(8,128)(2,1)S(1)} %all_to_all.19) | copy-start | bytes 2555908
  216.8 2.4 %collective-permute-start.39 = (bf16[256,1664]{1,0:T(8,128)(2,1)S(1)}, bf16[256,1664]{1,0:T(8,128)(2,1)S(1)}, u32[]{:S(2)}, u32[]{:S(2)}) collective-permute-start(bf16[256,1664]{1,0:T(8,128)(2,1)S(1)} %bitcast.44), channel_id=1, source_target_pairs={{0,1},{1,0},{2,3},{3,2},{4,5},{5,4},{6,7},{7,6},{8,9},{9,8},{10,11... | collective-permute-start | bytes 2555912 | tf_op jit(solution)/shard_map/ppermute | solution.py:1123
  (25 other events, 17.3 us)

commit v5 on v4

--- a/solution.py
+++ b/solution.py
@@ -991,7 +991,7 @@
 
 
 def combine(*items, deps=()):
-    steps = next(n for n in (4, 2, 1) if all(v[0].shape[0] % (16 * n * p) == 0 for v, p in items))
+    steps = next(n for n in (2, 1) if all(v[0].shape[0] % (16 * n * p) == 0 for v, p in items))
     ins, in_specs, outs, out_specs = [], [], [], []
     for terms, parts in items:
         rows, cols = terms[0].shape

time: 224 us -> 223 us (level)
  no operation moved by 1% of the time
where the time goes in v5:
time: 223 us; the launch traced here: 222 us
  Pallas kernels  127 us (57%)
  starting transfers between devices  42.1 us (19%)
  blocking collectives  29 us (13%)
  local copies, waits for them, and re-layouts  12.2 us (5%)
  waiting for transfers between devices  10 us (4%)
    pallas_call x18, Pallas kernels, launch(): return lambda *args: call(*args, *deps)  127 us
    ppermute x24, starting transfers between devices, swap_img(): lax.ppermute(value, 'img', [(k, k ^ mask) for k in range(lax.axis_size('i...  33.4 us
    all_to_all x1, blocking collectives, spread(): return lax.all_to_all(value, 'img', split_axis=0, concat_axis=0, tiled=True)  29 us
    unnamed x97, local copies, waits for them, and re-layouts  10.4 us
    ppermute x16, waiting for transfers between devices, swap_row(): return lax.ppermute(value, 'row', [(0, 1), (1, 0)])  6.33 us
    all_to_all x1, starting transfers between devices, spread(): return lax.all_to_all(value, 'img', split_axis=0, concat_axis=0, tiled=True)  5.42 us
  transfers between devices with their start and end apart: 41, of which 8 were waited for; matrix products, arithmetic and copies ran while one was open for 2% of the time, Pallas kernels for 36%

profile of v5, /device:TPU:0, one launch (start us, length us, event | category | flops | bytes accessed | tf_op | source)
XLA Modules:
  0.0 222.2 jit_solution(4401590690480645322)
XLA Ops:
  0.7 0.5 collective-permute-start.1
  1.2 2.7 %collective-permute-start.2 = (bf16[16,1024]{1,0:T(8,128)(2,1)}, bf16[16,1024]{1,0:T(8,128)(2,1)S(1)}, u32[]{:S(2)}, u32[]{:S(2)}) collective-permute-start(bf16[16,1024]{1,0:T(8,128)(2,1)} %refs_0_.1), channel_id=1, source_target_pairs={{0,8},{2,10},{4,12},{6,14},{8,0},{10,2},{12,4},{14,6},{16,24},{18,... | collective-permute-start | bytes 98312 | tf_op jit(solution)/shard_map/ppermute | solution.py:1119
  3.8 2.6 %collective-permute-start.3 = (bf16[16,1024]{1,0:T(8,128)(2,1)}, bf16[16,1024]{1,0:T(8,128)(2,1)S(1)}, u32[]{:S(2)}, u32[]{:S(2)}) collective-permute-start(bf16[16,1024]{1,0:T(8,128)(2,1)} %refs_0_.1), channel_id=1, source_target_pairs={{0,16},{2,18},{4,20},{6,22},{8,24},{10,26},{12,28},{14,30},{16,0},... | collective-permute-start | bytes 98312 | tf_op jit(solution)/shard_map/ppermute | solution.py:1119
  6.4 0.8 constant_dynamic-update-slice_fusion.1
  7.3 0.7 constant_dynamic-update-slice_fusion.refs_0_
  8.0 0.9 collective-permute-start.12
  8.9 3.5 %collective-permute-start.13 = (bf16[16,2560]{1,0:T(8,128)(2,1)S(1)}, bf16[16,2560]{1,0:T(8,128)(2,1)S(1)}, u32[]{:S(2)}, u32[]{:S(2)}) collective-permute-start(bf16[16,2560]{1,0:T(8,128)(2,1)S(1)} %constant_dynamic-update-slice_fusion.refs_0_), channel_id=1, source_target_pairs={{0,16},{2,18},{4,20},{6,22},{8,24},{10,26},{12,28},{14,30},{16,0},... | collective-permute-start | bytes 245768 | tf_op jit(solution)/shard_map/ppermute | solution.py:1119
  13.4 1.5 join.3
  14.8 1.5 collective-permute-start.5
  16.3 1.5 collective-permute-start.6
  18.3 0.5 copy-done.7
  18.8 5.0 %prepare.1 = (bf16[4,256,512]{2,1,0:T(8,128)(2,1)}, bf16[4,256,512]{2,1,0:T(8,128)(2,1)}, bf16[4,256,512]{2,1,0:T(8,128)(2,1)}, bf16[4,64,512]{2,1,0:T(8,128)(2,...) custom-call(s32[32,32]{1,0:T(8,128)} %bitcast.68, s32[32,32]{1,0:T(8,128)} %copy-done.43, ...), custom_call_target="tpu_custom_call" | custom-call | flops 4000000000 | tf_op jit(solution)/shard_map/prepare/pallas_call | solution.py:179
  25.1 1.8 join.4
  26.8 1.6 collective-permute-start.15
  28.4 1.1 broadcast_in_dim.2
  29.5 5.4 %all-to-all-start = ((bf16[16,64,512]{2,1,0:T(8,128)(2,1)}), bf16[16,64,512]{2,1,0:T(8,128)(2,1)S(1)}, u32[]{:S(2)}, u32[]{:S(2)}) async-start(bf16[16,64,512]{2,1,0:T(8,128)(2,1)} %broadcast_in_dim.2), calls=%async_computation | async-start | bytes 2097152 | tf_op jit(solution)/shard_map/all_to_all | solution.py:1149
  35.0 0.5 collective-permute-start.10
  36.0 0.8 pad_convert_fusion.refs_13_.refs_3_
  36.8 0.7 copy-done.17
  37.6 2.0 join.5
  39.6 1.9 collective-permute-start.16
  41.5 0.6 copy-done.30
  42.3 20.9 %forward.1 = (f32[4,256,1024]{2,1,0:T(8,128)}, bf16[16,13,5,16,256]{4,3,2,1,0:T(8,128)(2,1)}, f32[4,256,128]{2,1,0:T(8,128)}, f32[8,128]{1,0:T(8,128)}) custom-call(s32[32,32]{1,0:T(8,128)} %bitcast.69, s32[32,32]{1,0:T(8,128)} %copy-done.43, bf16[4,256,512]{2,1,0:T(8,128)(2,1)} %get-tuple-element.119.refs_2_, ...), custom_call_target="tpu_custom_call" | custom-call | flops 24000000000 | tf_op jit(solution)/shard_map/forward/pallas_call | solution.py:179
  63.3 0.5 collective-permute-start.17
  63.8 0.9 collective-permute-done.16.refs_6_.refs_10_
  64.7 2.3 %collective-permute-done.17.refs_7_.refs_11_ = bf16[128,2560]{1,0:T(8,128)(2,1)} collective-permute-done((bf16[128,2560]{1,0:T(8,128)(2,1)S(1)}, bf16[128,2560]{1,0:T(8,128)(2,1)}, u32[]{:S(2)}, u32[]{:S(2)}) %collective-permute-start.17) | collective-permute-done | bytes 655392 | tf_op jit(solution)/shard_map/ppermute | solution.py:1123
  67.0 0.9 collective-permute-done.18.refs_8_.refs_12_
  68.0 1.0 copy-done.8
  69.0 25.8 %middle.1 = (bf16[2,512,512]{2,1,0:T(8,128)(2,1)}, bf16[2048,1024]{1,0:T(8,128)(2,1)}, bf16[512,1024]{1,0:T(8,128)(2,1)}, bf16[1024,1024]{1,0:T(8,128)(2,1)}, bf...) custom-call(s32[32,32]{1,0:T(8,128)} %bitcast.70, ...), custom_call_target="tpu_custom_call" | custom-call | flops 30000001024 | tf_op jit(solution)/shard_map/middle/pallas_call | solution.py:179
  94.8 11.3 %feed_grads.1 = (bf16[256,2048]{1,0:T(8,128)(2,1)}, bf16[256,2048]{1,0:T(8,128)(2,1)}, bf16[1280,512]{1,0:T(8,128)(2,1)}, bf16[1280,512]{1,0:T(8,128)(2,1)}, f32[8,128]{1,0:T(8,128)}) custom-call(bf16[512,1024]{1,0:T(8,128)(2,1)} %get-tuple-element.136.refs_0_, bf16[1024,2048]{1,0:T(8,128)(2,1)} %get-tuple-element.137.refs_1_, ...), custom_call_target="tpu_custom_call" | custom-call | flops 11000000512 | tf_op jit(solution)/shard_map/feed_grads/pallas_call | solution.py:179
  106.9 12.9 %kernel_grad.1 = (f32[16,32,128]{2,1,0:T(8,128)}, f32[8,128]{1,0:T(8,128)}) custom-call(bf16[4,256,1024]{2,1,0:T(8,128)(2,1)} %bitcast.47, bf16[16,13,5,16,256]{4,3,2,1,0:T(8,128)(2,1)} %get-tuple-element.150.refs_1_, f32[8,128]{1,0:T(8,128)} %get-tuple-element.151.refs_2_), custom_call_target="tpu_custom_call" | custom-call | flops 12999999488 | tf_op jit(solution)/shard_map/kernel_grad/pallas_call | solution.py:179
  119.8 3.4 %gate_grads.1 = (bf16[256,512]{1,0:T(8,128)(2,1)}, bf16[256,512]{1,0:T(8,128)(2,1)}, f32[8,128]{1,0:T(8,128)}) custom-call(bf16[1024,1024]{1,0:T(8,128)(2,1)} %get-tuple-element.140.refs_4_.refs_0_, bf16[1024,1024]{1,0:T(8,128)(2,1)} %get-tuple-element.146.refs_1_, f32[8,512]{1,0:T(8,128)} %get-tuple-element.147.refs_2_, ...), custom_call_target="tpu_custom_call" | custom-call | flops 3000000000 | tf_op jit(solution)/shard_map/gate_grads/pallas_call | solution.py:179
  123.5 1.5 collective-permute-done.23
  125.0 0.7 copy-done.19
  126.1 3.8 %combine.2 = (bf16[2,320,512]{2,1,0:T(8,128)(2,1)}, bf16[2,320,512]{2,1,0:T(8,128)(2,1)}, bf16[2,64,2048]{2,1,0:T(8,128)(2,1)}, bf16[2,64,2048]{2,1,0:T(8,128)(2...) custom-call(bf16[2,2,320,512]{3,2,1,0:T(8,128)(2,1)} %bitcast.79, ...), custom_call_target="tpu_custom_call" | custom-call | flops 2000000000 | tf_op jit(solution)/shard_map/combine/pallas_call | solution.py:179
  130.0 1.5 collective-permute-start.24
  131.5 0.6 collective-permute-start.25
  132.1 1.5 collective-permute-start.26
  133.5 0.6 collective-permute-start.27
  134.1 1.5 collective-permute-start.28
  135.6 15.9 %conv_back.1 = (bf16[4,256,1024]{2,1,0:T(8,128)(2,1)}, f32[8,128]{1,0:T(8,128)}) custom-call(s32[32,32]{1,0:T(8,128)} %bitcast.71, bf16[4,256,1024]{2,1,0:T(8,128)(2,1)} %bitcast.48, bf16[4,64,1024]{2,1,0:T(8,128)(2,1)} %copy-done.14, f32[7,7,1024]{2,1,0:T(8,128)} %pad_convert_fusion.refs_13_.refs_3_, f32[8,128]{1,0:T(8,128)} %get-tuple-element.157.refs_4_), custom_call_target="tpu_custom_call" | custom-call | flops 16000000000 | tf_op jit(solution)/shard_map/conv_back/pallas_call | solution.py:179
  151.5 0.5 copy-done.37
  152.5 2.8 %combine.3 = (bf16[1,320,512]{2,1,0:T(8,128)(2,1)}, bf16[1,320,512]{2,1,0:T(8,128)(2,1)}, bf16[1,64,2048]{2,1,0:T(8,128)(2,1)}, bf16[1,64,2048]{2,1,0:T(8,128)(2...) custom-call(bf16[2,1,320,512]{3,2,1,0:T(8,128)(2,1)} %bitcast.86, ...), custom_call_target="tpu_custom_call" | custom-call | flops 2000000000 | tf_op jit(solution)/shard_map/combine/pallas_call | solution.py:179
  155.3 1.5 collective-permute-start.29
  156.8 0.6 collective-permute-start.30
  157.3 1.5 collective-permute-start.31
  158.8 2.4 %collective-permute-start.32 = (bf16[16,512]{1,0:T(8,128)(2,1)}, bf16[16,512]{1,0:T(8,128)(2,1)S(1)}, u32[]{:S(2)}, u32[]{:S(2)}) collective-permute-start(bf16[16,512]{1,0:T(8,128)(2,1)} %bitcast.74), channel_id=1, source_target_pairs={{0,16},{2,18},{4,20},{6,22},{8,24},{10,26},{12,28},{14,30},{16,0},... | collective-permute-start | bytes 49160 | tf_op jit(solution)/shard_map/ppermute | solution.py:1119
  161.2 0.6 collective-permute-start.33
  161.7 4.2 %in_grad.1 = (bf16[256,1024]{1,0:T(8,128)(2,1)}, bf16[256,1024]{1,0:T(8,128)(2,1)}, f32[8,128]{1,0:T(8,128)}) custom-call(bf16[512,1024]{1,0:T(8,128)(2,1)} %get-tuple-element.173.refs_0_, bf16[1024,1024]{1,0:T(8,128)(2,1)} %bitcast.77, f32[8,128]{1,0:T(8,128)} %get-tuple-element.174.refs_2_), custom_call_target="tpu_custom_call" | custom-call | flops 4000000000 | tf_op jit(solution)/shard_map/in_grad/pallas_call | solution.py:179
  166.0 0.6 copy-done.18
  166.7 2.1 merge.1
  168.8 0.6 collective-permute-start.36
  169.4 3.3 %collective-permute-start.37 = (bf16[144,512]{1,0:T(8,128)(2,1)}, bf16[144,512]{1,0:T(8,128)(2,1)S(1)}, u32[]{:S(2)}, u32[]{:S(2)}) collective-permute-start(bf16[144,512]{1,0:T(8,128)(2,1)} %get-tuple-element.187), channel_id=1, source_target_pairs={{0,16},{2,18},{4,20},{6,22},{8,24},{10,26},{12,28},{14,30},{16,0},... | collective-permute-start | bytes 442376 | tf_op jit(solution)/shard_map/ppermute | solution.py:1119
  172.6 0.6 collective-permute-start.38
  173.2 0.6 copy-done.46
  173.8 6.4 %last.1 = (bf16[2,512,512]{2,1,0:T(8,128)(2,1)}, f32[8,512]{1,0:T(8,128)}, f32[8,128]{1,0:T(8,128)}) custom-call(s32[32,32]{1,0:T(8,128)} %bitcast.72, bf16[1024,1024]{1,0:T(8,128)(2,1)} %bitcast.78, bf16[1024,512]{1,0:T(8,128)(2,1)} %bitcast.81, f32[1024,512]{1,0:T(8,128)} %get-tuple-element.159.refs_3_, bf16[64,1024]{1,0:T(8,128)(2,1)} %get-tuple-element.121.refs_4_, ...), custom_call_target="tpu_custom_call" | custom-call | flops 7000000000 | tf_op jit(solution)/shard_map/last/pallas_call | solution.py:179
  180.2 1.4 collective-permute-done.35.refs_3_
  181.6 2.3 %collective-permute-done.37.refs_10_.refs_2_ = bf16[144,512]{1,0:T(8,128)(2,1)S(1)} collective-permute-done((bf16[144,512]{1,0:T(8,128)(2,1)}, bf16[144,512]{1,0:T(8,128)(2,1)S(1)}, u32[]{:S(2)}, u32[]{:S(2)}) %collective-permute-start.37) | collective-permute-done | bytes 147488 | tf_op jit(solution)/shard_map/ppermute | solution.py:1119
  183.9 0.6 copy-done.21
  184.7 2.4 %deal.1 = (bf16[256,1664]{1,0:T(8,128)(2,1)}, f32[8,128]{1,0:T(8,128)}) custom-call(bf16[256,1024]{1,0:T(8,128)(2,1)} %get-tuple-element.181.refs_0_, bf16[256,1024]{1,0:T(8,128)(2,1)} %copy-done.13, f32[8,512]{1,0:T(8,128)} %get-tuple-element.183.refs_2_, f32[8,512]{1,0:T(8,128)} %copy-done.47, bf16[16,512]{1,0:T(8,128)(2,1)} %bitcast.94, ...), custom_call_target="tpu_custom_call" | custom-call | flops 2000000000 | tf_op jit(solution)/shard_map/deal/pallas_call | solution.py:179
  187.2 29.0 %all_to_all.19 = bf16[16,16,1664]{2,1,0:T(8,128)(2,1)S(1)} all-to-all(bf16[16,16,1664]{2,1,0:T(8,128)(2,1)} %bitcast.46), channel_id=1, replica_groups=mesh['img'=16,'row'=2] {'img'}, dimensions={0} | all-to-all | bytes 1703936 | tf_op jit(solution)/shard_map/all_to_all | solution.py:1149
  216.1 2.2 finish.1
  218.5 0.9 copy-done.9
  219.4 2.6 %unpack.1 = (f32[16,1024]{1,0:T(8,128)}, f32[7,7,992]{2,1,0:T(8,128)}, f32[992]{0:T(1024)}, f32[32,64]{1,0:T(8,128)}, f32[64,128]{1,0:T(8,128)}, /*index=5*/f32[...) custom-call(bf16[256,1664]{1,0:T(8,128)(2,1)} %bitcast.45, ...), custom_call_target="tpu_custom_call" | custom-call | flops 3000000000 | tf_op jit(solution)/shard_map/unpack/pallas_call | solution.py:179
  (138 shorter events, 6.3 us)
Async XLA Ops:
  0.7 17.2 %collective-permute-start.1 = (bf16[2,512,512]{2,1,0:T(8,128)(2,1)}, bf16[2,512,512]{2,1,0:T(8,128)(2,1)S(1)}, u32[]{:S(2)}, u32[]{:S(2)}) collective-permute-start(bf16[2,512,512]{2,1,0:T(8,128)(2,1)} %bitcast.51), channel_id=1, source_target_pairs={{0,1},{1,0},{2,3},{3,2},{4,5},{5,4},{6,7},{7,6},{8,9},{9,8},{10,11... | collective-permute-start | bytes 3145736 | tf_op jit(solution)/shard_map/ppermute | solution.py:1123
  1.2 7.7 %collective-permute-start.2 = (bf16[16,1024]{1,0:T(8,128)(2,1)}, bf16[16,1024]{1,0:T(8,128)(2,1)S(1)}, u32[]{:S(2)}, u32[]{:S(2)}) collective-permute-start(bf16[16,1024]{1,0:T(8,128)(2,1)} %refs_0_.1), channel_id=1, source_target_pairs={{0,8},{2,10},{4,12},{6,14},{8,0},{10,2},{12,4},{14,6},{16,24},{18,... | collective-permute-start | bytes 98312 | tf_op jit(solution)/shard_map/ppermute | solution.py:1119
  3.8 8.6 %collective-permute-start.3 = (bf16[16,1024]{1,0:T(8,128)(2,1)}, bf16[16,1024]{1,0:T(8,128)(2,1)S(1)}, u32[]{:S(2)}, u32[]{:S(2)}) collective-permute-start(bf16[16,1024]{1,0:T(8,128)(2,1)} %refs_0_.1), channel_id=1, source_target_pairs={{0,16},{2,18},{4,20},{6,22},{8,24},{10,26},{12,28},{14,30},{16,0},... | collective-permute-start | bytes 98312 | tf_op jit(solution)/shard_map/ppermute | solution.py:1119
  6.4 6.3 %collective-permute-start.4 = (bf16[16,1024]{1,0:T(8,128)(2,1)}, bf16[16,1024]{1,0:T(8,128)(2,1)S(1)}, u32[]{:S(2)}, u32[]{:S(2)}) collective-permute-start(bf16[16,1024]{1,0:T(8,128)(2,1)} %refs_0_.1), channel_id=1, source_target_pairs={{0,24},{2,26},{4,28},{6,30},{8,16},{10,18},{12,20},{14,22},{16,8},... | collective-permute-start | bytes 98312 | tf_op jit(solution)/shard_map/ppermute | solution.py:1119
  8.0 15.9 %copy-start.5 = (bf16[16,2560]{1,0:T(8,128)(2,1)}, bf16[16,2560]{1,0:T(8,128)(2,1)S(1)}, u32[]{:S(2)}) copy-start(bf16[16,2560]{1,0:T(8,128)(2,1)S(1)} %constant_dynamic-update-slice_fusion.refs_0_) | copy-start | bytes 245764
  8.0 8.3 %collective-permute-start.12 = (bf16[16,2560]{1,0:T(8,128)(2,1)S(1)}, bf16[16,2560]{1,0:T(8,128)(2,1)S(1)}, u32[]{:S(2)}, u32[]{:S(2)}) collective-permute-start(bf16[16,2560]{1,0:T(8,128)(2,1)S(1)} %constant_dynamic-update-slice_fusion.refs_0_), channel_id=1, source_target_pairs={{0,8},{2,10},{4,12},{6,14},{8,0},{10,2},{12,4},{14,6},{16,24},{18,... | collective-permute-start | bytes 245768 | tf_op jit(solution)/shard_map/ppermute | solution.py:1119
  8.9 3.9 %copy-start.40 = (bf16[16,1024]{1,0:T(8,128)(2,1)}, bf16[16,1024]{1,0:T(8,128)(2,1)S(1)}, u32[]{:S(2)}) copy-start(bf16[16,1024]{1,0:T(8,128)(2,1)S(1)} %collective-permute-done.2.refs_1_) | copy-start | bytes 98308
  8.9 15.0 %collective-permute-start.13 = (bf16[16,2560]{1,0:T(8,128)(2,1)S(1)}, bf16[16,2560]{1,0:T(8,128)(2,1)S(1)}, u32[]{:S(2)}, u32[]{:S(2)}) collective-permute-start(bf16[16,2560]{1,0:T(8,128)(2,1)S(1)} %constant_dynamic-update-slice_fusion.refs_0_), channel_id=1, source_target_pairs={{0,16},{2,18},{4,20},{6,22},{8,24},{10,26},{12,28},{14,30},{16,0},... | collective-permute-start | bytes 245768 | tf_op jit(solution)/shard_map/ppermute | solution.py:1119
  12.4 11.5 %collective-permute-start.14 = (bf16[16,2560]{1,0:T(8,128)(2,1)S(1)}, bf16[16,2560]{1,0:T(8,128)(2,1)S(1)}, u32[]{:S(2)}, u32[]{:S(2)}) collective-permute-start(bf16[16,2560]{1,0:T(8,128)(2,1)S(1)} %constant_dynamic-update-slice_fusion.refs_0_), channel_id=1, source_target_pairs={{0,24},{2,26},{4,28},{6,30},{8,16},{10,18},{12,20},{14,22},{16,8},... | collective-permute-start | bytes 245768 | tf_op jit(solution)/shard_map/ppermute | solution.py:1119
  12.7 2.1 collective-permute-start
  14.8 3.5 %copy-start.43 = (s32[32,32]{1,0:T(8,128)}, s32[32,32]{1,0:T(8,128)S(1)}, u32[]{:S(2)}) copy-start(s32[32,32]{1,0:T(8,128)S(1)} %collective-permute-done.refs_1_) | copy-start | bytes 12292
  14.8 9.1 %collective-permute-start.5 = (bf16[64,1024]{1,0:T(8,128)(2,1)}, bf16[64,1024]{1,0:T(8,128)(2,1)S(1)}, u32[]{:S(2)}, u32[]{:S(2)}) collective-permute-start(bf16[64,1024]{1,0:T(8,128)(2,1)} %get-tuple-element.121.refs_4_), channel_id=1, source_target_pairs={{0,2},{2,0},{4,6},{6,4},{8,10},{10,8},{12,14},{14,12},{16,18},{18,... | collective-permute-start | bytes 393224 | tf_op jit(solution)/shard_map/ppermute | solution.py:1119
  16.3 7.5 %copy-start.34 = (bf16[16,2560]{1,0:T(8,128)(2,1)}, bf16[16,2560]{1,0:T(8,128)(2,1)S(1)}, u32[]{:S(2)}) copy-start(bf16[16,2560]{1,0:T(8,128)(2,1)S(1)} %collective-permute-done.12.refs_1_) | copy-start | bytes 245764
  16.3 8.0 %collective-permute-start.6 = (bf16[64,1024]{1,0:T(8,128)(2,1)}, bf16[64,1024]{1,0:T(8,128)(2,1)S(1)}, u32[]{:S(2)}, u32[]{:S(2)}) collective-permute-start(bf16[64,1024]{1,0:T(8,128)(2,1)} %get-tuple-element.121.refs_4_), channel_id=1, source_target_pairs={{0,4},{2,6},{4,0},{6,2},{8,12},{10,14},{12,8},{14,10},{16,20},{18,... | collective-permute-start | bytes 393224 | tf_op jit(solution)/shard_map/ppermute | solution.py:1119
  17.8 1.0 copy-start.7
  17.9 6.5 %collective-permute-start.7 = (bf16[64,1024]{1,0:T(8,128)(2,1)}, bf16[64,1024]{1,0:T(8,128)(2,1)S(1)}, u32[]{:S(2)}, u32[]{:S(2)}) collective-permute-start(bf16[64,1024]{1,0:T(8,128)(2,1)} %get-tuple-element.121.refs_4_), channel_id=1, source_target_pairs={{0,6},{2,4},{4,2},{6,0},{8,14},{10,12},{12,10},{14,8},{16,22},{18,... | collective-permute-start | bytes 393224 | tf_op jit(solution)/shard_map/ppermute | solution.py:1119
  23.9 4.6 %copy-start.4 = (bf16[64,512]{1,0:T(8,128)(2,1)S(1)}, bf16[64,512]{1,0:T(8,128)(2,1)}, u32[]{:S(2)}) copy-start(bf16[64,512]{1,0:T(8,128)(2,1)} %param.45) | copy-start | bytes 196612
  26.8 8.1 %copy-start.23 = (bf16[64,1024]{1,0:T(8,128)(2,1)S(1)}, bf16[64,1024]{1,0:T(8,128)(2,1)}, u32[]{:S(2)}) copy-start(bf16[64,1024]{1,0:T(8,128)(2,1)} %get-tuple-element.121.refs_4_) | copy-start | bytes 393220
  26.8 8.2 %copy-start.27 = (bf16[64,1024]{1,0:T(8,128)(2,1)S(1)}, bf16[64,1024]{1,0:T(8,128)(2,1)}, u32[]{:S(2)}) copy-start(bf16[64,1024]{1,0:T(8,128)(2,1)} %copy-done.26) | copy-start | bytes 393220
  26.8 8.7 %copy-start.29 = (bf16[64,1024]{1,0:T(8,128)(2,1)S(1)}, bf16[64,1024]{1,0:T(8,128)(2,1)}, u32[]{:S(2)}) copy-start(bf16[64,1024]{1,0:T(8,128)(2,1)} %copy-done.28) | copy-start | bytes 393220
  26.8 8.8 %copy-start.25 = (bf16[64,1024]{1,0:T(8,128)(2,1)S(1)}, bf16[64,1024]{1,0:T(8,128)(2,1)}, u32[]{:S(2)}) copy-start(bf16[64,1024]{1,0:T(8,128)(2,1)} %copy-done.24) | copy-start | bytes 393220
  26.8 9.2 %copy-start.3 = (bf16[7,7,992]{2,1,0:T(8,128)(2,1)S(1)}, bf16[7,7,992]{2,1,0:T(8,128)(2,1)}, u32[]{:S(2)}) copy-start(bf16[7,7,992]{2,1,0:T(8,128)(2,1)} %param.31) | copy-start | bytes 291652
  26.8 10.0 %collective-permute-start.15 = (bf16[64,2560]{1,0:T(8,128)(2,1)}, bf16[64,2560]{1,0:T(8,128)(2,1)S(1)}, u32[]{:S(2)}, u32[]{:S(2)}) collective-permute-start(bf16[64,2560]{1,0:T(8,128)(2,1)} %get-tuple-element.124.refs_0_), channel_id=1, source_target_pairs={{0,4},{2,6},{4,0},{6,2},{8,12},{10,14},{12,8},{14,10},{16,20},{18,... | collective-permute-start | bytes 983048 | tf_op jit(solution)/shard_map/ppermute | solution.py:1119
  29.5 33.7 %all-to-all-start = ((bf16[16,64,512]{2,1,0:T(8,128)(2,1)}), bf16[16,64,512]{2,1,0:T(8,128)(2,1)S(1)}, u32[]{:S(2)}, u32[]{:S(2)}) async-start(bf16[16,64,512]{2,1,0:T(8,128)(2,1)} %broadcast_in_dim.2), calls=%async_computation | async-start | bytes 2097152 | tf_op jit(solution)/shard_map/all_to_all | solution.py:1149
  34.9 6.5 %collective-permute-start.8 = (bf16[64,1024]{1,0:T(8,128)(2,1)S(1)}, bf16[64,1024]{1,0:T(8,128)(2,1)S(1)}, u32[]{:S(2)}, u32[]{:S(2)}) collective-permute-start(bf16[64,1024]{1,0:T(8,128)(2,1)S(1)} %copy-done.23), channel_id=1, source_target_pairs={{0,1},{1,0},{2,3},{3,2},{4,5},{5,4},{6,7},{7,6},{8,9},{9,8},{10,11... | collective-permute-start | bytes 393224 | tf_op jit(solution)/shard_map/ppermute | solution.py:1123
  35.0 6.5 %collective-permute-start.10 = (bf16[64,1024]{1,0:T(8,128)(2,1)S(1)}, bf16[64,1024]{1,0:T(8,128)(2,1)S(1)}, u32[]{:S(2)}, u32[]{:S(2)}) collective-permute-start(bf16[64,1024]{1,0:T(8,128)(2,1)S(1)} %copy-done.27), channel_id=1, source_target_pairs={{0,1},{1,0},{2,3},{3,2},{4,5},{5,4},{6,7},{7,6},{8,9},{9,8},{10,11... | collective-permute-start | bytes 393224 | tf_op jit(solution)/shard_map/ppermute | solution.py:1123
  35.5 6.0 %collective-permute-start.11 = (bf16[64,1024]{1,0:T(8,128)(2,1)S(1)}, bf16[64,1024]{1,0:T(8,128)(2,1)S(1)}, u32[]{:S(2)}, u32[]{:S(2)}) collective-permute-start(bf16[64,1024]{1,0:T(8,128)(2,1)S(1)} %copy-done.29), channel_id=1, source_target_pairs={{0,1},{1,0},{2,3},{3,2},{4,5},{5,4},{6,7},{7,6},{8,9},{9,8},{10,11... | collective-permute-start | bytes 393224 | tf_op jit(solution)/shard_map/ppermute | solution.py:1123
  35.6 5.9 %collective-permute-start.9 = (bf16[64,1024]{1,0:T(8,128)(2,1)S(1)}, bf16[64,1024]{1,0:T(8,128)(2,1)S(1)}, u32[]{:S(2)}, u32[]{:S(2)}) collective-permute-start(bf16[64,1024]{1,0:T(8,128)(2,1)S(1)} %copy-done.25), channel_id=1, source_target_pairs={{0,1},{1,0},{2,3},{3,2},{4,5},{5,4},{6,7},{7,6},{8,9},{9,8},{10,11... | collective-permute-start | bytes 393224 | tf_op jit(solution)/shard_map/ppermute | solution.py:1123
  39.6 25.2 %collective-permute-start.16 = (bf16[128,2560]{1,0:T(8,128)(2,1)}, bf16[128,2560]{1,0:T(8,128)(2,1)S(1)}, u32[]{:S(2)}, u32[]{:S(2)}) collective-permute-start(bf16[128,2560]{1,0:T(8,128)(2,1)} %get-tuple-element.131.refs_5_.refs_9_), channel_id=1, source_target_pairs={{0,2},{2,0},{4,6},{6,4},{8,10},{10,8},{12,14},{14,12},{16,18},{18,... | collective-permute-start | bytes 1966088 | tf_op jit(solution)/shard_map/ppermute | solution.py:1119
  42.3 21.0 %copy-start.10 = (bf16[128,2560]{1,0:T(8,128)(2,1)S(1)}, bf16[128,2560]{1,0:T(8,128)(2,1)}, u32[]{:S(2)}) copy-start(bf16[128,2560]{1,0:T(8,128)(2,1)} %get-tuple-element.131.refs_5_.refs_9_) | copy-start | bytes 1966084
  63.2 4.8 %copy-start = (bf16[16,64,512]{2,1,0:T(8,128)(2,1)}, bf16[16,64,512]{2,1,0:T(8,128)(2,1)S(1)}, u32[]{:S(2)}) copy-start(bf16[16,64,512]{2,1,0:T(8,128)(2,1)S(1)} %all-to-all-done) | copy-start | bytes 3145732
  63.2 4.7 %collective-permute-start.19 = (bf16[1024,512]{1,0:T(8,128)(2,1)S(1)}, bf16[1024,512]{1,0:T(8,128)(2,1)S(1)}, u32[]{:S(2)}, u32[]{:S(2)}) collective-permute-start(bf16[1024,512]{1,0:T(8,128)(2,1)S(1)} %bitcast.42), channel_id=1, source_target_pairs={{0,1},{1,0},{2,3},{3,2},{4,5},{5,4},{6,7},{7,6},{8,9},{9,8},{10,11... | collective-permute-start | bytes 3145736 | tf_op jit(solution)/shard_map/ppermute | solution.py:1123
  63.3 3.7 %collective-permute-start.17 = (bf16[128,2560]{1,0:T(8,128)(2,1)S(1)}, bf16[128,2560]{1,0:T(8,128)(2,1)}, u32[]{:S(2)}, u32[]{:S(2)}) collective-permute-start(bf16[128,2560]{1,0:T(8,128)(2,1)S(1)} %copy-done.10), channel_id=1, source_target_pairs={{0,1},{1,0},{2,3},{3,2},{4,5},{5,4},{6,7},{7,6},{8,9},{9,8},{10,11... | collective-permute-start | bytes 1966088 | tf_op jit(solution)/shard_map/ppermute | solution.py:1123
  64.7 3.3 %copy-start.11 = (bf16[128,2560]{1,0:T(8,128)(2,1)}, bf16[128,2560]{1,0:T(8,128)(2,1)S(1)}, u32[]{:S(2)}) copy-start(bf16[128,2560]{1,0:T(8,128)(2,1)S(1)} %collective-permute-done.16.refs_6_.refs_10_) | copy-start | bytes 1966084
  64.7 3.2 %collective-permute-start.18 = (bf16[128,2560]{1,0:T(8,128)(2,1)S(1)}, bf16[128,2560]{1,0:T(8,128)(2,1)}, u32[]{:S(2)}, u32[]{:S(2)}) collective-permute-start(bf16[128,2560]{1,0:T(8,128)(2,1)S(1)} %collective-permute-done.16.refs_6_.refs_10_), channel_id=1, source_target_pairs={{0,1},{1,0},{2,3},{3,2},{4,5},{5,4},{6,7},{7,6},{8,9},{9,8},{10,11... | collective-permute-start | bytes 1966088 | tf_op jit(solution)/shard_map/ppermute | solution.py:1123
  68.0 1.0 copy-start.8
  94.8 11.9 %copy-start.2 = (bf16[1024,1024]{1,0:T(8,128)(2,1)S(1)}, bf16[1024,1024]{1,0:T(8,128)(2,1)}, u32[]{:S(2)}) copy-start(bf16[1024,1024]{1,0:T(8,128)(2,1)} %get-tuple-element.135) | copy-start | bytes 6291460
  106.1 18.9 %collective-permute-start.21 = (bf16[1280,512]{1,0:T(8,128)(2,1)}, bf16[1280,512]{1,0:T(8,128)(2,1)S(1)}, u32[]{:S(2)}, u32[]{:S(2)}) collective-permute-start(bf16[1280,512]{1,0:T(8,128)(2,1)} %get-tuple-element.143), channel_id=1, source_target_pairs={{0,1},{1,0},{2,3},{3,2},{4,5},{5,4},{6,7},{7,6},{8,9},{9,8},{10,11... | collective-permute-start | bytes 3932168 | tf_op jit(solution)/shard_map/ppermute | solution.py:1123
  106.3 18.6 %collective-permute-start.22 = (bf16[256,2048]{1,0:T(8,128)(2,1)}, bf16[256,2048]{1,0:T(8,128)(2,1)}, u32[]{:S(2)}, u32[]{:S(2)}) collective-permute-start(bf16[256,2048]{1,0:T(8,128)(2,1)} %get-tuple-element.145), channel_id=1, source_target_pairs={{0,1},{1,0},{2,3},{3,2},{4,5},{5,4},{6,7},{7,6},{8,9},{9,8},{10,11... | collective-permute-start | bytes 3145736 | tf_op jit(solution)/shard_map/ppermute | solution.py:1123
  106.8 27.3 %collective-permute-start.20 = (bf16[4,64,1024]{2,1,0:T(8,128)(2,1)S(1)}, bf16[4,64,1024]{2,1,0:T(8,128)(2,1)S(1)}, u32[]{:S(2)}, u32[]{:S(2)}) collective-permute-start(bf16[4,64,1024]{2,1,0:T(8,128)(2,1)S(1)} %slice_select_fusion), channel_id=1, source_target_pairs={{0,1},{1,0},{2,3},{3,2},{4,5},{5,4},{6,7},{7,6},{8,9},{9,8},{10,11... | collective-permute-start | bytes 1572872 | tf_op jit(solution)/shard_map/ppermute | solution.py:1123
  123.2 1.7 collective-permute-start.23
  125.0 1.2 copy-start.6
  130.0 21.5 %collective-permute-start.24 = (bf16[640,512]{1,0:T(8,128)(2,1)}, bf16[640,512]{1,0:T(8,128)(2,1)S(1)}, u32[]{:S(2)}, u32[]{:S(2)}) collective-permute-start(bf16[640,512]{1,0:T(8,128)(2,1)} %bitcast.55), channel_id=1, source_target_pairs={{0,4},{2,6},{4,0},{6,2},{8,12},{10,14},{12,8},{14,10},{16,20},{18,... | collective-permute-start | bytes 1966088 | tf_op jit(solution)/shard_map/ppermute | solution.py:1119
  131.5 20.0 %collective-permute-start.25 = (bf16[128,2048]{1,0:T(8,128)(2,1)}, bf16[128,2048]{1,0:T(8,128)(2,1)S(1)}, u32[]{:S(2)}, u32[]{:S(2)}) collective-permute-start(bf16[128,2048]{1,0:T(8,128)(2,1)} %bitcast.57), channel_id=1, source_target_pairs={{0,2},{2,0},{4,6},{6,4},{8,10},{10,8},{12,14},{14,12},{16,18},{18,... | collective-permute-start | bytes 1572872 | tf_op jit(solution)/shard_map/ppermute | solution.py:1119
  132.1 19.4 %collective-permute-start.26 = (bf16[64,512]{1,0:T(8,128)(2,1)}, bf16[64,512]{1,0:T(8,128)(2,1)S(1)}, u32[]{:S(2)}, u32[]{:S(2)}) collective-permute-start(bf16[64,512]{1,0:T(8,128)(2,1)} %bitcast.65), channel_id=1, source_target_pairs={{0,2},{2,0},{4,6},{6,4},{8,10},{10,8},{12,14},{14,12},{16,18},{18,... | collective-permute-start | bytes 196616 | tf_op jit(solution)/shard_map/ppermute | solution.py:1119
  133.5 17.9 %collective-permute-start.27 = (bf16[64,512]{1,0:T(8,128)(2,1)}, bf16[64,512]{1,0:T(8,128)(2,1)S(1)}, u32[]{:S(2)}, u32[]{:S(2)}) collective-permute-start(bf16[64,512]{1,0:T(8,128)(2,1)} %bitcast.64), channel_id=1, source_target_pairs={{0,4},{2,6},{4,0},{6,2},{8,12},{10,14},{12,8},{14,10},{16,20},{18,... | collective-permute-start | bytes 196616 | tf_op jit(solution)/shard_map/ppermute | solution.py:1119
  134.1 1.5 copy-start.14
  134.1 17.4 %collective-permute-start.28 = (bf16[64,512]{1,0:T(8,128)(2,1)}, bf16[64,512]{1,0:T(8,128)(2,1)S(1)}, u32[]{:S(2)}, u32[]{:S(2)}) collective-permute-start(bf16[64,512]{1,0:T(8,128)(2,1)} %bitcast.62), channel_id=1, source_target_pairs={{0,6},{2,4},{4,2},{6,0},{8,14},{10,12},{12,10},{14,8},{16,22},{18,... | collective-permute-start | bytes 196616 | tf_op jit(solution)/shard_map/ppermute | solution.py:1119
  151.5 1.0 copy-start.12
  155.3 10.7 %collective-permute-start.29 = (bf16[320,512]{1,0:T(8,128)(2,1)}, bf16[320,512]{1,0:T(8,128)(2,1)S(1)}, u32[]{:S(2)}, u32[]{:S(2)}) collective-permute-start(bf16[320,512]{1,0:T(8,128)(2,1)} %bitcast.58), channel_id=1, source_target_pairs={{0,2},{2,0},{4,6},{6,4},{8,10},{10,8},{12,14},{14,12},{16,18},{18,... | collective-permute-start | bytes 983048 | tf_op jit(solution)/shard_map/ppermute | solution.py:1119
  156.8 9.1 %collective-permute-start.30 = (bf16[64,2048]{1,0:T(8,128)(2,1)}, bf16[64,2048]{1,0:T(8,128)(2,1)S(1)}, u32[]{:S(2)}, u32[]{:S(2)}) collective-permute-start(bf16[64,2048]{1,0:T(8,128)(2,1)} %bitcast.59), channel_id=1, source_target_pairs={{0,4},{2,6},{4,0},{6,2},{8,12},{10,14},{12,8},{14,10},{16,20},{18,... | collective-permute-start | bytes 786440 | tf_op jit(solution)/shard_map/ppermute | solution.py:1119
  157.3 12.0 %collective-permute-start.31 = (bf16[16,512]{1,0:T(8,128)(2,1)}, bf16[16,512]{1,0:T(8,128)(2,1)S(1)}, u32[]{:S(2)}, u32[]{:S(2)}) collective-permute-start(bf16[16,512]{1,0:T(8,128)(2,1)} %bitcast.75), channel_id=1, source_target_pairs={{0,8},{2,10},{4,12},{6,14},{8,0},{10,2},{12,4},{14,6},{16,24},{18,... | collective-permute-start | bytes 49160 | tf_op jit(solution)/shard_map/ppermute | solution.py:1119
  158.8 13.8 %collective-permute-start.32 = (bf16[16,512]{1,0:T(8,128)(2,1)}, bf16[16,512]{1,0:T(8,128)(2,1)S(1)}, u32[]{:S(2)}, u32[]{:S(2)}) collective-permute-start(bf16[16,512]{1,0:T(8,128)(2,1)} %bitcast.74), channel_id=1, source_target_pairs={{0,16},{2,18},{4,20},{6,22},{8,24},{10,26},{12,28},{14,30},{16,0},... | collective-permute-start | bytes 49160 | tf_op jit(solution)/shard_map/ppermute | solution.py:1119
  161.2 12.0 %collective-permute-start.33 = (bf16[16,512]{1,0:T(8,128)(2,1)}, bf16[16,512]{1,0:T(8,128)(2,1)S(1)}, u32[]{:S(2)}, u32[]{:S(2)}) collective-permute-start(bf16[16,512]{1,0:T(8,128)(2,1)} %bitcast.73), channel_id=1, source_target_pairs={{0,24},{2,26},{4,28},{6,30},{8,16},{10,18},{12,20},{14,22},{16,8},... | collective-permute-start | bytes 49160 | tf_op jit(solution)/shard_map/ppermute | solution.py:1119
  165.9 17.9 %collective-permute-start.34 = (bf16[256,1024]{1,0:T(8,128)(2,1)}, bf16[256,1024]{1,0:T(8,128)(2,1)S(1)}, u32[]{:S(2)}, u32[]{:S(2)}) collective-permute-start(bf16[256,1024]{1,0:T(8,128)(2,1)} %get-tuple-element.182), channel_id=1, source_target_pairs={{0,1},{1,0},{2,3},{3,2},{4,5},{5,4},{6,7},{7,6},{8,9},{9,8},{10,11... | collective-permute-start | bytes 1572872 | tf_op jit(solution)/shard_map/ppermute | solution.py:1123
  168.8 12.8 %collective-permute-start.36 = (bf16[144,512]{1,0:T(8,128)(2,1)}, bf16[144,512]{1,0:T(8,128)(2,1)S(1)}, u32[]{:S(2)}, u32[]{:S(2)}) collective-permute-start(bf16[144,512]{1,0:T(8,128)(2,1)} %get-tuple-element.186), channel_id=1, source_target_pairs={{0,8},{2,10},{4,12},{6,14},{8,0},{10,2},{12,4},{14,6},{16,24},{18,... | collective-permute-start | bytes 442376 | tf_op jit(solution)/shard_map/ppermute | solution.py:1119
  169.4 3.8 %copy-start.44 = (bf16[16,512]{1,0:T(8,128)(2,1)}, bf16[16,512]{1,0:T(8,128)(2,1)S(1)}, u32[]{:S(2)}) copy-start(bf16[16,512]{1,0:T(8,128)(2,1)S(1)} %collective-permute-done.31.refs_14_.refs_5_) | copy-start | bytes 49156
  169.4 14.5 %collective-permute-start.37 = (bf16[144,512]{1,0:T(8,128)(2,1)}, bf16[144,512]{1,0:T(8,128)(2,1)S(1)}, u32[]{:S(2)}, u32[]{:S(2)}) collective-permute-start(bf16[144,512]{1,0:T(8,128)(2,1)} %get-tuple-element.187), channel_id=1, source_target_pairs={{0,16},{2,18},{4,20},{6,22},{8,24},{10,26},{12,28},{14,30},{16,0},... | collective-permute-start | bytes 442376 | tf_op jit(solution)/shard_map/ppermute | solution.py:1119
  172.6 11.2 %collective-permute-start.38 = (bf16[144,512]{1,0:T(8,128)(2,1)}, bf16[144,512]{1,0:T(8,128)(2,1)S(1)}, u32[]{:S(2)}, u32[]{:S(2)}) collective-permute-start(bf16[144,512]{1,0:T(8,128)(2,1)} %get-tuple-element.188), channel_id=1, source_target_pairs={{0,24},{2,26},{4,28},{6,30},{8,16},{10,18},{12,20},{14,22},{16,8},... | collective-permute-start | bytes 442376 | tf_op jit(solution)/shard_map/ppermute | solution.py:1119
  180.2 1.4 collective-permute-start.35
  181.6 2.3 %copy-start.47 = (f32[8,512]{1,0:T(8,128)}, f32[8,512]{1,0:T(8,128)S(1)}, u32[]{:S(2)}) copy-start(f32[8,512]{1,0:T(8,128)S(1)} %collective-permute-done.35.refs_3_) | copy-start | bytes 49156
  181.6 2.3 %copy-start.20 = (bf16[144,512]{1,0:T(8,128)(2,1)}, bf16[144,512]{1,0:T(8,128)(2,1)S(1)}, u32[]{:S(2)}) copy-start(bf16[144,512]{1,0:T(8,128)(2,1)S(1)} %collective-permute-done.36.refs_9_.refs_1_) | copy-start | bytes 442372
  216.1 2.4 %copy-start.1 = (bf16[16,16,1664]{2,1,0:T(8,128)(2,1)}, bf16[16,16,1664]{2,1,0:T(8,128)(2,1)S(1)}, u32[]{:S(2)}) copy-start(bf16[16,16,1664]{2,1,0:T(8,128)(2,1)S(1)} %all_to_all.19) | copy-start | bytes 2555908
  216.1 2.4 %collective-permute-start.39 = (bf16[256,1664]{1,0:T(8,128)(2,1)S(1)}, bf16[256,1664]{1,0:T(8,128)(2,1)S(1)}, u32[]{:S(2)}, u32[]{:S(2)}) collective-permute-start(bf16[256,1664]{1,0:T(8,128)(2,1)S(1)} %bitcast.44), channel_id=1, source_target_pairs={{0,1},{1,0},{2,3},{3,2},{4,5},{5,4},{6,7},{7,6},{8,9},{9,8},{10,11... | collective-permute-start | bytes 2555912 | tf_op jit(solution)/shard_map/ppermute | solution.py:1123
  (25 other events, 17.3 us)
